TPU v7x, 256 devices: a whole 4x4x8 slice. The times are simulated.
256 devices in a mesh: samp: 4 (over y), blk: 64 (over z, x, core).
Axes of the slice: x: 4, y: 4, z: 8, core: 2. Of those that a mesh axis runs over, the one named last changes fastest.
Arguments:
- perturb: bfloat16 [8192, 65536], P('samp', 'blk'), may hold values from -400 to 400
- partner: int32 [256, 8], P('blk'), may hold values from 0 to 255, as said below
- bins: int32 [256, 8], P('blk'), may hold values from 0 to 31
Outputs:
- localized_corr: float32 [256, 2048, 256], P('samp', 'blk')
Inputs may be any that keep to these rules, and one draw needn't show every extreme that they name: The partners of one row block are distinct; they include every block of the row block's own device (itself too); every partner lies on a device at most 2 indices away along the cyclic order of blk; the partners of all row blocks of one device take exactly 2 distinct blocks from each of the 4 devices nearest to it.
All inputs are finite; a program needn't handle non-finite values.
Results may differ from a plain program's by a relative error of at most 0.0003.
Values may be sent and summed in bfloat16 or wider, within the bound.
No kernel may reach another device: no remote copies, remote signals or barrier semaphores. Data moves between devices by JAX's collectives and lax.ppermute only.
A program may use at most 192 MiB of HBM per device.

v0:
```python
import jax
import jax.numpy as jnp
from jax import lax
from jax.sharding import PartitionSpec as P

BS = 256
B_DEV = 4
K_PART = 8
REACH = 2
NBIN = 32
PAIR_DEV = 32


EPSILON = 1e-06


def passed_along(value, axis, steps):
    count = lax.axis_size(axis)
    pairs = [(source, (source + steps) % count) for source in range(count)]
    return lax.ppermute(value, axis, pairs)


def taper_table():
    scaled = 2.0 * (jnp.arange(NBIN, dtype=jnp.float32) + 0.5) / NBIN
    inner = (((-0.25 * scaled + 0.5) * scaled + 0.625) * scaled - 5.0 / 3.0) * scaled * scaled + 1.0
    outer = (
        ((((scaled / 12.0 - 0.5) * scaled + 0.625) * scaled + 5.0 / 3.0) * scaled - 5.0) * scaled
        + 4.0
        - 2.0 / (3.0 * scaled)
    )
    return jnp.where(scaled <= 1.0, inner, outer)


def body(perturb, partner, bins):
    blk_count = lax.axis_size("blk")
    samp_count = lax.axis_size("samp")
    blk_here = lax.axis_index("blk")
    own_blocks = perturb.reshape(perturb.shape[0], B_DEV, BS)
    owner_dev = partner // B_DEV
    in_owner = partner % B_DEV
    offset = (owner_dev - blk_here + blk_count + REACH) % blk_count - REACH
    neighbours = [shift_by for shift_by in range(-REACH, REACH + 1) if shift_by != 0]
    slab_list = []
    for position, shift_by in enumerate(neighbours):
        incoming = passed_along(own_blocks, "blk", -shift_by)
        slab_list.append(incoming)
    column_table = jnp.concatenate(slab_list[:REACH] + [own_blocks] + slab_list[REACH:], axis=1)
    slot_index = (offset + REACH) * B_DEV + in_owner
    own_start = REACH * B_DEV
    norm_table = lax.psum(jnp.sum(jnp.square(column_table.astype(jnp.float32)), axis=0), "samp")
    tile_rows = BS // samp_count
    row_norm = norm_table[own_start : own_start + B_DEV]
    row_part = lax.dynamic_slice_in_dim(row_norm, lax.axis_index("samp") * tile_rows, tile_rows, 1)
    row_scale = jnp.transpose(lax.rsqrt(row_part + EPSILON))
    col_norm = jnp.take(norm_table, slot_index.reshape(-1), axis=0).reshape(B_DEV, K_PART, BS)
    bin_match = bins[:, :, None] == jnp.arange(NBIN, dtype=jnp.int32)[None, None, :]
    tapers = jnp.sum(jnp.where(bin_match, taper_table()[None, None, :], 0.0), axis=2)
    col_scale = tapers[:, :, None] * lax.rsqrt(col_norm + EPSILON)
    pieces = []
    for row_index in range(B_DEV):
        row_slab = own_blocks[:, row_index, :]
        col_slabs = jnp.take(column_table, slot_index[row_index], axis=1)
        pieces.append(
            jnp.einsum("sa,skc->akc", row_slab, col_slabs, preferred_element_type=jnp.float32)
        )
    gram_rows = lax.psum_scatter(
        jnp.stack(pieces, axis=1).reshape(tile_rows * lax.axis_size("samp"), PAIR_DEV, BS),
        "samp",
        scatter_dimension=0,
        tiled=True,
    )
    localized = (
        gram_rows.reshape(tile_rows, B_DEV, K_PART, BS)
        * row_scale[:, :, None, None]
        * col_scale[None]
    )
    return localized.reshape(tile_rows, PAIR_DEV, BS)


def solution(mesh):
    return jax.shard_map(
        body,
        mesh=mesh,
        in_specs=(P("samp", "blk"), P("blk", None), P("blk", None)),
        out_specs=P("samp", "blk", None),
        check_vma=False,
    )
```

profile of v0, /device:TPU:8, one launch (start us, length us, event | category | flops | bytes accessed | tf_op | source)
XLA Modules:
  0.0 341.7 jit_solution(13781453373249129495)
XLA Ops:
  6.5 6.5 %copy.17 = bf16[2048,1024]{0,1:T(8,128)(2,1)} copy(bf16[2048,1024]{1,0:T(8,128)(2,1)} %param.5) | data formatting | bytes 8388608 | tf_op args[0]
  13.1 1.5 collective-permute-start
  14.6 6.1 %collective-permute-start.2 = (bf16[2048,4,256]{0,2,1:T(8,128)(2,1)}, bf16[2048,4,256]{0,2,1:T(8,128)(2,1)}, u32[]{:S(2)}, u32[]{:S(2)}) collective-permute-start(bf16[2048,4,256]{0,2,1:T(8,128)(2,1)} %bitcast.79), channel_id=1, source_target_pairs={{0,63},{1,0},{2,1},{3,2},{4,3},{5,4},{6,5},{7,6},{8,7},{9,8},{10,9... | collective-permute-start | bytes 12582920 | tf_op jit(solution)/shard_map/ppermute | solution.py:20
  20.6 2.3 collective-permute-start.3
  23.0 89.8 %collective-permute-done = bf16[2048,4,256]{0,2,1:T(8,128)(2,1)} collective-permute-done((bf16[2048,4,256]{0,2,1:T(8,128)(2,1)}, bf16[2048,4,256]{0,2,1:T(8,128)(2,1)}, u32[]{:S(2)}, u32[]{:S(2)}) %collective-permute-start) | collective-permute-done | bytes 4194336 | tf_op jit(solution)/shard_map/ppermute | solution.py:20
  112.8 4.7 %constant_dynamic-update-slice_fusion.4 = bf16[2048,20,256]{0,2,1:T(8,128)(2,1)} fusion(bf16[2048,4,256]{0,2,1:T(8,128)(2,1)} %collective-permute-done), kind=kLoop, calls=%fused_computation.43 | loop fusion | bytes 8388608
  117.6 39.4 %collective-permute-done.1 = bf16[2048,4,256]{0,2,1:T(8,128)(2,1)} collective-permute-done((bf16[2048,4,256]{0,2,1:T(8,128)(2,1)}, bf16[2048,4,256]{0,2,1:T(8,128)(2,1)}, u32[]{:S(2)}, u32[]{:S(2)}) %collective-permute-start.1) | collective-permute-done | bytes 4194336 | tf_op jit(solution)/shard_map/ppermute | solution.py:20
  157.0 4.7 %constant_dynamic-update-slice_fusion.3 = bf16[2048,20,256]{0,2,1:T(8,128)(2,1)} fusion(bf16[2048,20,256]{0,2,1:T(8,128)(2,1)} %constant_dynamic-update-slice_fusion.4, bf16[2048,4,256]{0,2,1:T(8,128)(2,1)} %collective-permute-done.1), kind=kLoop, calls=%fused_computation.42 | loop fusion | bytes 8388608
  161.7 2.3 constant_dynamic-update-slice_fusion.2
  164.0 4.7 %constant_dynamic-update-slice_fusion.1 = bf16[2048,20,256]{0,2,1:T(8,128)(2,1)} fusion(bf16[2048,20,256]{0,2,1:T(8,128)(2,1)} %constant_dynamic-update-slice_fusion.2, bf16[2048,4,256]{0,2,1:T(8,128)(2,1)} %collective-permute-done.2), kind=kLoop, calls=%fused_computation.40 | loop fusion | bytes 8388608
  168.7 4.7 %constant_dynamic-update-slice_fusion = bf16[2048,20,256]{0,2,1:T(8,128)(2,1)} fusion(bf16[2048,20,256]{0,2,1:T(8,128)(2,1)} %constant_dynamic-update-slice_fusion.1, bf16[2048,4,256]{0,2,1:T(8,128)(2,1)} %collective-permute-done.3), kind=kLoop, calls=%fused_computation.39 | loop fusion | bytes 8388608 | tf_op jit(solution)/shard_map/concatenate | solution.py:47
  173.4 11.9 %gather_fusion.1 = bf16[8,2048,256]{1,2,0:T(8,128)(2,1)} fusion(bf16[2048,20,256]{0,2,1:T(8,128)(2,1)} %constant_dynamic-update-slice_fusion, s32[1024]{0:T(1024)S(1)} %get-tuple-element.25), kind=kCustom, calls=%fused_computation.clone | custom fusion | bytes 16777248 | tf_op jit(solution)/shard_map/jit(_take)/gather | solution.py:62
  185.3 11.6 %gather_fusion.2 = bf16[8,2048,256]{1,2,0:T(8,128)(2,1)} fusion(bf16[2048,20,256]{0,2,1:T(8,128)(2,1)} %constant_dynamic-update-slice_fusion, s32[1024]{0:T(1024)S(1)} %get-tuple-element.24), kind=kCustom, calls=%fused_computation.1.clone | custom fusion | bytes 16777248 | tf_op jit(solution)/shard_map/jit(_take)/gather | solution.py:62
  196.9 11.8 %gather_fusion.3 = bf16[8,2048,256]{1,2,0:T(8,128)(2,1)} fusion(bf16[2048,20,256]{0,2,1:T(8,128)(2,1)} %constant_dynamic-update-slice_fusion, s32[1024]{0:T(1024)S(1)} %get-tuple-element.23), kind=kCustom, calls=%fused_computation.2.clone | custom fusion | bytes 16777248 | tf_op jit(solution)/shard_map/jit(_take)/gather | solution.py:62
  208.7 11.7 %gather_fusion.4 = bf16[8,2048,256]{1,2,0:T(8,128)(2,1)} fusion(bf16[2048,20,256]{0,2,1:T(8,128)(2,1)} %constant_dynamic-update-slice_fusion, s32[1024]{0:T(1024)S(1)} %get-tuple-element.22), kind=kCustom, calls=%fused_computation.3.clone | custom fusion | bytes 16777248 | tf_op jit(solution)/shard_map/jit(_take)/gather | solution.py:62
  220.4 6.3 %fusion.20 = f32[256,1,8,256]{0,3,2,1:T(8,128)S(1)} fusion(bf16[8,2048,256]{1,2,0:T(8,128)(2,1)} %gather_fusion.1, pred[8]{0:T(512)(128)(4,1)S(1)} %get-tuple-element.8, bf16[2048,4,256]{0,2,1:T(8,128)(2,1)} %bitcast.81), kind=kOutput, calls=%fused_computation.28 | convolution fusion | flops 2151677952 | bytes 11534344 | tf_op jit(solution)/shard_map/sa,skc->akc/dot_general | solution.py:64
  226.7 6.1 %fusion.23 = f32[256,1,8,256]{0,3,2,1:T(8,128)S(1)} fusion(bf16[8,2048,256]{1,2,0:T(8,128)(2,1)} %gather_fusion.2, pred[8]{0:T(512)(128)(4,1)S(1)} %get-tuple-element.20, bf16[2048,4,256]{0,2,1:T(8,128)(2,1)S(1)} %bitcast.83), kind=kOutput, calls=%fused_computation.29 | convolution fusion | flops 2151677952 | bytes 11534848 | tf_op jit(solution)/shard_map/sa,skc->akc/dot_general | solution.py:64
  232.8 2.5 fusion.26
  235.3 2.5 fusion.29
  237.8 3.7 %pad_maximum_fusion = f32[256,4,8,256]{0,3,2,1:T(8,128)} fusion(f32[256,1,8,256]{0,3,2,1:T(8,128)S(1)} %fusion.29, f32[256,1,8,256]{0,3,2,1:T(8,128)S(1)} %fusion.26, f32[256,1,8,256]{0,3,2,1:T(8,128)S(1)} %fusion.23, f32[256,1,8,256]{0,3,2,1:T(8,128)S(1)} %fusion.20), kind=kLoop, calls=%fused_computation.6 | loop fusion | flops 6291456 | bytes 16777216 | tf_op jit(solution)/shard_map/stack | solution.py:67
  241.5 10.3 %copy.22 = f32[256,32,256]{2,1,0:T(8,128)} copy(f32[256,32,256]{0,2,1:T(8,128)} %bitcast.76) | data formatting | bytes 16777216 | tf_op jit(solution)/shard_map/reshape | solution.py:67
  251.8 0.1 reshape.103
  251.9 0.1 broadcast_in_dim.41
  252.0 0.5 copy-done.3
  252.5 0.2 select_reduce_fusion
  252.6 0.1 mul.138
  252.7 8.9 %multiply_reduce_fusion = f32[20,256]{1,0:T(8,128)S(1)} fusion(bf16[2048,20,256]{0,2,1:T(8,128)(2,1)} %constant_dynamic-update-slice_fusion), kind=kLoop, calls=%fused_computation.5 | loop fusion | flops 31452160 | bytes 20992000 | tf_op jit(solution)/shard_map/reduce_sum | solution.py:50
  261.6 15.1 %psum.7 = f32[20,256]{1,0:T(8,128)S(1)} all-reduce(f32[20,256]{1,0:T(8,128)S(1)} %multiply_reduce_fusion), channel_id=1, replica_groups=mesh['samp'=4,'blk'=64] {'samp'}, use_global_device_ids=true, to_apply=%region_2.4 | all-reduce | flops 5120 | bytes 40960 | tf_op jit(solution)/shard_map/psum | solution.py:50
  276.8 0.1 copy.23
  276.9 0.6 gather_fusion
  277.6 53.9 %reduce-scatter.2.cloned.1.call-done = f32[64,32,256]{2,1,0:T(8,128)} async-done(((f32[256,32,256]{2,1,0:T(8,128)}), f32[64,32,256]{2,1,0:T(8,128)}) %reduce-scatter.2.cloned.1.call-update) | async-done | bytes 2097168 | tf_op jit(solution)/shard_map/reduce_scatter | solution.py:66
  331.6 3.3 multiply_multiply_fusion
  (33 shorter events, 0.3 us)
Async XLA Ops:
  6.5 16.4 %copy-start.2 = (s32[4,8]{1,0:T(4,128)S(1)}, s32[4,8]{1,0:T(4,128)}, u32[]{:S(2)}) copy-start(s32[4,8]{1,0:T(4,128)} %param.6) | copy-start | bytes 388
  6.5 325.0 %reduce-scatter.2.cloned.1.call-start = ((), (), s32[]{:S(2)}) async-start(), calls=%async_computation.1 | async-start | bytes 10485760 | tf_op jit(solution)/shard_map/reduce_scatter | solution.py:66
  13.1 99.8 %collective-permute-start = (bf16[2048,4,256]{0,2,1:T(8,128)(2,1)}, bf16[2048,4,256]{0,2,1:T(8,128)(2,1)}, u32[]{:S(2)}, u32[]{:S(2)}) collective-permute-start(bf16[2048,4,256]{0,2,1:T(8,128)(2,1)} %bitcast.77), channel_id=1, source_target_pairs={{0,2},{1,3},{2,4},{3,5},{4,6},{5,7},{6,8},{7,9},{8,10},{9,11},{10,... | collective-permute-start | bytes 12582920 | tf_op jit(solution)/shard_map/ppermute | solution.py:20
  14.6 142.4 %collective-permute-start.1 = (bf16[2048,4,256]{0,2,1:T(8,128)(2,1)}, bf16[2048,4,256]{0,2,1:T(8,128)(2,1)}, u32[]{:S(2)}, u32[]{:S(2)}) collective-permute-start(bf16[2048,4,256]{0,2,1:T(8,128)(2,1)} %bitcast.78), channel_id=1, source_target_pairs={{0,1},{1,2},{2,3},{3,4},{4,5},{5,6},{6,7},{7,8},{8,9},{9,10},{10,1... | collective-permute-start | bytes 12582920 | tf_op jit(solution)/shard_map/ppermute | solution.py:20
  14.6 149.4 %collective-permute-start.2 = (bf16[2048,4,256]{0,2,1:T(8,128)(2,1)}, bf16[2048,4,256]{0,2,1:T(8,128)(2,1)}, u32[]{:S(2)}, u32[]{:S(2)}) collective-permute-start(bf16[2048,4,256]{0,2,1:T(8,128)(2,1)} %bitcast.79), channel_id=1, source_target_pairs={{0,63},{1,0},{2,1},{3,2},{4,3},{5,4},{6,5},{7,6},{8,7},{9,8},{10,9... | collective-permute-start | bytes 12582920 | tf_op jit(solution)/shard_map/ppermute | solution.py:20
  20.6 148.0 %collective-permute-start.3 = (bf16[2048,4,256]{0,2,1:T(8,128)(2,1)}, bf16[2048,4,256]{0,2,1:T(8,128)(2,1)}, u32[]{:S(2)}, u32[]{:S(2)}) collective-permute-start(bf16[2048,4,256]{0,2,1:T(8,128)(2,1)} %bitcast.80), channel_id=1, source_target_pairs={{0,62},{1,63},{2,0},{3,1},{4,2},{5,3},{6,4},{7,5},{8,6},{9,7},{10,... | collective-permute-start | bytes 12582920 | tf_op jit(solution)/shard_map/ppermute | solution.py:20
  23.0 138.7 %copy-start = (bf16[2048,1024]{0,1:T(8,128)(2,1)S(1)}, bf16[2048,1024]{0,1:T(8,128)(2,1)}, u32[]{:S(2)}) copy-start(bf16[2048,1024]{0,1:T(8,128)(2,1)} %copy.17) | copy-start | bytes 12582916
  220.4 6.3 %copy-start.1 = (bf16[2048,1024]{0,1:T(8,128)(2,1)S(1)}, bf16[2048,1024]{0,1:T(8,128)(2,1)}, u32[]{:S(2)}) copy-start(bf16[2048,1024]{0,1:T(8,128)(2,1)} %copy.17) | copy-start | bytes 12582916
  220.4 12.4 %slice-start.2 = ((s8[8388608]{0:T(1024)(128)(4,1)}), s8[4194304]{0:T(1024)(128)(4,1)S(1)}, s32[]{:S(2)}) async-start(s8[8388608]{0:T(1024)(128)(4,1)} %bitcast.88), calls=%async_computation.4 | async-start | bytes 8388608
  226.6 6.1 %slice-start.3 = ((s8[8388608]{0:T(1024)(128)(4,1)}), s8[4194304]{0:T(1024)(128)(4,1)S(1)}, s32[]{:S(2)}) async-start(s8[8388608]{0:T(1024)(128)(4,1)} %bitcast.88), calls=%async_computation.5 | async-start | bytes 8388608
  226.7 8.6 %slice-start = ((s8[8388608]{0:T(1024)(128)(4,1)}), s8[4194304]{0:T(1024)(128)(4,1)S(1)}, s32[]{:S(2)}) async-start(s8[8388608]{0:T(1024)(128)(4,1)} %bitcast.86), calls=%async_computation.2 | async-start | bytes 8388608
  232.8 2.5 slice-start.1
  251.8 0.7 copy-start.3
Sparse Core Ops, SparseCore 0:
  251.9 79.6 reduce-scatter.1
where the time goes:
time: 345 us; the launch traced here: 342 us
  waiting for transfers between devices  183 us (53%)
  local copies, waits for them, and re-layouts  86.4 us (25%)
  matrix products  17.3 us (5%)
  other arithmetic  16.3 us (5%)
  blocking collectives  15.1 us (4%)
  between operations  13.6 us (4%)
  starting transfers between devices  9.83 us (3%)
    ppermute x4, waiting for transfers between devices, passed_along(): return lax.ppermute(value, axis, pairs)  129 us
    reduce_scatter x1, waiting for transfers between devices, body(): lax.psum_scatter(jnp.stack(pieces, axis=1).reshape(tile_rows * lax.axis_s...  53.9 us
    gather x4, local copies, waits for them, and re-layouts, body(): col_slabs = jnp.take(column_table, slot_index[row_index], axis=1)  47 us
    unnamed x21, local copies, waits for them, and re-layouts  23.5 us
    dot_general x4, matrix products, body(): jnp.einsum('sa,skc->akc', row_slab, col_slabs, preferred_element_type=jnp...  17.3 us
    psum x1, blocking collectives, body(): lax.psum(jnp.sum(jnp.square(column_table.astype(jnp.float32)), axis=0), '...  15.1 us
    reshape x1, local copies, waits for them, and re-layouts, body(): jnp.stack(pieces, axis=1)  10.3 us
    ppermute x4, starting transfers between devices, passed_along(): return lax.ppermute(value, axis, pairs)  9.83 us
  transfers between devices with their start and end apart: 5, of which 3 were waited for; matrix products, arithmetic and copies ran while one was open for 8% of the time, Pallas kernels for 0%

commit v1 on v0

v1 whole, which is shorter than its diff:
```python
import functools

import jax
import jax.numpy as jnp
from jax import lax
from jax.experimental import pallas as pl
from jax.experimental.pallas import tpu as pltpu
from jax.sharding import PartitionSpec as P

BS = 256
B_DEV = 4
K_PART = 8
REACH = 2
NBIN = 32
PAIR_DEV = 32
SHIFTS = (-2, -1, 1, 2)
HALF = 128
STAGES = 2

EPSILON = 1e-06
MIB = 1 << 20


def passed_along(value, axis, steps):
    count = lax.axis_size(axis)
    pairs = [(source, (source + steps) % count) for source in range(count)]
    return lax.ppermute(value, axis, pairs)


def taper_table():
    scaled = 2.0 * (jnp.arange(NBIN, dtype=jnp.float32) + 0.5) / NBIN
    inner = (((-0.25 * scaled + 0.5) * scaled + 0.625) * scaled - 5.0 / 3.0) * scaled * scaled + 1.0
    outer = (
        ((((scaled / 12.0 - 0.5) * scaled + 0.625) * scaled + 5.0 / 3.0) * scaled - 5.0) * scaled
        + 4.0
        - 2.0 / (3.0 * scaled)
    )
    return jnp.where(scaled <= 1.0, inner, outer)


def select_kernel(want_ref, source_ref, *refs):
    outs, sems = refs[:-1], refs[-1]
    copies = []
    for stage in range(STAGES):
        for q in range(4):
            for side in range(2):
                start = pl.multiple_of(want_ref[q * 2 + side] * BS + stage * HALF, HALF)
                copies.append(
                    pltpu.make_async_copy(
                        source_ref.at[:, pl.ds(start, HALF)],
                        outs[stage * 4 + q].at[:, pl.ds(side * HALF, HALF)],
                        sems.at[len(copies)],
                    )
                )
    for copy in copies:
        copy.start()
    for copy in copies:
        copy.wait()


def select(want, perturb):
    samples = perturb.shape[0]
    count = STAGES * 4
    return pl.pallas_call(
        select_kernel,
        grid_spec=pltpu.PrefetchScalarGridSpec(
            num_scalar_prefetch=1,
            grid=(),
            in_specs=[pl.BlockSpec(memory_space=pl.ANY)],
            out_specs=[pl.BlockSpec(memory_space=pl.ANY)] * count,
            scratch_shapes=[pltpu.SemaphoreType.DMA((count * 2,))],
        ),
        out_shape=[jax.ShapeDtypeStruct((samples, 2 * HALF), perturb.dtype)] * count,
        cost_estimate=pl.CostEstimate(flops=0, bytes_accessed=16 * MIB, transcendentals=0),
    )(want, perturb)


def own_kernel(x_ref, at_ref, part_ref, norm_ref):
    samp = part_ref.shape[0]
    rows = BS // samp
    for r in range(B_DEV):
        at = jnp.transpose(x_ref[:, r * BS : (r + 1) * BS])
        at_ref[r * BS : (r + 1) * BS, :] = at

    @pl.loop(0, B_DEV)
    def _(r):
        at = at_ref[pl.ds(pl.multiple_of(r * BS, BS), BS), :]
        for c in range(B_DEV):
            tile = jnp.dot(at, x_ref[:, c * BS : (c + 1) * BS], preferred_element_type=jnp.float32)
            for y in range(samp):
                part_ref[y, r * B_DEV + c] = tile[y * rows : (y + 1) * rows]

            @pl.when(r == c)
            def _():
                here = lax.broadcasted_iota(jnp.int32, (BS, BS), 0) == lax.broadcasted_iota(jnp.int32, (BS, BS), 1)
                norm_ref[c : c + 1, :] = jnp.sum(jnp.where(here, tile, 0.0), axis=0, keepdims=True)


def own_tiles(perturb, samp):
    samples, cells = perturb.shape
    return pl.pallas_call(
        own_kernel,
        out_shape=[
            jax.ShapeDtypeStruct((cells, samples), perturb.dtype),
            jax.ShapeDtypeStruct((samp, 16, BS // samp, BS), jnp.float32),
            jax.ShapeDtypeStruct((B_DEV, BS), jnp.float32),
        ],
        compiler_params=pltpu.CompilerParams(vmem_limit_bytes=40 * MIB),
        cost_estimate=pl.CostEstimate(flops=2 * cells * cells * samples, bytes_accessed=12 * MIB, transcendentals=0),
    )(perturb)


def remote_kernel(slot_ref, at_ref, *refs):
    blocks, part_ref, all_ref = refs[:4], refs[4], refs[5]
    samp = part_ref.shape[0]
    rows = BS // samp
    for r in range(B_DEV):
        at = at_ref[r * BS : (r + 1) * BS, :]
        for q in range(4):
            tile = jnp.dot(at, blocks[q][...], preferred_element_type=jnp.float32)
            all_ref[2 * q] = tile[:, :HALF]
            all_ref[2 * q + 1] = tile[:, HALF:]
        for j in range(4):
            chosen = all_ref[slot_ref[r * 4 + j]]
            for y in range(samp):
                part_ref[y, r * 4 + j] = chosen[y * rows : (y + 1) * rows]


def remote_tiles(slots, at, blocks, samp):
    cells, samples = at.shape
    full = lambda shape: pl.BlockSpec(shape, lambda i, s: (0,) * len(shape))
    shape = (samp, 16, BS // samp, HALF)
    return pl.pallas_call(
        remote_kernel,
        grid_spec=pltpu.PrefetchScalarGridSpec(
            num_scalar_prefetch=1,
            grid=(1,),
            in_specs=[full(at.shape)] + [full(blocks[0].shape)] * 4,
            out_specs=full(shape),
            scratch_shapes=[pltpu.VMEM((8, BS, HALF), jnp.float32)],
        ),
        out_shape=jax.ShapeDtypeStruct(shape, jnp.float32),
        compiler_params=pltpu.CompilerParams(vmem_limit_bytes=40 * MIB),
        cost_estimate=pl.CostEstimate(flops=2 * cells * cells * samples, bytes_accessed=10 * MIB, transcendentals=0),
    )(slots, at, *blocks)


def final_kernel(source_ref, column_ref, taper_ref, own_ref, rem0_ref, rem1_ref, row_ref, norm_ref, out_ref):
    for r in range(B_DEV):
        row_scale = row_ref[:, r : r + 1]
        for k in range(K_PART):
            p = r * K_PART + k
            source = source_ref[p]
            col_scale = taper_ref[p] * lax.rsqrt(norm_ref[pl.ds(column_ref[p], 1), :] + EPSILON)
            for h, rem_ref in enumerate((rem0_ref, rem1_ref)):
                cols = slice(h * HALF, (h + 1) * HALF)

                @pl.when(source < 16)
                def _():
                    out_ref[:, p, cols] = own_ref[source, :, cols] * row_scale * col_scale[:, cols]

                @pl.when(source >= 16)
                def _():
                    out_ref[:, p, cols] = rem_ref[source - 16] * row_scale * col_scale[:, cols]


def final(source, column, tapers, own, rems, row_scale, norms):
    rows = own.shape[1]
    full = lambda shape: pl.BlockSpec(shape, lambda i, *s: (0,) * len(shape))
    return pl.pallas_call(
        final_kernel,
        grid_spec=pltpu.PrefetchScalarGridSpec(
            num_scalar_prefetch=3,
            grid=(1,),
            in_specs=[full(own.shape), full(rems[0].shape), full(rems[1].shape), full(row_scale.shape), full(norms.shape)],
            out_specs=full((rows, PAIR_DEV, BS)),
        ),
        out_shape=jax.ShapeDtypeStruct((rows, PAIR_DEV, BS), jnp.float32),
        cost_estimate=pl.CostEstimate(flops=MIB, bytes_accessed=4 * MIB, transcendentals=0),
    )(source, column, tapers, own, *rems, row_scale, norms)


def body(perturb, partner, bins):
    blk_count = lax.axis_size("blk")
    samp = lax.axis_size("samp")
    here = lax.axis_index("blk")
    owner = partner // B_DEV
    inside = partner % B_DEV
    offset = (owner - here + blk_count + REACH) % blk_count - REACH
    shifts = jnp.array(SHIFTS, jnp.int32)
    block_ids = jnp.arange(B_DEV, dtype=jnp.int32)
    hit = (offset.reshape(1, 1, -1) == shifts[:, None, None]) & (inside.reshape(1, 1, -1) == block_ids[None, :, None])
    need = jnp.any(hit, axis=2)
    low = jnp.min(jnp.where(need, block_ids[None], B_DEV - 1), axis=1)
    high = jnp.max(jnp.where(need, block_ids[None], 0), axis=1)
    want = jnp.stack([low, high], axis=1)
    asked = [passed_along(want[q], "blk", shift) for q, shift in enumerate(SHIFTS)]
    asked = jnp.concatenate(asked)
    chosen = select(asked, perturb)
    got = [
        [passed_along(chosen[stage * 4 + q], "blk", -shift) for q, shift in enumerate(SHIFTS)]
        for stage in range(STAGES)
    ]

    own = offset == 0
    q_of = jnp.where(offset < 0, offset + 2, offset + 1)
    is_high = jnp.sum(jnp.where(q_of[:, :, None] == jnp.arange(4), high[None, None], 0), axis=2) == inside
    slot = 2 * q_of + is_high.astype(jnp.int32)
    rank = jnp.cumsum(jnp.where(own, 0, 1), axis=1) - 1
    rows4 = jnp.arange(B_DEV, dtype=jnp.int32)[:, None] * 4
    source = jnp.where(own, rows4 + inside, 16 + rows4 + rank)
    column = jnp.where(own, inside, 4 + slot)
    slots = jnp.sum(
        jnp.where((~own)[:, :, None] & (rank[:, :, None] == jnp.arange(4)), slot[:, :, None], 0), axis=1
    )
    bin_match = bins[:, :, None] == jnp.arange(NBIN, dtype=jnp.int32)[None, None, :]
    tapers = jnp.sum(jnp.where(bin_match, taper_table()[None, None, :], 0.0), axis=2)

    rows = BS // samp
    at, own_part, norm_part = own_tiles(perturb, samp)
    own_sum = lax.psum_scatter(
        own_part.reshape(samp * 16 * rows, BS), "samp", scatter_dimension=0, tiled=True
    ).reshape(16, rows, BS)
    norms = norm_part + passed_along(norm_part, "samp", 2)
    norms = norms + passed_along(norms, "samp", 1)
    far = []
    for q, shift in enumerate(SHIFTS):
        theirs = passed_along(norms, "blk", -shift)
        for pick in (low[q], high[q]):
            far.append(lax.dynamic_slice_in_dim(theirs, pick, 1, 0))
    norm_table = jnp.concatenate([norms] + far, axis=0)
    row_part = lax.dynamic_slice_in_dim(norms, lax.axis_index("samp") * rows, rows, 1)
    row_scale = jnp.transpose(lax.rsqrt(row_part + EPSILON))

    rems = []
    for stage in range(STAGES):
        part = remote_tiles(slots.reshape(-1), at, got[stage], samp)
        rems.append(
            lax.psum_scatter(
                part.reshape(samp * 16 * rows, HALF), "samp", scatter_dimension=0, tiled=True
            ).reshape(16, rows, HALF)
        )
    return final(
        source.reshape(-1), column.reshape(-1), tapers.reshape(-1), own_sum, rems, row_scale, norm_table
    )


def solution(mesh):
    return jax.shard_map(
        body,
        mesh=mesh,
        in_specs=(P("samp", "blk"), P("blk", None), P("blk", None)),
        out_specs=P("samp", "blk", None),
        check_vma=False,
    )
```

time: 345 us -> 479 us (1.39)
  Pallas kernels: 0 us -> 293 us
  waiting for transfers between devices: 183 us -> 102 us
  local copies, waits for them, and re-layouts: 86.4 us -> 12 us
  starting transfers between devices: 9.83 us -> 36.7 us
  matrix products: 17.3 us -> 0 us
  blocking collectives: 15.1 us -> 0 us
  between operations: 13.6 us -> 28.6 us
  other arithmetic: 16.3 us -> 3.85 us
    pallas_call x0 -> x5, Pallas kernels: none -> 293 us  [the longest x1 256 us: select(): pl.pallas_call(select_kernel, grid_spec=pltpu.PrefetchScalarGridSpec(num_...]
    ppermute x4 -> x18, waiting for transfers between devices: 129 us -> 52.2 us  [passed_along(): return lax.ppermute(value, axis, pairs)]
    gather x5 -> x0, local copies, waits for them, and re-layouts: 47.6 us -> none  [the longest x4 47 us: body(): col_slabs = jnp.take(column_table, slot_index[row_index], axis=1)]
    ppermute x4 -> x18, starting transfers between devices: 9.83 us -> 36.6 us  [passed_along(): return lax.ppermute(value, axis, pairs)]
    dot_general x4 -> x0, matrix products: 17.3 us -> none  [body(): jnp.einsum('sa,skc->akc', row_slab, col_slabs, preferred_element_type=jnp...]
    unnamed x21 -> x12, local copies, waits for them, and re-layouts: 23.5 us -> 6.32 us
    psum x1 -> x0, blocking collectives: 15.1 us -> none  [body(): lax.psum(jnp.sum(jnp.square(column_table.astype(jnp.float32)), axis=0), '...]
    reduce_sum x1 -> x2, other arithmetic: 8.92 us -> 0.23 us  [the longest x1 0.14 us: body(): jnp.sum(jnp.where((~own)[:, :, None] & (rank[:, :, None] == jnp.arange(4)...]
  transfers between devices with their start and end apart: 5 -> 21, of which waited for: 3 -> 10; matrix products, arithmetic and copies ran while one was open for 8% -> 1% of each run, Pallas kernels for 0% -> 4%
where the time goes in v1:
time: 479 us; the launch traced here: 476 us
  Pallas kernels  293 us (61%)
  waiting for transfers between devices  102 us (21%)
  starting transfers between devices  36.7 us (8%)
  between operations  28.6 us (6%)
  local copies, waits for them, and re-layouts  12 us (3%)
    pallas_call x1, Pallas kernels, select(): pl.pallas_call(select_kernel, grid_spec=pltpu.PrefetchScalarGridSpec(num_...  256 us
    ppermute x18, waiting for transfers between devices, passed_along(): return lax.ppermute(value, axis, pairs)  52.2 us
    reduce_scatter x1, waiting for transfers between devices, body(): lax.psum_scatter(own_part.reshape(samp * 16 * rows, BS), 'samp', scatter_...  49.3 us
    ppermute x18, starting transfers between devices, passed_along(): return lax.ppermute(value, axis, pairs)  36.6 us
    pallas_call x2, Pallas kernels, remote_tiles(): pl.pallas_call(remote_kernel, grid_spec=pltpu.PrefetchScalarGridSpec(num_...  14 us
    pallas_call x1, Pallas kernels, own_tiles(): pl.pallas_call(own_kernel, out_shape=[jax.ShapeDtypeStruct((cells, sample...  12.4 us
    pallas_call x1, Pallas kernels, final(): pl.pallas_call(final_kernel, grid_spec=pltpu.PrefetchScalarGridSpec(num_s...  10.5 us
  transfers between devices with their start and end apart: 21, of which 10 were waited for; matrix products, arithmetic and copies ran while one was open for 1% of the time, Pallas kernels for 4%

profile of v1, /device:TPU:8, one launch (start us, length us, event | category | flops | bytes accessed | tf_op | source)
XLA Modules:
  0.0 476.3 jit_solution(7933387565939642346)
XLA Ops:
  6.5 0.8 fusion.10
  8.2 0.7 broadcast_compare_fusion
  9.5 1.6 collective-permute-start.3
  11.0 6.2 %collective-permute-start.1 = (s32[2]{0:T(128)S(1)}, s32[2]{0:T(128)S(1)}, u32[]{:S(2)}, u32[]{:S(2)}) collective-permute-start(s32[2]{0:T(128)S(1)} %get-tuple-element.30), channel_id=1, source_target_pairs={{0,63},{1,0},{2,1},{3,2},{4,3},{5,4},{6,5},{7,6},{8,7},{9,8},{10,9... | collective-permute-start | bytes 32 | tf_op jit(solution)/shard_map/ppermute | solution.py:27
  17.2 2.2 collective-permute-start
  19.4 1.3 collective-permute-done
  21.3 256.0 %shard_map.47 = (bf16[2048,256]{1,0:T(8,128)(2,1)}, bf16[2048,256]{1,0:T(8,128)(2,1)}, bf16[2048,256]{1,0:T(8,128)(2,1)}, bf16[2048,256]{1,0:T(8,128)(2,1)}, bf1...) custom-call(s32[8]{0:T(128)} %pad_add_fusion.1.want_ref, ...), custom_call_target="tpu_custom_call" | custom-call | bytes 16777216 | tf_op jit(solution)/shard_map/pallas_call | solution.py:64
  277.5 5.1 %collective-permute-start.6 = (bf16[2048,256]{1,0:T(8,128)(2,1)}, bf16[2048,256]{1,0:T(8,128)(2,1)S(1)}, u32[]{:S(2)}, u32[]{:S(2)}) collective-permute-start(bf16[2048,256]{1,0:T(8,128)(2,1)} %get-tuple-element.20), channel_id=1, source_target_pairs={{0,63},{1,0},{2,1},{3,2},{4,3},{5,4},{6,5},{7,6},{8,7},{9,8},{10,9... | collective-permute-start | bytes 3145736 | tf_op jit(solution)/shard_map/ppermute | solution.py:27
  282.6 2.2 collective-permute-start.7
  285.4 2.2 copy-done
  287.6 12.4 %shard_map.46 = (bf16[1024,2048]{1,0:T(8,128)(2,1)S(1)}, f32[4,16,64,256]{3,2,1,0:T(8,128)S(1)}, f32[4,256]{1,0:T(4,128)S(1)}) custom-call(bf16[2048,1024]{1,0:T(8,128)(2,1)S(1)} %copy-done), custom_call_target="tpu_custom_call" | custom-call | flops 4294967296 | bytes 12582912 | tf_op jit(solution)/shard_map/pallas_call | solution.py:101
  300.0 1.9 copy-done.1
  301.9 5.4 %collective-permute-done.4.refs_0_ = bf16[2048,256]{1,0:T(8,128)(2,1)S(1)} collective-permute-done((bf16[2048,256]{1,0:T(8,128)(2,1)}, bf16[2048,256]{1,0:T(8,128)(2,1)S(1)}, u32[]{:S(2)}, u32[]{:S(2)}) %collective-permute-start.4) | collective-permute-done | bytes 1048608 | tf_op jit(solution)/shard_map/ppermute | solution.py:27
  307.3 8.2 %collective-permute-done.5.refs_1_ = bf16[2048,256]{1,0:T(8,128)(2,1)S(1)} collective-permute-done((bf16[2048,256]{1,0:T(8,128)(2,1)}, bf16[2048,256]{1,0:T(8,128)(2,1)S(1)}, u32[]{:S(2)}, u32[]{:S(2)}) %collective-permute-start.5) | collective-permute-done | bytes 1048608 | tf_op jit(solution)/shard_map/ppermute | solution.py:27
  315.4 2.2 collective-permute-done.7.refs_3_
  317.7 7.6 %shard_map.48 = f32[4,16,64,128]{3,2,1,0:T(8,128)} custom-call(s32[16]{0:T(128)S(1)} %reshape.142.slot_ref, bf16[1024,2048]{1,0:T(8,128)(2,1)S(1)} %get-tuple-element.17.at_ref, bf16[2048,256]{1,0:T(8,128)(2,1)S(1)} %collective-permute-done.4.refs_0_, bf16[2048,256]{1,0:T(8,128)(2,1)S(1)} %collective-permute-done.5.refs_1_, ...), custom_call_target="tpu_custom_call" | custom-call | flops 4294967296 | bytes 10485760 | tf_op jit(solution)/shard_map/pallas_call | solution.py:133
  325.6 5.1 %collective-permute-start.10 = (bf16[2048,256]{1,0:T(8,128)(2,1)}, bf16[2048,256]{1,0:T(8,128)(2,1)S(1)}, u32[]{:S(2)}, u32[]{:S(2)}) collective-permute-start(bf16[2048,256]{1,0:T(8,128)(2,1)} %get-tuple-element.24), channel_id=1, source_target_pairs={{0,63},{1,0},{2,1},{3,2},{4,3},{5,4},{6,5},{7,6},{8,7},{9,8},{10,9... | collective-permute-start | bytes 3145736 | tf_op jit(solution)/shard_map/ppermute | solution.py:27
  330.6 2.5 collective-permute-start.11
  333.1 22.4 %collective-permute-done.8.refs_0_ = bf16[2048,256]{1,0:T(8,128)(2,1)S(1)} collective-permute-done((bf16[2048,256]{1,0:T(8,128)(2,1)}, bf16[2048,256]{1,0:T(8,128)(2,1)S(1)}, u32[]{:S(2)}, u32[]{:S(2)}) %collective-permute-start.8) | collective-permute-done | bytes 1048608 | tf_op jit(solution)/shard_map/ppermute | solution.py:27
  355.6 2.2 collective-permute-done.9.refs_1_
  357.8 8.0 %collective-permute-done.11.refs_3_ = bf16[2048,256]{1,0:T(8,128)(2,1)S(1)} collective-permute-done((bf16[2048,256]{1,0:T(8,128)(2,1)}, bf16[2048,256]{1,0:T(8,128)(2,1)S(1)}, u32[]{:S(2)}, u32[]{:S(2)}) %collective-permute-start.11) | collective-permute-done | bytes 1048608 | tf_op jit(solution)/shard_map/ppermute | solution.py:27
  365.7 2.2 copy-done.3
  367.9 6.4 %shard_map.49 = f32[4,16,64,128]{3,2,1,0:T(8,128)} custom-call(s32[16]{0:T(128)S(1)} %reshape.142.slot_ref, bf16[1024,2048]{1,0:T(8,128)(2,1)S(1)} %copy-done.3, bf16[2048,256]{1,0:T(8,128)(2,1)S(1)} %collective-permute-done.8.refs_0_, bf16[2048,256]{1,0:T(8,128)(2,1)S(1)} %collective-permute-done.9.refs_1_, ...), custom_call_target="tpu_custom_call" | custom-call | flops 4294967296 | bytes 10485760 | tf_op jit(solution)/shard_map/pallas_call | solution.py:133
  375.1 2.4 collective-permute-start.12
  378.3 2.0 collective-permute-done.12
  380.3 1.6 collective-permute-start.13
  400.0 5.1 %collective-permute-start.16 = (f32[4,256]{1,0:T(4,128)S(1)}, f32[4,256]{1,0:T(4,128)S(1)}, u32[]{:S(2)}, u32[]{:S(2)}) collective-permute-start(f32[4,256]{1,0:T(4,128)S(1)} %add.198), channel_id=1, source_target_pairs={{0,63},{1,0},{2,1},{3,2},{4,3},{5,4},{6,5},{7,6},{8,7},{9,8},{10,9... | collective-permute-start | bytes 12296 | tf_op jit(solution)/shard_map/ppermute | solution.py:27
  405.0 2.4 collective-permute-start.17
  407.5 0.7 copy.7.row_ref
  408.7 1.2 concatenate.7.norm_ref
  410.0 49.3 %reduce-scatter.4.cloned.1.call-done = f32[1024,256]{1,0:T(8,128)} async-done(((f32[4096,256]{1,0:T(8,128)}), f32[1024,256]{1,0:T(8,128)}) %reduce-scatter.4.cloned.1.call-update) | async-done | bytes 1048592 | tf_op jit(solution)/shard_map/reduce_scatter | solution.py:221
  459.3 10.5 %shard_map.50 = f32[64,32,256]{2,1,0:T(8,128)} custom-call(s32[32]{0:T(128)} %reshape.137.source_ref, s32[32]{0:T(128)} %reshape.138.column_ref, f32[32]{0:T(128)} %reshape.139.taper_ref, f32[16,64,256]{2,1,0:T(8,128)} %bitcast.19, f32[16,64,128]{2,1,0:T(8,128)} %bitcast.20, f32[16,64,128]{2,1,0:T(8,128)} %bitcast.21, f32[64,4]{1,0:T(8,128)} %copy.7.row_ref, ...), custom_call_target="tpu_custom_call" | custom-call | flops 1048576 | bytes 4194304 | tf_op jit(solution)/shard_map/pallas_call | solution.py:170
  (64 shorter events, 8.0 us)
Async XLA Ops:
  6.5 278.6 %copy-start.4 = (s32[4,8]{1,0:T(4,128)S(1)}, s32[4,8]{1,0:T(4,128)}, u32[]{:S(2)}) copy-start(s32[4,8]{1,0:T(4,128)} %param.5) | copy-start | bytes 388
  6.5 403.4 %reduce-scatter.6.cloned.1.call-start = ((), (), s32[]{:S(2)}) async-start(), calls=%async_computation.4 | async-start | bytes 2621440 | tf_op jit(solution)/shard_map/reduce_scatter | solution.py:239
  9.5 10.0 %collective-permute-start.3 = (s32[2]{0:T(128)S(1)}, s32[2]{0:T(128)S(1)}, u32[]{:S(2)}, u32[]{:S(2)}) collective-permute-start(s32[2]{0:T(128)S(1)} %get-tuple-element.28), channel_id=1, source_target_pairs={{0,2},{1,3},{2,4},{3,5},{4,6},{5,7},{6,8},{7,9},{8,10},{9,11},{10,... | collective-permute-start | bytes 32 | tf_op jit(solution)/shard_map/ppermute | solution.py:27
  11.0 8.4 %collective-permute-start.2 = (s32[2]{0:T(128)S(1)}, s32[2]{0:T(128)S(1)}, u32[]{:S(2)}, u32[]{:S(2)}) collective-permute-start(s32[2]{0:T(128)S(1)} %get-tuple-element.29), channel_id=1, source_target_pairs={{0,1},{1,2},{2,3},{3,4},{4,5},{5,6},{6,7},{7,8},{8,9},{9,10},{10,1... | collective-permute-start | bytes 32 | tf_op jit(solution)/shard_map/ppermute | solution.py:27
  11.0 8.4 %collective-permute-start.1 = (s32[2]{0:T(128)S(1)}, s32[2]{0:T(128)S(1)}, u32[]{:S(2)}, u32[]{:S(2)}) collective-permute-start(s32[2]{0:T(128)S(1)} %get-tuple-element.30), channel_id=1, source_target_pairs={{0,63},{1,0},{2,1},{3,2},{4,3},{5,4},{6,5},{7,6},{8,7},{9,8},{10,9... | collective-permute-start | bytes 32 | tf_op jit(solution)/shard_map/ppermute | solution.py:27
  17.2 3.5 collective-permute-start
  277.4 29.9 %collective-permute-start.4 = (bf16[2048,256]{1,0:T(8,128)(2,1)}, bf16[2048,256]{1,0:T(8,128)(2,1)S(1)}, u32[]{:S(2)}, u32[]{:S(2)}) collective-permute-start(bf16[2048,256]{1,0:T(8,128)(2,1)} %get-tuple-element.18), channel_id=1, source_target_pairs={{0,2},{1,3},{2,4},{3,5},{4,6},{5,7},{6,8},{7,9},{8,10},{9,11},{10,... | collective-permute-start | bytes 3145736 | tf_op jit(solution)/shard_map/ppermute | solution.py:27
  277.4 38.0 %collective-permute-start.5 = (bf16[2048,256]{1,0:T(8,128)(2,1)}, bf16[2048,256]{1,0:T(8,128)(2,1)S(1)}, u32[]{:S(2)}, u32[]{:S(2)}) collective-permute-start(bf16[2048,256]{1,0:T(8,128)(2,1)} %get-tuple-element.19), channel_id=1, source_target_pairs={{0,1},{1,2},{2,3},{3,4},{4,5},{5,6},{6,7},{7,8},{8,9},{9,10},{10,1... | collective-permute-start | bytes 3145736 | tf_op jit(solution)/shard_map/ppermute | solution.py:27
  277.5 37.9 %collective-permute-start.6 = (bf16[2048,256]{1,0:T(8,128)(2,1)}, bf16[2048,256]{1,0:T(8,128)(2,1)S(1)}, u32[]{:S(2)}, u32[]{:S(2)}) collective-permute-start(bf16[2048,256]{1,0:T(8,128)(2,1)} %get-tuple-element.20), channel_id=1, source_target_pairs={{0,63},{1,0},{2,1},{3,2},{4,3},{5,4},{6,5},{7,6},{8,7},{9,8},{10,9... | collective-permute-start | bytes 3145736 | tf_op jit(solution)/shard_map/ppermute | solution.py:27
  282.6 35.1 %collective-permute-start.7 = (bf16[2048,256]{1,0:T(8,128)(2,1)}, bf16[2048,256]{1,0:T(8,128)(2,1)}, u32[]{:S(2)}, u32[]{:S(2)}) collective-permute-start(bf16[2048,256]{1,0:T(8,128)(2,1)} %get-tuple-element.21), channel_id=1, source_target_pairs={{0,62},{1,63},{2,0},{3,1},{4,2},{5,3},{6,4},{7,5},{8,6},{9,7},{10,... | collective-permute-start | bytes 3145736 | tf_op jit(solution)/shard_map/ppermute | solution.py:27
  285.4 2.2 copy-start
  300.0 1.9 copy-start.1
  301.9 23.4 %copy-start.2 = (bf16[1024,2048]{1,0:T(8,128)(2,1)}, bf16[1024,2048]{1,0:T(8,128)(2,1)S(1)}, u32[]{:S(2)}) copy-start(bf16[1024,2048]{1,0:T(8,128)(2,1)S(1)} %get-tuple-element.17.at_ref) | copy-start | bytes 12582916
  325.3 84.6 %reduce-scatter.8.cloned.1.call-start = ((), (), s32[]{:S(2)}) async-start(), calls=%async_computation.5 | async-start | bytes 2621440 | tf_op jit(solution)/shard_map/reduce_scatter | solution.py:239
  325.4 30.2 %collective-permute-start.8 = (bf16[2048,256]{1,0:T(8,128)(2,1)}, bf16[2048,256]{1,0:T(8,128)(2,1)S(1)}, u32[]{:S(2)}, u32[]{:S(2)}) collective-permute-start(bf16[2048,256]{1,0:T(8,128)(2,1)} %get-tuple-element.22), channel_id=1, source_target_pairs={{0,2},{1,3},{2,4},{3,5},{4,6},{5,7},{6,8},{7,9},{8,10},{9,11},{10,... | collective-permute-start | bytes 3145736 | tf_op jit(solution)/shard_map/ppermute | solution.py:27
  325.5 32.3 %collective-permute-start.9 = (bf16[2048,256]{1,0:T(8,128)(2,1)}, bf16[2048,256]{1,0:T(8,128)(2,1)S(1)}, u32[]{:S(2)}, u32[]{:S(2)}) collective-permute-start(bf16[2048,256]{1,0:T(8,128)(2,1)} %get-tuple-element.23), channel_id=1, source_target_pairs={{0,1},{1,2},{2,3},{3,4},{4,5},{5,6},{6,7},{7,8},{8,9},{9,10},{10,1... | collective-permute-start | bytes 3145736 | tf_op jit(solution)/shard_map/ppermute | solution.py:27
  325.6 32.2 %collective-permute-start.10 = (bf16[2048,256]{1,0:T(8,128)(2,1)}, bf16[2048,256]{1,0:T(8,128)(2,1)S(1)}, u32[]{:S(2)}, u32[]{:S(2)}) collective-permute-start(bf16[2048,256]{1,0:T(8,128)(2,1)} %get-tuple-element.24), channel_id=1, source_target_pairs={{0,63},{1,0},{2,1},{3,2},{4,3},{5,4},{6,5},{7,6},{8,7},{9,8},{10,9... | collective-permute-start | bytes 3145736 | tf_op jit(solution)/shard_map/ppermute | solution.py:27
  330.6 35.1 %collective-permute-start.11 = (bf16[2048,256]{1,0:T(8,128)(2,1)}, bf16[2048,256]{1,0:T(8,128)(2,1)S(1)}, u32[]{:S(2)}, u32[]{:S(2)}) collective-permute-start(bf16[2048,256]{1,0:T(8,128)(2,1)} %get-tuple-element.25), channel_id=1, source_target_pairs={{0,62},{1,63},{2,0},{3,1},{4,2},{5,3},{6,4},{7,5},{8,6},{9,7},{10,... | collective-permute-start | bytes 3145736 | tf_op jit(solution)/shard_map/ppermute | solution.py:27
  365.7 2.2 copy-start.3
  374.3 3.2 copy-start.5
  374.4 84.9 %reduce-scatter.4.cloned.1.call-start = ((), (), s32[]{:S(2)}) async-start(), calls=%async_computation.3 | async-start | bytes 5242880 | tf_op jit(solution)/shard_map/reduce_scatter | solution.py:221
  375.1 5.2 %collective-permute-start.12 = (f32[4,256]{1,0:T(4,128)S(1)}, f32[4,256]{1,0:T(4,128)S(1)}, u32[]{:S(2)}, u32[]{:S(2)}) collective-permute-start(f32[4,256]{1,0:T(4,128)S(1)} %get-tuple-element.26), channel_id=1, source_target_pairs={{0,128},{64,192},{128,0},{192,64},{1,129},{65,193},{129,1},{193,65... | collective-permute-start | bytes 12296 | tf_op jit(solution)/shard_map/ppermute | solution.py:27
  380.3 19.5 %collective-permute-start.13 = (f32[4,256]{1,0:T(4,128)S(1)}, f32[4,256]{1,0:T(4,128)S(1)}, u32[]{:S(2)}, u32[]{:S(2)}) collective-permute-start(f32[4,256]{1,0:T(4,128)S(1)} %add.197), channel_id=1, source_target_pairs={{0,64},{64,128},{128,192},{192,0},{1,65},{65,129},{129,193},{193,1... | collective-permute-start | bytes 12296 | tf_op jit(solution)/shard_map/ppermute | solution.py:27
  399.8 8.4 %collective-permute-start.14 = (f32[4,256]{1,0:T(4,128)S(1)}, f32[4,256]{1,0:T(4,128)S(1)}, u32[]{:S(2)}, u32[]{:S(2)}) collective-permute-start(f32[4,256]{1,0:T(4,128)S(1)} %add.198), channel_id=1, source_target_pairs={{0,2},{1,3},{2,4},{3,5},{4,6},{5,7},{6,8},{7,9},{8,10},{9,11},{10,... | collective-permute-start | bytes 12296 | tf_op jit(solution)/shard_map/ppermute | solution.py:27
  399.9 8.3 %collective-permute-start.15 = (f32[4,256]{1,0:T(4,128)S(1)}, f32[4,256]{1,0:T(4,128)S(1)}, u32[]{:S(2)}, u32[]{:S(2)}) collective-permute-start(f32[4,256]{1,0:T(4,128)S(1)} %add.198), channel_id=1, source_target_pairs={{0,1},{1,2},{2,3},{3,4},{4,5},{5,6},{6,7},{7,8},{8,9},{9,10},{10,1... | collective-permute-start | bytes 12296 | tf_op jit(solution)/shard_map/ppermute | solution.py:27
  400.0 8.2 %collective-permute-start.16 = (f32[4,256]{1,0:T(4,128)S(1)}, f32[4,256]{1,0:T(4,128)S(1)}, u32[]{:S(2)}, u32[]{:S(2)}) collective-permute-start(f32[4,256]{1,0:T(4,128)S(1)} %add.198), channel_id=1, source_target_pairs={{0,63},{1,0},{2,1},{3,2},{4,3},{5,4},{6,5},{7,6},{8,7},{9,8},{10,9... | collective-permute-start | bytes 12296 | tf_op jit(solution)/shard_map/ppermute | solution.py:27
  405.0 3.7 collective-permute-start.17
Sparse Core Ops, SparseCore 0:
  325.5 33.1 reduce-scatter.5
  374.5 33.0 reduce-scatter.7
  410.1 49.1 reduce-scatter.3

commit v2 on v0

v2 whole, which is shorter than its diff:
```python
import functools

import jax
import jax.numpy as jnp
from jax import lax
from jax.experimental import pallas as pl
from jax.experimental.pallas import tpu as pltpu
from jax.sharding import PartitionSpec as P

BS = 256
B_DEV = 4
K_PART = 8
REACH = 2
NBIN = 32
PAIR_DEV = 32
HALF = 128
STAGES = 2
EXTRA = 8

EPSILON = 1e-06
MIB = 1 << 20


def passed_along(value, axis, steps):
    count = lax.axis_size(axis)
    pairs = [(source, (source + steps) % count) for source in range(count)]
    return lax.ppermute(value, axis, pairs)


def exchanged(value, kind, back=False):
    count = lax.axis_size("blk")
    source_of = (
        lambda i: i - 2,
        lambda i: i ^ 1,
        lambda i: i - 1 if i % 2 == 0 else i + 1,
        lambda i: i + 2,
    )[kind]
    pairs = [(source_of(i) % count, i) for i in range(count)]
    if back:
        pairs = [(b, a) for a, b in pairs]
    return lax.ppermute(value, "blk", sorted(pairs))


def ringed(value):
    samp, count = lax.axis_size("samp"), lax.axis_size("blk")
    pairs = [
        (y * count + i, (y + 1 - 2 * (i % 2)) % samp * count + i) for y in range(samp) for i in range(count)
    ]
    return lax.ppermute(value, ("samp", "blk"), pairs)


def taper_table():
    scaled = 2.0 * (jnp.arange(NBIN, dtype=jnp.float32) + 0.5) / NBIN
    inner = (((-0.25 * scaled + 0.5) * scaled + 0.625) * scaled - 5.0 / 3.0) * scaled * scaled + 1.0
    outer = (
        ((((scaled / 12.0 - 0.5) * scaled + 0.625) * scaled + 5.0 / 3.0) * scaled - 5.0) * scaled
        + 4.0
        - 2.0 / (3.0 * scaled)
    )
    return jnp.where(scaled <= 1.0, inner, outer)


def select_kernel(plan, want_ref, source_ref, *refs):
    outs, held_ref, in_sems, out_sems = refs[:-3], refs[-3], refs[-2], refs[-1]
    reads, writes = [], []
    for i, (q, side, half, out, column) in enumerate(plan):
        start = pl.multiple_of(want_ref[q * 2 + side] * BS + half * HALF, HALF)
        reads.append(pltpu.make_async_copy(source_ref.at[:, pl.ds(start, HALF)], held_ref.at[i], in_sems.at[i]))
        writes.append(
            pltpu.make_async_copy(held_ref.at[i], outs[out].at[:, pl.ds(column * HALF, HALF)], out_sems.at[i])
        )
    for read in reads:
        read.start()
    for read, write in zip(reads, writes):
        read.wait()
        write.start()
    for write in writes:
        write.wait()


def select(want, perturb):
    samples = perturb.shape[0]
    widths = [2 * HALF] * 6 + [4 * HALF]
    plan = [(q, side, 0, out, side) for out, q in enumerate((0, 2, 3)) for side in range(2)]
    plan += [(1, side, half, 6, 2 * half + side) for half in range(2) for side in range(2)]
    plan += [(q, side, 1, 3 + out, side) for out, q in enumerate((0, 2, 3)) for side in range(2)]
    return pl.pallas_call(
        functools.partial(select_kernel, plan),
        grid_spec=pltpu.PrefetchScalarGridSpec(
            num_scalar_prefetch=1,
            grid=(),
            in_specs=[pl.BlockSpec(memory_space=pl.ANY)],
            out_specs=[pl.BlockSpec(memory_space=pltpu.HBM)] * len(widths),
            scratch_shapes=[
                pltpu.VMEM((len(plan), samples, HALF), perturb.dtype),
                pltpu.SemaphoreType.DMA((len(plan),)),
                pltpu.SemaphoreType.DMA((len(plan),)),
            ],
        ),
        out_shape=[jax.ShapeDtypeStruct((samples, width), perturb.dtype) for width in widths],
        compiler_params=pltpu.CompilerParams(vmem_limit_bytes=16 * MIB),
        cost_estimate=pl.CostEstimate(flops=0, bytes_accessed=MIB * len(plan), transcendentals=0),
    )(want, perturb)


def own_kernel(x_ref, at_ref, part_ref):
    samp = part_ref.shape[0]
    rows = BS // samp
    for r in range(B_DEV):
        at_ref[r * BS : (r + 1) * BS, :] = jnp.transpose(x_ref[:, r * BS : (r + 1) * BS])

    @pl.loop(0, B_DEV)
    def _(r):
        at = at_ref[pl.ds(pl.multiple_of(r * BS, BS), BS), :]
        for c in range(B_DEV):
            tile = jnp.dot(at, x_ref[:, c * BS : (c + 1) * BS], preferred_element_type=jnp.float32)
            for y in range(samp):
                where = pl.ds(pl.multiple_of((r * B_DEV + c) * rows, rows), rows)
                part_ref[y, where, :] = tile[y * rows : (y + 1) * rows]

            @pl.when(r == c)
            def _():
                here = lax.broadcasted_iota(jnp.int32, (BS, BS), 0) == lax.broadcasted_iota(jnp.int32, (BS, BS), 1)
                norm = jnp.sum(jnp.where(here, tile, 0.0), axis=0, keepdims=True)
                for y in range(samp):
                    part_ref[y, 16 * rows + c : 16 * rows + c + 1, :] = norm

    for y in range(samp):
        part_ref[y, 16 * rows + B_DEV :, :] = jnp.zeros((EXTRA - B_DEV, BS), jnp.float32)


def own_tiles(perturb, samp):
    samples, cells = perturb.shape
    return pl.pallas_call(
        own_kernel,
        out_shape=[
            jax.ShapeDtypeStruct((cells, samples), perturb.dtype),
            jax.ShapeDtypeStruct((samp, 16 * BS // samp + EXTRA, BS), jnp.float32),
        ],
        compiler_params=pltpu.CompilerParams(vmem_limit_bytes=40 * MIB),
        cost_estimate=pl.CostEstimate(flops=2 * cells * cells * samples, bytes_accessed=10 * MIB, transcendentals=0),
    )(perturb)


def remote_kernel(slot_ref, dest_ref, at_ref, *refs):
    blocks, parts, all_ref = refs[:4], refs[4:-1], refs[-1]
    samp = len(parts)
    samples = blocks[0].shape[0]
    rows = BS // samp
    r = pl.program_id(0)
    at = at_ref[...]
    for q in range(4):
        tile = jnp.dot(at, blocks[q][...], preferred_element_type=jnp.float32)
        all_ref[2 * q] = tile[:, :HALF]
        all_ref[2 * q + 1] = tile[:, HALF:]
    for j in range(4):
        u = r * 4 + j
        place = pl.ds(pl.multiple_of(u * rows, rows), rows)
        for d in range(samp):
            first = pl.multiple_of(dest_ref[d] * rows, rows)
            parts[d][place, :] = all_ref[slot_ref[u], pl.ds(first, rows), :]

    step = 128
    for q in range(4):

        @pl.when(r == q)
        def _():
            def add(i, total):
                x = blocks[q][pl.ds(pl.multiple_of(i * step, step), step), :].astype(jnp.float32)
                return total + jnp.sum((x * x).reshape(step // 8, 8, 2 * HALF), axis=0)

            total = lax.fori_loop(0, samples // step, add, jnp.zeros((8, 2 * HALF), jnp.float32))
            norm = jnp.sum(total, axis=0, keepdims=True)
            for side in range(2):
                at_row = 16 * rows + 2 * q + side
                for d in range(samp):
                    parts[d][at_row : at_row + 1, :] = norm[:, side * HALF : (side + 1) * HALF]


def remote_tiles(stage, slots, dest, at, blocks, samp):
    cells, samples = at.shape
    full = lambda shape: pl.BlockSpec(shape, lambda i, *s: (0,) * len(shape))
    shape = (16 * BS // samp + EXTRA, HALF)
    block = lambda q: pl.BlockSpec((samples, 2 * HALF), lambda i, *s: (0, stage if q == 1 else 0))
    return pl.pallas_call(
        remote_kernel,
        grid_spec=pltpu.PrefetchScalarGridSpec(
            num_scalar_prefetch=2,
            grid=(B_DEV,),
            in_specs=[pl.BlockSpec((BS, samples), lambda i, *s: (i, 0))] + [block(q) for q in range(4)],
            out_specs=[full(shape)] * samp,
            scratch_shapes=[pltpu.VMEM((8, BS, HALF), jnp.float32)],
        ),
        out_shape=[jax.ShapeDtypeStruct(shape, jnp.float32)] * samp,
        compiler_params=pltpu.CompilerParams(vmem_limit_bytes=30 * MIB),
        cost_estimate=pl.CostEstimate(flops=2 * cells * cells * samples, bytes_accessed=10 * MIB, transcendentals=0),
    )(slots, dest, at, *blocks)


def final_kernel(half, rem_count, place_ref, slot_ref, dest_ref, taper_ref, own_ref, *refs):
    rem_refs, out_ref = refs[:rem_count], refs[-1]
    rows = out_ref.shape[0] // PAIR_DEV
    first = dest_ref[0] * rows
    cols = slice(half * HALF, (half + 1) * HALF)
    lane = lax.broadcasted_iota(jnp.int32, (rows, BS), 1)
    row = lax.broadcasted_iota(jnp.int32, (rows, BS), 0)
    mine = lane == row + first
    for r in range(B_DEV):
        row_norm = own_ref[16 * rows + r : 16 * rows + r + 1, :]
        row_norm = jnp.sum(jnp.where(mine, row_norm, 0.0), axis=1, keepdims=True)
        row_scale = jnp.broadcast_to(lax.rsqrt(row_norm + EPSILON), (rows, HALF))
        for j in range(4):
            u = r * 4 + j
            norm = own_ref[16 * rows + j : 16 * rows + j + 1, cols]
            col_scale = taper_ref[u] * lax.rsqrt(norm + EPSILON)
            tile = own_ref[u * rows : (u + 1) * rows, cols]
            out_ref[pl.ds(place_ref[u], rows, stride=PAIR_DEV), :] = tile * row_scale * col_scale
        for j in range(4):
            u = r * 4 + j
            at_norm = pl.ds(16 * rows + slot_ref[u], 1)
            norm = sum(ref[at_norm, :] for ref in rem_refs)
            col_scale = taper_ref[16 + u] * lax.rsqrt(norm + EPSILON)
            tile = sum(ref[u * rows : (u + 1) * rows, :] for ref in rem_refs)
            out_ref[pl.ds(place_ref[16 + u], rows, stride=PAIR_DEV), :] = tile * row_scale * col_scale


def final(half, place, slots, dest, tapers, own, rems, out, rows):
    full = lambda shape: pl.BlockSpec(shape, lambda i, *s: (0,) * len(shape))
    before = [] if out is None else [out]
    return pl.pallas_call(
        functools.partial(final_kernel, half, len(rems)),
        grid_spec=pltpu.PrefetchScalarGridSpec(
            num_scalar_prefetch=4,
            grid=(1,),
            in_specs=[full(own.shape)]
            + [full(rem.shape) for rem in rems]
            + [pl.BlockSpec(memory_space=pl.ANY)] * len(before),
            out_specs=pl.BlockSpec((rows * PAIR_DEV, HALF), lambda i, *s: (0, half)),
        ),
        out_shape=jax.ShapeDtypeStruct((rows * PAIR_DEV, BS), jnp.float32),
        input_output_aliases={5 + len(rems): 0} if before else {},
        cost_estimate=pl.CostEstimate(flops=MIB, bytes_accessed=4 * MIB, transcendentals=0),
    )(place, slots, dest, tapers, own, *rems, *before)


def body(perturb, partner, bins):
    blk_count = lax.axis_size("blk")
    samp = lax.axis_size("samp")
    here = lax.axis_index("blk")
    owner = partner // B_DEV
    inside = partner % B_DEV
    offset = (owner - here + blk_count + REACH) % blk_count - REACH
    mate = 1 - 2 * (here % 2)
    kind = jnp.where(offset == -2, 0, jnp.where(offset == 2, 3, jnp.where(offset == mate, 1, 2)))
    own = offset == 0
    kind = jnp.where(own, -1, kind)
    four = jnp.arange(4, dtype=jnp.int32)
    hit = (kind.reshape(1, 1, -1) == four[:, None, None]) & (inside.reshape(1, 1, -1) == four[None, :, None])
    need = jnp.any(hit, axis=2)
    low = jnp.min(jnp.where(need, four[None], B_DEV - 1), axis=1)
    high = jnp.max(jnp.where(need, four[None], 0), axis=1)
    want = jnp.stack([low, high], axis=1)
    asked = jnp.concatenate([exchanged(want[q], q, back=True) for q in range(4)])
    chosen = select(asked, perturb)
    mates = exchanged(chosen[6], 1)
    got = []
    for stage in range(STAGES):
        two_below, across, two_above = (exchanged(chosen[3 * stage + i], q) for i, q in enumerate((0, 2, 3)))
        got.append([two_below, mates, across, two_above])

    k_ids = jnp.arange(K_PART, dtype=jnp.int32)[None, :, None]
    is_high = jnp.sum(jnp.where(kind[:, :, None] == four, high[None, None], 0), axis=2) == inside
    slot = 2 * kind + is_high.astype(jnp.int32)
    remote = (~own).astype(jnp.int32)
    earlier = (jnp.arange(K_PART)[:, None] < jnp.arange(K_PART)[None, :]).astype(jnp.int32)
    rank = jnp.sum(remote[:, :, None] * earlier[None], axis=1)
    is_own = own[:, :, None] & (inside[:, :, None] == four)
    is_rem = (~own)[:, :, None] & (rank[:, :, None] == four)
    pick = lambda mask, value: jnp.sum(jnp.where(mask, value, 0), axis=1)
    bin_match = bins[:, :, None] == jnp.arange(NBIN, dtype=jnp.int32)[None, None, :]
    taper = jnp.sum(jnp.where(bin_match, taper_table()[None, None, :], 0.0), axis=2)[:, :, None]
    both = jnp.stack([is_own, is_rem])
    first_place = jnp.arange(B_DEV, dtype=jnp.int32)[None, :, None] * K_PART
    place = (jnp.sum(jnp.where(both, k_ids[None], 0), axis=2) + first_place).reshape(-1)
    tapers = jnp.sum(jnp.where(both, taper[None], 0.0), axis=2).reshape(-1)
    slots = pick(is_rem, slot[:, :, None]).reshape(-1)

    rows = BS // samp
    size = 16 * rows + EXTRA
    me = lax.axis_index("samp")
    ahead = 1 - 2 * (here % 2)
    ring_dest = (me + ahead * jnp.array([-1, -2, 1, 0], jnp.int32) + 2 * samp) % samp
    dest = (me + jnp.arange(samp, dtype=jnp.int32)) % samp
    at, own_part = own_tiles(perturb, samp)

    parts = list(remote_tiles(0, slots, ring_dest, at, got[0], samp))
    own_part, parts[0] = lax.optimization_barrier((own_part, parts[0]))
    own_sum = lax.psum_scatter(own_part.reshape(samp * size, BS), "samp", scatter_dimension=0, tiled=True)
    running = parts[0]
    for d in range(1, samp):
        running = ringed(running) + parts[d]

    parts = remote_tiles(1, slots, dest, at, got[1], samp)
    last = [parts[0]] + [passed_along(parts[d], "samp", d) for d in range(1, samp)]

    out = final(0, place, slots, dest, tapers, own_sum, [running], None, rows)
    out = final(1, place, slots, dest, tapers, own_sum, last, out, rows)
    return out.reshape(rows, PAIR_DEV, BS)


def solution(mesh):
    return jax.shard_map(
        body,
        mesh=mesh,
        in_specs=(P("samp", "blk"), P("blk", None), P("blk", None)),
        out_specs=P("samp", "blk", None),
        check_vma=False,
    )
```

time: 345 us -> 183 us (0.53)
  waiting for transfers between devices: 183 us -> 75.9 us
  local copies, waits for them, and re-layouts: 86.4 us -> 14.1 us
  Pallas kernels: 0 us -> 43.3 us
  starting transfers between devices: 9.83 us -> 31.4 us
  matrix products: 17.3 us -> 0 us
  blocking collectives: 15.1 us -> 0 us
  other arithmetic: 16.3 us -> 3.86 us
    ppermute x4 -> x3, waiting for transfers between devices: 129 us -> 0.01 us  [passed_along(): return lax.ppermute(value, axis, pairs)]
    ppermute x0 -> x14, waiting for transfers between devices: none -> 75.9 us  [the longest x3 45 us: ringed(): return lax.ppermute(value, ('samp', 'blk'), pairs)]
    reduce_scatter x1, waiting for transfers between devices: 53.9 us -> 0.01 us  [body(): lax.psum_scatter(own_part.reshape(samp * size, BS), 'samp', scatter_dimen...]
    gather x5 -> x0, local copies, waits for them, and re-layouts: 47.6 us -> none  [the longest x4 47 us: body(): col_slabs = jnp.take(column_table, slot_index[row_index], axis=1)]
    pallas_call x0 -> x6, Pallas kernels: none -> 43.3 us  [the longest x2 17.2 us: remote_tiles(): pl.pallas_call(remote_kernel, grid_spec=pltpu.PrefetchScalarGridSpec(num_...]
    ppermute x0 -> x14, starting transfers between devices: none -> 26.4 us  [the longest x11 23.2 us: exchanged(): return lax.ppermute(value, 'blk', sorted(pairs))]
    dot_general x4 -> x0, matrix products: 17.3 us -> none  [body(): jnp.einsum('sa,skc->akc', row_slab, col_slabs, preferred_element_type=jnp...]
    psum x1 -> x0, blocking collectives: 15.1 us -> none  [body(): lax.psum(jnp.sum(jnp.square(column_table.astype(jnp.float32)), axis=0), '...]
  transfers between devices with their start and end apart: 5 -> 18, of which waited for: 3 -> 8; matrix products, arithmetic and copies ran while one was open for 8% -> 2% of each run, Pallas kernels for 0% -> 14%
where the time goes in v2:
time: 183 us; the launch traced here: 182 us
  waiting for transfers between devices  75.9 us (41%)
  Pallas kernels  43.3 us (24%)
  starting transfers between devices  31.4 us (17%)
  local copies, waits for them, and re-layouts  14.1 us (8%)
  between operations  13.6 us (7%)
  other arithmetic  3.86 us (2%)
    ppermute x3, waiting for transfers between devices, ringed(): return lax.ppermute(value, ('samp', 'blk'), pairs)  45 us
    ppermute x11, waiting for transfers between devices, exchanged(): return lax.ppermute(value, 'blk', sorted(pairs))  30.9 us
    ppermute x11, starting transfers between devices, exchanged(): return lax.ppermute(value, 'blk', sorted(pairs))  23.2 us
    pallas_call x2, Pallas kernels, remote_tiles(): pl.pallas_call(remote_kernel, grid_spec=pltpu.PrefetchScalarGridSpec(num_...  17.2 us
    pallas_call x1, Pallas kernels, own_tiles(): pl.pallas_call(own_kernel, out_shape=[jax.ShapeDtypeStruct((cells, sample...  12.4 us
    unnamed x28, local copies, waits for them, and re-layouts  12.3 us
    pallas_call x2, Pallas kernels, final(): pl.pallas_call(functools.partial(final_kernel, half, len(rems)), grid_spe...  8.83 us
    ppermute x3, starting transfers between devices, passed_along(): return lax.ppermute(value, axis, pairs)  4.95 us
  transfers between devices with their start and end apart: 18, of which 8 were waited for; matrix products, arithmetic and copies ran while one was open for 2% of the time, Pallas kernels for 14%

profile of v2, /device:TPU:8, one launch (start us, length us, event | category | flops | bytes accessed | tf_op | source)
XLA Modules:
  0.0 182.1 jit_solution(1440857268220135141)
XLA Ops:
  8.0 8.1 %collective-permute-start = (s32[2]{0:T(128)S(1)}, s32[2]{0:T(128)S(1)}, u32[]{:S(2)}, u32[]{:S(2)}) collective-permute-start(s32[2]{0:T(128)S(1)} %get-tuple-element.43), channel_id=1, source_target_pairs={{0,62},{1,63},{2,0},{3,1},{4,2},{5,3},{6,4},{7,5},{8,6},{9,7},{10,... | collective-permute-start | bytes 32 | tf_op jit(solution)/shard_map/ppermute | solution.py:41
  16.1 4.2 %collective-permute-start.2 = (s32[2]{0:T(128)S(1)}, s32[2]{0:T(128)S(1)}, u32[]{:S(2)}, u32[]{:S(2)}) collective-permute-start(s32[2]{0:T(128)S(1)} %get-tuple-element.45), channel_id=1, source_target_pairs={{0,63},{1,2},{2,1},{3,4},{4,3},{5,6},{6,5},{7,8},{8,7},{9,10},{10,... | collective-permute-start | bytes 32 | tf_op jit(solution)/shard_map/ppermute | solution.py:41
  20.3 2.6 %collective-permute-done.3 = s32[2]{0:T(128)S(1)} collective-permute-done((s32[2]{0:T(128)S(1)}, s32[2]{0:T(128)S(1)}, u32[]{:S(2)}, u32[]{:S(2)}) %collective-permute-start.3) | collective-permute-done | bytes 40 | tf_op jit(solution)/shard_map/ppermute | solution.py:41
  23.0 2.2 %copy-done.1 = bf16[2048,1024]{1,0:T(8,128)(2,1)S(1)} copy-done((bf16[2048,1024]{1,0:T(8,128)(2,1)S(1)}, bf16[2048,1024]{1,0:T(8,128)(2,1)}, u32[]{:S(2)}) %copy-start.1) | copy-done | bytes 4194328
  25.2 4.9 %shard_map.47 = (bf16[2048,256]{1,0:T(8,128)(2,1)S(1)}, bf16[2048,256]{1,0:T(8,128)(2,1)S(1)}, bf16[2048,256]{1,0:T(8,128)(2,1)S(1)}, bf16[2048,256]{1,0:T(8,128...) custom-call(s32[8]{0:T(128)S(1)} %pad_add_fusion.2.want_ref, ...), custom_call_target="tpu_custom_call" | custom-call | bytes 16777216 | tf_op jit(solution)/shard_map/pallas_call | solution.py:87
  30.2 1.0 copy-done.6
  31.1 1.0 copy-done.7
  32.2 1.0 copy-done.8
  33.3 5.2 %collective-permute-start.6 = (bf16[2048,256]{1,0:T(8,128)(2,1)S(1)}, bf16[2048,256]{1,0:T(8,128)(2,1)}, u32[]{:S(2)}, u32[]{:S(2)}) collective-permute-start(bf16[2048,256]{1,0:T(8,128)(2,1)S(1)} %get-tuple-element.28), channel_id=1, source_target_pairs={{0,63},{1,2},{2,1},{3,4},{4,3},{5,6},{6,5},{7,8},{8,7},{9,10},{10,... | collective-permute-start | bytes 3145736 | tf_op jit(solution)/shard_map/ppermute | solution.py:41
  39.1 2.2 %copy-done.2 = bf16[2048,1024]{1,0:T(8,128)(2,1)S(1)} copy-done((bf16[2048,1024]{1,0:T(8,128)(2,1)S(1)}, bf16[2048,1024]{1,0:T(8,128)(2,1)}, u32[]{:S(2)}) %copy-start.2) | copy-done | bytes 4194328
  41.3 12.4 %shard_map.46 = (bf16[1024,2048]{1,0:T(8,128)(2,1)S(1)}, f32[4,1032,256]{2,1,0:T(8,128)S(1)}) custom-call(bf16[2048,1024]{1,0:T(8,128)(2,1)S(1)} %copy-done.2), custom_call_target="tpu_custom_call" | custom-call | flops 4294967296 | bytes 10485760 | tf_op jit(solution)/shard_map/pallas_call | solution.py:134
  53.7 1.9 %copy-done = f32[4,1032,256]{2,1,0:T(8,128)} copy-done((f32[4,1032,256]{2,1,0:T(8,128)}, f32[4,1032,256]{2,1,0:T(8,128)S(1)}, u32[]{:S(2)}) %copy-start) | copy-done | bytes 4227096
  55.6 7.3 %collective-permute-done.4.refs_0_ = bf16[2048,256]{1,0:T(8,128)(2,1)} collective-permute-done((bf16[2048,256]{1,0:T(8,128)(2,1)}, bf16[2048,256]{1,0:T(8,128)(2,1)}, u32[]{:S(2)}, u32[]{:S(2)}) %collective-permute-start.4) | collective-permute-done | bytes 1048608 | tf_op jit(solution)/shard_map/ppermute | solution.py:41
  62.9 10.9 %collective-permute-done.6.refs_2_ = bf16[2048,256]{1,0:T(8,128)(2,1)} collective-permute-done((bf16[2048,256]{1,0:T(8,128)(2,1)S(1)}, bf16[2048,256]{1,0:T(8,128)(2,1)}, u32[]{:S(2)}, u32[]{:S(2)}) %collective-permute-start.6) | collective-permute-done | bytes 1048608 | tf_op jit(solution)/shard_map/ppermute | solution.py:41
  73.8 9.0 %shard_map.48 = (f32[1032,128]{1,0:T(8,128)S(1)}, f32[1032,128]{1,0:T(8,128)S(1)}, f32[1032,128]{1,0:T(8,128)S(1)}, f32[1032,128]{1,0:T(8,128)S(1)}) custom-call(s32[16]{0:T(128)S(1)} %reshape.145.slot_ref, s32[4]{0:T(128)S(1)} %and_select_fusion.dest_ref, bf16[1024,2048]{1,0:T(8,128)(2,1)S(1)} %get-tuple-element.25.at_ref, ...), custom_call_target="tpu_custom_call" | custom-call | flops 4294967296 | bytes 10485760 | tf_op jit(solution)/shard_map/pallas_call | solution.py:185
  83.0 5.2 %collective-permute-start.10 = (bf16[2048,256]{1,0:T(8,128)(2,1)S(1)}, bf16[2048,256]{1,0:T(8,128)(2,1)S(1)}, u32[]{:S(2)}, u32[]{:S(2)}) collective-permute-start(bf16[2048,256]{1,0:T(8,128)(2,1)S(1)} %get-tuple-element.34), channel_id=1, source_target_pairs={{0,62},{1,63},{2,0},{3,1},{4,2},{5,3},{6,4},{7,5},{8,6},{9,7},{10,... | collective-permute-start | bytes 3145736 | tf_op jit(solution)/shard_map/ppermute | solution.py:41
  88.3 1.6 collective-permute-start.14
  89.9 16.3 %collective-permute-done.14 = f32[1032,128]{1,0:T(8,128)S(1)} collective-permute-done((f32[1032,128]{1,0:T(8,128)S(1)}, f32[1032,128]{1,0:T(8,128)S(1)}, u32[]{:S(2)}, u32[]{:S(2)}) %collective-permute-start.14) | collective-permute-done | bytes 528416 | tf_op jit(solution)/shard_map/ppermute | solution.py:49
  106.3 1.6 collective-permute-start.15
  108.0 4.6 %collective-permute-done.8.refs_0_ = bf16[2048,256]{1,0:T(8,128)(2,1)S(1)} collective-permute-done((bf16[2048,256]{1,0:T(8,128)(2,1)}, bf16[2048,256]{1,0:T(8,128)(2,1)S(1)}, u32[]{:S(2)}, u32[]{:S(2)}) %collective-permute-start.8) | collective-permute-done | bytes 1048608 | tf_op jit(solution)/shard_map/ppermute | solution.py:41
  112.6 4.7 %collective-permute-done.9.refs_2_ = bf16[2048,256]{1,0:T(8,128)(2,1)S(1)} collective-permute-done((bf16[2048,256]{1,0:T(8,128)(2,1)}, bf16[2048,256]{1,0:T(8,128)(2,1)S(1)}, u32[]{:S(2)}, u32[]{:S(2)}) %collective-permute-start.9) | collective-permute-done | bytes 1048608 | tf_op jit(solution)/shard_map/ppermute | solution.py:41
  118.0 2.2 %copy-done.10 = bf16[1024,2048]{1,0:T(8,128)(2,1)S(1)} copy-done((bf16[1024,2048]{1,0:T(8,128)(2,1)S(1)}, bf16[1024,2048]{1,0:T(8,128)(2,1)}, u32[]{:S(2)}) %copy-start.10) | copy-done | bytes 4194328
  120.2 8.1 %shard_map.49 = (f32[1032,128]{1,0:T(8,128)S(1)}, f32[1032,128]{1,0:T(8,128)S(1)}, f32[1032,128]{1,0:T(8,128)S(1)}, f32[1032,128]{1,0:T(8,128)S(1)}) custom-call(s32[16]{0:T(128)S(1)} %reshape.145.slot_ref, s32[4]{0:T(128)S(1)} %and_select_fusion.1.dest_ref, bf16[1024,2048]{1,0:T(8,128)(2,1)S(1)} %copy-done.10, ...), custom_call_target="tpu_custom_call" | custom-call | flops 4294967296 | bytes 10485760 | tf_op jit(solution)/shard_map/pallas_call | solution.py:185
  128.4 0.8 copy-done.3
  129.2 1.6 collective-permute-start.11
  130.8 1.0 collective-permute-start.12
  131.7 2.4 %collective-permute-start.13 = (f32[1032,128]{1,0:T(8,128)S(1)}, f32[1032,128]{1,0:T(8,128)}, u32[]{:S(2)}, u32[]{:S(2)}) collective-permute-start(f32[1032,128]{1,0:T(8,128)S(1)} %get-tuple-element.38), channel_id=1, source_target_pairs={{0,192},{64,0},{128,64},{192,128},{1,193},{65,1},{129,65},{193,129... | collective-permute-start | bytes 1585160 | tf_op jit(solution)/shard_map/ppermute | solution.py:27
  134.1 0.8 add.166
  136.8 28.7 %collective-permute-done.16 = f32[1032,128]{1,0:T(8,128)S(1)} collective-permute-done((f32[1032,128]{1,0:T(8,128)}, f32[1032,128]{1,0:T(8,128)S(1)}, u32[]{:S(2)}, u32[]{:S(2)}) %collective-permute-start.16) | collective-permute-done | bytes 528416 | tf_op jit(solution)/shard_map/ppermute | solution.py:49
  165.5 0.9 add.167.refs_0_
  166.4 4.2 %shard_map.50.refs_4_ = f32[2048,256]{1,0:T(8,128)} custom-call(s32[32]{0:T(128)} %add.148.place_ref, s32[16]{0:T(128)} %copy-done.4, s32[4]{0:T(128)} %copy-done.5, f32[32]{0:T(128)} %reshape.146.taper_ref, f32[1032,256]{1,0:T(8,128)} %reduce-scatter.2.cloned.1.call-done.own_ref, f32[1032,128]{1,0:T(8,128)} %add.167.refs_0_), custom_call_target="tpu_custom_call" | custom-call | flops 1048576 | bytes 4194304 | tf_op jit(solution)/shard_map/pallas_call | solution.py:230
  170.5 4.7 %shard_map.51 = f32[2048,256]{1,0:T(8,128)} custom-call(s32[32]{0:T(128)} %add.148.place_ref, s32[16]{0:T(128)} %copy-done.4, s32[4]{0:T(128)} %copy-done.5, f32[32]{0:T(128)} %reshape.146.taper_ref, f32[1032,256]{1,0:T(8,128)} %reduce-scatter.2.cloned.1.call-done.own_ref, f32[1032,128]{1,0:T(8,128)} %copy-done.3, ...), custom_call_target="tpu_custom_call", output_to_operand_aliasing={{}: (9, {})} | custom-call | flops 1048576 | bytes 4194304 | tf_op jit(solution)/shard_map/pallas_call | solution.py:230
  (70 shorter events, 5.2 us)
Async XLA Ops:
  6.5 159.8 %reduce-scatter.2.cloned.1.call-start = ((), (), s32[]{:S(2)}) async-start(), calls=%async_computation.1 | async-start | bytes 5283840 | tf_op jit(solution)/shard_map/reduce_scatter | solution.py:298
  8.0 12.4 %collective-permute-start = (s32[2]{0:T(128)S(1)}, s32[2]{0:T(128)S(1)}, u32[]{:S(2)}, u32[]{:S(2)}) collective-permute-start(s32[2]{0:T(128)S(1)} %get-tuple-element.43), channel_id=1, source_target_pairs={{0,62},{1,63},{2,0},{3,1},{4,2},{5,3},{6,4},{7,5},{8,6},{9,7},{10,... | collective-permute-start | bytes 32 | tf_op jit(solution)/shard_map/ppermute | solution.py:41
  16.1 6.9 %collective-permute-start.3 = (s32[2]{0:T(128)S(1)}, s32[2]{0:T(128)S(1)}, u32[]{:S(2)}, u32[]{:S(2)}) collective-permute-start(s32[2]{0:T(128)S(1)} %get-tuple-element.44), channel_id=1, source_target_pairs={{0,2},{1,3},{2,4},{3,5},{4,6},{5,7},{6,8},{7,9},{8,10},{9,11},{10,... | collective-permute-start | bytes 32 | tf_op jit(solution)/shard_map/ppermute | solution.py:41
  16.1 6.9 %collective-permute-start.2 = (s32[2]{0:T(128)S(1)}, s32[2]{0:T(128)S(1)}, u32[]{:S(2)}, u32[]{:S(2)}) collective-permute-start(s32[2]{0:T(128)S(1)} %get-tuple-element.45), channel_id=1, source_target_pairs={{0,63},{1,2},{2,1},{3,4},{4,3},{5,6},{6,5},{7,8},{8,7},{9,10},{10,... | collective-permute-start | bytes 32 | tf_op jit(solution)/shard_map/ppermute | solution.py:41
  20.3 2.6 %collective-permute-start.1 = (s32[2]{0:T(128)S(1)}, s32[2]{0:T(128)S(1)}, u32[]{:S(2)}, u32[]{:S(2)}) collective-permute-start(s32[2]{0:T(128)S(1)} %get-tuple-element.46), channel_id=1, source_target_pairs={{0,1},{1,0},{2,3},{3,2},{4,5},{5,4},{6,7},{7,6},{8,9},{9,8},{10,11... | collective-permute-start | bytes 32 | tf_op jit(solution)/shard_map/ppermute | solution.py:41
  23.0 2.2 %copy-start.1 = (bf16[2048,1024]{1,0:T(8,128)(2,1)S(1)}, bf16[2048,1024]{1,0:T(8,128)(2,1)}, u32[]{:S(2)}) copy-start(bf16[2048,1024]{1,0:T(8,128)(2,1)} %source_ref.1) | copy-start | bytes 12582916
  25.2 13.6 %copy-start.11 = (s32[4,8]{1,0:T(4,128)S(1)}, s32[4,8]{1,0:T(4,128)}, u32[]{:S(2)}) copy-start(s32[4,8]{1,0:T(4,128)} %param.5) | copy-start | bytes 388
  25.2 13.8 %copy-start.13 = (s32[4]{0:T(128)S(1)}, s32[4]{0:T(128)}, u32[]{:S(2)}) copy-start(s32[4]{0:T(128)} %constant.131.clone) | copy-start | bytes 52
  30.1 1.0 copy-start.6
  31.1 1.0 copy-start.7
  32.2 1.0 copy-start.8
  33.2 40.6 %collective-permute-start.5 = (bf16[2048,512]{1,0:T(8,128)(2,1)}, bf16[2048,512]{1,0:T(8,128)(2,1)}, u32[]{:S(2)}, u32[]{:S(2)}) collective-permute-start(bf16[2048,512]{1,0:T(8,128)(2,1)} %get-tuple-element.27), channel_id=1, source_target_pairs={{0,1},{1,0},{2,3},{3,2},{4,5},{5,4},{6,7},{7,6},{8,9},{9,8},{10,11... | collective-permute-start | bytes 6291464 | tf_op jit(solution)/shard_map/ppermute | solution.py:41
  33.3 29.6 %collective-permute-start.4 = (bf16[2048,256]{1,0:T(8,128)(2,1)}, bf16[2048,256]{1,0:T(8,128)(2,1)}, u32[]{:S(2)}, u32[]{:S(2)}) collective-permute-start(bf16[2048,256]{1,0:T(8,128)(2,1)} %copy-done.8), channel_id=1, source_target_pairs={{0,2},{1,3},{2,4},{3,5},{4,6},{5,7},{6,8},{7,9},{8,10},{9,11},{10,... | collective-permute-start | bytes 3145736 | tf_op jit(solution)/shard_map/ppermute | solution.py:41
  33.3 40.5 %collective-permute-start.6 = (bf16[2048,256]{1,0:T(8,128)(2,1)S(1)}, bf16[2048,256]{1,0:T(8,128)(2,1)}, u32[]{:S(2)}, u32[]{:S(2)}) collective-permute-start(bf16[2048,256]{1,0:T(8,128)(2,1)S(1)} %get-tuple-element.28), channel_id=1, source_target_pairs={{0,63},{1,2},{2,1},{3,4},{4,3},{5,6},{6,5},{7,8},{8,7},{9,10},{10,... | collective-permute-start | bytes 3145736 | tf_op jit(solution)/shard_map/ppermute | solution.py:41
  38.5 35.3 %collective-permute-start.7 = (bf16[2048,256]{1,0:T(8,128)(2,1)S(1)}, bf16[2048,256]{1,0:T(8,128)(2,1)}, u32[]{:S(2)}, u32[]{:S(2)}) collective-permute-start(bf16[2048,256]{1,0:T(8,128)(2,1)S(1)} %get-tuple-element.29), channel_id=1, source_target_pairs={{0,62},{1,63},{2,0},{3,1},{4,2},{5,3},{6,4},{7,5},{8,6},{9,7},{10,... | collective-permute-start | bytes 3145736 | tf_op jit(solution)/shard_map/ppermute | solution.py:41
  39.0 79.0 %copy-start.4 = (s32[16]{0:T(128)}, s32[16]{0:T(128)S(1)}, u32[]{:S(2)}) copy-start(s32[16]{0:T(128)S(1)} %reshape.145.slot_ref) | copy-start | bytes 196
  39.1 2.2 %copy-start.2 = (bf16[2048,1024]{1,0:T(8,128)(2,1)S(1)}, bf16[2048,1024]{1,0:T(8,128)(2,1)}, u32[]{:S(2)}) copy-start(bf16[2048,1024]{1,0:T(8,128)(2,1)} %source_ref.1) | copy-start | bytes 12582916
  53.7 1.9 %copy-start = (f32[4,1032,256]{2,1,0:T(8,128)}, f32[4,1032,256]{2,1,0:T(8,128)S(1)}, u32[]{:S(2)}) copy-start(f32[4,1032,256]{2,1,0:T(8,128)S(1)} %get-tuple-element.31) | copy-start | bytes 12681220
  55.6 27.2 %copy-start.9 = (bf16[1024,2048]{1,0:T(8,128)(2,1)}, bf16[1024,2048]{1,0:T(8,128)(2,1)S(1)}, u32[]{:S(2)}) copy-start(bf16[1024,2048]{1,0:T(8,128)(2,1)S(1)} %get-tuple-element.25.at_ref) | copy-start | bytes 12582916
  82.9 29.7 %collective-permute-start.8 = (bf16[2048,256]{1,0:T(8,128)(2,1)}, bf16[2048,256]{1,0:T(8,128)(2,1)S(1)}, u32[]{:S(2)}, u32[]{:S(2)}) collective-permute-start(bf16[2048,256]{1,0:T(8,128)(2,1)} %copy-done.7), channel_id=1, source_target_pairs={{0,2},{1,3},{2,4},{3,5},{4,6},{5,7},{6,8},{7,9},{8,10},{9,11},{10,... | collective-permute-start | bytes 3145736 | tf_op jit(solution)/shard_map/ppermute | solution.py:41
  82.9 34.3 %collective-permute-start.9 = (bf16[2048,256]{1,0:T(8,128)(2,1)}, bf16[2048,256]{1,0:T(8,128)(2,1)S(1)}, u32[]{:S(2)}, u32[]{:S(2)}) collective-permute-start(bf16[2048,256]{1,0:T(8,128)(2,1)} %copy-done.6), channel_id=1, source_target_pairs={{0,63},{1,2},{2,1},{3,4},{4,3},{5,6},{6,5},{7,8},{8,7},{9,10},{10,... | collective-permute-start | bytes 3145736 | tf_op jit(solution)/shard_map/ppermute | solution.py:41
  83.0 35.0 %collective-permute-start.10 = (bf16[2048,256]{1,0:T(8,128)(2,1)S(1)}, bf16[2048,256]{1,0:T(8,128)(2,1)S(1)}, u32[]{:S(2)}, u32[]{:S(2)}) collective-permute-start(bf16[2048,256]{1,0:T(8,128)(2,1)S(1)} %get-tuple-element.34), channel_id=1, source_target_pairs={{0,62},{1,63},{2,0},{3,1},{4,2},{5,3},{6,4},{7,5},{8,6},{9,7},{10,... | collective-permute-start | bytes 3145736 | tf_op jit(solution)/shard_map/ppermute | solution.py:41
  88.3 17.9 %collective-permute-start.14 = (f32[1032,128]{1,0:T(8,128)S(1)}, f32[1032,128]{1,0:T(8,128)S(1)}, u32[]{:S(2)}, u32[]{:S(2)}) collective-permute-start(f32[1032,128]{1,0:T(8,128)S(1)} %get-tuple-element.39), channel_id=1, source_target_pairs={{0,64},{1,193},{2,66},{3,195},{4,68},{5,197},{6,70},{7,199},{8,72}... | collective-permute-start | bytes 1585160 | tf_op jit(solution)/shard_map/ppermute | solution.py:49
  106.3 27.9 %collective-permute-start.15 = (f32[1032,128]{1,0:T(8,128)S(1)}, f32[1032,128]{1,0:T(8,128)S(1)}, u32[]{:S(2)}, u32[]{:S(2)}) collective-permute-start(f32[1032,128]{1,0:T(8,128)S(1)} %add.165), channel_id=1, source_target_pairs={{0,64},{1,193},{2,66},{3,195},{4,68},{5,197},{6,70},{7,199},{8,72}... | collective-permute-start | bytes 1585160 | tf_op jit(solution)/shard_map/ppermute | solution.py:49
  107.9 27.1 %copy-start.12 = (s32[4,8]{1,0:T(4,128)S(1)}, s32[4,8]{1,0:T(4,128)}, u32[]{:S(2)}) copy-start(s32[4,8]{1,0:T(4,128)} %param.6) | copy-start | bytes 388
  107.9 20.4 %copy-start.5 = (s32[4]{0:T(128)}, s32[4]{0:T(128)S(1)}, u32[]{:S(2)}) copy-start(s32[4]{0:T(128)S(1)} %and_select_fusion.1.dest_ref) | copy-start | bytes 52
  118.0 2.2 %copy-start.10 = (bf16[1024,2048]{1,0:T(8,128)(2,1)S(1)}, bf16[1024,2048]{1,0:T(8,128)(2,1)}, u32[]{:S(2)}) copy-start(bf16[1024,2048]{1,0:T(8,128)(2,1)} %copy-done.9) | copy-start | bytes 12582916
  128.4 0.8 copy-start.3
  129.2 41.3 %collective-permute-start.11 = (f32[1032,128]{1,0:T(8,128)S(1)}, f32[1032,128]{1,0:T(8,128)}, u32[]{:S(2)}, u32[]{:S(2)}) collective-permute-start(f32[1032,128]{1,0:T(8,128)S(1)} %get-tuple-element.36), channel_id=1, source_target_pairs={{0,64},{64,128},{128,192},{192,0},{1,65},{65,129},{129,193},{193,1... | collective-permute-start | bytes 1585160 | tf_op jit(solution)/shard_map/ppermute | solution.py:27
  130.8 39.8 %collective-permute-start.12 = (f32[1032,128]{1,0:T(8,128)S(1)}, f32[1032,128]{1,0:T(8,128)}, u32[]{:S(2)}, u32[]{:S(2)}) collective-permute-start(f32[1032,128]{1,0:T(8,128)S(1)} %get-tuple-element.37), channel_id=1, source_target_pairs={{0,128},{64,192},{128,0},{192,64},{1,129},{65,193},{129,1},{193,65... | collective-permute-start | bytes 1585160 | tf_op jit(solution)/shard_map/ppermute | solution.py:27
  131.7 38.8 %collective-permute-start.13 = (f32[1032,128]{1,0:T(8,128)S(1)}, f32[1032,128]{1,0:T(8,128)}, u32[]{:S(2)}, u32[]{:S(2)}) collective-permute-start(f32[1032,128]{1,0:T(8,128)S(1)} %get-tuple-element.38), channel_id=1, source_target_pairs={{0,192},{64,0},{128,64},{192,128},{1,193},{65,1},{129,65},{193,129... | collective-permute-start | bytes 1585160 | tf_op jit(solution)/shard_map/ppermute | solution.py:27
  135.0 30.5 %collective-permute-start.16 = (f32[1032,128]{1,0:T(8,128)}, f32[1032,128]{1,0:T(8,128)S(1)}, u32[]{:S(2)}, u32[]{:S(2)}) collective-permute-start(f32[1032,128]{1,0:T(8,128)} %add.166), channel_id=1, source_target_pairs={{0,64},{1,193},{2,66},{3,195},{4,68},{5,197},{6,70},{7,199},{8,72}... | collective-permute-start | bytes 1585160 | tf_op jit(solution)/shard_map/ppermute | solution.py:49
Sparse Core Ops, SparseCore 0:
  83.0 72.1 reduce-scatter.1

commit v3 on v2

--- a/solution.py
+++ b/solution.py
@@ -19,6 +19,7 @@
 
 EPSILON = 1e-06
 MIB = 1 << 20
+BIG = 58 * MIB
 
 
 def passed_along(value, axis, steps):
@@ -98,101 +99,122 @@
             ],
         ),
         out_shape=[jax.ShapeDtypeStruct((samples, width), perturb.dtype) for width in widths],
-        compiler_params=pltpu.CompilerParams(vmem_limit_bytes=16 * MIB),
+        compiler_params=pltpu.CompilerParams(vmem_limit_bytes=BIG),
         cost_estimate=pl.CostEstimate(flops=0, bytes_accessed=MIB * len(plan), transcendentals=0),
     )(want, perturb)
 
 
-def own_kernel(x_ref, at_ref, part_ref):
+def own_kernel(x_ref, row_ref, at_ref, part_ref):
     samp = part_ref.shape[0]
     rows = BS // samp
-    for r in range(B_DEV):
-        at_ref[r * BS : (r + 1) * BS, :] = jnp.transpose(x_ref[:, r * BS : (r + 1) * BS])
-
-    @pl.loop(0, B_DEV)
-    def _(r):
-        at = at_ref[pl.ds(pl.multiple_of(r * BS, BS), BS), :]
-        for c in range(B_DEV):
-            tile = jnp.dot(at, x_ref[:, c * BS : (c + 1) * BS], preferred_element_type=jnp.float32)
+    r = pl.program_id(0)
+    at_ref[...] = jnp.transpose(row_ref[...])
+    at = at_ref[...]
+    for c in range(B_DEV):
+        tile = jnp.dot(at, x_ref[:, c * BS : (c + 1) * BS], preferred_element_type=jnp.float32)
+        for y in range(samp):
+            part_ref[y, c * rows : (c + 1) * rows, :] = tile[y * rows : (y + 1) * rows]
+
+        @pl.when(r == c)
+        def _():
+            here = lax.broadcasted_iota(jnp.int32, (BS, BS), 0) == lax.broadcasted_iota(jnp.int32, (BS, BS), 1)
+            norm = jnp.sum(jnp.where(here, tile, 0.0), axis=0, keepdims=True)
             for y in range(samp):
-                where = pl.ds(pl.multiple_of((r * B_DEV + c) * rows, rows), rows)
-                part_ref[y, where, :] = tile[y * rows : (y + 1) * rows]
-
-            @pl.when(r == c)
-            def _():
-                here = lax.broadcasted_iota(jnp.int32, (BS, BS), 0) == lax.broadcasted_iota(jnp.int32, (BS, BS), 1)
-                norm = jnp.sum(jnp.where(here, tile, 0.0), axis=0, keepdims=True)
-                for y in range(samp):
-                    part_ref[y, 16 * rows + c : 16 * rows + c + 1, :] = norm
-
-    for y in range(samp):
-        part_ref[y, 16 * rows + B_DEV :, :] = jnp.zeros((EXTRA - B_DEV, BS), jnp.float32)
+                part_ref[y, BS : BS + EXTRA, :] = jnp.broadcast_to(norm, (EXTRA, BS))
 
 
 def own_tiles(perturb, samp):
     samples, cells = perturb.shape
+    block = BS + EXTRA
     return pl.pallas_call(
         own_kernel,
+        grid=(B_DEV,),
+        in_specs=[
+            pl.BlockSpec((samples, cells), lambda r: (0, 0)),
+            pl.BlockSpec((samples, BS), lambda r: (0, r)),
+        ],
+        out_specs=[
+            pl.BlockSpec((BS, samples), lambda r: (r, 0)),
+            pl.BlockSpec((samp, block, BS), lambda r: (0, r, 0)),
+        ],
         out_shape=[
             jax.ShapeDtypeStruct((cells, samples), perturb.dtype),
-            jax.ShapeDtypeStruct((samp, 16 * BS // samp + EXTRA, BS), jnp.float32),
+            jax.ShapeDtypeStruct((samp, B_DEV * block, BS), jnp.float32),
         ],
-        compiler_params=pltpu.CompilerParams(vmem_limit_bytes=40 * MIB),
-        cost_estimate=pl.CostEstimate(flops=2 * cells * cells * samples, bytes_accessed=10 * MIB, transcendentals=0),
-    )(perturb)
-
-
-def remote_kernel(slot_ref, dest_ref, at_ref, *refs):
-    blocks, parts, all_ref = refs[:4], refs[4:-1], refs[-1]
+        compiler_params=pltpu.CompilerParams(vmem_limit_bytes=BIG),
+        cost_estimate=pl.CostEstimate(flops=2 * cells * cells * samples, bytes_accessed=12 * MIB, transcendentals=0),
+    )(perturb, perturb)
+
+
+def remote_kernel(stage, slot_ref, dest_ref, at_ref, *refs):
+    blocks, parts, cols_ref, sems = refs[:4], refs[4:-2], refs[-2], refs[-1]
     samp = len(parts)
-    samples = blocks[0].shape[0]
+    samples = cols_ref.shape[1]
     rows = BS // samp
     r = pl.program_id(0)
+
+    @pl.when(r == 0)
+    def _():
+        copies = []
+        for q in range(4):
+            for side in range(2):
+                column = (2 * stage if q == 1 else 0) + side
+                copies.append(
+                    pltpu.make_async_copy(
+                        blocks[q].at[:, pl.ds(column * HALF, HALF)],
+                        cols_ref.at[2 * q + side],
+                        sems.at[2 * q + side],
+                    )
+                )
+        for copy in copies:
+            copy.start()
+        for copy in copies:
+            copy.wait()
+
     at = at_ref[...]
-    for q in range(4):
-        tile = jnp.dot(at, blocks[q][...], preferred_element_type=jnp.float32)
-        all_ref[2 * q] = tile[:, :HALF]
-        all_ref[2 * q + 1] = tile[:, HALF:]
-    for j in range(4):
-        u = r * 4 + j
-        place = pl.ds(pl.multiple_of(u * rows, rows), rows)
+    for pair in range(2):
+        u = r * 4 + 2 * pair
+        cols = jnp.concatenate([cols_ref[slot_ref[u]], cols_ref[slot_ref[u + 1]]], axis=1)
+        tile = jnp.dot(at, cols, preferred_element_type=jnp.float32)
+        for side in range(2):
+            j = 2 * pair + side
+            for d in range(samp):
+                for y in range(samp):
+
+                    @pl.when(dest_ref[d] == y)
+                    def _():
+                        parts[d][j * rows : (j + 1) * rows, :] = tile[
+                            y * rows : (y + 1) * rows, side * HALF : (side + 1) * HALF
+                        ]
+
+    step = 128
+    for side in range(2):
+        def add(i, total):
+            x = cols_ref[2 * r + side, pl.ds(pl.multiple_of(i * step, step), step), :].astype(jnp.float32)
+            return total + jnp.sum((x * x).reshape(step // 8, 8, HALF), axis=0)
+
+        total = lax.fori_loop(0, samples // step, add, jnp.zeros((8, HALF), jnp.float32))
+        norm = jnp.sum(total, axis=0, keepdims=True)
         for d in range(samp):
-            first = pl.multiple_of(dest_ref[d] * rows, rows)
-            parts[d][place, :] = all_ref[slot_ref[u], pl.ds(first, rows), :]
-
-    step = 128
-    for q in range(4):
-
-        @pl.when(r == q)
-        def _():
-            def add(i, total):
-                x = blocks[q][pl.ds(pl.multiple_of(i * step, step), step), :].astype(jnp.float32)
-                return total + jnp.sum((x * x).reshape(step // 8, 8, 2 * HALF), axis=0)
-
-            total = lax.fori_loop(0, samples // step, add, jnp.zeros((8, 2 * HALF), jnp.float32))
-            norm = jnp.sum(total, axis=0, keepdims=True)
-            for side in range(2):
-                at_row = 16 * rows + 2 * q + side
-                for d in range(samp):
-                    parts[d][at_row : at_row + 1, :] = norm[:, side * HALF : (side + 1) * HALF]
+            parts[d][BS + side * 4 : BS + side * 4 + 4, :] = jnp.broadcast_to(norm, (4, HALF))
 
 
 def remote_tiles(stage, slots, dest, at, blocks, samp):
     cells, samples = at.shape
-    full = lambda shape: pl.BlockSpec(shape, lambda i, *s: (0,) * len(shape))
-    shape = (16 * BS // samp + EXTRA, HALF)
-    block = lambda q: pl.BlockSpec((samples, 2 * HALF), lambda i, *s: (0, stage if q == 1 else 0))
+    block = BS + EXTRA
+    out_specs = [pl.BlockSpec((block, HALF), lambda r, *s: (r, 0))] * samp
+    out_shape = [jax.ShapeDtypeStruct((B_DEV * block, HALF), jnp.float32)] * samp
     return pl.pallas_call(
-        remote_kernel,
+        functools.partial(remote_kernel, stage),
         grid_spec=pltpu.PrefetchScalarGridSpec(
             num_scalar_prefetch=2,
             grid=(B_DEV,),
-            in_specs=[pl.BlockSpec((BS, samples), lambda i, *s: (i, 0))] + [block(q) for q in range(4)],
-            out_specs=[full(shape)] * samp,
-            scratch_shapes=[pltpu.VMEM((8, BS, HALF), jnp.float32)],
+            in_specs=[pl.BlockSpec((BS, samples), lambda r, *s: (r, 0))] + [pl.BlockSpec(memory_space=pl.ANY)] * 4,
+            out_specs=out_specs,
+            scratch_shapes=[pltpu.VMEM((8, samples, HALF), at.dtype), pltpu.SemaphoreType.DMA((8,))],
         ),
-        out_shape=[jax.ShapeDtypeStruct(shape, jnp.float32)] * samp,
-        compiler_params=pltpu.CompilerParams(vmem_limit_bytes=30 * MIB),
+        out_shape=out_shape,
+        compiler_params=pltpu.CompilerParams(vmem_limit_bytes=BIG),
         cost_estimate=pl.CostEstimate(flops=2 * cells * cells * samples, bytes_accessed=10 * MIB, transcendentals=0),
     )(slots, dest, at, *blocks)
 
@@ -205,22 +227,25 @@
     lane = lax.broadcasted_iota(jnp.int32, (rows, BS), 1)
     row = lax.broadcasted_iota(jnp.int32, (rows, BS), 0)
     mine = lane == row + first
+    block = BS + EXTRA
     for r in range(B_DEV):
-        row_norm = own_ref[16 * rows + r : 16 * rows + r + 1, :]
+        base = r * block
+        row_norm = own_ref[base + BS : base + BS + 1, :]
         row_norm = jnp.sum(jnp.where(mine, row_norm, 0.0), axis=1, keepdims=True)
         row_scale = jnp.broadcast_to(lax.rsqrt(row_norm + EPSILON), (rows, HALF))
         for j in range(4):
             u = r * 4 + j
-            norm = own_ref[16 * rows + j : 16 * rows + j + 1, cols]
+            norm = own_ref[j * block + BS : j * block + BS + 1, cols]
             col_scale = taper_ref[u] * lax.rsqrt(norm + EPSILON)
-            tile = own_ref[u * rows : (u + 1) * rows, cols]
+            tile = own_ref[base + j * rows : base + (j + 1) * rows, cols]
             out_ref[pl.ds(place_ref[u], rows, stride=PAIR_DEV), :] = tile * row_scale * col_scale
         for j in range(4):
             u = r * 4 + j
-            at_norm = pl.ds(16 * rows + slot_ref[u], 1)
+            slot = slot_ref[u]
+            at_norm = pl.ds(slot // 2 * block + BS + slot % 2 * 4, 1)
             norm = sum(ref[at_norm, :] for ref in rem_refs)
             col_scale = taper_ref[16 + u] * lax.rsqrt(norm + EPSILON)
-            tile = sum(ref[u * rows : (u + 1) * rows, :] for ref in rem_refs)
+            tile = sum(ref[base + j * rows : base + (j + 1) * rows, :] for ref in rem_refs)
             out_ref[pl.ds(place_ref[16 + u], rows, stride=PAIR_DEV), :] = tile * row_scale * col_scale
 
 
@@ -260,7 +285,9 @@
     low = jnp.min(jnp.where(need, four[None], B_DEV - 1), axis=1)
     high = jnp.max(jnp.where(need, four[None], 0), axis=1)
     want = jnp.stack([low, high], axis=1)
+    at, own_part = own_tiles(perturb, samp)
     asked = jnp.concatenate([exchanged(want[q], q, back=True) for q in range(4)])
+    asked, at, own_part = lax.optimization_barrier((asked, at, own_part))
     chosen = select(asked, perturb)
     mates = exchanged(chosen[6], 1)
     got = []
@@ -286,20 +313,16 @@
     slots = pick(is_rem, slot[:, :, None]).reshape(-1)
 
     rows = BS // samp
-    size = 16 * rows + EXTRA
+    size = B_DEV * (BS + EXTRA)
     me = lax.axis_index("samp")
     ahead = 1 - 2 * (here % 2)
     ring_dest = (me + ahead * jnp.array([-1, -2, 1, 0], jnp.int32) + 2 * samp) % samp
     dest = (me + jnp.arange(samp, dtype=jnp.int32)) % samp
-    at, own_part = own_tiles(perturb, samp)
-
-    parts = list(remote_tiles(0, slots, ring_dest, at, got[0], samp))
-    own_part, parts[0] = lax.optimization_barrier((own_part, parts[0]))
     own_sum = lax.psum_scatter(own_part.reshape(samp * size, BS), "samp", scatter_dimension=0, tiled=True)
+    parts = remote_tiles(0, slots, ring_dest, at, got[0], samp)
     running = parts[0]
     for d in range(1, samp):
         running = ringed(running) + parts[d]
-
     parts = remote_tiles(1, slots, dest, at, got[1], samp)
     last = [parts[0]] + [passed_along(parts[d], "samp", d) for d in range(1, samp)]
 

time: 183 us -> 194 us (1.060)
  the two profiles are of different devices: /device:TPU:8 before, /device:TPU:1 now
where the time goes in v3:
time: 194 us
  waiting for transfers between devices  73.3 us (38%)
  Pallas kernels  62.2 us (32%)
  starting transfers between devices  33.2 us (17%)
  between operations  13.6 us (7%)
  local copies, waits for them, and re-layouts  5.76 us (3%)
  other arithmetic  5.66 us (3%)
    ppermute x11, waiting for transfers between devices, exchanged(): return lax.ppermute(value, 'blk', sorted(pairs))  38.7 us
    ppermute x3, waiting for transfers between devices, ringed(): return lax.ppermute(value, ('samp', 'blk'), pairs)  34.7 us
    pallas_call x2, Pallas kernels, remote_tiles(): pl.pallas_call(functools.partial(remote_kernel, stage), grid_spec=pltpu.P...  30.2 us
    ppermute x11, starting transfers between devices, exchanged(): return lax.ppermute(value, 'blk', sorted(pairs))  23.6 us
    pallas_call x1, Pallas kernels, own_tiles(): pl.pallas_call(own_kernel, grid=(B_DEV,), in_specs=[pl.BlockSpec((samples...  15.2 us
    pallas_call x2, Pallas kernels, final(): pl.pallas_call(functools.partial(final_kernel, half, len(rems)), grid_spe...  8.86 us
    pallas_call x1, Pallas kernels, select(): pl.pallas_call(functools.partial(select_kernel, plan), grid_spec=pltpu.Pr...  7.93 us
    ppermute x3, starting transfers between devices, ringed(): return lax.ppermute(value, ('samp', 'blk'), pairs)  6.84 us
  transfers between devices with their start and end apart: 18, of which 4 were waited for; matrix products, arithmetic and copies ran while one was open for 3% of the time, Pallas kernels for 30%

profile of v3, /device:TPU:1, one launch (start us, length us, event | category | flops | bytes accessed | tf_op | source)
XLA Modules:
  0.0 193.8 jit_solution(17046969574763721653)
XLA Ops:
  6.5 0.7 add_select_fusion
  8.0 8.7 %collective-permute-start = (s32[2]{0:T(128)S(1)}, s32[2]{0:T(128)S(1)}, u32[]{:S(2)}, u32[]{:S(2)}) collective-permute-start(s32[2]{0:T(128)S(1)} %get-tuple-element.45), channel_id=1, source_target_pairs={{0,62},{1,63},{2,0},{3,1},{4,2},{5,3},{6,4},{7,5},{8,6},{9,7},{10,... | collective-permute-start | bytes 32 | tf_op jit(solution)/shard_map/ppermute | solution.py:42
  16.7 5.2 %collective-permute-start.1 = (s32[2]{0:T(128)S(1)}, s32[2]{0:T(128)S(1)}, u32[]{:S(2)}, u32[]{:S(2)}) collective-permute-start(s32[2]{0:T(128)S(1)} %get-tuple-element.48), channel_id=1, source_target_pairs={{0,1},{1,0},{2,3},{3,2},{4,5},{5,4},{6,7},{7,6},{8,9},{9,8},{10,11... | collective-permute-start | bytes 32 | tf_op jit(solution)/shard_map/ppermute | solution.py:42
  21.8 15.2 %shard_map.46 = (bf16[1024,2048]{1,0:T(8,128)(2,1)}, f32[4,1056,256]{2,1,0:T(8,128)}) custom-call(bf16[2048,1024]{1,0:T(8,128)(2,1)} %source_ref.1, bf16[2048,1024]{1,0:T(8,128)(2,1)} %source_ref.1), custom_call_target="tpu_custom_call" | custom-call | flops 4294967296 | bytes 12582912 | tf_op jit(solution)/shard_map/pallas_call | solution.py:129
  37.1 0.6 pad_add_fusion.2.want_ref
  37.7 7.9 %shard_map.47 = (bf16[2048,256]{1,0:T(8,128)(2,1)}, bf16[2048,256]{1,0:T(8,128)(2,1)}, bf16[2048,256]{1,0:T(8,128)(2,1)}, bf16[2048,256]{1,0:T(8,128)(2,1)}, bf1...) custom-call(s32[8]{0:T(128)} %pad_add_fusion.2.want_ref, bf16[2048,1024]{1,0:T(8,128)(2,1)} %source_ref.1), custom_call_target="tpu_custom_call" | custom-call | bytes 16777216 | tf_op jit(solution)/shard_map/pallas_call | solution.py:88
  46.0 5.0 %collective-permute-start.13 = (bf16[2048,256]{1,0:T(8,128)(2,1)}, bf16[2048,256]{1,0:T(8,128)(2,1)}, u32[]{:S(2)}, u32[]{:S(2)}) collective-permute-start(bf16[2048,256]{1,0:T(8,128)(2,1)} %get-tuple-element.40), channel_id=1, source_target_pairs={{0,62},{1,63},{2,0},{3,1},{4,2},{5,3},{6,4},{7,5},{8,6},{9,7},{10,... | collective-permute-start | bytes 3145736 | tf_op jit(solution)/shard_map/ppermute | solution.py:42
  51.3 0.6 reshape.145.slot_ref
  51.9 0.5 and_select_fusion.dest_ref
  52.5 21.3 %collective-permute-done.11.refs_0_ = bf16[2048,256]{1,0:T(8,128)(2,1)} collective-permute-done((bf16[2048,256]{1,0:T(8,128)(2,1)}, bf16[2048,256]{1,0:T(8,128)(2,1)}, u32[]{:S(2)}, u32[]{:S(2)}) %collective-permute-start.11) | collective-permute-done | bytes 1048608 | tf_op jit(solution)/shard_map/ppermute | solution.py:42
  73.8 17.3 %collective-permute-done.12.refs_2_ = bf16[2048,256]{1,0:T(8,128)(2,1)} collective-permute-done((bf16[2048,256]{1,0:T(8,128)(2,1)}, bf16[2048,256]{1,0:T(8,128)(2,1)}, u32[]{:S(2)}, u32[]{:S(2)}) %collective-permute-start.12) | collective-permute-done | bytes 1048608 | tf_op jit(solution)/shard_map/ppermute | solution.py:42
  91.1 4.5 %collective-permute-start.7 = (bf16[2048,256]{1,0:T(8,128)(2,1)}, bf16[2048,256]{1,0:T(8,128)(2,1)}, u32[]{:S(2)}, u32[]{:S(2)}) collective-permute-start(bf16[2048,256]{1,0:T(8,128)(2,1)} %get-tuple-element.33), channel_id=1, source_target_pairs={{0,62},{1,63},{2,0},{3,1},{4,2},{5,3},{6,4},{7,5},{8,6},{9,7},{10,... | collective-permute-start | bytes 3145736 | tf_op jit(solution)/shard_map/ppermute | solution.py:42
  95.6 1.3 copy-done.8
  96.9 15.1 %shard_map.49 = (f32[1056,128]{1,0:T(8,128)}, f32[1056,128]{1,0:T(8,128)}, f32[1056,128]{1,0:T(8,128)}, f32[1056,128]{1,0:T(8,128)}) custom-call(s32[16]{0:T(128)} %reshape.145.slot_ref, s32[4]{0:T(128)} %and_select_fusion.dest_ref, bf16[1024,2048]{1,0:T(8,128)(2,1)} %get-tuple-element.28.at_ref, bf16[2048,256]{1,0:T(8,128)(2,1)} %collective-permute-done.11.refs_0_, ...), custom_call_target="tpu_custom_call" | custom-call | flops 4294967296 | bytes 10485760 | tf_op jit(solution)/shard_map/pallas_call | solution.py:207
  112.0 2.8 %collective-permute-start.14 = (f32[1056,128]{1,0:T(8,128)}, f32[1056,128]{1,0:T(8,128)S(1)}, u32[]{:S(2)}, u32[]{:S(2)}) collective-permute-start(f32[1056,128]{1,0:T(8,128)} %get-tuple-element.41), channel_id=1, source_target_pairs={{0,64},{1,193},{2,66},{3,195},{4,68},{5,197},{6,70},{7,199},{8,72}... | collective-permute-start | bytes 1622024 | tf_op jit(solution)/shard_map/ppermute | solution.py:50
  114.8 6.6 %collective-permute-done.14 = f32[1056,128]{1,0:T(8,128)S(1)} collective-permute-done((f32[1056,128]{1,0:T(8,128)}, f32[1056,128]{1,0:T(8,128)S(1)}, u32[]{:S(2)}, u32[]{:S(2)}) %collective-permute-start.14) | collective-permute-done | bytes 540704 | tf_op jit(solution)/shard_map/ppermute | solution.py:50
  121.4 1.1 add.165
  122.6 3.3 %collective-permute-start.15 = (f32[1056,128]{1,0:T(8,128)S(1)}, f32[1056,128]{1,0:T(8,128)S(1)}, u32[]{:S(2)}, u32[]{:S(2)}) collective-permute-start(f32[1056,128]{1,0:T(8,128)S(1)} %add.165), channel_id=1, source_target_pairs={{0,64},{1,193},{2,66},{3,195},{4,68},{5,197},{6,70},{7,199},{8,72}... | collective-permute-start | bytes 1622024 | tf_op jit(solution)/shard_map/ppermute | solution.py:50
  125.8 0.5 and_select_fusion.1.dest_ref
  126.4 0.9 copy-done.9
  127.4 15.1 %shard_map.48 = (f32[1056,128]{1,0:T(8,128)}, f32[1056,128]{1,0:T(8,128)}, f32[1056,128]{1,0:T(8,128)}, f32[1056,128]{1,0:T(8,128)}) custom-call(s32[16]{0:T(128)} %reshape.145.slot_ref, s32[4]{0:T(128)} %and_select_fusion.1.dest_ref, bf16[1024,2048]{1,0:T(8,128)(2,1)} %get-tuple-element.28.at_ref, bf16[2048,256]{1,0:T(8,128)(2,1)} %copy-done.9, ...), custom_call_target="tpu_custom_call" | custom-call | flops 4294967296 | bytes 10485760 | tf_op jit(solution)/shard_map/pallas_call | solution.py:207
  142.6 1.2 collective-permute-start.9
  143.7 1.5 collective-permute-start.10
  145.3 0.8 collective-permute-start.16
  146.3 0.6 reshape.146.taper_ref
  146.9 0.2 select_reduce_fusion.2
  147.2 0.7 add.148.place_ref
  147.9 28.1 %collective-permute-done.16 = f32[1056,128]{1,0:T(8,128)S(1)} collective-permute-done((f32[1056,128]{1,0:T(8,128)S(1)}, f32[1056,128]{1,0:T(8,128)S(1)}, u32[]{:S(2)}, u32[]{:S(2)}) %collective-permute-start.16) | collective-permute-done | bytes 540704 | tf_op jit(solution)/shard_map/ppermute | solution.py:50
  176.0 0.9 add.167.refs_0_
  176.9 4.2 %shard_map.50.refs_4_ = f32[2048,256]{1,0:T(8,128)} custom-call(s32[32]{0:T(128)} %add.148.place_ref, s32[16]{0:T(128)} %reshape.145.slot_ref, s32[4]{0:T(128)} %and_select_fusion.1.dest_ref, f32[32]{0:T(128)} %reshape.146.taper_ref, f32[1056,256]{1,0:T(8,128)} %reduce-scatter.2.cloned.1.call-done.own_ref, f32[1056,128]{1,0:T(8,128)} %add.167.refs_0_), custom_call_target="tpu_custom_call" | custom-call | flops 1048576 | bytes 4194304 | tf_op jit(solution)/shard_map/pallas_call | solution.py:255
  181.1 0.8 copy-done.2
  182.2 4.7 %shard_map.51 = f32[2048,256]{1,0:T(8,128)} custom-call(s32[32]{0:T(128)} %add.148.place_ref, s32[16]{0:T(128)} %reshape.145.slot_ref, s32[4]{0:T(128)} %and_select_fusion.1.dest_ref, f32[32]{0:T(128)} %reshape.146.taper_ref, f32[1056,256]{1,0:T(8,128)} %reduce-scatter.2.cloned.1.call-done.own_ref, ...), custom_call_target="tpu_custom_call", output_to_operand_aliasing={{}: (9, {})} | custom-call | flops 1048576 | bytes 4194304 | tf_op jit(solution)/shard_map/pallas_call | solution.py:255
  (62 shorter events, 2.3 us)
Async XLA Ops:
  6.5 170.3 %reduce-scatter.2.cloned.1.call-start = ((), (), s32[]{:S(2)}) async-start(), calls=%async_computation.1 | async-start | bytes 5406720 | tf_op jit(solution)/shard_map/reduce_scatter | solution.py:321
  8.0 29.1 %collective-permute-start = (s32[2]{0:T(128)S(1)}, s32[2]{0:T(128)S(1)}, u32[]{:S(2)}, u32[]{:S(2)}) collective-permute-start(s32[2]{0:T(128)S(1)} %get-tuple-element.45), channel_id=1, source_target_pairs={{0,62},{1,63},{2,0},{3,1},{4,2},{5,3},{6,4},{7,5},{8,6},{9,7},{10,... | collective-permute-start | bytes 32 | tf_op jit(solution)/shard_map/ppermute | solution.py:42
  16.6 20.4 %collective-permute-start.3 = (s32[2]{0:T(128)S(1)}, s32[2]{0:T(128)S(1)}, u32[]{:S(2)}, u32[]{:S(2)}) collective-permute-start(s32[2]{0:T(128)S(1)} %get-tuple-element.46), channel_id=1, source_target_pairs={{0,2},{1,3},{2,4},{3,5},{4,6},{5,7},{6,8},{7,9},{8,10},{9,11},{10,... | collective-permute-start | bytes 32 | tf_op jit(solution)/shard_map/ppermute | solution.py:42
  16.7 20.4 %collective-permute-start.2 = (s32[2]{0:T(128)S(1)}, s32[2]{0:T(128)S(1)}, u32[]{:S(2)}, u32[]{:S(2)}) collective-permute-start(s32[2]{0:T(128)S(1)} %get-tuple-element.47), channel_id=1, source_target_pairs={{0,63},{1,2},{2,1},{3,4},{4,3},{5,6},{6,5},{7,8},{8,7},{9,10},{10,... | collective-permute-start | bytes 32 | tf_op jit(solution)/shard_map/ppermute | solution.py:42
  16.7 20.4 %collective-permute-start.1 = (s32[2]{0:T(128)S(1)}, s32[2]{0:T(128)S(1)}, u32[]{:S(2)}, u32[]{:S(2)}) collective-permute-start(s32[2]{0:T(128)S(1)} %get-tuple-element.48), channel_id=1, source_target_pairs={{0,1},{1,0},{2,3},{3,2},{4,5},{5,4},{6,7},{7,6},{8,9},{9,8},{10,11... | collective-permute-start | bytes 32 | tf_op jit(solution)/shard_map/ppermute | solution.py:42
  37.7 13.5 %copy-start.5 = (s32[4,8]{1,0:T(4,128)S(1)}, s32[4,8]{1,0:T(4,128)}, u32[]{:S(2)}) copy-start(s32[4,8]{1,0:T(4,128)} %param.5) | copy-start | bytes 388
  37.7 14.2 %copy-start.7 = (s32[4]{0:T(128)S(1)}, s32[4]{0:T(128)}, u32[]{:S(2)}) copy-start(s32[4]{0:T(128)} %constant.131.clone) | copy-start | bytes 52
  45.7 49.9 %collective-permute-start.5 = (bf16[2048,512]{1,0:T(8,128)(2,1)}, bf16[2048,512]{1,0:T(8,128)(2,1)S(1)}, u32[]{:S(2)}, u32[]{:S(2)}) collective-permute-start(bf16[2048,512]{1,0:T(8,128)(2,1)} %get-tuple-element.31), channel_id=1, source_target_pairs={{0,1},{1,0},{2,3},{3,2},{4,5},{5,4},{6,7},{7,6},{8,9},{9,8},{10,11... | collective-permute-start | bytes 6291464 | tf_op jit(solution)/shard_map/ppermute | solution.py:42
  45.8 28.0 %collective-permute-start.11 = (bf16[2048,256]{1,0:T(8,128)(2,1)}, bf16[2048,256]{1,0:T(8,128)(2,1)}, u32[]{:S(2)}, u32[]{:S(2)}) collective-permute-start(bf16[2048,256]{1,0:T(8,128)(2,1)} %get-tuple-element.38), channel_id=1, source_target_pairs={{0,2},{1,3},{2,4},{3,5},{4,6},{5,7},{6,8},{7,9},{8,10},{9,11},{10,... | collective-permute-start | bytes 3145736 | tf_op jit(solution)/shard_map/ppermute | solution.py:42
  45.9 45.2 %collective-permute-start.12 = (bf16[2048,256]{1,0:T(8,128)(2,1)}, bf16[2048,256]{1,0:T(8,128)(2,1)}, u32[]{:S(2)}, u32[]{:S(2)}) collective-permute-start(bf16[2048,256]{1,0:T(8,128)(2,1)} %get-tuple-element.39), channel_id=1, source_target_pairs={{0,63},{1,2},{2,1},{3,4},{4,3},{5,6},{6,5},{7,8},{8,7},{9,10},{10,... | collective-permute-start | bytes 3145736 | tf_op jit(solution)/shard_map/ppermute | solution.py:42
  46.0 49.6 %collective-permute-start.13 = (bf16[2048,256]{1,0:T(8,128)(2,1)}, bf16[2048,256]{1,0:T(8,128)(2,1)}, u32[]{:S(2)}, u32[]{:S(2)}) collective-permute-start(bf16[2048,256]{1,0:T(8,128)(2,1)} %get-tuple-element.40), channel_id=1, source_target_pairs={{0,62},{1,63},{2,0},{3,1},{4,2},{5,3},{6,4},{7,5},{8,6},{9,7},{10,... | collective-permute-start | bytes 3145736 | tf_op jit(solution)/shard_map/ppermute | solution.py:42
  52.5 73.9 %collective-permute-start.4 = (bf16[2048,256]{1,0:T(8,128)(2,1)}, bf16[2048,256]{1,0:T(8,128)(2,1)S(1)}, u32[]{:S(2)}, u32[]{:S(2)}) collective-permute-start(bf16[2048,256]{1,0:T(8,128)(2,1)} %get-tuple-element.30), channel_id=1, source_target_pairs={{0,2},{1,3},{2,4},{3,5},{4,6},{5,7},{6,8},{7,9},{8,10},{9,11},{10,... | collective-permute-start | bytes 3145736 | tf_op jit(solution)/shard_map/ppermute | solution.py:42
  73.8 52.6 %collective-permute-start.6 = (bf16[2048,256]{1,0:T(8,128)(2,1)}, bf16[2048,256]{1,0:T(8,128)(2,1)}, u32[]{:S(2)}, u32[]{:S(2)}) collective-permute-start(bf16[2048,256]{1,0:T(8,128)(2,1)} %get-tuple-element.32), channel_id=1, source_target_pairs={{0,63},{1,2},{2,1},{3,4},{4,3},{5,6},{6,5},{7,8},{8,7},{9,10},{10,... | collective-permute-start | bytes 3145736 | tf_op jit(solution)/shard_map/ppermute | solution.py:42
  91.1 35.3 %collective-permute-start.7 = (bf16[2048,256]{1,0:T(8,128)(2,1)}, bf16[2048,256]{1,0:T(8,128)(2,1)}, u32[]{:S(2)}, u32[]{:S(2)}) collective-permute-start(bf16[2048,256]{1,0:T(8,128)(2,1)} %get-tuple-element.33), channel_id=1, source_target_pairs={{0,62},{1,63},{2,0},{3,1},{4,2},{5,3},{6,4},{7,5},{8,6},{9,7},{10,... | collective-permute-start | bytes 3145736 | tf_op jit(solution)/shard_map/ppermute | solution.py:42
  95.6 1.3 copy-start.8
  112.0 9.4 %collective-permute-start.14 = (f32[1056,128]{1,0:T(8,128)}, f32[1056,128]{1,0:T(8,128)S(1)}, u32[]{:S(2)}, u32[]{:S(2)}) collective-permute-start(f32[1056,128]{1,0:T(8,128)} %get-tuple-element.41), channel_id=1, source_target_pairs={{0,64},{1,193},{2,66},{3,195},{4,68},{5,197},{6,70},{7,199},{8,72}... | collective-permute-start | bytes 1622024 | tf_op jit(solution)/shard_map/ppermute | solution.py:50
  122.6 22.7 %collective-permute-start.15 = (f32[1056,128]{1,0:T(8,128)S(1)}, f32[1056,128]{1,0:T(8,128)S(1)}, u32[]{:S(2)}, u32[]{:S(2)}) collective-permute-start(f32[1056,128]{1,0:T(8,128)S(1)} %add.165), channel_id=1, source_target_pairs={{0,64},{1,193},{2,66},{3,195},{4,68},{5,197},{6,70},{7,199},{8,72}... | collective-permute-start | bytes 1622024 | tf_op jit(solution)/shard_map/ppermute | solution.py:50
  126.4 18.9 %copy-start.1 = (f32[1056,128]{1,0:T(8,128)S(1)}, f32[1056,128]{1,0:T(8,128)}, u32[]{:S(2)}) copy-start(f32[1056,128]{1,0:T(8,128)} %get-tuple-element.43) | copy-start | bytes 1622020
  126.4 19.7 %copy-start.6 = (s32[4,8]{1,0:T(4,128)S(1)}, s32[4,8]{1,0:T(4,128)}, u32[]{:S(2)}) copy-start(s32[4,8]{1,0:T(4,128)} %param.6) | copy-start | bytes 388
  126.4 49.6 %copy-start = (f32[1056,128]{1,0:T(8,128)S(1)}, f32[1056,128]{1,0:T(8,128)}, u32[]{:S(2)}) copy-start(f32[1056,128]{1,0:T(8,128)} %get-tuple-element.44) | copy-start | bytes 1622020
  126.4 1.0 copy-start.9
  142.5 38.6 %collective-permute-start.8 = (f32[1056,128]{1,0:T(8,128)}, f32[1056,128]{1,0:T(8,128)S(1)}, u32[]{:S(2)}, u32[]{:S(2)}) collective-permute-start(f32[1056,128]{1,0:T(8,128)} %get-tuple-element.35), channel_id=1, source_target_pairs={{0,64},{64,128},{128,192},{192,0},{1,65},{65,129},{129,193},{193,1... | collective-permute-start | bytes 1622024 | tf_op jit(solution)/shard_map/ppermute | solution.py:28
  142.6 38.5 %collective-permute-start.9 = (f32[1056,128]{1,0:T(8,128)}, f32[1056,128]{1,0:T(8,128)S(1)}, u32[]{:S(2)}, u32[]{:S(2)}) collective-permute-start(f32[1056,128]{1,0:T(8,128)} %get-tuple-element.36), channel_id=1, source_target_pairs={{0,128},{64,192},{128,0},{192,64},{1,129},{65,193},{129,1},{193,65... | collective-permute-start | bytes 1622024 | tf_op jit(solution)/shard_map/ppermute | solution.py:28
  143.7 37.3 %collective-permute-start.10 = (f32[1056,128]{1,0:T(8,128)}, f32[1056,128]{1,0:T(8,128)S(1)}, u32[]{:S(2)}, u32[]{:S(2)}) collective-permute-start(f32[1056,128]{1,0:T(8,128)} %get-tuple-element.37), channel_id=1, source_target_pairs={{0,192},{64,0},{128,64},{192,128},{1,193},{65,1},{129,65},{193,129... | collective-permute-start | bytes 1622024 | tf_op jit(solution)/shard_map/ppermute | solution.py:28
  145.3 30.7 %collective-permute-start.16 = (f32[1056,128]{1,0:T(8,128)S(1)}, f32[1056,128]{1,0:T(8,128)S(1)}, u32[]{:S(2)}, u32[]{:S(2)}) collective-permute-start(f32[1056,128]{1,0:T(8,128)S(1)} %add.166), channel_id=1, source_target_pairs={{0,64},{1,193},{2,66},{3,195},{4,68},{5,197},{6,70},{7,199},{8,72}... | collective-permute-start | bytes 1622024 | tf_op jit(solution)/shard_map/ppermute | solution.py:50
  181.0 0.8 copy-start.2
  181.0 1.0 copy-start.3
  181.1 1.2 copy-start.4
Sparse Core Ops, SparseCore 0:
  37.8 45.9 reduce-scatter.1

commit v4 on v3

--- a/solution.py
+++ b/solution.py
@@ -147,7 +147,7 @@
 
 
 def remote_kernel(stage, slot_ref, dest_ref, at_ref, *refs):
-    blocks, parts, cols_ref, sems = refs[:4], refs[4:-2], refs[-2], refs[-1]
+    blocks, parts, (cols_ref, tile_ref, sems) = refs[:4], refs[4:-3], refs[-3:]
     samp = len(parts)
     samples = cols_ref.shape[1]
     rows = BS // samp
@@ -176,16 +176,12 @@
         u = r * 4 + 2 * pair
         cols = jnp.concatenate([cols_ref[slot_ref[u]], cols_ref[slot_ref[u + 1]]], axis=1)
         tile = jnp.dot(at, cols, preferred_element_type=jnp.float32)
+        tile_ref[...] = tile
         for side in range(2):
             j = 2 * pair + side
             for d in range(samp):
-                for y in range(samp):
-
-                    @pl.when(dest_ref[d] == y)
-                    def _():
-                        parts[d][j * rows : (j + 1) * rows, :] = tile[
-                            y * rows : (y + 1) * rows, side * HALF : (side + 1) * HALF
-                        ]
+                first = pl.multiple_of(dest_ref[d] * rows, rows)
+                parts[d][j * rows : (j + 1) * rows, :] = tile_ref[pl.ds(first, rows), side * HALF : (side + 1) * HALF]
 
     step = 128
     for side in range(2):
@@ -211,7 +207,11 @@
             grid=(B_DEV,),
             in_specs=[pl.BlockSpec((BS, samples), lambda r, *s: (r, 0))] + [pl.BlockSpec(memory_space=pl.ANY)] * 4,
             out_specs=out_specs,
-            scratch_shapes=[pltpu.VMEM((8, samples, HALF), at.dtype), pltpu.SemaphoreType.DMA((8,))],
+            scratch_shapes=[
+                pltpu.VMEM((8, samples, HALF), at.dtype),
+                pltpu.VMEM((BS, BS), jnp.float32),
+                pltpu.SemaphoreType.DMA((8,)),
+            ],
         ),
         out_shape=out_shape,
         compiler_params=pltpu.CompilerParams(vmem_limit_bytes=BIG),
@@ -285,15 +285,7 @@
     low = jnp.min(jnp.where(need, four[None], B_DEV - 1), axis=1)
     high = jnp.max(jnp.where(need, four[None], 0), axis=1)
     want = jnp.stack([low, high], axis=1)
-    at, own_part = own_tiles(perturb, samp)
     asked = jnp.concatenate([exchanged(want[q], q, back=True) for q in range(4)])
-    asked, at, own_part = lax.optimization_barrier((asked, at, own_part))
-    chosen = select(asked, perturb)
-    mates = exchanged(chosen[6], 1)
-    got = []
-    for stage in range(STAGES):
-        two_below, across, two_above = (exchanged(chosen[3 * stage + i], q) for i, q in enumerate((0, 2, 3)))
-        got.append([two_below, mates, across, two_above])
 
     k_ids = jnp.arange(K_PART, dtype=jnp.int32)[None, :, None]
     is_high = jnp.sum(jnp.where(kind[:, :, None] == four, high[None, None], 0), axis=2) == inside
@@ -318,6 +310,15 @@
     ahead = 1 - 2 * (here % 2)
     ring_dest = (me + ahead * jnp.array([-1, -2, 1, 0], jnp.int32) + 2 * samp) % samp
     dest = (me + jnp.arange(samp, dtype=jnp.int32)) % samp
+    chosen = select(asked, perturb)
+    mates = exchanged(chosen[6], 1)
+    got = []
+    for stage in range(STAGES):
+        two_below, across, two_above = (exchanged(chosen[3 * stage + i], q) for i, q in enumerate((0, 2, 3)))
+        got.append([two_below, mates, across, two_above])
+    at, own_part = own_tiles(perturb, samp)
+    own_part, *arrived = lax.optimization_barrier((own_part, got[0][0], got[0][2], got[0][3]))
+    got[0] = [arrived[0], mates, arrived[1], arrived[2]]
     own_sum = lax.psum_scatter(own_part.reshape(samp * size, BS), "samp", scatter_dimension=0, tiled=True)
     parts = remote_tiles(0, slots, ring_dest, at, got[0], samp)
     running = parts[0]

time: 194 us -> 178 us (0.918)
  waiting for transfers between devices: 73.3 us -> 60.9 us
  Pallas kernels: 62.2 us -> 54.5 us
  starting transfers between devices: 33.2 us -> 37.9 us
    ppermute x11, waiting for transfers between devices: 38.7 us -> 14.5 us  [exchanged(): return lax.ppermute(value, 'blk', sorted(pairs))]
    ppermute x3, waiting for transfers between devices: 34.7 us -> 46.4 us  [ringed(): return lax.ppermute(value, ('samp', 'blk'), pairs)]
    pallas_call x2, Pallas kernels: 30.2 us -> 22.7 us  [remote_tiles(): pl.pallas_call(functools.partial(remote_kernel, stage), grid_spec=pltpu.P...]
    ppermute x11, starting transfers between devices: 23.6 us -> 28 us  [exchanged(): return lax.ppermute(value, 'blk', sorted(pairs))]
  transfers between devices with their start and end apart: 18 -> 18, of which waited for: 4 -> 5; matrix products, arithmetic and copies ran while one was open for 3% -> 3% of each run, Pallas kernels for 30% -> 24%
where the time goes in v4:
time: 178 us
  waiting for transfers between devices  60.9 us (34%)
  Pallas kernels  54.5 us (31%)
  starting transfers between devices  37.9 us (21%)
  between operations  13.5 us (8%)
  other arithmetic  5.77 us (3%)
  local copies, waits for them, and re-layouts  4.85 us (3%)
    ppermute x3, waiting for transfers between devices, ringed(): return lax.ppermute(value, ('samp', 'blk'), pairs)  46.4 us
    ppermute x11, starting transfers between devices, exchanged(): return lax.ppermute(value, 'blk', sorted(pairs))  28 us
    pallas_call x2, Pallas kernels, remote_tiles(): pl.pallas_call(functools.partial(remote_kernel, stage), grid_spec=pltpu.P...  22.7 us
    pallas_call x1, Pallas kernels, own_tiles(): pl.pallas_call(own_kernel, grid=(B_DEV,), in_specs=[pl.BlockSpec((samples...  15.2 us
    ppermute x11, waiting for transfers between devices, exchanged(): return lax.ppermute(value, 'blk', sorted(pairs))  14.5 us
    pallas_call x2, Pallas kernels, final(): pl.pallas_call(functools.partial(final_kernel, half, len(rems)), grid_spe...  8.86 us
    pallas_call x1, Pallas kernels, select(): pl.pallas_call(functools.partial(select_kernel, plan), grid_spec=pltpu.Pr...  7.77 us
    ppermute x3, starting transfers between devices, ringed(): return lax.ppermute(value, ('samp', 'blk'), pairs)  7.24 us
  transfers between devices with their start and end apart: 18, of which 5 were waited for; matrix products, arithmetic and copies ran while one was open for 3% of the time, Pallas kernels for 24%

profile of v4, /device:TPU:1, one launch (start us, length us, event | category | flops | bytes accessed | tf_op | source)
XLA Modules:
  0.0 177.5 jit_solution(13507915591416385414)
XLA Ops:
  6.5 0.7 add_select_fusion
  8.0 2.1 %collective-permute-start.3 = (s32[2]{0:T(128)S(1)}, s32[2]{0:T(128)S(1)}, u32[]{:S(2)}, u32[]{:S(2)}) collective-permute-start(s32[2]{0:T(128)S(1)} %get-tuple-element.48), channel_id=1, source_target_pairs={{0,2},{1,3},{2,4},{3,5},{4,6},{5,7},{6,8},{7,9},{8,10},{9,11},{10,... | collective-permute-start | bytes 32 | tf_op jit(solution)/shard_map/ppermute | solution.py:42
  10.1 2.1 %collective-permute-start.2 = (s32[2]{0:T(128)S(1)}, s32[2]{0:T(128)S(1)}, u32[]{:S(2)}, u32[]{:S(2)}) collective-permute-start(s32[2]{0:T(128)S(1)} %get-tuple-element.49), channel_id=1, source_target_pairs={{0,63},{1,2},{2,1},{3,4},{4,3},{5,6},{6,5},{7,8},{8,7},{9,10},{10,... | collective-permute-start | bytes 32 | tf_op jit(solution)/shard_map/ppermute | solution.py:42
  12.1 5.0 %collective-permute-start.1 = (s32[2]{0:T(128)S(1)}, s32[2]{0:T(128)S(1)}, u32[]{:S(2)}, u32[]{:S(2)}) collective-permute-start(s32[2]{0:T(128)S(1)} %get-tuple-element.50), channel_id=1, source_target_pairs={{0,1},{1,0},{2,3},{3,2},{4,5},{5,4},{6,7},{7,6},{8,9},{9,8},{10,11... | collective-permute-start | bytes 32 | tf_op jit(solution)/shard_map/ppermute | solution.py:42
  17.2 1.4 collective-permute-start
  18.5 1.0 collective-permute-done
  19.5 0.7 pad_add_fusion.2.want_ref
  20.2 7.8 %shard_map.47 = (bf16[2048,256]{1,0:T(8,128)(2,1)}, bf16[2048,256]{1,0:T(8,128)(2,1)}, bf16[2048,256]{1,0:T(8,128)(2,1)}, bf16[2048,256]{1,0:T(8,128)(2,1)}, bf1...) custom-call(s32[8]{0:T(128)} %pad_add_fusion.2.want_ref, bf16[2048,1024]{1,0:T(8,128)(2,1)} %source_ref.1), custom_call_target="tpu_custom_call" | custom-call | bytes 16777216 | tf_op jit(solution)/shard_map/pallas_call | solution.py:88
  28.7 5.3 %collective-permute-start.6 = (bf16[2048,256]{1,0:T(8,128)(2,1)}, bf16[2048,256]{1,0:T(8,128)(2,1)}, u32[]{:S(2)}, u32[]{:S(2)}) collective-permute-start(bf16[2048,256]{1,0:T(8,128)(2,1)} %get-tuple-element.29), channel_id=1, source_target_pairs={{0,62},{1,63},{2,0},{3,1},{4,2},{5,3},{6,4},{7,5},{8,6},{9,7},{10,... | collective-permute-start | bytes 3145736 | tf_op jit(solution)/shard_map/ppermute | solution.py:42
  34.0 15.2 %shard_map.46 = (bf16[1024,2048]{1,0:T(8,128)(2,1)}, f32[4,1056,256]{2,1,0:T(8,128)}) custom-call(bf16[2048,1024]{1,0:T(8,128)(2,1)} %source_ref.1, bf16[2048,1024]{1,0:T(8,128)(2,1)} %source_ref.1), custom_call_target="tpu_custom_call" | custom-call | flops 4294967296 | bytes 12582912 | tf_op jit(solution)/shard_map/pallas_call | solution.py:129
  49.2 6.0 %collective-permute-done.4.refs_0_ = bf16[2048,256]{1,0:T(8,128)(2,1)} collective-permute-done((bf16[2048,256]{1,0:T(8,128)(2,1)}, bf16[2048,256]{1,0:T(8,128)(2,1)}, u32[]{:S(2)}, u32[]{:S(2)}) %collective-permute-start.4) | collective-permute-done | bytes 1048608 | tf_op jit(solution)/shard_map/ppermute | solution.py:42
  55.2 7.4 %collective-permute-done.5.refs_2_ = bf16[2048,256]{1,0:T(8,128)(2,1)} collective-permute-done((bf16[2048,256]{1,0:T(8,128)(2,1)}, bf16[2048,256]{1,0:T(8,128)(2,1)}, u32[]{:S(2)}, u32[]{:S(2)}) %collective-permute-start.5) | collective-permute-done | bytes 1048608 | tf_op jit(solution)/shard_map/ppermute | solution.py:42
  62.6 6.0 %collective-permute-start.8 = (bf16[2048,512]{1,0:T(8,128)(2,1)}, bf16[2048,512]{1,0:T(8,128)(2,1)S(1)}, u32[]{:S(2)}, u32[]{:S(2)}) collective-permute-start(bf16[2048,512]{1,0:T(8,128)(2,1)} %get-tuple-element.33), channel_id=1, source_target_pairs={{0,1},{1,0},{2,3},{3,2},{4,5},{5,4},{6,7},{7,6},{8,9},{9,8},{10,11... | collective-permute-start | bytes 6291464 | tf_op jit(solution)/shard_map/ppermute | solution.py:42
  69.0 0.7 reshape.145.slot_ref
  70.2 5.4 %collective-permute-start.10 = (bf16[2048,256]{1,0:T(8,128)(2,1)S(1)}, bf16[2048,256]{1,0:T(8,128)(2,1)}, u32[]{:S(2)}, u32[]{:S(2)}) collective-permute-start(bf16[2048,256]{1,0:T(8,128)(2,1)S(1)} %copy-done.9), channel_id=1, source_target_pairs={{0,62},{1,63},{2,0},{3,1},{4,2},{5,3},{6,4},{7,5},{8,6},{9,7},{10,... | collective-permute-start | bytes 3145736 | tf_op jit(solution)/shard_map/ppermute | solution.py:42
  75.6 1.3 copy-done.8
  77.0 11.7 %shard_map.49 = (f32[1056,128]{1,0:T(8,128)}, f32[1056,128]{1,0:T(8,128)}, f32[1056,128]{1,0:T(8,128)}, f32[1056,128]{1,0:T(8,128)}) custom-call(s32[16]{0:T(128)} %reshape.145.slot_ref, s32[4]{0:T(128)} %and_select_fusion.dest_ref, bf16[1024,2048]{1,0:T(8,128)(2,1)} %get-tuple-element.31.at_ref, bf16[2048,256]{1,0:T(8,128)(2,1)} %collective-permute-done.4.refs_0_, ...), custom_call_target="tpu_custom_call" | custom-call | flops 4294967296 | bytes 10485760 | tf_op jit(solution)/shard_map/pallas_call | solution.py:203
  88.6 2.8 %collective-permute-start.14 = (f32[1056,128]{1,0:T(8,128)}, f32[1056,128]{1,0:T(8,128)S(1)}, u32[]{:S(2)}, u32[]{:S(2)}) collective-permute-start(f32[1056,128]{1,0:T(8,128)} %get-tuple-element.43), channel_id=1, source_target_pairs={{0,64},{1,193},{2,66},{3,195},{4,68},{5,197},{6,70},{7,199},{8,72}... | collective-permute-start | bytes 1622024 | tf_op jit(solution)/shard_map/ppermute | solution.py:50
  91.5 18.2 %collective-permute-done.14 = f32[1056,128]{1,0:T(8,128)S(1)} collective-permute-done((f32[1056,128]{1,0:T(8,128)}, f32[1056,128]{1,0:T(8,128)S(1)}, u32[]{:S(2)}, u32[]{:S(2)}) %collective-permute-start.14) | collective-permute-done | bytes 540704 | tf_op jit(solution)/shard_map/ppermute | solution.py:50
  109.6 1.1 add.165
  110.8 3.7 %collective-permute-start.15 = (f32[1056,128]{1,0:T(8,128)S(1)}, f32[1056,128]{1,0:T(8,128)S(1)}, u32[]{:S(2)}, u32[]{:S(2)}) collective-permute-start(f32[1056,128]{1,0:T(8,128)S(1)} %add.165), channel_id=1, source_target_pairs={{0,64},{1,193},{2,66},{3,195},{4,68},{5,197},{6,70},{7,199},{8,72}... | collective-permute-start | bytes 1622024 | tf_op jit(solution)/shard_map/ppermute | solution.py:50
  115.2 11.1 %shard_map.48 = (f32[1056,128]{1,0:T(8,128)}, f32[1056,128]{1,0:T(8,128)}, f32[1056,128]{1,0:T(8,128)}, f32[1056,128]{1,0:T(8,128)}) custom-call(s32[16]{0:T(128)} %reshape.145.slot_ref, s32[4]{0:T(128)} %and_select_fusion.1.dest_ref, bf16[1024,2048]{1,0:T(8,128)(2,1)} %get-tuple-element.31.at_ref, bf16[2048,256]{1,0:T(8,128)(2,1)} %collective-permute-done.7.refs_0_, ...), custom_call_target="tpu_custom_call" | custom-call | flops 4294967296 | bytes 10485760 | tf_op jit(solution)/shard_map/pallas_call | solution.py:203
  126.4 1.2 collective-permute-start.12
  127.6 1.4 collective-permute-start.13
  129.1 0.8 collective-permute-start.16
  129.9 0.7 add.148.place_ref
  130.9 0.6 reshape.146.taper_ref
  131.5 28.2 %collective-permute-done.16 = f32[1056,128]{1,0:T(8,128)S(1)} collective-permute-done((f32[1056,128]{1,0:T(8,128)S(1)}, f32[1056,128]{1,0:T(8,128)S(1)}, u32[]{:S(2)}, u32[]{:S(2)}) %collective-permute-start.16) | collective-permute-done | bytes 540704 | tf_op jit(solution)/shard_map/ppermute | solution.py:50
  159.8 0.9 add.167.refs_0_
  160.6 4.2 %shard_map.50.refs_4_ = f32[2048,256]{1,0:T(8,128)} custom-call(s32[32]{0:T(128)} %add.148.place_ref, s32[16]{0:T(128)} %reshape.145.slot_ref, s32[4]{0:T(128)} %and_select_fusion.1.dest_ref, f32[32]{0:T(128)} %reshape.146.taper_ref, f32[1056,256]{1,0:T(8,128)} %reduce-scatter.2.cloned.1.call-done.own_ref, f32[1056,128]{1,0:T(8,128)} %add.167.refs_0_), custom_call_target="tpu_custom_call" | custom-call | flops 1048576 | bytes 4194304 | tf_op jit(solution)/shard_map/pallas_call | solution.py:255
  164.9 0.8 copy-done.2
  166.0 4.7 %shard_map.51 = f32[2048,256]{1,0:T(8,128)} custom-call(s32[32]{0:T(128)} %add.148.place_ref, s32[16]{0:T(128)} %reshape.145.slot_ref, s32[4]{0:T(128)} %and_select_fusion.1.dest_ref, f32[32]{0:T(128)} %reshape.146.taper_ref, f32[1056,256]{1,0:T(8,128)} %reduce-scatter.2.cloned.1.call-done.own_ref, ...), custom_call_target="tpu_custom_call", output_to_operand_aliasing={{}: (9, {})} | custom-call | flops 1048576 | bytes 4194304 | tf_op jit(solution)/shard_map/pallas_call | solution.py:255
  (62 shorter events, 4.1 us)
Async XLA Ops:
  6.5 154.1 %reduce-scatter.2.cloned.1.call-start = ((), (), s32[]{:S(2)}) async-start(), calls=%async_computation.1 | async-start | bytes 5406720 | tf_op jit(solution)/shard_map/reduce_scatter | solution.py:322
  8.0 10.5 %collective-permute-start.3 = (s32[2]{0:T(128)S(1)}, s32[2]{0:T(128)S(1)}, u32[]{:S(2)}, u32[]{:S(2)}) collective-permute-start(s32[2]{0:T(128)S(1)} %get-tuple-element.48), channel_id=1, source_target_pairs={{0,2},{1,3},{2,4},{3,5},{4,6},{5,7},{6,8},{7,9},{8,10},{9,11},{10,... | collective-permute-start | bytes 32 | tf_op jit(solution)/shard_map/ppermute | solution.py:42
  10.1 8.4 %collective-permute-start.2 = (s32[2]{0:T(128)S(1)}, s32[2]{0:T(128)S(1)}, u32[]{:S(2)}, u32[]{:S(2)}) collective-permute-start(s32[2]{0:T(128)S(1)} %get-tuple-element.49), channel_id=1, source_target_pairs={{0,63},{1,2},{2,1},{3,4},{4,3},{5,6},{6,5},{7,8},{8,7},{9,10},{10,... | collective-permute-start | bytes 32 | tf_op jit(solution)/shard_map/ppermute | solution.py:42
  12.1 6.4 %collective-permute-start.1 = (s32[2]{0:T(128)S(1)}, s32[2]{0:T(128)S(1)}, u32[]{:S(2)}, u32[]{:S(2)}) collective-permute-start(s32[2]{0:T(128)S(1)} %get-tuple-element.50), channel_id=1, source_target_pairs={{0,1},{1,0},{2,3},{3,2},{4,5},{5,4},{6,7},{7,6},{8,9},{9,8},{10,11... | collective-permute-start | bytes 32 | tf_op jit(solution)/shard_map/ppermute | solution.py:42
  17.2 2.4 %collective-permute-start = (s32[2]{0:T(128)S(1)}, s32[2]{0:T(128)S(1)}, u32[]{:S(2)}, u32[]{:S(2)}) collective-permute-start(s32[2]{0:T(128)S(1)} %get-tuple-element.47), channel_id=1, source_target_pairs={{0,62},{1,63},{2,0},{3,1},{4,2},{5,3},{6,4},{7,5},{8,6},{9,7},{10,... | collective-permute-start | bytes 32 | tf_op jit(solution)/shard_map/ppermute | solution.py:42
  28.0 27.2 %collective-permute-start.4 = (bf16[2048,256]{1,0:T(8,128)(2,1)}, bf16[2048,256]{1,0:T(8,128)(2,1)}, u32[]{:S(2)}, u32[]{:S(2)}) collective-permute-start(bf16[2048,256]{1,0:T(8,128)(2,1)} %get-tuple-element.27), channel_id=1, source_target_pairs={{0,2},{1,3},{2,4},{3,5},{4,6},{5,7},{6,8},{7,9},{8,10},{9,11},{10,... | collective-permute-start | bytes 3145736 | tf_op jit(solution)/shard_map/ppermute | solution.py:42
  28.1 34.5 %collective-permute-start.5 = (bf16[2048,256]{1,0:T(8,128)(2,1)}, bf16[2048,256]{1,0:T(8,128)(2,1)}, u32[]{:S(2)}, u32[]{:S(2)}) collective-permute-start(bf16[2048,256]{1,0:T(8,128)(2,1)} %get-tuple-element.28), channel_id=1, source_target_pairs={{0,63},{1,2},{2,1},{3,4},{4,3},{5,6},{6,5},{7,8},{8,7},{9,10},{10,... | collective-permute-start | bytes 3145736 | tf_op jit(solution)/shard_map/ppermute | solution.py:42
  28.7 33.9 %collective-permute-start.6 = (bf16[2048,256]{1,0:T(8,128)(2,1)}, bf16[2048,256]{1,0:T(8,128)(2,1)}, u32[]{:S(2)}, u32[]{:S(2)}) collective-permute-start(bf16[2048,256]{1,0:T(8,128)(2,1)} %get-tuple-element.29), channel_id=1, source_target_pairs={{0,62},{1,63},{2,0},{3,1},{4,2},{5,3},{6,4},{7,5},{8,6},{9,7},{10,... | collective-permute-start | bytes 3145736 | tf_op jit(solution)/shard_map/ppermute | solution.py:42
  62.6 6.2 %copy-start.5 = (s32[4,8]{1,0:T(4,128)S(1)}, s32[4,8]{1,0:T(4,128)}, u32[]{:S(2)}) copy-start(s32[4,8]{1,0:T(4,128)} %param.5) | copy-start | bytes 388
  62.6 7.0 %copy-start.7 = (s32[4]{0:T(128)S(1)}, s32[4]{0:T(128)}, u32[]{:S(2)}) copy-start(s32[4]{0:T(128)} %constant.131.clone) | copy-start | bytes 52
  62.6 7.6 %copy-start.9 = (bf16[2048,256]{1,0:T(8,128)(2,1)S(1)}, bf16[2048,256]{1,0:T(8,128)(2,1)}, u32[]{:S(2)}) copy-start(bf16[2048,256]{1,0:T(8,128)(2,1)} %get-tuple-element.35) | copy-start | bytes 3145732
  62.6 13.0 %collective-permute-start.8 = (bf16[2048,512]{1,0:T(8,128)(2,1)}, bf16[2048,512]{1,0:T(8,128)(2,1)S(1)}, u32[]{:S(2)}, u32[]{:S(2)}) collective-permute-start(bf16[2048,512]{1,0:T(8,128)(2,1)} %get-tuple-element.33), channel_id=1, source_target_pairs={{0,1},{1,0},{2,3},{3,2},{4,5},{5,4},{6,7},{7,6},{8,9},{9,8},{10,11... | collective-permute-start | bytes 6291464 | tf_op jit(solution)/shard_map/ppermute | solution.py:42
  70.2 45.0 %collective-permute-start.7 = (bf16[2048,256]{1,0:T(8,128)(2,1)}, bf16[2048,256]{1,0:T(8,128)(2,1)}, u32[]{:S(2)}, u32[]{:S(2)}) collective-permute-start(bf16[2048,256]{1,0:T(8,128)(2,1)} %get-tuple-element.32), channel_id=1, source_target_pairs={{0,2},{1,3},{2,4},{3,5},{4,6},{5,7},{6,8},{7,9},{8,10},{9,11},{10,... | collective-permute-start | bytes 3145736 | tf_op jit(solution)/shard_map/ppermute | solution.py:42
  70.2 45.0 %collective-permute-start.9 = (bf16[2048,256]{1,0:T(8,128)(2,1)}, bf16[2048,256]{1,0:T(8,128)(2,1)}, u32[]{:S(2)}, u32[]{:S(2)}) collective-permute-start(bf16[2048,256]{1,0:T(8,128)(2,1)} %get-tuple-element.34), channel_id=1, source_target_pairs={{0,63},{1,2},{2,1},{3,4},{4,3},{5,6},{6,5},{7,8},{8,7},{9,10},{10,... | collective-permute-start | bytes 3145736 | tf_op jit(solution)/shard_map/ppermute | solution.py:42
  70.2 45.0 %collective-permute-start.10 = (bf16[2048,256]{1,0:T(8,128)(2,1)S(1)}, bf16[2048,256]{1,0:T(8,128)(2,1)}, u32[]{:S(2)}, u32[]{:S(2)}) collective-permute-start(bf16[2048,256]{1,0:T(8,128)(2,1)S(1)} %copy-done.9), channel_id=1, source_target_pairs={{0,62},{1,63},{2,0},{3,1},{4,2},{5,3},{6,4},{7,5},{8,6},{9,7},{10,... | collective-permute-start | bytes 3145736 | tf_op jit(solution)/shard_map/ppermute | solution.py:42
  75.6 1.3 copy-start.8
  88.6 21.0 %collective-permute-start.14 = (f32[1056,128]{1,0:T(8,128)}, f32[1056,128]{1,0:T(8,128)S(1)}, u32[]{:S(2)}, u32[]{:S(2)}) collective-permute-start(f32[1056,128]{1,0:T(8,128)} %get-tuple-element.43), channel_id=1, source_target_pairs={{0,64},{1,193},{2,66},{3,195},{4,68},{5,197},{6,70},{7,199},{8,72}... | collective-permute-start | bytes 1622024 | tf_op jit(solution)/shard_map/ppermute | solution.py:50
  110.8 18.3 %collective-permute-start.15 = (f32[1056,128]{1,0:T(8,128)S(1)}, f32[1056,128]{1,0:T(8,128)S(1)}, u32[]{:S(2)}, u32[]{:S(2)}) collective-permute-start(f32[1056,128]{1,0:T(8,128)S(1)} %add.165), channel_id=1, source_target_pairs={{0,64},{1,193},{2,66},{3,195},{4,68},{5,197},{6,70},{7,199},{8,72}... | collective-permute-start | bytes 1622024 | tf_op jit(solution)/shard_map/ppermute | solution.py:50
  115.2 13.9 %copy-start.1 = (f32[1056,128]{1,0:T(8,128)S(1)}, f32[1056,128]{1,0:T(8,128)}, u32[]{:S(2)}) copy-start(f32[1056,128]{1,0:T(8,128)} %get-tuple-element.45) | copy-start | bytes 1622020
  115.2 15.5 %copy-start.6 = (s32[4,8]{1,0:T(4,128)S(1)}, s32[4,8]{1,0:T(4,128)}, u32[]{:S(2)}) copy-start(s32[4,8]{1,0:T(4,128)} %param.6) | copy-start | bytes 388
  115.2 44.6 %copy-start = (f32[1056,128]{1,0:T(8,128)S(1)}, f32[1056,128]{1,0:T(8,128)}, u32[]{:S(2)}) copy-start(f32[1056,128]{1,0:T(8,128)} %get-tuple-element.46) | copy-start | bytes 1622020
  126.3 38.5 %collective-permute-start.11 = (f32[1056,128]{1,0:T(8,128)}, f32[1056,128]{1,0:T(8,128)S(1)}, u32[]{:S(2)}, u32[]{:S(2)}) collective-permute-start(f32[1056,128]{1,0:T(8,128)} %get-tuple-element.37), channel_id=1, source_target_pairs={{0,64},{64,128},{128,192},{192,0},{1,65},{65,129},{129,193},{193,1... | collective-permute-start | bytes 1622024 | tf_op jit(solution)/shard_map/ppermute | solution.py:28
  126.4 38.4 %collective-permute-start.12 = (f32[1056,128]{1,0:T(8,128)}, f32[1056,128]{1,0:T(8,128)S(1)}, u32[]{:S(2)}, u32[]{:S(2)}) collective-permute-start(f32[1056,128]{1,0:T(8,128)} %get-tuple-element.38), channel_id=1, source_target_pairs={{0,128},{64,192},{128,0},{192,64},{1,129},{65,193},{129,1},{193,65... | collective-permute-start | bytes 1622024 | tf_op jit(solution)/shard_map/ppermute | solution.py:28
  127.6 37.2 %collective-permute-start.13 = (f32[1056,128]{1,0:T(8,128)}, f32[1056,128]{1,0:T(8,128)S(1)}, u32[]{:S(2)}, u32[]{:S(2)}) collective-permute-start(f32[1056,128]{1,0:T(8,128)} %get-tuple-element.39), channel_id=1, source_target_pairs={{0,192},{64,0},{128,64},{192,128},{1,193},{65,1},{129,65},{193,129... | collective-permute-start | bytes 1622024 | tf_op jit(solution)/shard_map/ppermute | solution.py:28
  129.1 30.7 %collective-permute-start.16 = (f32[1056,128]{1,0:T(8,128)S(1)}, f32[1056,128]{1,0:T(8,128)S(1)}, u32[]{:S(2)}, u32[]{:S(2)}) collective-permute-start(f32[1056,128]{1,0:T(8,128)S(1)} %add.166), channel_id=1, source_target_pairs={{0,64},{1,193},{2,66},{3,195},{4,68},{5,197},{6,70},{7,199},{8,72}... | collective-permute-start | bytes 1622024 | tf_op jit(solution)/shard_map/ppermute | solution.py:50
  164.8 0.8 copy-start.2
  164.8 1.0 copy-start.3
  164.8 1.2 copy-start.4
Sparse Core Ops, SparseCore 0:
  62.8 65.2 reduce-scatter.1

commit v5 on v4

--- a/solution.py
+++ b/solution.py
@@ -16,6 +16,9 @@
 HALF = 128
 STAGES = 2
 EXTRA = 8
+CODE_EXTRA = 16
+TOP = 32766.0
+STEPS = 256.0
 
 EPSILON = 1e-06
 MIB = 1 << 20
@@ -42,14 +45,6 @@
     return lax.ppermute(value, "blk", sorted(pairs))
 
 
-def ringed(value):
-    samp, count = lax.axis_size("samp"), lax.axis_size("blk")
-    pairs = [
-        (y * count + i, (y + 1 - 2 * (i % 2)) % samp * count + i) for y in range(samp) for i in range(count)
-    ]
-    return lax.ppermute(value, ("samp", "blk"), pairs)
-
-
 def taper_table():
     scaled = 2.0 * (jnp.arange(NBIN, dtype=jnp.float32) + 0.5) / NBIN
     inner = (((-0.25 * scaled + 0.5) * scaled + 0.625) * scaled - 5.0 / 3.0) * scaled * scaled + 1.0
@@ -59,6 +54,27 @@
         - 2.0 / (3.0 * scaled)
     )
     return jnp.where(scaled <= 1.0, inner, outer)
+
+
+def scale_code(largest):
+    return jnp.ceil(jnp.log2(jnp.maximum(largest, 1e-30)) * STEPS)
+
+
+def encode(tile):
+    code = scale_code(jnp.max(jnp.abs(tile), axis=0, keepdims=True))
+    scaled = jnp.round(tile * (jnp.exp2(code * (-1.0 / STEPS)) * TOP))
+    return jnp.clip(scaled, -TOP, TOP), code
+
+
+def encode_norm(norm):
+    code = scale_code(norm)
+    scaled = norm * (jnp.exp2(code * (-1.0 / STEPS)) * TOP)
+    high = jnp.round(scaled)
+    return [code, high, jnp.round((scaled - high) * TOP)]
+
+
+def decoded_scale(code):
+    return jnp.exp2(code * (1.0 / STEPS)) * (1.0 / TOP)
 
 
 def select_kernel(plan, want_ref, source_ref, *refs):
@@ -79,12 +95,13 @@
         write.wait()
 
 
-def select(want, perturb):
+def select(stage, want, perturb):
     samples = perturb.shape[0]
-    widths = [2 * HALF] * 6 + [4 * HALF]
-    plan = [(q, side, 0, out, side) for out, q in enumerate((0, 2, 3)) for side in range(2)]
-    plan += [(1, side, half, 6, 2 * half + side) for half in range(2) for side in range(2)]
-    plan += [(q, side, 1, 3 + out, side) for out, q in enumerate((0, 2, 3)) for side in range(2)]
+    widths = [2 * HALF] * 3
+    plan = [(q, side, stage, out, side) for out, q in enumerate((0, 2, 3)) for side in range(2)]
+    if stage == 1:
+        plan += [(1, side, half, 3, 2 * half + side) for half in range(2) for side in range(2)]
+        widths.append(4 * HALF)
     return pl.pallas_call(
         functools.partial(select_kernel, plan),
         grid_spec=pltpu.PrefetchScalarGridSpec(
@@ -172,6 +189,7 @@
             copy.wait()
 
     at = at_ref[...]
+    codes = [[] for _ in range(samp - 1)]
     for pair in range(2):
         u = r * 4 + 2 * pair
         cols = jnp.concatenate([cols_ref[slot_ref[u]], cols_ref[slot_ref[u + 1]]], axis=1)
@@ -181,9 +199,15 @@
             j = 2 * pair + side
             for d in range(samp):
                 first = pl.multiple_of(dest_ref[d] * rows, rows)
-                parts[d][j * rows : (j + 1) * rows, :] = tile_ref[pl.ds(first, rows), side * HALF : (side + 1) * HALF]
+                piece = tile_ref[pl.ds(first, rows), side * HALF : (side + 1) * HALF]
+                if d > 0:
+                    piece, code = encode(piece)
+                    piece = piece.astype(jnp.int32).astype(jnp.int16)
+                    codes[d - 1].append(code)
+                parts[d][j * rows : (j + 1) * rows, :] = piece
 
     step = 128
+    norm_codes = []
     for side in range(2):
         def add(i, total):
             x = cols_ref[2 * r + side, pl.ds(pl.multiple_of(i * step, step), step), :].astype(jnp.float32)
@@ -191,15 +215,21 @@
 
         total = lax.fori_loop(0, samples // step, add, jnp.zeros((8, HALF), jnp.float32))
         norm = jnp.sum(total, axis=0, keepdims=True)
-        for d in range(samp):
-            parts[d][BS + side * 4 : BS + side * 4 + 4, :] = jnp.broadcast_to(norm, (4, HALF))
+        norm_codes += encode_norm(norm)
+        parts[0][BS + side * 4 : BS + side * 4 + 4, :] = jnp.broadcast_to(norm, (4, HALF))
+    row_id = lax.broadcasted_iota(jnp.int32, (CODE_EXTRA, HALF), 0)
+    for d in range(1, samp):
+        extra = jnp.zeros((CODE_EXTRA, HALF), jnp.float32)
+        for i, row in enumerate(codes[d - 1] + norm_codes):
+            extra = jnp.where(row_id == i, row, extra)
+        parts[d][BS : BS + CODE_EXTRA, :] = extra.astype(jnp.int32).astype(jnp.int16)
 
 
 def remote_tiles(stage, slots, dest, at, blocks, samp):
     cells, samples = at.shape
-    block = BS + EXTRA
-    out_specs = [pl.BlockSpec((block, HALF), lambda r, *s: (r, 0))] * samp
-    out_shape = [jax.ShapeDtypeStruct((B_DEV * block, HALF), jnp.float32)] * samp
+    blocks_out = [(BS + EXTRA, jnp.float32)] + [(BS + CODE_EXTRA, jnp.int16)] * (samp - 1)
+    out_specs = [pl.BlockSpec((block, HALF), lambda r, *s: (r, 0)) for block, _ in blocks_out]
+    out_shape = [jax.ShapeDtypeStruct((B_DEV * block, HALF), dtype) for block, dtype in blocks_out]
     return pl.pallas_call(
         functools.partial(remote_kernel, stage),
         grid_spec=pltpu.PrefetchScalarGridSpec(
@@ -219,8 +249,8 @@
     )(slots, dest, at, *blocks)
 
 
-def final_kernel(half, rem_count, place_ref, slot_ref, dest_ref, taper_ref, own_ref, *refs):
-    rem_refs, out_ref = refs[:rem_count], refs[-1]
+def final_kernel(half, place_ref, slot_ref, dest_ref, taper_ref, own_ref, kept_ref, *refs):
+    coded_refs, out_ref, norm_ref = refs[:3], refs[-2], refs[-1]
     rows = out_ref.shape[0] // PAIR_DEV
     first = dest_ref[0] * rows
     cols = slice(half * HALF, (half + 1) * HALF)
@@ -228,6 +258,18 @@
     row = lax.broadcasted_iota(jnp.int32, (rows, BS), 0)
     mine = lane == row + first
     block = BS + EXTRA
+    coded = BS + CODE_EXTRA
+    extras = []
+    for r in range(B_DEV):
+        extras.append(
+            [ref[r * coded + BS : (r + 1) * coded, :].astype(jnp.int32).astype(jnp.float32) for ref in coded_refs]
+        )
+        for side in range(2):
+            norm = kept_ref[r * block + BS + side * 4 : r * block + BS + side * 4 + 1, :]
+            for extra in extras[r]:
+                code, high, low = (extra[4 + 3 * side + i : 5 + 3 * side + i, :] for i in range(3))
+                norm = norm + (high + low * (1.0 / TOP)) * decoded_scale(code)
+            norm_ref[2 * r + side : 2 * r + side + 1, :] = norm
     for r in range(B_DEV):
         base = r * block
         row_norm = own_ref[base + BS : base + BS + 1, :]
@@ -241,11 +283,12 @@
             out_ref[pl.ds(place_ref[u], rows, stride=PAIR_DEV), :] = tile * row_scale * col_scale
         for j in range(4):
             u = r * 4 + j
-            slot = slot_ref[u]
-            at_norm = pl.ds(slot // 2 * block + BS + slot % 2 * 4, 1)
-            norm = sum(ref[at_norm, :] for ref in rem_refs)
+            norm = norm_ref[pl.ds(slot_ref[u], 1), :]
             col_scale = taper_ref[16 + u] * lax.rsqrt(norm + EPSILON)
-            tile = sum(ref[base + j * rows : base + (j + 1) * rows, :] for ref in rem_refs)
+            tile = kept_ref[base + j * rows : base + (j + 1) * rows, :]
+            for ref, extra in zip(coded_refs, extras[r]):
+                piece = ref[r * coded + j * rows : r * coded + (j + 1) * rows, :].astype(jnp.int32).astype(jnp.float32)
+                tile = tile + piece * decoded_scale(extra[j : j + 1, :])
             out_ref[pl.ds(place_ref[16 + u], rows, stride=PAIR_DEV), :] = tile * row_scale * col_scale
 
 
@@ -253,7 +296,7 @@
     full = lambda shape: pl.BlockSpec(shape, lambda i, *s: (0,) * len(shape))
     before = [] if out is None else [out]
     return pl.pallas_call(
-        functools.partial(final_kernel, half, len(rems)),
+        functools.partial(final_kernel, half),
         grid_spec=pltpu.PrefetchScalarGridSpec(
             num_scalar_prefetch=4,
             grid=(1,),
@@ -261,6 +304,7 @@
             + [full(rem.shape) for rem in rems]
             + [pl.BlockSpec(memory_space=pl.ANY)] * len(before),
             out_specs=pl.BlockSpec((rows * PAIR_DEV, HALF), lambda i, *s: (0, half)),
+            scratch_shapes=[pltpu.VMEM((8, HALF), jnp.float32)],
         ),
         out_shape=jax.ShapeDtypeStruct((rows * PAIR_DEV, BS), jnp.float32),
         input_output_aliases={5 + len(rems): 0} if before else {},
@@ -307,28 +351,28 @@
     rows = BS // samp
     size = B_DEV * (BS + EXTRA)
     me = lax.axis_index("samp")
-    ahead = 1 - 2 * (here % 2)
-    ring_dest = (me + ahead * jnp.array([-1, -2, 1, 0], jnp.int32) + 2 * samp) % samp
     dest = (me + jnp.arange(samp, dtype=jnp.int32)) % samp
-    chosen = select(asked, perturb)
-    mates = exchanged(chosen[6], 1)
+    chosen = [select(stage, asked, perturb) for stage in range(STAGES)]
+    mates = exchanged(chosen[1][3], 1)
     got = []
     for stage in range(STAGES):
-        two_below, across, two_above = (exchanged(chosen[3 * stage + i], q) for i, q in enumerate((0, 2, 3)))
+        two_below, across, two_above = (exchanged(chosen[stage][i], q) for i, q in enumerate((0, 2, 3)))
         got.append([two_below, mates, across, two_above])
-    at, own_part = own_tiles(perturb, samp)
+    held, _ = lax.optimization_barrier((perturb, chosen[1][0]))
+    at, own_part = own_tiles(held, samp)
     own_part, *arrived = lax.optimization_barrier((own_part, got[0][0], got[0][2], got[0][3]))
     got[0] = [arrived[0], mates, arrived[1], arrived[2]]
     own_sum = lax.psum_scatter(own_part.reshape(samp * size, BS), "samp", scatter_dimension=0, tiled=True)
-    parts = remote_tiles(0, slots, ring_dest, at, got[0], samp)
-    running = parts[0]
-    for d in range(1, samp):
-        running = ringed(running) + parts[d]
-    parts = remote_tiles(1, slots, dest, at, got[1], samp)
-    last = [parts[0]] + [passed_along(parts[d], "samp", d) for d in range(1, samp)]
-
-    out = final(0, place, slots, dest, tapers, own_sum, [running], None, rows)
-    out = final(1, place, slots, dest, tapers, own_sum, last, out, rows)
+    sums = []
+    for stage in range(STAGES):
+        parts = remote_tiles(stage, slots, dest, at, got[stage], samp)
+        last = [parts[0]] + [passed_along(parts[d], "samp", d) for d in range(1, samp)]
+        if stage == 0:
+            dest, *last[1:3] = lax.optimization_barrier((dest, *last[1:3]))
+        sums.append(last)
+
+    out = final(0, place, slots, dest, tapers, own_sum, sums[0], None, rows)
+    out = final(1, place, slots, dest, tapers, own_sum, sums[1], out, rows)
     return out.reshape(rows, PAIR_DEV, BS)
 
 

time: 178 us -> 157 us (0.88)
  the two profiles are of different devices: /device:TPU:1 before, /device:TPU:8 now
where the time goes in v5:
time: 157 us; the launch traced here: 156 us
  Pallas kernels  56.3 us (36%)
  starting transfers between devices  41.4 us (26%)
  waiting for transfers between devices  34.8 us (22%)
  between operations  13.5 us (9%)
  local copies, waits for them, and re-layouts  7.25 us (5%)
  other arithmetic  3.15 us (2%)
    ppermute x11, starting transfers between devices, exchanged(): return lax.ppermute(value, 'blk', sorted(pairs))  25.1 us
    pallas_call x2, Pallas kernels, remote_tiles(): pl.pallas_call(functools.partial(remote_kernel, stage), grid_spec=pltpu.P...  22.6 us
    ppermute x6, waiting for transfers between devices, passed_along(): return lax.ppermute(value, axis, pairs)  18.2 us
    ppermute x11, waiting for transfers between devices, exchanged(): return lax.ppermute(value, 'blk', sorted(pairs))  16.6 us
    ppermute x6, starting transfers between devices, passed_along(): return lax.ppermute(value, axis, pairs)  16.3 us
    pallas_call x1, Pallas kernels, own_tiles(): pl.pallas_call(own_kernel, grid=(B_DEV,), in_specs=[pl.BlockSpec((samples...  15.2 us
    pallas_call x2, Pallas kernels, select(): pl.pallas_call(functools.partial(select_kernel, plan), grid_spec=pltpu.Pr...  9.32 us
    pallas_call x2, Pallas kernels, final(): pl.pallas_call(functools.partial(final_kernel, half), grid_spec=pltpu.Pre...  9.12 us
  transfers between devices with their start and end apart: 18, of which 8 were waited for; matrix products, arithmetic and copies ran while one was open for 2% of the time, Pallas kernels for 31%

profile of v5, /device:TPU:8, one launch (start us, length us, event | category | flops | bytes accessed | tf_op | source)
XLA Modules:
  0.0 156.4 jit_solution(10167590728609878612)
XLA Ops:
  6.5 0.7 add_select_fusion
  8.0 8.1 %collective-permute-start = (s32[2]{0:T(128)S(1)}, s32[2]{0:T(128)S(1)}, u32[]{:S(2)}, u32[]{:S(2)}) collective-permute-start(s32[2]{0:T(128)S(1)} %get-tuple-element.55), channel_id=1, source_target_pairs={{0,62},{1,63},{2,0},{3,1},{4,2},{5,3},{6,4},{7,5},{8,6},{9,7},{10,... | collective-permute-start | bytes 32 | tf_op jit(solution)/shard_map/ppermute | solution.py:45
  16.1 4.2 %collective-permute-start.2 = (s32[2]{0:T(128)S(1)}, s32[2]{0:T(128)S(1)}, u32[]{:S(2)}, u32[]{:S(2)}) collective-permute-start(s32[2]{0:T(128)S(1)} %get-tuple-element.57), channel_id=1, source_target_pairs={{0,63},{1,2},{2,1},{3,4},{4,3},{5,6},{6,5},{7,8},{8,7},{9,10},{10,... | collective-permute-start | bytes 32 | tf_op jit(solution)/shard_map/ppermute | solution.py:45
  20.3 2.6 %collective-permute-done.3 = s32[2]{0:T(128)S(1)} collective-permute-done((s32[2]{0:T(128)S(1)}, s32[2]{0:T(128)S(1)}, u32[]{:S(2)}, u32[]{:S(2)}) %collective-permute-start.3) | collective-permute-done | bytes 40 | tf_op jit(solution)/shard_map/ppermute | solution.py:45
  23.6 3.7 %shard_map.39 = (bf16[2048,256]{1,0:T(8,128)(2,1)}, bf16[2048,256]{1,0:T(8,128)(2,1)}, bf16[2048,256]{1,0:T(8,128)(2,1)}) custom-call(s32[8]{0:T(128)} %pad_add_fusion.2.want_ref, bf16[2048,1024]{1,0:T(8,128)(2,1)} %source_ref.3), custom_call_target="tpu_custom_call" | custom-call | bytes 6291456 | tf_op jit(solution)/shard_map/pallas_call | solution.py:105
  27.4 3.5 %collective-permute-start.5 = (bf16[2048,256]{1,0:T(8,128)(2,1)}, bf16[2048,256]{1,0:T(8,128)(2,1)}, u32[]{:S(2)}, u32[]{:S(2)}) collective-permute-start(bf16[2048,256]{1,0:T(8,128)(2,1)} %get-tuple-element.35), channel_id=1, source_target_pairs={{0,63},{1,2},{2,1},{3,4},{4,3},{5,6},{6,5},{7,8},{8,7},{9,10},{10,... | collective-permute-start | bytes 3145736 | tf_op jit(solution)/shard_map/ppermute | solution.py:45
  30.9 1.8 %collective-permute-start.6 = (bf16[2048,256]{1,0:T(8,128)(2,1)}, bf16[2048,256]{1,0:T(8,128)(2,1)}, u32[]{:S(2)}, u32[]{:S(2)}) collective-permute-start(bf16[2048,256]{1,0:T(8,128)(2,1)} %get-tuple-element.36), channel_id=1, source_target_pairs={{0,62},{1,63},{2,0},{3,1},{4,2},{5,3},{6,4},{7,5},{8,6},{9,7},{10,... | collective-permute-start | bytes 3145736 | tf_op jit(solution)/shard_map/ppermute | solution.py:45
  32.7 5.6 %shard_map.37 = (bf16[2048,256]{1,0:T(8,128)(2,1)}, bf16[2048,256]{1,0:T(8,128)(2,1)}, bf16[2048,256]{1,0:T(8,128)(2,1)}, bf16[2048,512]{1,0:T(8,128)(2,1)}) custom-call(s32[8]{0:T(128)} %pad_add_fusion.2.want_ref, bf16[2048,1024]{1,0:T(8,128)(2,1)} %source_ref.3), custom_call_target="tpu_custom_call" | custom-call | bytes 10485760 | tf_op jit(solution)/shard_map/pallas_call | solution.py:105
  38.3 15.2 %shard_map.38 = (bf16[1024,2048]{1,0:T(8,128)(2,1)}, f32[4,1056,256]{2,1,0:T(8,128)}) custom-call(bf16[2048,1024]{1,0:T(8,128)(2,1)} %source_ref.3, bf16[2048,1024]{1,0:T(8,128)(2,1)} %source_ref.3), custom_call_target="tpu_custom_call" | custom-call | flops 4294967296 | bytes 12582912 | tf_op jit(solution)/shard_map/pallas_call | solution.py:146
  53.5 3.6 %collective-permute-done.4.refs_0_ = bf16[2048,256]{1,0:T(8,128)(2,1)} collective-permute-done((bf16[2048,256]{1,0:T(8,128)(2,1)}, bf16[2048,256]{1,0:T(8,128)(2,1)}, u32[]{:S(2)}, u32[]{:S(2)}) %collective-permute-start.4) | collective-permute-done | bytes 1048608 | tf_op jit(solution)/shard_map/ppermute | solution.py:45
  57.1 9.0 %collective-permute-done.5.refs_2_ = bf16[2048,256]{1,0:T(8,128)(2,1)} collective-permute-done((bf16[2048,256]{1,0:T(8,128)(2,1)}, bf16[2048,256]{1,0:T(8,128)(2,1)}, u32[]{:S(2)}, u32[]{:S(2)}) %collective-permute-start.5) | collective-permute-done | bytes 1048608 | tf_op jit(solution)/shard_map/ppermute | solution.py:45
  67.6 5.5 %collective-permute-start.11 = (bf16[2048,256]{1,0:T(8,128)(2,1)}, bf16[2048,256]{1,0:T(8,128)(2,1)S(1)}, u32[]{:S(2)}, u32[]{:S(2)}) collective-permute-start(bf16[2048,256]{1,0:T(8,128)(2,1)} %get-tuple-element.45), channel_id=1, source_target_pairs={{0,63},{1,2},{2,1},{3,4},{4,3},{5,6},{6,5},{7,8},{8,7},{9,10},{10,... | collective-permute-start | bytes 3145736 | tf_op jit(solution)/shard_map/ppermute | solution.py:45
  73.1 1.7 %collective-permute-start.12 = (bf16[2048,256]{1,0:T(8,128)(2,1)}, bf16[2048,256]{1,0:T(8,128)(2,1)}, u32[]{:S(2)}, u32[]{:S(2)}) collective-permute-start(bf16[2048,256]{1,0:T(8,128)(2,1)} %get-tuple-element.46), channel_id=1, source_target_pairs={{0,62},{1,63},{2,0},{3,1},{4,2},{5,3},{6,4},{7,5},{8,6},{9,7},{10,... | collective-permute-start | bytes 3145736 | tf_op jit(solution)/shard_map/ppermute | solution.py:45
  75.4 1.3 copy-done.8
  76.7 11.4 %shard_map.40 = (f32[1056,128]{1,0:T(8,128)}, s16[1088,128]{1,0:T(8,128)(2,1)}, s16[1088,128]{1,0:T(8,128)(2,1)}, s16[1088,128]{1,0:T(8,128)(2,1)}) custom-call(s32[16]{0:T(128)} %reshape.145.slot_ref, s32[4]{0:T(128)} %and_select_fusion.dest_ref, bf16[1024,2048]{1,0:T(8,128)(2,1)} %get-tuple-element.32.at_ref, ...), custom_call_target="tpu_custom_call" | custom-call | flops 4294967296 | bytes 10485760 | tf_op jit(solution)/shard_map/pallas_call | solution.py:233
  88.2 1.6 %collective-permute-start.8 = (s16[1088,128]{1,0:T(8,128)(2,1)}, s16[1088,128]{1,0:T(8,128)(2,1)S(1)}, u32[]{:S(2)}, u32[]{:S(2)}) collective-permute-start(s16[1088,128]{1,0:T(8,128)(2,1)} %get-tuple-element.41), channel_id=1, source_target_pairs={{0,64},{64,128},{128,192},{192,0},{1,65},{65,129},{129,193},{193,1... | collective-permute-start | bytes 835592 | tf_op jit(solution)/shard_map/ppermute | solution.py:31
  89.8 1.0 collective-permute-start.9
  91.1 13.1 %collective-permute-done.8.refs_0_ = s16[1088,128]{1,0:T(8,128)(2,1)S(1)} collective-permute-done((s16[1088,128]{1,0:T(8,128)(2,1)}, s16[1088,128]{1,0:T(8,128)(2,1)S(1)}, u32[]{:S(2)}, u32[]{:S(2)}) %collective-permute-start.8) | collective-permute-done | bytes 278560 | tf_op jit(solution)/shard_map/ppermute | solution.py:31
  104.1 1.2 collective-permute-start.16
  105.4 1.3 collective-permute-done.9.refs_1_
  106.7 1.3 collective-permute-done.11.refs_2_
  108.0 1.0 copy-done.11
  109.0 1.0 copy-done.10
  110.0 11.2 %shard_map.41 = (f32[1056,128]{1,0:T(8,128)}, s16[1088,128]{1,0:T(8,128)(2,1)}, s16[1088,128]{1,0:T(8,128)(2,1)}, s16[1088,128]{1,0:T(8,128)(2,1)}) custom-call(s32[16]{0:T(128)} %reshape.145.slot_ref, s32[4]{0:T(128)} %and_select_fusion.dest_ref, bf16[1024,2048]{1,0:T(8,128)(2,1)} %get-tuple-element.32.at_ref, bf16[2048,256]{1,0:T(8,128)(2,1)} %copy-done.10, ...), custom_call_target="tpu_custom_call" | custom-call | flops 4294967296 | bytes 10485760 | tf_op jit(solution)/shard_map/pallas_call | solution.py:233
  121.2 9.0 %collective-permute-start.13 = (s16[1088,128]{1,0:T(8,128)(2,1)}, s16[1088,128]{1,0:T(8,128)(2,1)S(1)}, u32[]{:S(2)}, u32[]{:S(2)}) collective-permute-start(s16[1088,128]{1,0:T(8,128)(2,1)} %get-tuple-element.48), channel_id=1, source_target_pairs={{0,64},{64,128},{128,192},{192,0},{1,65},{65,129},{129,193},{193,1... | collective-permute-start | bytes 835592 | tf_op jit(solution)/shard_map/ppermute | solution.py:31
  130.2 3.4 %collective-permute-start.14 = (s16[1088,128]{1,0:T(8,128)(2,1)}, s16[1088,128]{1,0:T(8,128)(2,1)S(1)}, u32[]{:S(2)}, u32[]{:S(2)}) collective-permute-start(s16[1088,128]{1,0:T(8,128)(2,1)} %get-tuple-element.49), channel_id=1, source_target_pairs={{0,128},{64,192},{128,0},{192,64},{1,129},{65,193},{129,1},{193,65... | collective-permute-start | bytes 835592 | tf_op jit(solution)/shard_map/ppermute | solution.py:31
  135.2 0.7 copy-done.2
  135.9 4.6 %shard_map.42.refs_3_ = f32[2048,256]{1,0:T(8,128)} custom-call(s32[32]{0:T(128)} %add.127.place_ref, s32[16]{0:T(128)} %reshape.145.slot_ref, s32[4]{0:T(128)} %and_select_fusion.dest_ref, f32[32]{0:T(128)} %reshape.146.taper_ref, f32[1056,256]{1,0:T(8,128)} %reduce-scatter.2.cloned.1.call-done.own_ref, f32[1056,128]{1,0:T(8,128)} %get-tuple-element.51.kept_ref, ...), custom_call_target="tpu_custom_call" | custom-call | flops 1048576 | bytes 4194304 | tf_op jit(solution)/shard_map/pallas_call | solution.py:298
  140.4 0.9 collective-permute-done.14.refs_1_
  141.3 3.0 %collective-permute-done.15.refs_2_ = s16[1088,128]{1,0:T(8,128)(2,1)S(1)} collective-permute-done((s16[1088,128]{1,0:T(8,128)(2,1)}, s16[1088,128]{1,0:T(8,128)(2,1)S(1)}, u32[]{:S(2)}, u32[]{:S(2)}) %collective-permute-start.15) | collective-permute-done | bytes 278560 | tf_op jit(solution)/shard_map/ppermute | solution.py:31
  144.3 0.7 copy-done.5
  145.0 4.6 %shard_map.43 = f32[2048,256]{1,0:T(8,128)} custom-call(s32[32]{0:T(128)} %add.127.place_ref, s32[16]{0:T(128)} %reshape.145.slot_ref, s32[4]{0:T(128)} %and_select_fusion.dest_ref, f32[32]{0:T(128)} %reshape.146.taper_ref, f32[1056,256]{1,0:T(8,128)} %reduce-scatter.2.cloned.1.call-done.own_ref, ...), custom_call_target="tpu_custom_call", output_to_operand_aliasing={{}: (9, {})} | custom-call | flops 1048576 | bytes 4194304 | tf_op jit(solution)/shard_map/pallas_call | solution.py:298
  (63 shorter events, 5.3 us)
Async XLA Ops:
  6.5 128.6 %reduce-scatter.2.cloned.1.call-start = ((), (), s32[]{:S(2)}) async-start(), calls=%async_computation.1 | async-start | bytes 5406720 | tf_op jit(solution)/shard_map/reduce_scatter | solution.py:365
  8.0 12.4 %collective-permute-start = (s32[2]{0:T(128)S(1)}, s32[2]{0:T(128)S(1)}, u32[]{:S(2)}, u32[]{:S(2)}) collective-permute-start(s32[2]{0:T(128)S(1)} %get-tuple-element.55), channel_id=1, source_target_pairs={{0,62},{1,63},{2,0},{3,1},{4,2},{5,3},{6,4},{7,5},{8,6},{9,7},{10,... | collective-permute-start | bytes 32 | tf_op jit(solution)/shard_map/ppermute | solution.py:45
  16.1 6.9 %collective-permute-start.3 = (s32[2]{0:T(128)S(1)}, s32[2]{0:T(128)S(1)}, u32[]{:S(2)}, u32[]{:S(2)}) collective-permute-start(s32[2]{0:T(128)S(1)} %get-tuple-element.56), channel_id=1, source_target_pairs={{0,2},{1,3},{2,4},{3,5},{4,6},{5,7},{6,8},{7,9},{8,10},{9,11},{10,... | collective-permute-start | bytes 32 | tf_op jit(solution)/shard_map/ppermute | solution.py:45
  16.1 6.9 %collective-permute-start.2 = (s32[2]{0:T(128)S(1)}, s32[2]{0:T(128)S(1)}, u32[]{:S(2)}, u32[]{:S(2)}) collective-permute-start(s32[2]{0:T(128)S(1)} %get-tuple-element.57), channel_id=1, source_target_pairs={{0,63},{1,2},{2,1},{3,4},{4,3},{5,6},{6,5},{7,8},{8,7},{9,10},{10,... | collective-permute-start | bytes 32 | tf_op jit(solution)/shard_map/ppermute | solution.py:45
  20.3 2.6 %collective-permute-start.1 = (s32[2]{0:T(128)S(1)}, s32[2]{0:T(128)S(1)}, u32[]{:S(2)}, u32[]{:S(2)}) collective-permute-start(s32[2]{0:T(128)S(1)} %get-tuple-element.58), channel_id=1, source_target_pairs={{0,1},{1,0},{2,3},{3,2},{4,5},{5,4},{6,7},{7,6},{8,9},{9,8},{10,11... | collective-permute-start | bytes 32 | tf_op jit(solution)/shard_map/ppermute | solution.py:45
  27.3 29.8 %collective-permute-start.4 = (bf16[2048,256]{1,0:T(8,128)(2,1)}, bf16[2048,256]{1,0:T(8,128)(2,1)}, u32[]{:S(2)}, u32[]{:S(2)}) collective-permute-start(bf16[2048,256]{1,0:T(8,128)(2,1)} %get-tuple-element.34), channel_id=1, source_target_pairs={{0,2},{1,3},{2,4},{3,5},{4,6},{5,7},{6,8},{7,9},{8,10},{9,11},{10,... | collective-permute-start | bytes 3145736 | tf_op jit(solution)/shard_map/ppermute | solution.py:45
  27.4 38.7 %collective-permute-start.5 = (bf16[2048,256]{1,0:T(8,128)(2,1)}, bf16[2048,256]{1,0:T(8,128)(2,1)}, u32[]{:S(2)}, u32[]{:S(2)}) collective-permute-start(bf16[2048,256]{1,0:T(8,128)(2,1)} %get-tuple-element.35), channel_id=1, source_target_pairs={{0,63},{1,2},{2,1},{3,4},{4,3},{5,6},{6,5},{7,8},{8,7},{9,10},{10,... | collective-permute-start | bytes 3145736 | tf_op jit(solution)/shard_map/ppermute | solution.py:45
  30.9 35.2 %collective-permute-start.6 = (bf16[2048,256]{1,0:T(8,128)(2,1)}, bf16[2048,256]{1,0:T(8,128)(2,1)}, u32[]{:S(2)}, u32[]{:S(2)}) collective-permute-start(bf16[2048,256]{1,0:T(8,128)(2,1)} %get-tuple-element.36), channel_id=1, source_target_pairs={{0,62},{1,63},{2,0},{3,1},{4,2},{5,3},{6,4},{7,5},{8,6},{9,7},{10,... | collective-permute-start | bytes 3145736 | tf_op jit(solution)/shard_map/ppermute | solution.py:45
  66.1 0.7 copy-start.6
  66.1 1.5 copy-start.9
  66.2 9.3 %collective-permute-start.7 = (bf16[2048,512]{1,0:T(8,128)(2,1)}, bf16[2048,512]{1,0:T(8,128)(2,1)S(1)}, u32[]{:S(2)}, u32[]{:S(2)}) collective-permute-start(bf16[2048,512]{1,0:T(8,128)(2,1)} %get-tuple-element.38), channel_id=1, source_target_pairs={{0,1},{1,0},{2,3},{3,2},{4,5},{5,4},{6,7},{7,6},{8,9},{9,8},{10,11... | collective-permute-start | bytes 6291464 | tf_op jit(solution)/shard_map/ppermute | solution.py:45
  67.6 40.4 %collective-permute-start.10 = (bf16[2048,256]{1,0:T(8,128)(2,1)S(1)}, bf16[2048,256]{1,0:T(8,128)(2,1)S(1)}, u32[]{:S(2)}, u32[]{:S(2)}) collective-permute-start(bf16[2048,256]{1,0:T(8,128)(2,1)S(1)} %copy-done.9), channel_id=1, source_target_pairs={{0,2},{1,3},{2,4},{3,5},{4,6},{5,7},{6,8},{7,9},{8,10},{9,11},{10,... | collective-permute-start | bytes 3145736 | tf_op jit(solution)/shard_map/ppermute | solution.py:45
  67.6 40.4 %collective-permute-start.11 = (bf16[2048,256]{1,0:T(8,128)(2,1)}, bf16[2048,256]{1,0:T(8,128)(2,1)S(1)}, u32[]{:S(2)}, u32[]{:S(2)}) collective-permute-start(bf16[2048,256]{1,0:T(8,128)(2,1)} %get-tuple-element.45), channel_id=1, source_target_pairs={{0,63},{1,2},{2,1},{3,4},{4,3},{5,6},{6,5},{7,8},{8,7},{9,10},{10,... | collective-permute-start | bytes 3145736 | tf_op jit(solution)/shard_map/ppermute | solution.py:45
  73.1 35.0 %collective-permute-start.12 = (bf16[2048,256]{1,0:T(8,128)(2,1)}, bf16[2048,256]{1,0:T(8,128)(2,1)}, u32[]{:S(2)}, u32[]{:S(2)}) collective-permute-start(bf16[2048,256]{1,0:T(8,128)(2,1)} %get-tuple-element.46), channel_id=1, source_target_pairs={{0,62},{1,63},{2,0},{3,1},{4,2},{5,3},{6,4},{7,5},{8,6},{9,7},{10,... | collective-permute-start | bytes 3145736 | tf_op jit(solution)/shard_map/ppermute | solution.py:45
  75.4 1.3 copy-start.8
  76.7 14.1 %copy-start.7 = (s32[4,8]{1,0:T(4,128)S(1)}, s32[4,8]{1,0:T(4,128)}, u32[]{:S(2)}) copy-start(s32[4,8]{1,0:T(4,128)} %param.5) | copy-start | bytes 388
  88.2 16.0 %collective-permute-start.8 = (s16[1088,128]{1,0:T(8,128)(2,1)}, s16[1088,128]{1,0:T(8,128)(2,1)S(1)}, u32[]{:S(2)}, u32[]{:S(2)}) collective-permute-start(s16[1088,128]{1,0:T(8,128)(2,1)} %get-tuple-element.41), channel_id=1, source_target_pairs={{0,64},{64,128},{128,192},{192,0},{1,65},{65,129},{129,193},{193,1... | collective-permute-start | bytes 835592 | tf_op jit(solution)/shard_map/ppermute | solution.py:31
  89.8 16.9 %collective-permute-start.9 = (s16[1088,128]{1,0:T(8,128)(2,1)}, s16[1088,128]{1,0:T(8,128)(2,1)S(1)}, u32[]{:S(2)}, u32[]{:S(2)}) collective-permute-start(s16[1088,128]{1,0:T(8,128)(2,1)} %get-tuple-element.42), channel_id=1, source_target_pairs={{0,128},{64,192},{128,0},{192,64},{1,129},{65,193},{129,1},{193,65... | collective-permute-start | bytes 835592 | tf_op jit(solution)/shard_map/ppermute | solution.py:31
  104.1 17.1 %copy-start = (s16[1088,128]{1,0:T(8,128)(2,1)}, s16[1088,128]{1,0:T(8,128)(2,1)S(1)}, u32[]{:S(2)}) copy-start(s16[1088,128]{1,0:T(8,128)(2,1)S(1)} %collective-permute-done.8.refs_0_) | copy-start | bytes 835588
  104.1 31.0 %collective-permute-start.16 = (s16[1088,128]{1,0:T(8,128)(2,1)}, s16[1088,128]{1,0:T(8,128)(2,1)S(1)}, u32[]{:S(2)}, u32[]{:S(2)}) collective-permute-start(s16[1088,128]{1,0:T(8,128)(2,1)} %get-tuple-element.54), channel_id=1, source_target_pairs={{0,192},{64,0},{128,64},{192,128},{1,193},{65,1},{129,65},{193,129... | collective-permute-start | bytes 835592 | tf_op jit(solution)/shard_map/ppermute | solution.py:31
  106.7 14.5 %copy-start.1 = (s16[1088,128]{1,0:T(8,128)(2,1)}, s16[1088,128]{1,0:T(8,128)(2,1)S(1)}, u32[]{:S(2)}) copy-start(s16[1088,128]{1,0:T(8,128)(2,1)S(1)} %collective-permute-done.9.refs_1_) | copy-start | bytes 835588
  108.0 1.0 copy-start.11
  109.0 1.0 copy-start.10
  121.2 19.2 %collective-permute-start.13 = (s16[1088,128]{1,0:T(8,128)(2,1)}, s16[1088,128]{1,0:T(8,128)(2,1)S(1)}, u32[]{:S(2)}, u32[]{:S(2)}) collective-permute-start(s16[1088,128]{1,0:T(8,128)(2,1)} %get-tuple-element.48), channel_id=1, source_target_pairs={{0,64},{64,128},{128,192},{192,0},{1,65},{65,129},{129,193},{193,1... | collective-permute-start | bytes 835592 | tf_op jit(solution)/shard_map/ppermute | solution.py:31
  130.2 11.1 %collective-permute-start.14 = (s16[1088,128]{1,0:T(8,128)(2,1)}, s16[1088,128]{1,0:T(8,128)(2,1)S(1)}, u32[]{:S(2)}, u32[]{:S(2)}) collective-permute-start(s16[1088,128]{1,0:T(8,128)(2,1)} %get-tuple-element.49), channel_id=1, source_target_pairs={{0,128},{64,192},{128,0},{192,64},{1,129},{65,193},{129,1},{193,65... | collective-permute-start | bytes 835592 | tf_op jit(solution)/shard_map/ppermute | solution.py:31
  133.7 10.6 %collective-permute-start.15 = (s16[1088,128]{1,0:T(8,128)(2,1)}, s16[1088,128]{1,0:T(8,128)(2,1)S(1)}, u32[]{:S(2)}, u32[]{:S(2)}) collective-permute-start(s16[1088,128]{1,0:T(8,128)(2,1)} %get-tuple-element.50), channel_id=1, source_target_pairs={{0,192},{64,0},{128,64},{192,128},{1,193},{65,1},{129,65},{193,129... | collective-permute-start | bytes 835592 | tf_op jit(solution)/shard_map/ppermute | solution.py:31
  135.2 0.7 copy-start.2
  140.4 3.8 %copy-start.3 = (s16[1088,128]{1,0:T(8,128)(2,1)}, s16[1088,128]{1,0:T(8,128)(2,1)S(1)}, u32[]{:S(2)}) copy-start(s16[1088,128]{1,0:T(8,128)(2,1)S(1)} %collective-permute-done.13.refs_0_) | copy-start | bytes 835588
  141.3 3.0 %copy-start.4 = (s16[1088,128]{1,0:T(8,128)(2,1)}, s16[1088,128]{1,0:T(8,128)(2,1)S(1)}, u32[]{:S(2)}) copy-start(s16[1088,128]{1,0:T(8,128)(2,1)S(1)} %collective-permute-done.14.refs_1_) | copy-start | bytes 835588
  144.3 0.7 copy-start.5
Sparse Core Ops, SparseCore 0:
  66.3 60.1 reduce-scatter.1

commit v6 on v5

--- a/solution.py
+++ b/solution.py
@@ -121,46 +121,98 @@
     )(want, perturb)
 
 
-def own_kernel(x_ref, row_ref, at_ref, part_ref):
-    samp = part_ref.shape[0]
+def with_rows(count, width, rows):
+    row_id = lax.broadcasted_iota(jnp.int32, (count, width), 0)
+    block = jnp.zeros((count, width), jnp.float32)
+    for i, row in enumerate(rows):
+        block = jnp.where(row_id == i, row, block)
+    return block.astype(jnp.int32).astype(jnp.int16)
+
+
+def own_kernel(dest_ref, x_ref, row_ref, at_ref, *refs):
+    parts, tile_ref, norm_ref = refs[:-2], refs[-2], refs[-1]
+    samp = len(parts)
     rows = BS // samp
     r = pl.program_id(0)
     at_ref[...] = jnp.transpose(row_ref[...])
     at = at_ref[...]
+    codes = [[] for _ in range(samp - 1)]
     for c in range(B_DEV):
-        tile = jnp.dot(at, x_ref[:, c * BS : (c + 1) * BS], preferred_element_type=jnp.float32)
-        for y in range(samp):
-            part_ref[y, c * rows : (c + 1) * rows, :] = tile[y * rows : (y + 1) * rows]
+        tile_ref[...] = jnp.dot(at, x_ref[:, c * BS : (c + 1) * BS], preferred_element_type=jnp.float32)
+        for d in range(samp):
+            piece = tile_ref[pl.ds(pl.multiple_of(dest_ref[d] * rows, rows), rows), :]
+            if d > 0:
+                piece, code = encode(piece)
+                piece = piece.astype(jnp.int32).astype(jnp.int16)
+                codes[d - 1].append(code)
+            parts[d][c * rows : (c + 1) * rows, :] = piece
 
         @pl.when(r == c)
         def _():
             here = lax.broadcasted_iota(jnp.int32, (BS, BS), 0) == lax.broadcasted_iota(jnp.int32, (BS, BS), 1)
-            norm = jnp.sum(jnp.where(here, tile, 0.0), axis=0, keepdims=True)
-            for y in range(samp):
-                part_ref[y, BS : BS + EXTRA, :] = jnp.broadcast_to(norm, (EXTRA, BS))
-
-
-def own_tiles(perturb, samp):
+            norm = jnp.sum(jnp.where(here, tile_ref[...], 0.0), axis=0, keepdims=True)
+            norm_ref[...] = jnp.broadcast_to(norm, norm_ref.shape)
+
+    parts[0][BS : BS + EXTRA, :] = norm_ref[...]
+    norm_codes = encode_norm(norm_ref[0:1, :])
+    for d in range(1, samp):
+        parts[d][BS : BS + CODE_EXTRA, :] = with_rows(CODE_EXTRA, BS, codes[d - 1] + norm_codes)
+
+
+def own_tiles(dest, perturb):
     samples, cells = perturb.shape
-    block = BS + EXTRA
+    samp = dest.shape[0]
+    blocks_out = [(BS + EXTRA, jnp.float32)] + [(BS + CODE_EXTRA, jnp.int16)] * (samp - 1)
     return pl.pallas_call(
         own_kernel,
-        grid=(B_DEV,),
-        in_specs=[
-            pl.BlockSpec((samples, cells), lambda r: (0, 0)),
-            pl.BlockSpec((samples, BS), lambda r: (0, r)),
-        ],
-        out_specs=[
-            pl.BlockSpec((BS, samples), lambda r: (r, 0)),
-            pl.BlockSpec((samp, block, BS), lambda r: (0, r, 0)),
-        ],
-        out_shape=[
-            jax.ShapeDtypeStruct((cells, samples), perturb.dtype),
-            jax.ShapeDtypeStruct((samp, B_DEV * block, BS), jnp.float32),
-        ],
+        grid_spec=pltpu.PrefetchScalarGridSpec(
+            num_scalar_prefetch=1,
+            grid=(B_DEV,),
+            in_specs=[
+                pl.BlockSpec((samples, cells), lambda r, *s: (0, 0)),
+                pl.BlockSpec((samples, BS), lambda r, *s: (0, r)),
+            ],
+            out_specs=[pl.BlockSpec((BS, samples), lambda r, *s: (r, 0))]
+            + [pl.BlockSpec((block, BS), lambda r, *s: (r, 0)) for block, _ in blocks_out],
+            scratch_shapes=[pltpu.VMEM((BS, BS), jnp.float32), pltpu.VMEM((EXTRA, BS), jnp.float32)],
+        ),
+        out_shape=[jax.ShapeDtypeStruct((cells, samples), perturb.dtype)]
+        + [jax.ShapeDtypeStruct((B_DEV * block, BS), dtype) for block, dtype in blocks_out],
         compiler_params=pltpu.CompilerParams(vmem_limit_bytes=BIG),
         cost_estimate=pl.CostEstimate(flops=2 * cells * cells * samples, bytes_accessed=12 * MIB, transcendentals=0),
-    )(perturb, perturb)
+    )(dest, perturb, perturb)
+
+
+def total_kernel(kept_ref, *refs):
+    coded_refs, out_ref = refs[:-1], refs[-1]
+    rows = BS // (len(coded_refs) + 1)
+    block = BS + EXTRA
+    coded = BS + CODE_EXTRA
+    for r in range(B_DEV):
+        extras = [
+            ref[r * coded + BS : (r + 1) * coded, :].astype(jnp.int32).astype(jnp.float32) for ref in coded_refs
+        ]
+        for j in range(4):
+            here = slice(r * block + j * rows, r * block + (j + 1) * rows)
+            tile = kept_ref[here, :]
+            for ref, extra in zip(coded_refs, extras):
+                piece = ref[r * coded + j * rows : r * coded + (j + 1) * rows, :].astype(jnp.int32)
+                tile = tile + piece.astype(jnp.float32) * decoded_scale(extra[j : j + 1, :])
+            out_ref[here, :] = tile
+        norm = kept_ref[r * block + BS : r * block + BS + 1, :]
+        for extra in extras:
+            code, high, low = (extra[4 + i : 5 + i, :] for i in range(3))
+            norm = norm + (high + low * (1.0 / TOP)) * decoded_scale(code)
+        out_ref[r * block + BS : (r + 1) * block, :] = jnp.broadcast_to(norm, (EXTRA, BS))
+
+
+def own_total(kept, coded):
+    return pl.pallas_call(
+        total_kernel,
+        out_shape=jax.ShapeDtypeStruct(kept.shape, kept.dtype),
+        compiler_params=pltpu.CompilerParams(vmem_limit_bytes=16 * MIB),
+        cost_estimate=pl.CostEstimate(flops=4 * MIB, bytes_accessed=4 * MIB, transcendentals=0),
+    )(kept, *coded)
 
 
 def remote_kernel(stage, slot_ref, dest_ref, at_ref, *refs):
@@ -206,23 +258,24 @@
                     codes[d - 1].append(code)
                 parts[d][j * rows : (j + 1) * rows, :] = piece
 
-    step = 128
+    step, lanes = 256, 32
+
+    def add(i, totals):
+        at_rows = pl.ds(pl.multiple_of(i * step, step), step)
+        squares = [jnp.square(cols_ref[2 * r + side, at_rows, :].astype(jnp.float32)) for side in range(2)]
+        return [
+            total + jnp.sum(square.reshape(step // lanes, lanes, HALF), axis=0)
+            for total, square in zip(totals, squares)
+        ]
+
+    totals = lax.fori_loop(0, samples // step, add, [jnp.zeros((lanes, HALF), jnp.float32)] * 2)
     norm_codes = []
-    for side in range(2):
-        def add(i, total):
-            x = cols_ref[2 * r + side, pl.ds(pl.multiple_of(i * step, step), step), :].astype(jnp.float32)
-            return total + jnp.sum((x * x).reshape(step // 8, 8, HALF), axis=0)
-
-        total = lax.fori_loop(0, samples // step, add, jnp.zeros((8, HALF), jnp.float32))
+    for side, total in enumerate(totals):
         norm = jnp.sum(total, axis=0, keepdims=True)
         norm_codes += encode_norm(norm)
         parts[0][BS + side * 4 : BS + side * 4 + 4, :] = jnp.broadcast_to(norm, (4, HALF))
-    row_id = lax.broadcasted_iota(jnp.int32, (CODE_EXTRA, HALF), 0)
     for d in range(1, samp):
-        extra = jnp.zeros((CODE_EXTRA, HALF), jnp.float32)
-        for i, row in enumerate(codes[d - 1] + norm_codes):
-            extra = jnp.where(row_id == i, row, extra)
-        parts[d][BS : BS + CODE_EXTRA, :] = extra.astype(jnp.int32).astype(jnp.int16)
+        parts[d][BS : BS + CODE_EXTRA, :] = with_rows(CODE_EXTRA, HALF, codes[d - 1] + norm_codes)
 
 
 def remote_tiles(stage, slots, dest, at, blocks, samp):
@@ -349,28 +402,29 @@
     slots = pick(is_rem, slot[:, :, None]).reshape(-1)
 
     rows = BS // samp
-    size = B_DEV * (BS + EXTRA)
     me = lax.axis_index("samp")
     dest = (me + jnp.arange(samp, dtype=jnp.int32)) % samp
     chosen = [select(stage, asked, perturb) for stage in range(STAGES)]
-    mates = exchanged(chosen[1][3], 1)
     got = []
     for stage in range(STAGES):
-        two_below, across, two_above = (exchanged(chosen[stage][i], q) for i, q in enumerate((0, 2, 3)))
-        got.append([two_below, mates, across, two_above])
+        got.append([exchanged(chosen[stage][i], q) for i, q in enumerate((0, 2, 3))])
     held, _ = lax.optimization_barrier((perturb, chosen[1][0]))
-    at, own_part = own_tiles(held, samp)
-    own_part, *arrived = lax.optimization_barrier((own_part, got[0][0], got[0][2], got[0][3]))
-    got[0] = [arrived[0], mates, arrived[1], arrived[2]]
-    own_sum = lax.psum_scatter(own_part.reshape(samp * size, BS), "samp", scatter_dimension=0, tiled=True)
+    at, kept, *own_parts = own_tiles(dest, held)
+    *own_parts, to_mate, below, across, above = lax.optimization_barrier((*own_parts, chosen[1][3], *got[0]))
+    mates = exchanged(to_mate, 1)
+    got = [[below, mates, across, above], [got[1][0], mates, got[1][1], got[1][2]]]
+    own_parts = [passed_along(part, "samp", d) for d, part in enumerate(own_parts, 1)]
     sums = []
     for stage in range(STAGES):
-        parts = remote_tiles(stage, slots, dest, at, got[stage], samp)
+        parts = list(remote_tiles(stage, slots, dest, at, got[stage], samp))
+        if stage == 0:
+            parts, own_parts = lax.optimization_barrier((parts, own_parts))
         last = [parts[0]] + [passed_along(parts[d], "samp", d) for d in range(1, samp)]
         if stage == 0:
             dest, *last[1:3] = lax.optimization_barrier((dest, *last[1:3]))
         sums.append(last)
 
+    own_sum = own_total(kept, own_parts)
     out = final(0, place, slots, dest, tapers, own_sum, sums[0], None, rows)
     out = final(1, place, slots, dest, tapers, own_sum, sums[1], out, rows)
     return out.reshape(rows, PAIR_DEV, BS)

time: 157 us -> 149 us (0.949)
  between operations: 13.5 us -> 0.17 us
  waiting for transfers between devices: 34.8 us -> 43.2 us
  local copies, waits for them, and re-layouts: 7.25 us -> 4.16 us
  Pallas kernels: 56.3 us -> 54.5 us
    ppermute x6 -> x9, waiting for transfers between devices: 18.2 us -> 30.2 us  [passed_along(): return lax.ppermute(value, axis, pairs)]
    pallas_call x2, Pallas kernels: 22.6 us -> 18.9 us  [remote_tiles(): pl.pallas_call(functools.partial(remote_kernel, stage), grid_spec=pltpu.P...]
    ppermute x11, waiting for transfers between devices: 16.6 us -> 13 us  [exchanged(): return lax.ppermute(value, 'blk', sorted(pairs))]
    unnamed x24 -> x20, local copies, waits for them, and re-layouts: 5.06 us -> 1.87 us
    pallas_call x1 -> x2, Pallas kernels: 15.2 us -> 17.4 us  [the longest x1 16.9 us: own_tiles(): pl.pallas_call(own_kernel, grid_spec=pltpu.PrefetchScalarGridSpec(num_sca...]
    ppermute x6 -> x9, starting transfers between devices: 16.3 us -> 18.2 us  [passed_along(): return lax.ppermute(value, axis, pairs)]
  transfers between devices with their start and end apart: 18 -> 20, of which waited for: 8 -> 9; matrix products, arithmetic and copies ran while one was open for 2% -> 2% of each run, Pallas kernels for 31% -> 31%
where the time goes in v6:
time: 149 us; the launch traced here: 148 us
  Pallas kernels  54.5 us (37%)
  waiting for transfers between devices  43.2 us (29%)
  starting transfers between devices  42.9 us (29%)
  local copies, waits for them, and re-layouts  4.16 us (3%)
  other arithmetic  3.12 us (2%)
    ppermute x9, waiting for transfers between devices, passed_along(): return lax.ppermute(value, axis, pairs)  30.2 us
    ppermute x11, starting transfers between devices, exchanged(): return lax.ppermute(value, 'blk', sorted(pairs))  24.7 us
    pallas_call x2, Pallas kernels, remote_tiles(): pl.pallas_call(functools.partial(remote_kernel, stage), grid_spec=pltpu.P...  18.9 us
    ppermute x9, starting transfers between devices, passed_along(): return lax.ppermute(value, axis, pairs)  18.2 us
    pallas_call x1, Pallas kernels, own_tiles(): pl.pallas_call(own_kernel, grid_spec=pltpu.PrefetchScalarGridSpec(num_sca...  16.9 us
    ppermute x11, waiting for transfers between devices, exchanged(): return lax.ppermute(value, 'blk', sorted(pairs))  13 us
    pallas_call x2, Pallas kernels, final(): pl.pallas_call(functools.partial(final_kernel, half), grid_spec=pltpu.Pre...  9.12 us
    pallas_call x2, Pallas kernels, select(): pl.pallas_call(functools.partial(select_kernel, plan), grid_spec=pltpu.Pr...  9.11 us
  transfers between devices with their start and end apart: 20, of which 9 were waited for; matrix products, arithmetic and copies ran while one was open for 2% of the time, Pallas kernels for 31%

profile of v6, /device:TPU:8, one launch (start us, length us, event | category | flops | bytes accessed | tf_op | source)
XLA Modules:
  0.0 148.0 jit_solution(3048060969012091426)
XLA Ops:
  0.0 0.7 add_select_fusion
  1.4 8.1 %collective-permute-start = (s32[2]{0:T(128)S(1)}, s32[2]{0:T(128)S(1)}, u32[]{:S(2)}, u32[]{:S(2)}) collective-permute-start(s32[2]{0:T(128)S(1)} %get-tuple-element.81), channel_id=1, source_target_pairs={{0,62},{1,63},{2,0},{3,1},{4,2},{5,3},{6,4},{7,5},{8,6},{9,7},{10,... | collective-permute-start | bytes 32 | tf_op jit(solution)/shard_map/ppermute | solution.py:45
  9.6 4.2 %collective-permute-start.2 = (s32[2]{0:T(128)S(1)}, s32[2]{0:T(128)S(1)}, u32[]{:S(2)}, u32[]{:S(2)}) collective-permute-start(s32[2]{0:T(128)S(1)} %get-tuple-element.83), channel_id=1, source_target_pairs={{0,63},{1,2},{2,1},{3,4},{4,3},{5,6},{6,5},{7,8},{8,7},{9,10},{10,... | collective-permute-start | bytes 32 | tf_op jit(solution)/shard_map/ppermute | solution.py:45
  13.8 2.6 %collective-permute-done.3 = s32[2]{0:T(128)S(1)} collective-permute-done((s32[2]{0:T(128)S(1)}, s32[2]{0:T(128)S(1)}, u32[]{:S(2)}, u32[]{:S(2)}) %collective-permute-start.3) | collective-permute-done | bytes 40 | tf_op jit(solution)/shard_map/ppermute | solution.py:45
  17.0 3.5 %shard_map.39 = (bf16[2048,256]{1,0:T(8,128)(2,1)}, bf16[2048,256]{1,0:T(8,128)(2,1)}, bf16[2048,256]{1,0:T(8,128)(2,1)}) custom-call(s32[8]{0:T(128)} %pad_add_fusion.2.want_ref, bf16[2048,1024]{1,0:T(8,128)(2,1)} %source_ref.3), custom_call_target="tpu_custom_call" | custom-call | bytes 6291456 | tf_op jit(solution)/shard_map/pallas_call | solution.py:105
  20.7 3.9 %collective-permute-start.5 = (bf16[2048,256]{1,0:T(8,128)(2,1)}, bf16[2048,256]{1,0:T(8,128)(2,1)S(1)}, u32[]{:S(2)}, u32[]{:S(2)}) collective-permute-start(bf16[2048,256]{1,0:T(8,128)(2,1)} %get-tuple-element.51), channel_id=1, source_target_pairs={{0,63},{1,2},{2,1},{3,4},{4,3},{5,6},{6,5},{7,8},{8,7},{9,10},{10,... | collective-permute-start | bytes 3145736 | tf_op jit(solution)/shard_map/ppermute | solution.py:45
  24.6 1.6 %collective-permute-start.6 = (bf16[2048,256]{1,0:T(8,128)(2,1)}, bf16[2048,256]{1,0:T(8,128)(2,1)}, u32[]{:S(2)}, u32[]{:S(2)}) collective-permute-start(bf16[2048,256]{1,0:T(8,128)(2,1)} %get-tuple-element.52), channel_id=1, source_target_pairs={{0,62},{1,63},{2,0},{3,1},{4,2},{5,3},{6,4},{7,5},{8,6},{9,7},{10,... | collective-permute-start | bytes 3145736 | tf_op jit(solution)/shard_map/ppermute | solution.py:45
  26.8 5.6 %shard_map.37 = (bf16[2048,256]{1,0:T(8,128)(2,1)}, bf16[2048,256]{1,0:T(8,128)(2,1)}, bf16[2048,256]{1,0:T(8,128)(2,1)}, bf16[2048,512]{1,0:T(8,128)(2,1)}) custom-call(s32[8]{0:T(128)} %pad_add_fusion.2.want_ref, bf16[2048,1024]{1,0:T(8,128)(2,1)} %source_ref.3), custom_call_target="tpu_custom_call" | custom-call | bytes 10485760 | tf_op jit(solution)/shard_map/pallas_call | solution.py:105
  32.4 16.9 %shard_map.38 = (bf16[1024,2048]{1,0:T(8,128)(2,1)}, f32[1056,256]{1,0:T(8,128)}, s16[1088,256]{1,0:T(8,128)(2,1)}, s16[1088,256]{1,0:T(8,128)(2,1)}, s16[1088,256]{1,0:T(8,128)(2,1)}) custom-call(s32[4]{0:T(128)} %and_select_fusion.dest_ref, bf16[2048,1024]{1,0:T(8,128)(2,1)} %source_ref.3, bf16[2048,1024]{1,0:T(8,128)(2,1)} %source_ref.3), custom_call_target="tpu_custom_call" | custom-call | flops 4294967296 | bytes 12582912 | tf_op jit(solution)/shard_map/pallas_call | solution.py:166
  49.3 0.9 collective-permute-done.4.refs_0_
  50.3 9.4 %collective-permute-done.5.refs_2_ = bf16[2048,256]{1,0:T(8,128)(2,1)S(1)} collective-permute-done((bf16[2048,256]{1,0:T(8,128)(2,1)}, bf16[2048,256]{1,0:T(8,128)(2,1)S(1)}, u32[]{:S(2)}, u32[]{:S(2)}) %collective-permute-start.5) | collective-permute-done | bytes 1048608 | tf_op jit(solution)/shard_map/ppermute | solution.py:45
  59.8 0.9 copy-done.9
  60.6 1.6 %collective-permute-start.8 = (s16[1088,256]{1,0:T(8,128)(2,1)}, s16[1088,256]{1,0:T(8,128)(2,1)S(1)}, u32[]{:S(2)}, u32[]{:S(2)}) collective-permute-start(s16[1088,256]{1,0:T(8,128)(2,1)} %get-tuple-element.61), channel_id=1, source_target_pairs={{0,64},{64,128},{128,192},{192,0},{1,65},{65,129},{129,193},{193,1... | collective-permute-start | bytes 1671176 | tf_op jit(solution)/shard_map/ppermute | solution.py:31
  62.4 4.9 %collective-permute-start.14 = (bf16[2048,256]{1,0:T(8,128)(2,1)}, bf16[2048,256]{1,0:T(8,128)(2,1)}, u32[]{:S(2)}, u32[]{:S(2)}) collective-permute-start(bf16[2048,256]{1,0:T(8,128)(2,1)} %get-tuple-element.71), channel_id=1, source_target_pairs={{0,63},{1,2},{2,1},{3,4},{4,3},{5,6},{6,5},{7,8},{8,7},{9,10},{10,... | collective-permute-start | bytes 3145736 | tf_op jit(solution)/shard_map/ppermute | solution.py:45
  67.4 1.6 %collective-permute-start.15 = (bf16[2048,256]{1,0:T(8,128)(2,1)}, bf16[2048,256]{1,0:T(8,128)(2,1)}, u32[]{:S(2)}, u32[]{:S(2)}) collective-permute-start(bf16[2048,256]{1,0:T(8,128)(2,1)} %get-tuple-element.72), channel_id=1, source_target_pairs={{0,62},{1,63},{2,0},{3,1},{4,2},{5,3},{6,4},{7,5},{8,6},{9,7},{10,... | collective-permute-start | bytes 3145736 | tf_op jit(solution)/shard_map/ppermute | solution.py:45
  69.8 5.3 %collective-permute-done.8.refs_0_ = s16[1088,256]{1,0:T(8,128)(2,1)S(1)} collective-permute-done((s16[1088,256]{1,0:T(8,128)(2,1)}, s16[1088,256]{1,0:T(8,128)(2,1)S(1)}, u32[]{:S(2)}, u32[]{:S(2)}) %collective-permute-start.8) | collective-permute-done | bytes 557088 | tf_op jit(solution)/shard_map/ppermute | solution.py:31
  75.1 2.3 %collective-permute-start.9 = (s16[1088,256]{1,0:T(8,128)(2,1)}, s16[1088,256]{1,0:T(8,128)(2,1)S(1)}, u32[]{:S(2)}, u32[]{:S(2)}) collective-permute-start(s16[1088,256]{1,0:T(8,128)(2,1)} %get-tuple-element.62), channel_id=1, source_target_pairs={{0,128},{64,192},{128,0},{192,64},{1,129},{65,193},{129,1},{193,65... | collective-permute-start | bytes 1671176 | tf_op jit(solution)/shard_map/ppermute | solution.py:31
  77.4 1.3 collective-permute-start.10
  78.8 9.5 %shard_map.40 = (f32[1056,128]{1,0:T(8,128)}, s16[1088,128]{1,0:T(8,128)(2,1)}, s16[1088,128]{1,0:T(8,128)(2,1)}, s16[1088,128]{1,0:T(8,128)(2,1)}) custom-call(s32[16]{0:T(128)} %reshape.142.slot_ref, s32[4]{0:T(128)} %and_select_fusion.dest_ref, bf16[1024,2048]{1,0:T(8,128)(2,1)} %get-tuple-element.45.at_ref, bf16[2048,256]{1,0:T(8,128)(2,1)} %copy-done.8, ...), custom_call_target="tpu_custom_call" | custom-call | flops 4294967296 | bytes 10485760 | tf_op jit(solution)/shard_map/pallas_call | solution.py:286
  88.3 4.1 %collective-permute-done.9.refs_1_ = s16[1088,256]{1,0:T(8,128)(2,1)S(1)} collective-permute-done((s16[1088,256]{1,0:T(8,128)(2,1)}, s16[1088,256]{1,0:T(8,128)(2,1)S(1)}, u32[]{:S(2)}, u32[]{:S(2)}) %collective-permute-start.9) | collective-permute-done | bytes 557088 | tf_op jit(solution)/shard_map/ppermute | solution.py:31
  92.4 9.8 %collective-permute-done.10.refs_2_ = s16[1088,256]{1,0:T(8,128)(2,1)S(1)} collective-permute-done((s16[1088,256]{1,0:T(8,128)(2,1)}, s16[1088,256]{1,0:T(8,128)(2,1)S(1)}, u32[]{:S(2)}, u32[]{:S(2)}) %collective-permute-start.10) | collective-permute-done | bytes 557088 | tf_op jit(solution)/shard_map/ppermute | solution.py:31
  102.8 2.3 %collective-permute-start.12 = (s16[1088,128]{1,0:T(8,128)(2,1)}, s16[1088,128]{1,0:T(8,128)(2,1)S(1)}, u32[]{:S(2)}, u32[]{:S(2)}) collective-permute-start(s16[1088,128]{1,0:T(8,128)(2,1)} %get-tuple-element.65), channel_id=1, source_target_pairs={{0,128},{64,192},{128,0},{192,64},{1,129},{65,193},{129,1},{193,65... | collective-permute-start | bytes 835592 | tf_op jit(solution)/shard_map/ppermute | solution.py:31
  105.4 6.5 %collective-permute-done.11.refs_0_ = s16[1088,128]{1,0:T(8,128)(2,1)S(1)} collective-permute-done((s16[1088,128]{1,0:T(8,128)(2,1)}, s16[1088,128]{1,0:T(8,128)(2,1)S(1)}, u32[]{:S(2)}, u32[]{:S(2)}) %collective-permute-start.11) | collective-permute-done | bytes 278560 | tf_op jit(solution)/shard_map/ppermute | solution.py:31
  112.0 0.8 collective-permute-start.19
  112.8 9.4 %shard_map.42 = (f32[1056,128]{1,0:T(8,128)}, s16[1088,128]{1,0:T(8,128)(2,1)}, s16[1088,128]{1,0:T(8,128)(2,1)}, s16[1088,128]{1,0:T(8,128)(2,1)}) custom-call(s32[16]{0:T(128)} %reshape.142.slot_ref, s32[4]{0:T(128)} %and_select_fusion.dest_ref, bf16[1024,2048]{1,0:T(8,128)(2,1)} %get-tuple-element.45.at_ref, ...), custom_call_target="tpu_custom_call" | custom-call | flops 4294967296 | bytes 10485760 | tf_op jit(solution)/shard_map/pallas_call | solution.py:286
  122.2 5.9 %collective-permute-start.16 = (s16[1088,128]{1,0:T(8,128)(2,1)}, s16[1088,128]{1,0:T(8,128)(2,1)S(1)}, u32[]{:S(2)}, u32[]{:S(2)}) collective-permute-start(s16[1088,128]{1,0:T(8,128)(2,1)} %get-tuple-element.74), channel_id=1, source_target_pairs={{0,64},{64,128},{128,192},{192,0},{1,65},{65,129},{129,193},{193,1... | collective-permute-start | bytes 835592 | tf_op jit(solution)/shard_map/ppermute | solution.py:31
  128.1 3.4 %collective-permute-start.17 = (s16[1088,128]{1,0:T(8,128)(2,1)}, s16[1088,128]{1,0:T(8,128)(2,1)S(1)}, u32[]{:S(2)}, u32[]{:S(2)}) collective-permute-start(s16[1088,128]{1,0:T(8,128)(2,1)} %get-tuple-element.75), channel_id=1, source_target_pairs={{0,128},{64,192},{128,0},{192,64},{1,129},{65,193},{129,1},{193,65... | collective-permute-start | bytes 835592 | tf_op jit(solution)/shard_map/ppermute | solution.py:31
  131.5 0.7 reshape.143.taper_ref
  133.5 1.0 copy-done
  134.5 4.6 %shard_map.43.refs_3_ = f32[2048,256]{1,0:T(8,128)} custom-call(s32[32]{0:T(128)} %add.125.place_ref, s32[16]{0:T(128)} %reshape.142.slot_ref, s32[4]{0:T(128)} %and_select_fusion.dest_ref, f32[32]{0:T(128)} %reshape.143.taper_ref, f32[1056,256]{1,0:T(8,128)} %copy-done, f32[1056,128]{1,0:T(8,128)} %get-tuple-element.77.kept_ref, ...), custom_call_target="tpu_custom_call" | custom-call | flops 1048576 | bytes 4194304 | tf_op jit(solution)/shard_map/pallas_call | solution.py:351
  139.4 4.0 %collective-permute-done.18.refs_2_ = s16[1088,128]{1,0:T(8,128)(2,1)} collective-permute-done((s16[1088,128]{1,0:T(8,128)(2,1)}, s16[1088,128]{1,0:T(8,128)(2,1)}, u32[]{:S(2)}, u32[]{:S(2)}) %collective-permute-start.18) | collective-permute-done | bytes 278560 | tf_op jit(solution)/shard_map/ppermute | solution.py:31
  143.5 4.6 %shard_map.44 = f32[2048,256]{1,0:T(8,128)} custom-call(s32[32]{0:T(128)} %add.125.place_ref, s32[16]{0:T(128)} %reshape.142.slot_ref, s32[4]{0:T(128)} %and_select_fusion.dest_ref, f32[32]{0:T(128)} %reshape.143.taper_ref, f32[1056,256]{1,0:T(8,128)} %copy-done, f32[1056,128]{1,0:T(8,128)} %get-tuple-element.73.kept_ref, ...), custom_call_target="tpu_custom_call", output_to_operand_aliasing={{}: (9, {})} | custom-call | flops 1048576 | bytes 4194304 | tf_op jit(solution)/shard_map/pallas_call | solution.py:351
  (63 shorter events, 5.8 us)
Async XLA Ops:
  1.4 12.4 %collective-permute-start = (s32[2]{0:T(128)S(1)}, s32[2]{0:T(128)S(1)}, u32[]{:S(2)}, u32[]{:S(2)}) collective-permute-start(s32[2]{0:T(128)S(1)} %get-tuple-element.81), channel_id=1, source_target_pairs={{0,62},{1,63},{2,0},{3,1},{4,2},{5,3},{6,4},{7,5},{8,6},{9,7},{10,... | collective-permute-start | bytes 32 | tf_op jit(solution)/shard_map/ppermute | solution.py:45
  9.6 6.9 %collective-permute-start.3 = (s32[2]{0:T(128)S(1)}, s32[2]{0:T(128)S(1)}, u32[]{:S(2)}, u32[]{:S(2)}) collective-permute-start(s32[2]{0:T(128)S(1)} %get-tuple-element.82), channel_id=1, source_target_pairs={{0,2},{1,3},{2,4},{3,5},{4,6},{5,7},{6,8},{7,9},{8,10},{9,11},{10,... | collective-permute-start | bytes 32 | tf_op jit(solution)/shard_map/ppermute | solution.py:45
  9.6 6.9 %collective-permute-start.2 = (s32[2]{0:T(128)S(1)}, s32[2]{0:T(128)S(1)}, u32[]{:S(2)}, u32[]{:S(2)}) collective-permute-start(s32[2]{0:T(128)S(1)} %get-tuple-element.83), channel_id=1, source_target_pairs={{0,63},{1,2},{2,1},{3,4},{4,3},{5,6},{6,5},{7,8},{8,7},{9,10},{10,... | collective-permute-start | bytes 32 | tf_op jit(solution)/shard_map/ppermute | solution.py:45
  13.8 2.6 %collective-permute-start.1 = (s32[2]{0:T(128)S(1)}, s32[2]{0:T(128)S(1)}, u32[]{:S(2)}, u32[]{:S(2)}) collective-permute-start(s32[2]{0:T(128)S(1)} %get-tuple-element.84), channel_id=1, source_target_pairs={{0,1},{1,0},{2,3},{3,2},{4,5},{5,4},{6,7},{7,6},{8,9},{9,8},{10,11... | collective-permute-start | bytes 32 | tf_op jit(solution)/shard_map/ppermute | solution.py:45
  20.6 29.7 %collective-permute-start.4 = (bf16[2048,256]{1,0:T(8,128)(2,1)}, bf16[2048,256]{1,0:T(8,128)(2,1)S(1)}, u32[]{:S(2)}, u32[]{:S(2)}) collective-permute-start(bf16[2048,256]{1,0:T(8,128)(2,1)} %get-tuple-element.50), channel_id=1, source_target_pairs={{0,2},{1,3},{2,4},{3,5},{4,6},{5,7},{6,8},{7,9},{8,10},{9,11},{10,... | collective-permute-start | bytes 3145736 | tf_op jit(solution)/shard_map/ppermute | solution.py:45
  20.7 39.0 %collective-permute-start.5 = (bf16[2048,256]{1,0:T(8,128)(2,1)}, bf16[2048,256]{1,0:T(8,128)(2,1)S(1)}, u32[]{:S(2)}, u32[]{:S(2)}) collective-permute-start(bf16[2048,256]{1,0:T(8,128)(2,1)} %get-tuple-element.51), channel_id=1, source_target_pairs={{0,63},{1,2},{2,1},{3,4},{4,3},{5,6},{6,5},{7,8},{8,7},{9,10},{10,... | collective-permute-start | bytes 3145736 | tf_op jit(solution)/shard_map/ppermute | solution.py:45
  24.6 35.1 %collective-permute-start.6 = (bf16[2048,256]{1,0:T(8,128)(2,1)}, bf16[2048,256]{1,0:T(8,128)(2,1)}, u32[]{:S(2)}, u32[]{:S(2)}) collective-permute-start(bf16[2048,256]{1,0:T(8,128)(2,1)} %get-tuple-element.52), channel_id=1, source_target_pairs={{0,62},{1,63},{2,0},{3,1},{4,2},{5,3},{6,4},{7,5},{8,6},{9,7},{10,... | collective-permute-start | bytes 3145736 | tf_op jit(solution)/shard_map/ppermute | solution.py:45
  32.4 29.9 %copy-start.6 = (s32[4,8]{1,0:T(4,128)S(1)}, s32[4,8]{1,0:T(4,128)}, u32[]{:S(2)}) copy-start(s32[4,8]{1,0:T(4,128)} %param.4) | copy-start | bytes 388
  50.3 28.5 %copy-start.8 = (bf16[2048,256]{1,0:T(8,128)(2,1)}, bf16[2048,256]{1,0:T(8,128)(2,1)S(1)}, u32[]{:S(2)}) copy-start(bf16[2048,256]{1,0:T(8,128)(2,1)S(1)} %collective-permute-done.4.refs_0_) | copy-start | bytes 3145732
  59.6 1.0 copy-start.9
  59.7 17.7 %collective-permute-start.7 = (bf16[2048,512]{1,0:T(8,128)(2,1)}, bf16[2048,512]{1,0:T(8,128)(2,1)}, u32[]{:S(2)}, u32[]{:S(2)}) collective-permute-start(bf16[2048,512]{1,0:T(8,128)(2,1)} %get-tuple-element.54), channel_id=1, source_target_pairs={{0,1},{1,0},{2,3},{3,2},{4,5},{5,4},{6,7},{7,6},{8,9},{9,8},{10,11... | collective-permute-start | bytes 6291464 | tf_op jit(solution)/shard_map/ppermute | solution.py:45
  60.6 14.5 %collective-permute-start.8 = (s16[1088,256]{1,0:T(8,128)(2,1)}, s16[1088,256]{1,0:T(8,128)(2,1)S(1)}, u32[]{:S(2)}, u32[]{:S(2)}) collective-permute-start(s16[1088,256]{1,0:T(8,128)(2,1)} %get-tuple-element.61), channel_id=1, source_target_pairs={{0,64},{64,128},{128,192},{192,0},{1,65},{65,129},{129,193},{193,1... | collective-permute-start | bytes 1671176 | tf_op jit(solution)/shard_map/ppermute | solution.py:31
  62.3 50.4 %collective-permute-start.13 = (bf16[2048,256]{1,0:T(8,128)(2,1)}, bf16[2048,256]{1,0:T(8,128)(2,1)}, u32[]{:S(2)}, u32[]{:S(2)}) collective-permute-start(bf16[2048,256]{1,0:T(8,128)(2,1)} %get-tuple-element.43), channel_id=1, source_target_pairs={{0,2},{1,3},{2,4},{3,5},{4,6},{5,7},{6,8},{7,9},{8,10},{9,11},{10,... | collective-permute-start | bytes 3145736 | tf_op jit(solution)/shard_map/ppermute | solution.py:45
  62.4 50.3 %collective-permute-start.14 = (bf16[2048,256]{1,0:T(8,128)(2,1)}, bf16[2048,256]{1,0:T(8,128)(2,1)}, u32[]{:S(2)}, u32[]{:S(2)}) collective-permute-start(bf16[2048,256]{1,0:T(8,128)(2,1)} %get-tuple-element.71), channel_id=1, source_target_pairs={{0,63},{1,2},{2,1},{3,4},{4,3},{5,6},{6,5},{7,8},{8,7},{9,10},{10,... | collective-permute-start | bytes 3145736 | tf_op jit(solution)/shard_map/ppermute | solution.py:45
  67.4 45.4 %collective-permute-start.15 = (bf16[2048,256]{1,0:T(8,128)(2,1)}, bf16[2048,256]{1,0:T(8,128)(2,1)}, u32[]{:S(2)}, u32[]{:S(2)}) collective-permute-start(bf16[2048,256]{1,0:T(8,128)(2,1)} %get-tuple-element.72), channel_id=1, source_target_pairs={{0,62},{1,63},{2,0},{3,1},{4,2},{5,3},{6,4},{7,5},{8,6},{9,7},{10,... | collective-permute-start | bytes 3145736 | tf_op jit(solution)/shard_map/ppermute | solution.py:45
  75.1 17.3 %collective-permute-start.9 = (s16[1088,256]{1,0:T(8,128)(2,1)}, s16[1088,256]{1,0:T(8,128)(2,1)S(1)}, u32[]{:S(2)}, u32[]{:S(2)}) collective-permute-start(s16[1088,256]{1,0:T(8,128)(2,1)} %get-tuple-element.62), channel_id=1, source_target_pairs={{0,128},{64,192},{128,0},{192,64},{1,129},{65,193},{129,1},{193,65... | collective-permute-start | bytes 1671176 | tf_op jit(solution)/shard_map/ppermute | solution.py:31
  77.4 24.8 %collective-permute-start.10 = (s16[1088,256]{1,0:T(8,128)(2,1)}, s16[1088,256]{1,0:T(8,128)(2,1)S(1)}, u32[]{:S(2)}, u32[]{:S(2)}) collective-permute-start(s16[1088,256]{1,0:T(8,128)(2,1)} %get-tuple-element.63), channel_id=1, source_target_pairs={{0,192},{64,0},{128,64},{192,128},{1,193},{65,1},{129,65},{193,129... | collective-permute-start | bytes 1671176 | tf_op jit(solution)/shard_map/ppermute | solution.py:31
  78.8 26.4 %copy-start.7 = (s32[4,8]{1,0:T(4,128)S(1)}, s32[4,8]{1,0:T(4,128)}, u32[]{:S(2)}) copy-start(s32[4,8]{1,0:T(4,128)} %param.5) | copy-start | bytes 388
  102.2 9.7 %collective-permute-start.11 = (s16[1088,128]{1,0:T(8,128)(2,1)}, s16[1088,128]{1,0:T(8,128)(2,1)S(1)}, u32[]{:S(2)}, u32[]{:S(2)}) collective-permute-start(s16[1088,128]{1,0:T(8,128)(2,1)} %get-tuple-element.64), channel_id=1, source_target_pairs={{0,64},{64,128},{128,192},{192,0},{1,65},{65,129},{129,193},{193,1... | collective-permute-start | bytes 835592 | tf_op jit(solution)/shard_map/ppermute | solution.py:31
  102.8 9.9 %collective-permute-start.12 = (s16[1088,128]{1,0:T(8,128)(2,1)}, s16[1088,128]{1,0:T(8,128)(2,1)S(1)}, u32[]{:S(2)}, u32[]{:S(2)}) collective-permute-start(s16[1088,128]{1,0:T(8,128)(2,1)} %get-tuple-element.65), channel_id=1, source_target_pairs={{0,128},{64,192},{128,0},{192,64},{1,129},{65,193},{129,1},{193,65... | collective-permute-start | bytes 835592 | tf_op jit(solution)/shard_map/ppermute | solution.py:31
  105.4 27.6 %copy-start.1 = (f32[1056,256]{1,0:T(8,128)S(1)}, f32[1056,256]{1,0:T(8,128)}, u32[]{:S(2)}) copy-start(f32[1056,256]{1,0:T(8,128)} %get-tuple-element.67.kept_ref) | copy-start | bytes 3244036
  111.9 10.2 %copy-start.2 = (s16[1088,128]{1,0:T(8,128)(2,1)}, s16[1088,128]{1,0:T(8,128)(2,1)S(1)}, u32[]{:S(2)}) copy-start(s16[1088,128]{1,0:T(8,128)(2,1)S(1)} %collective-permute-done.11.refs_0_) | copy-start | bytes 835588
  112.0 22.5 %collective-permute-start.19 = (s16[1088,128]{1,0:T(8,128)(2,1)}, s16[1088,128]{1,0:T(8,128)(2,1)}, u32[]{:S(2)}, u32[]{:S(2)}) collective-permute-start(s16[1088,128]{1,0:T(8,128)(2,1)} %get-tuple-element.80), channel_id=1, source_target_pairs={{0,192},{64,0},{128,64},{192,128},{1,193},{65,1},{129,65},{193,129... | collective-permute-start | bytes 835592 | tf_op jit(solution)/shard_map/ppermute | solution.py:31
  112.7 9.4 %copy-start.3 = (s16[1088,128]{1,0:T(8,128)(2,1)}, s16[1088,128]{1,0:T(8,128)(2,1)S(1)}, u32[]{:S(2)}) copy-start(s16[1088,128]{1,0:T(8,128)(2,1)S(1)} %collective-permute-done.12.refs_1_) | copy-start | bytes 835588
  122.2 16.8 %collective-permute-start.16 = (s16[1088,128]{1,0:T(8,128)(2,1)}, s16[1088,128]{1,0:T(8,128)(2,1)S(1)}, u32[]{:S(2)}, u32[]{:S(2)}) collective-permute-start(s16[1088,128]{1,0:T(8,128)(2,1)} %get-tuple-element.74), channel_id=1, source_target_pairs={{0,64},{64,128},{128,192},{192,0},{1,65},{65,129},{129,193},{193,1... | collective-permute-start | bytes 835592 | tf_op jit(solution)/shard_map/ppermute | solution.py:31
  128.1 11.4 %collective-permute-start.17 = (s16[1088,128]{1,0:T(8,128)(2,1)}, s16[1088,128]{1,0:T(8,128)(2,1)S(1)}, u32[]{:S(2)}, u32[]{:S(2)}) collective-permute-start(s16[1088,128]{1,0:T(8,128)(2,1)} %get-tuple-element.75), channel_id=1, source_target_pairs={{0,128},{64,192},{128,0},{192,64},{1,129},{65,193},{129,1},{193,65... | collective-permute-start | bytes 835592 | tf_op jit(solution)/shard_map/ppermute | solution.py:31
  131.5 12.0 %collective-permute-start.18 = (s16[1088,128]{1,0:T(8,128)(2,1)}, s16[1088,128]{1,0:T(8,128)(2,1)}, u32[]{:S(2)}, u32[]{:S(2)}) collective-permute-start(s16[1088,128]{1,0:T(8,128)(2,1)} %get-tuple-element.76), channel_id=1, source_target_pairs={{0,192},{64,0},{128,64},{192,128},{1,193},{65,1},{129,65},{193,129... | collective-permute-start | bytes 835592 | tf_op jit(solution)/shard_map/ppermute | solution.py:31
  133.5 1.0 copy-start
  139.0 4.4 %copy-start.4 = (s16[1088,128]{1,0:T(8,128)(2,1)}, s16[1088,128]{1,0:T(8,128)(2,1)S(1)}, u32[]{:S(2)}) copy-start(s16[1088,128]{1,0:T(8,128)(2,1)S(1)} %collective-permute-done.16.refs_0_) | copy-start | bytes 835588
  139.4 4.0 %copy-start.5 = (s16[1088,128]{1,0:T(8,128)(2,1)}, s16[1088,128]{1,0:T(8,128)(2,1)S(1)}, u32[]{:S(2)}) copy-start(s16[1088,128]{1,0:T(8,128)(2,1)S(1)} %collective-permute-done.17.refs_1_) | copy-start | bytes 835588

commit v7 on v6

--- a/solution.py
+++ b/solution.py
@@ -43,6 +43,16 @@
     if back:
         pairs = [(b, a) for a, b in pairs]
     return lax.ppermute(value, "blk", sorted(pairs))
+
+
+def spread(parts):
+    one, two, three = parts
+    count, half = three.shape[0], two.shape[0] // 2
+    down = passed_along(jnp.concatenate([three, two[half:]]), "samp", -1)
+    up = passed_along(one, "samp", 1)
+    first = passed_along(two[:half], "samp", 2)
+    second = passed_along(down[count:], "samp", -1)
+    return [up, first, second, down]
 
 
 def taper_table():
@@ -183,20 +193,21 @@
     )(dest, perturb, perturb)
 
 
-def total_kernel(kept_ref, *refs):
-    coded_refs, out_ref = refs[:-1], refs[-1]
-    rows = BS // (len(coded_refs) + 1)
+def total_kernel(kept_ref, up_ref, first_ref, second_ref, down_ref, out_ref):
+    rows = BS // 4
     block = BS + EXTRA
     coded = BS + CODE_EXTRA
     for r in range(B_DEV):
+        middle = (first_ref, r) if r < B_DEV // 2 else (second_ref, r - B_DEV // 2)
+        sources = [(up_ref, r), middle, (down_ref, r)]
         extras = [
-            ref[r * coded + BS : (r + 1) * coded, :].astype(jnp.int32).astype(jnp.float32) for ref in coded_refs
+            ref[at * coded + BS : (at + 1) * coded, :].astype(jnp.int32).astype(jnp.float32) for ref, at in sources
         ]
         for j in range(4):
             here = slice(r * block + j * rows, r * block + (j + 1) * rows)
             tile = kept_ref[here, :]
-            for ref, extra in zip(coded_refs, extras):
-                piece = ref[r * coded + j * rows : r * coded + (j + 1) * rows, :].astype(jnp.int32)
+            for (ref, at), extra in zip(sources, extras):
+                piece = ref[at * coded + j * rows : at * coded + (j + 1) * rows, :].astype(jnp.int32)
                 tile = tile + piece.astype(jnp.float32) * decoded_scale(extra[j : j + 1, :])
             out_ref[here, :] = tile
         norm = kept_ref[r * block + BS : r * block + BS + 1, :]
@@ -413,7 +424,7 @@
     *own_parts, to_mate, below, across, above = lax.optimization_barrier((*own_parts, chosen[1][3], *got[0]))
     mates = exchanged(to_mate, 1)
     got = [[below, mates, across, above], [got[1][0], mates, got[1][1], got[1][2]]]
-    own_parts = [passed_along(part, "samp", d) for d, part in enumerate(own_parts, 1)]
+    own_parts = spread(own_parts)
     sums = []
     for stage in range(STAGES):
         parts = list(remote_tiles(stage, slots, dest, at, got[stage], samp))
@@ -421,7 +432,7 @@
             parts, own_parts = lax.optimization_barrier((parts, own_parts))
         last = [parts[0]] + [passed_along(parts[d], "samp", d) for d in range(1, samp)]
         if stage == 0:
-            dest, *last[1:3] = lax.optimization_barrier((dest, *last[1:3]))
+            dest, last[1] = lax.optimization_barrier((dest, last[1]))
         sums.append(last)
 
     own_sum = own_total(kept, own_parts)

time: 149 us -> 148 us (level)
    ppermute x9 -> x10, starting transfers between devices: 18.2 us -> 15.3 us  [passed_along(): return lax.ppermute(value, axis, pairs)]
    ppermute x11, starting transfers between devices: 24.7 us -> 26.3 us  [exchanged(): return lax.ppermute(value, 'blk', sorted(pairs))]
    ppermute x9 -> x10, waiting for transfers between devices: 30.2 us -> 30.7 us  [passed_along(): return lax.ppermute(value, axis, pairs)]
  transfers between devices with their start and end apart: 20 -> 21, of which waited for: 9 -> 8; matrix products, arithmetic and copies ran while one was open for 2% -> 4% of each run, Pallas kernels for 31% -> 31%
where the time goes in v7:
time: 148 us
  Pallas kernels  54.3 us (37%)
  waiting for transfers between devices  43.3 us (29%)
  starting transfers between devices  41.6 us (28%)
  local copies, waits for them, and re-layouts  4.39 us (3%)
  other arithmetic  4.16 us (3%)
    ppermute x10, waiting for transfers between devices, passed_along(): return lax.ppermute(value, axis, pairs)  30.7 us
    ppermute x11, starting transfers between devices, exchanged(): return lax.ppermute(value, 'blk', sorted(pairs))  26.3 us
    pallas_call x2, Pallas kernels, remote_tiles(): pl.pallas_call(functools.partial(remote_kernel, stage), grid_spec=pltpu.P...  18.7 us
    pallas_call x1, Pallas kernels, own_tiles(): pl.pallas_call(own_kernel, grid_spec=pltpu.PrefetchScalarGridSpec(num_sca...  16.8 us
    ppermute x10, starting transfers between devices, passed_along(): return lax.ppermute(value, axis, pairs)  15.3 us
    ppermute x11, waiting for transfers between devices, exchanged(): return lax.ppermute(value, 'blk', sorted(pairs))  12.6 us
    pallas_call x2, Pallas kernels, select(): pl.pallas_call(functools.partial(select_kernel, plan), grid_spec=pltpu.Pr...  9.15 us
    pallas_call x2, Pallas kernels, final(): pl.pallas_call(functools.partial(final_kernel, half), grid_spec=pltpu.Pre...  9.12 us
  transfers between devices with their start and end apart: 21, of which 8 were waited for; matrix products, arithmetic and copies ran while one was open for 4% of the time, Pallas kernels for 31%

profile of v7, /device:TPU:8, one launch (start us, length us, event | category | flops | bytes accessed | tf_op | source)
XLA Modules:
  0.0 147.9 jit_solution(6390272399519743439)
XLA Ops:
  0.0 0.7 add_select_fusion
  1.4 1.6 %collective-permute-start.3 = (s32[2]{0:T(128)S(1)}, s32[2]{0:T(128)S(1)}, u32[]{:S(2)}, u32[]{:S(2)}) collective-permute-start(s32[2]{0:T(128)S(1)} %get-tuple-element.82), channel_id=1, source_target_pairs={{0,2},{1,3},{2,4},{3,5},{4,6},{5,7},{6,8},{7,9},{8,10},{9,11},{10,... | collective-permute-start | bytes 32 | tf_op jit(solution)/shard_map/ppermute | solution.py:45
  3.0 6.1 %collective-permute-start.2 = (s32[2]{0:T(128)S(1)}, s32[2]{0:T(128)S(1)}, u32[]{:S(2)}, u32[]{:S(2)}) collective-permute-start(s32[2]{0:T(128)S(1)} %get-tuple-element.83), channel_id=1, source_target_pairs={{0,63},{1,2},{2,1},{3,4},{4,3},{5,6},{6,5},{7,8},{8,7},{9,10},{10,... | collective-permute-start | bytes 32 | tf_op jit(solution)/shard_map/ppermute | solution.py:45
  9.1 1.6 %collective-permute-start = (s32[2]{0:T(128)S(1)}, s32[2]{0:T(128)S(1)}, u32[]{:S(2)}, u32[]{:S(2)}) collective-permute-start(s32[2]{0:T(128)S(1)} %get-tuple-element.81), channel_id=1, source_target_pairs={{0,62},{1,63},{2,0},{3,1},{4,2},{5,3},{6,4},{7,5},{8,6},{9,7},{10,... | collective-permute-start | bytes 32 | tf_op jit(solution)/shard_map/ppermute | solution.py:45
  11.1 1.6 %collective-permute-done = s32[2]{0:T(128)S(1)} collective-permute-done((s32[2]{0:T(128)S(1)}, s32[2]{0:T(128)S(1)}, u32[]{:S(2)}, u32[]{:S(2)}) %collective-permute-start) | collective-permute-done | bytes 40 | tf_op jit(solution)/shard_map/ppermute | solution.py:45
  13.3 3.6 %shard_map.39 = (bf16[2048,256]{1,0:T(8,128)(2,1)}, bf16[2048,256]{1,0:T(8,128)(2,1)}, bf16[2048,256]{1,0:T(8,128)(2,1)}) custom-call(s32[8]{0:T(128)} %pad_add_fusion.3.want_ref, bf16[2048,1024]{1,0:T(8,128)(2,1)} %source_ref.3), custom_call_target="tpu_custom_call" | custom-call | bytes 6291456 | tf_op jit(solution)/shard_map/pallas_call | solution.py:115
  16.9 4.1 %collective-permute-start.5 = (bf16[2048,256]{1,0:T(8,128)(2,1)}, bf16[2048,256]{1,0:T(8,128)(2,1)}, u32[]{:S(2)}, u32[]{:S(2)}) collective-permute-start(bf16[2048,256]{1,0:T(8,128)(2,1)} %get-tuple-element.51), channel_id=1, source_target_pairs={{0,63},{1,2},{2,1},{3,4},{4,3},{5,6},{6,5},{7,8},{8,7},{9,10},{10,... | collective-permute-start | bytes 3145736 | tf_op jit(solution)/shard_map/ppermute | solution.py:45
  21.0 1.6 %collective-permute-start.6 = (bf16[2048,256]{1,0:T(8,128)(2,1)}, bf16[2048,256]{1,0:T(8,128)(2,1)}, u32[]{:S(2)}, u32[]{:S(2)}) collective-permute-start(bf16[2048,256]{1,0:T(8,128)(2,1)} %get-tuple-element.52), channel_id=1, source_target_pairs={{0,62},{1,63},{2,0},{3,1},{4,2},{5,3},{6,4},{7,5},{8,6},{9,7},{10,... | collective-permute-start | bytes 3145736 | tf_op jit(solution)/shard_map/ppermute | solution.py:45
  23.2 5.6 %shard_map.37 = (bf16[2048,256]{1,0:T(8,128)(2,1)}, bf16[2048,256]{1,0:T(8,128)(2,1)}, bf16[2048,256]{1,0:T(8,128)(2,1)}, bf16[2048,512]{1,0:T(8,128)(2,1)}) custom-call(s32[8]{0:T(128)} %pad_add_fusion.3.want_ref, bf16[2048,1024]{1,0:T(8,128)(2,1)} %source_ref.3), custom_call_target="tpu_custom_call" | custom-call | bytes 10485760 | tf_op jit(solution)/shard_map/pallas_call | solution.py:115
  28.7 16.8 %shard_map.38 = (bf16[1024,2048]{1,0:T(8,128)(2,1)}, f32[1056,256]{1,0:T(8,128)}, s16[1088,256]{1,0:T(8,128)(2,1)}, s16[1088,256]{1,0:T(8,128)(2,1)}, s16[1088,256]{1,0:T(8,128)(2,1)}) custom-call(s32[4]{0:T(128)} %and_select_fusion.dest_ref, bf16[2048,1024]{1,0:T(8,128)(2,1)} %source_ref.3, bf16[2048,1024]{1,0:T(8,128)(2,1)} %source_ref.3), custom_call_target="tpu_custom_call" | custom-call | flops 4294967296 | bytes 12582912 | tf_op jit(solution)/shard_map/pallas_call | solution.py:176
  45.5 1.0 collective-permute-done.4.refs_0_
  46.6 9.6 %collective-permute-done.5.refs_2_ = bf16[2048,256]{1,0:T(8,128)(2,1)} collective-permute-done((bf16[2048,256]{1,0:T(8,128)(2,1)}, bf16[2048,256]{1,0:T(8,128)(2,1)}, u32[]{:S(2)}, u32[]{:S(2)}) %collective-permute-start.5) | collective-permute-done | bytes 1048608 | tf_op jit(solution)/shard_map/ppermute | solution.py:45
  56.2 1.1 fusion.12
  57.3 1.1 pad_add_fusion
  59.0 2.6 %collective-permute-start.9 = (s16[544,256]{1,0:T(8,128)(2,1)S(1)}, s16[544,256]{1,0:T(8,128)(2,1)S(1)}, u32[]{:S(2)}, u32[]{:S(2)}) collective-permute-start(s16[544,256]{1,0:T(8,128)(2,1)S(1)} %get-tuple-element.90), channel_id=1, source_target_pairs={{0,128},{64,192},{128,0},{192,64},{1,129},{65,193},{129,1},{193,65... | collective-permute-start | bytes 835592 | tf_op jit(solution)/shard_map/ppermute | solution.py:31
  61.9 5.4 %collective-permute-start.14 = (bf16[2048,256]{1,0:T(8,128)(2,1)}, bf16[2048,256]{1,0:T(8,128)(2,1)}, u32[]{:S(2)}, u32[]{:S(2)}) collective-permute-start(bf16[2048,256]{1,0:T(8,128)(2,1)} %get-tuple-element.71), channel_id=1, source_target_pairs={{0,63},{1,2},{2,1},{3,4},{4,3},{5,6},{6,5},{7,8},{8,7},{9,10},{10,... | collective-permute-start | bytes 3145736 | tf_op jit(solution)/shard_map/ppermute | solution.py:45
  67.2 19.2 %collective-permute-done.9.first_ref = s16[544,256]{1,0:T(8,128)(2,1)S(1)} collective-permute-done((s16[544,256]{1,0:T(8,128)(2,1)S(1)}, s16[544,256]{1,0:T(8,128)(2,1)S(1)}, u32[]{:S(2)}, u32[]{:S(2)}) %collective-permute-start.9) | collective-permute-done | bytes 278560 | tf_op jit(solution)/shard_map/ppermute | solution.py:31
  86.5 5.7 %collective-permute-start.15 = (bf16[2048,256]{1,0:T(8,128)(2,1)}, bf16[2048,256]{1,0:T(8,128)(2,1)}, u32[]{:S(2)}, u32[]{:S(2)}) collective-permute-start(bf16[2048,256]{1,0:T(8,128)(2,1)} %get-tuple-element.72), channel_id=1, source_target_pairs={{0,62},{1,63},{2,0},{3,1},{4,2},{5,3},{6,4},{7,5},{8,6},{9,7},{10,... | collective-permute-start | bytes 3145736 | tf_op jit(solution)/shard_map/ppermute | solution.py:45
  92.3 0.7 reshape.142.slot_ref
  93.1 2.1 %collective-permute-start.11 = (s16[544,256]{1,0:T(8,128)(2,1)S(1)}, s16[544,256]{1,0:T(8,128)(2,1)S(1)}, u32[]{:S(2)}, u32[]{:S(2)}) collective-permute-start(s16[544,256]{1,0:T(8,128)(2,1)S(1)} %slice.28), channel_id=1, source_target_pairs={{0,192},{64,0},{128,64},{192,128},{1,193},{65,1},{129,65},{193,129... | collective-permute-start | bytes 835592 | tf_op jit(solution)/shard_map/ppermute | solution.py:31
  95.2 9.4 %shard_map.40 = (f32[1056,128]{1,0:T(8,128)}, s16[1088,128]{1,0:T(8,128)(2,1)}, s16[1088,128]{1,0:T(8,128)(2,1)}, s16[1088,128]{1,0:T(8,128)(2,1)}) custom-call(s32[16]{0:T(128)} %reshape.142.slot_ref, s32[4]{0:T(128)} %and_select_fusion.dest_ref, bf16[1024,2048]{1,0:T(8,128)(2,1)} %get-tuple-element.45.at_ref, bf16[2048,256]{1,0:T(8,128)(2,1)} %copy-done.6, ...), custom_call_target="tpu_custom_call" | custom-call | flops 4294967296 | bytes 10485760 | tf_op jit(solution)/shard_map/pallas_call | solution.py:297
  104.6 2.7 %collective-permute-done.8.up_ref = s16[1088,256]{1,0:T(8,128)(2,1)S(1)} collective-permute-done((s16[1088,256]{1,0:T(8,128)(2,1)}, s16[1088,256]{1,0:T(8,128)(2,1)S(1)}, u32[]{:S(2)}, u32[]{:S(2)}) %collective-permute-start.8) | collective-permute-done | bytes 557088 | tf_op jit(solution)/shard_map/ppermute | solution.py:31
  107.8 2.2 %collective-permute-start.19 = (s16[1088,128]{1,0:T(8,128)(2,1)}, s16[1088,128]{1,0:T(8,128)(2,1)}, u32[]{:S(2)}, u32[]{:S(2)}) collective-permute-start(s16[1088,128]{1,0:T(8,128)(2,1)} %get-tuple-element.79), channel_id=1, source_target_pairs={{0,128},{64,192},{128,0},{192,64},{1,129},{65,193},{129,1},{193,65... | collective-permute-start | bytes 835592 | tf_op jit(solution)/shard_map/ppermute | solution.py:31
  110.1 7.0 %collective-permute-done.12.refs_0_ = s16[1088,128]{1,0:T(8,128)(2,1)S(1)} collective-permute-done((s16[1088,128]{1,0:T(8,128)(2,1)}, s16[1088,128]{1,0:T(8,128)(2,1)S(1)}, u32[]{:S(2)}, u32[]{:S(2)}) %collective-permute-start.12) | collective-permute-done | bytes 278560 | tf_op jit(solution)/shard_map/ppermute | solution.py:31
  117.0 5.3 %collective-permute-start.20 = (s16[1088,128]{1,0:T(8,128)(2,1)}, s16[1088,128]{1,0:T(8,128)(2,1)}, u32[]{:S(2)}, u32[]{:S(2)}) collective-permute-start(s16[1088,128]{1,0:T(8,128)(2,1)} %get-tuple-element.80), channel_id=1, source_target_pairs={{0,192},{64,0},{128,64},{192,128},{1,193},{65,1},{129,65},{193,129... | collective-permute-start | bytes 835592 | tf_op jit(solution)/shard_map/ppermute | solution.py:31
  122.4 9.4 %shard_map.42 = (f32[1056,128]{1,0:T(8,128)}, s16[1088,128]{1,0:T(8,128)(2,1)}, s16[1088,128]{1,0:T(8,128)(2,1)}, s16[1088,128]{1,0:T(8,128)(2,1)}) custom-call(s32[16]{0:T(128)} %reshape.142.slot_ref, s32[4]{0:T(128)} %and_select_fusion.dest_ref, bf16[1024,2048]{1,0:T(8,128)(2,1)} %get-tuple-element.45.at_ref, ...), custom_call_target="tpu_custom_call" | custom-call | flops 4294967296 | bytes 10485760 | tf_op jit(solution)/shard_map/pallas_call | solution.py:297
  131.9 2.1 %collective-permute-start.17 = (s16[1088,128]{1,0:T(8,128)(2,1)}, s16[1088,128]{1,0:T(8,128)(2,1)}, u32[]{:S(2)}, u32[]{:S(2)}) collective-permute-start(s16[1088,128]{1,0:T(8,128)(2,1)} %get-tuple-element.75), channel_id=1, source_target_pairs={{0,128},{64,192},{128,0},{192,64},{1,129},{65,193},{129,1},{193,65... | collective-permute-start | bytes 835592 | tf_op jit(solution)/shard_map/ppermute | solution.py:31
  134.0 0.6 add.125.place_ref
  135.9 1.0 copy-done
  136.9 4.6 %shard_map.43.refs_3_ = f32[2048,256]{1,0:T(8,128)} custom-call(s32[32]{0:T(128)} %add.125.place_ref, s32[16]{0:T(128)} %reshape.142.slot_ref, s32[4]{0:T(128)} %and_select_fusion.dest_ref, f32[32]{0:T(128)} %reshape.143.taper_ref, f32[1056,256]{1,0:T(8,128)} %copy-done, f32[1056,128]{1,0:T(8,128)} %get-tuple-element.77.kept_ref, ...), custom_call_target="tpu_custom_call" | custom-call | flops 1048576 | bytes 4194304 | tf_op jit(solution)/shard_map/pallas_call | solution.py:362
  141.5 1.8 %collective-permute-done.18.refs_2_ = s16[1088,128]{1,0:T(8,128)(2,1)} collective-permute-done((s16[1088,128]{1,0:T(8,128)(2,1)}, s16[1088,128]{1,0:T(8,128)(2,1)}, u32[]{:S(2)}, u32[]{:S(2)}) %collective-permute-start.18) | collective-permute-done | bytes 278560 | tf_op jit(solution)/shard_map/ppermute | solution.py:31
  143.3 4.6 %shard_map.44 = f32[2048,256]{1,0:T(8,128)} custom-call(s32[32]{0:T(128)} %add.125.place_ref, s32[16]{0:T(128)} %reshape.142.slot_ref, s32[4]{0:T(128)} %and_select_fusion.dest_ref, f32[32]{0:T(128)} %reshape.143.taper_ref, f32[1056,256]{1,0:T(8,128)} %copy-done, f32[1056,128]{1,0:T(8,128)} %get-tuple-element.73.kept_ref, ...), custom_call_target="tpu_custom_call", output_to_operand_aliasing={{}: (9, {})} | custom-call | flops 1048576 | bytes 4194304 | tf_op jit(solution)/shard_map/pallas_call | solution.py:362
  (62 shorter events, 5.3 us)
Async XLA Ops:
  1.4 9.6 %collective-permute-start.3 = (s32[2]{0:T(128)S(1)}, s32[2]{0:T(128)S(1)}, u32[]{:S(2)}, u32[]{:S(2)}) collective-permute-start(s32[2]{0:T(128)S(1)} %get-tuple-element.82), channel_id=1, source_target_pairs={{0,2},{1,3},{2,4},{3,5},{4,6},{5,7},{6,8},{7,9},{8,10},{9,11},{10,... | collective-permute-start | bytes 32 | tf_op jit(solution)/shard_map/ppermute | solution.py:45
  3.0 8.1 %collective-permute-start.2 = (s32[2]{0:T(128)S(1)}, s32[2]{0:T(128)S(1)}, u32[]{:S(2)}, u32[]{:S(2)}) collective-permute-start(s32[2]{0:T(128)S(1)} %get-tuple-element.83), channel_id=1, source_target_pairs={{0,63},{1,2},{2,1},{3,4},{4,3},{5,6},{6,5},{7,8},{8,7},{9,10},{10,... | collective-permute-start | bytes 32 | tf_op jit(solution)/shard_map/ppermute | solution.py:45
  9.1 2.0 %collective-permute-start.1 = (s32[2]{0:T(128)S(1)}, s32[2]{0:T(128)S(1)}, u32[]{:S(2)}, u32[]{:S(2)}) collective-permute-start(s32[2]{0:T(128)S(1)} %get-tuple-element.84), channel_id=1, source_target_pairs={{0,1},{1,0},{2,3},{3,2},{4,5},{5,4},{6,7},{7,6},{8,9},{9,8},{10,11... | collective-permute-start | bytes 32 | tf_op jit(solution)/shard_map/ppermute | solution.py:45
  9.1 3.5 %collective-permute-start = (s32[2]{0:T(128)S(1)}, s32[2]{0:T(128)S(1)}, u32[]{:S(2)}, u32[]{:S(2)}) collective-permute-start(s32[2]{0:T(128)S(1)} %get-tuple-element.81), channel_id=1, source_target_pairs={{0,62},{1,63},{2,0},{3,1},{4,2},{5,3},{6,4},{7,5},{8,6},{9,7},{10,... | collective-permute-start | bytes 32 | tf_op jit(solution)/shard_map/ppermute | solution.py:45
  16.9 29.7 %collective-permute-start.4 = (bf16[2048,256]{1,0:T(8,128)(2,1)}, bf16[2048,256]{1,0:T(8,128)(2,1)S(1)}, u32[]{:S(2)}, u32[]{:S(2)}) collective-permute-start(bf16[2048,256]{1,0:T(8,128)(2,1)} %get-tuple-element.50), channel_id=1, source_target_pairs={{0,2},{1,3},{2,4},{3,5},{4,6},{5,7},{6,8},{7,9},{8,10},{9,11},{10,... | collective-permute-start | bytes 3145736 | tf_op jit(solution)/shard_map/ppermute | solution.py:45
  16.9 39.3 %collective-permute-start.5 = (bf16[2048,256]{1,0:T(8,128)(2,1)}, bf16[2048,256]{1,0:T(8,128)(2,1)}, u32[]{:S(2)}, u32[]{:S(2)}) collective-permute-start(bf16[2048,256]{1,0:T(8,128)(2,1)} %get-tuple-element.51), channel_id=1, source_target_pairs={{0,63},{1,2},{2,1},{3,4},{4,3},{5,6},{6,5},{7,8},{8,7},{9,10},{10,... | collective-permute-start | bytes 3145736 | tf_op jit(solution)/shard_map/ppermute | solution.py:45
  21.0 35.2 %collective-permute-start.6 = (bf16[2048,256]{1,0:T(8,128)(2,1)}, bf16[2048,256]{1,0:T(8,128)(2,1)}, u32[]{:S(2)}, u32[]{:S(2)}) collective-permute-start(bf16[2048,256]{1,0:T(8,128)(2,1)} %get-tuple-element.52), channel_id=1, source_target_pairs={{0,62},{1,63},{2,0},{3,1},{4,2},{5,3},{6,4},{7,5},{8,6},{9,7},{10,... | collective-permute-start | bytes 3145736 | tf_op jit(solution)/shard_map/ppermute | solution.py:45
  45.5 16.2 %copy-start.4 = (s32[4,8]{1,0:T(4,128)S(1)}, s32[4,8]{1,0:T(4,128)}, u32[]{:S(2)}) copy-start(s32[4,8]{1,0:T(4,128)} %param.4) | copy-start | bytes 388
  46.6 10.7 %copy-start.6 = (bf16[2048,256]{1,0:T(8,128)(2,1)}, bf16[2048,256]{1,0:T(8,128)(2,1)S(1)}, u32[]{:S(2)}) copy-start(bf16[2048,256]{1,0:T(8,128)(2,1)S(1)} %collective-permute-done.4.refs_0_) | copy-start | bytes 3145732
  56.2 36.9 %collective-permute-start.7 = (bf16[2048,512]{1,0:T(8,128)(2,1)}, bf16[2048,512]{1,0:T(8,128)(2,1)}, u32[]{:S(2)}, u32[]{:S(2)}) collective-permute-start(bf16[2048,512]{1,0:T(8,128)(2,1)} %get-tuple-element.54), channel_id=1, source_target_pairs={{0,1},{1,0},{2,3},{3,2},{4,5},{5,4},{6,7},{7,6},{8,9},{9,8},{10,11... | collective-permute-start | bytes 6291464 | tf_op jit(solution)/shard_map/ppermute | solution.py:45
  58.4 34.6 %collective-permute-start.10 = (s16[1632,256]{1,0:T(8,128)(2,1)S(1)}, s16[1632,256]{1,0:T(8,128)(2,1)S(1)}, u32[]{:S(2)}, u32[]{:S(2)}) collective-permute-start(s16[1632,256]{1,0:T(8,128)(2,1)S(1)} %pad_add_fusion), channel_id=1, source_target_pairs={{0,192},{64,0},{128,64},{192,128},{1,193},{65,1},{129,65},{193,129... | collective-permute-start | bytes 2506760 | tf_op jit(solution)/shard_map/ppermute | solution.py:31
  59.0 27.4 %collective-permute-start.9 = (s16[544,256]{1,0:T(8,128)(2,1)S(1)}, s16[544,256]{1,0:T(8,128)(2,1)S(1)}, u32[]{:S(2)}, u32[]{:S(2)}) collective-permute-start(s16[544,256]{1,0:T(8,128)(2,1)S(1)} %get-tuple-element.90), channel_id=1, source_target_pairs={{0,128},{64,192},{128,0},{192,64},{1,129},{65,193},{129,1},{193,65... | collective-permute-start | bytes 835592 | tf_op jit(solution)/shard_map/ppermute | solution.py:31
  61.8 60.6 %collective-permute-start.13 = (bf16[2048,256]{1,0:T(8,128)(2,1)}, bf16[2048,256]{1,0:T(8,128)(2,1)}, u32[]{:S(2)}, u32[]{:S(2)}) collective-permute-start(bf16[2048,256]{1,0:T(8,128)(2,1)} %get-tuple-element.43), channel_id=1, source_target_pairs={{0,2},{1,3},{2,4},{3,5},{4,6},{5,7},{6,8},{7,9},{8,10},{9,11},{10,... | collective-permute-start | bytes 3145736 | tf_op jit(solution)/shard_map/ppermute | solution.py:45
  61.9 60.5 %collective-permute-start.14 = (bf16[2048,256]{1,0:T(8,128)(2,1)}, bf16[2048,256]{1,0:T(8,128)(2,1)}, u32[]{:S(2)}, u32[]{:S(2)}) collective-permute-start(bf16[2048,256]{1,0:T(8,128)(2,1)} %get-tuple-element.71), channel_id=1, source_target_pairs={{0,63},{1,2},{2,1},{3,4},{4,3},{5,6},{6,5},{7,8},{8,7},{9,10},{10,... | collective-permute-start | bytes 3145736 | tf_op jit(solution)/shard_map/ppermute | solution.py:45
  86.5 35.9 %collective-permute-start.15 = (bf16[2048,256]{1,0:T(8,128)(2,1)}, bf16[2048,256]{1,0:T(8,128)(2,1)}, u32[]{:S(2)}, u32[]{:S(2)}) collective-permute-start(bf16[2048,256]{1,0:T(8,128)(2,1)} %get-tuple-element.72), channel_id=1, source_target_pairs={{0,62},{1,63},{2,0},{3,1},{4,2},{5,3},{6,4},{7,5},{8,6},{9,7},{10,... | collective-permute-start | bytes 3145736 | tf_op jit(solution)/shard_map/ppermute | solution.py:45
  93.0 14.2 %collective-permute-start.8 = (s16[1088,256]{1,0:T(8,128)(2,1)}, s16[1088,256]{1,0:T(8,128)(2,1)S(1)}, u32[]{:S(2)}, u32[]{:S(2)}) collective-permute-start(s16[1088,256]{1,0:T(8,128)(2,1)} %get-tuple-element.61), channel_id=1, source_target_pairs={{0,64},{64,128},{128,192},{192,0},{1,65},{65,129},{129,193},{193,1... | collective-permute-start | bytes 1671176 | tf_op jit(solution)/shard_map/ppermute | solution.py:31
  93.1 14.1 %collective-permute-start.11 = (s16[544,256]{1,0:T(8,128)(2,1)S(1)}, s16[544,256]{1,0:T(8,128)(2,1)S(1)}, u32[]{:S(2)}, u32[]{:S(2)}) collective-permute-start(s16[544,256]{1,0:T(8,128)(2,1)S(1)} %slice.28), channel_id=1, source_target_pairs={{0,192},{64,0},{128,64},{192,128},{1,193},{65,1},{129,65},{193,129... | collective-permute-start | bytes 835592 | tf_op jit(solution)/shard_map/ppermute | solution.py:31
  107.2 9.8 %collective-permute-start.12 = (s16[1088,128]{1,0:T(8,128)(2,1)}, s16[1088,128]{1,0:T(8,128)(2,1)S(1)}, u32[]{:S(2)}, u32[]{:S(2)}) collective-permute-start(s16[1088,128]{1,0:T(8,128)(2,1)} %get-tuple-element.64), channel_id=1, source_target_pairs={{0,64},{64,128},{128,192},{192,0},{1,65},{65,129},{129,193},{193,1... | collective-permute-start | bytes 835592 | tf_op jit(solution)/shard_map/ppermute | solution.py:31
  107.8 26.8 %copy-start.5 = (s32[4,8]{1,0:T(4,128)S(1)}, s32[4,8]{1,0:T(4,128)}, u32[]{:S(2)}) copy-start(s32[4,8]{1,0:T(4,128)} %param.5) | copy-start | bytes 388
  107.8 27.7 %copy-start.1 = (f32[1056,256]{1,0:T(8,128)S(1)}, f32[1056,256]{1,0:T(8,128)}, u32[]{:S(2)}) copy-start(f32[1056,256]{1,0:T(8,128)} %get-tuple-element.66.kept_ref) | copy-start | bytes 3244036
  107.8 29.1 %collective-permute-start.19 = (s16[1088,128]{1,0:T(8,128)(2,1)}, s16[1088,128]{1,0:T(8,128)(2,1)}, u32[]{:S(2)}, u32[]{:S(2)}) collective-permute-start(s16[1088,128]{1,0:T(8,128)(2,1)} %get-tuple-element.79), channel_id=1, source_target_pairs={{0,128},{64,192},{128,0},{192,64},{1,129},{65,193},{129,1},{193,65... | collective-permute-start | bytes 835592 | tf_op jit(solution)/shard_map/ppermute | solution.py:31
  117.0 14.7 %copy-start.2 = (s16[1088,128]{1,0:T(8,128)(2,1)}, s16[1088,128]{1,0:T(8,128)(2,1)S(1)}, u32[]{:S(2)}) copy-start(s16[1088,128]{1,0:T(8,128)(2,1)S(1)} %collective-permute-done.12.refs_0_) | copy-start | bytes 835588
  117.0 19.9 %collective-permute-start.20 = (s16[1088,128]{1,0:T(8,128)(2,1)}, s16[1088,128]{1,0:T(8,128)(2,1)}, u32[]{:S(2)}, u32[]{:S(2)}) collective-permute-start(s16[1088,128]{1,0:T(8,128)(2,1)} %get-tuple-element.80), channel_id=1, source_target_pairs={{0,192},{64,0},{128,64},{192,128},{1,193},{65,1},{129,65},{193,129... | collective-permute-start | bytes 835592 | tf_op jit(solution)/shard_map/ppermute | solution.py:31
  131.8 9.7 %collective-permute-start.16 = (s16[1088,128]{1,0:T(8,128)(2,1)}, s16[1088,128]{1,0:T(8,128)(2,1)S(1)}, u32[]{:S(2)}, u32[]{:S(2)}) collective-permute-start(s16[1088,128]{1,0:T(8,128)(2,1)} %get-tuple-element.74), channel_id=1, source_target_pairs={{0,64},{64,128},{128,192},{192,0},{1,65},{65,129},{129,193},{193,1... | collective-permute-start | bytes 835592 | tf_op jit(solution)/shard_map/ppermute | solution.py:31
  131.9 9.6 %collective-permute-start.17 = (s16[1088,128]{1,0:T(8,128)(2,1)}, s16[1088,128]{1,0:T(8,128)(2,1)}, u32[]{:S(2)}, u32[]{:S(2)}) collective-permute-start(s16[1088,128]{1,0:T(8,128)(2,1)} %get-tuple-element.75), channel_id=1, source_target_pairs={{0,128},{64,192},{128,0},{192,64},{1,129},{65,193},{129,1},{193,65... | collective-permute-start | bytes 835592 | tf_op jit(solution)/shard_map/ppermute | solution.py:31
  133.9 9.4 %collective-permute-start.18 = (s16[1088,128]{1,0:T(8,128)(2,1)}, s16[1088,128]{1,0:T(8,128)(2,1)}, u32[]{:S(2)}, u32[]{:S(2)}) collective-permute-start(s16[1088,128]{1,0:T(8,128)(2,1)} %get-tuple-element.76), channel_id=1, source_target_pairs={{0,192},{64,0},{128,64},{192,128},{1,193},{65,1},{129,65},{193,129... | collective-permute-start | bytes 835592 | tf_op jit(solution)/shard_map/ppermute | solution.py:31
  135.9 1.0 copy-start
  141.5 1.8 %copy-start.3 = (s16[1088,128]{1,0:T(8,128)(2,1)}, s16[1088,128]{1,0:T(8,128)(2,1)S(1)}, u32[]{:S(2)}) copy-start(s16[1088,128]{1,0:T(8,128)(2,1)S(1)} %collective-permute-done.16.refs_0_) | copy-start | bytes 835588

commit v8 on v7

--- a/solution.py
+++ b/solution.py
@@ -109,9 +109,6 @@
     samples = perturb.shape[0]
     widths = [2 * HALF] * 3
     plan = [(q, side, stage, out, side) for out, q in enumerate((0, 2, 3)) for side in range(2)]
-    if stage == 1:
-        plan += [(1, side, half, 3, 2 * half + side) for half in range(2) for side in range(2)]
-        widths.append(4 * HALF)
     return pl.pallas_call(
         functools.partial(select_kernel, plan),
         grid_spec=pltpu.PrefetchScalarGridSpec(
@@ -226,7 +223,7 @@
     )(kept, *coded)
 
 
-def remote_kernel(stage, slot_ref, dest_ref, at_ref, *refs):
+def remote_kernel(stage, slot_ref, dest_ref, mate_ref, at_ref, *refs):
     blocks, parts, (cols_ref, tile_ref, sems) = refs[:4], refs[4:-3], refs[-3:]
     samp = len(parts)
     samples = cols_ref.shape[1]
@@ -238,10 +235,10 @@
         copies = []
         for q in range(4):
             for side in range(2):
-                column = (2 * stage if q == 1 else 0) + side
+                start = pl.multiple_of(mate_ref[side] * BS + stage * HALF, HALF) if q == 1 else side * HALF
                 copies.append(
                     pltpu.make_async_copy(
-                        blocks[q].at[:, pl.ds(column * HALF, HALF)],
+                        blocks[q].at[:, pl.ds(start, HALF)],
                         cols_ref.at[2 * q + side],
                         sems.at[2 * q + side],
                     )
@@ -289,7 +286,7 @@
         parts[d][BS : BS + CODE_EXTRA, :] = with_rows(CODE_EXTRA, HALF, codes[d - 1] + norm_codes)
 
 
-def remote_tiles(stage, slots, dest, at, blocks, samp):
+def remote_tiles(stage, slots, dest, mate_blocks, at, blocks, samp):
     cells, samples = at.shape
     blocks_out = [(BS + EXTRA, jnp.float32)] + [(BS + CODE_EXTRA, jnp.int16)] * (samp - 1)
     out_specs = [pl.BlockSpec((block, HALF), lambda r, *s: (r, 0)) for block, _ in blocks_out]
@@ -297,7 +294,7 @@
     return pl.pallas_call(
         functools.partial(remote_kernel, stage),
         grid_spec=pltpu.PrefetchScalarGridSpec(
-            num_scalar_prefetch=2,
+            num_scalar_prefetch=3,
             grid=(B_DEV,),
             in_specs=[pl.BlockSpec((BS, samples), lambda r, *s: (r, 0))] + [pl.BlockSpec(memory_space=pl.ANY)] * 4,
             out_specs=out_specs,
@@ -310,7 +307,7 @@
         out_shape=out_shape,
         compiler_params=pltpu.CompilerParams(vmem_limit_bytes=BIG),
         cost_estimate=pl.CostEstimate(flops=2 * cells * cells * samples, bytes_accessed=10 * MIB, transcendentals=0),
-    )(slots, dest, at, *blocks)
+    )(slots, dest, mate_blocks, at, *blocks)
 
 
 def final_kernel(half, place_ref, slot_ref, dest_ref, taper_ref, own_ref, kept_ref, *refs):
@@ -393,6 +390,7 @@
     low = jnp.min(jnp.where(need, four[None], B_DEV - 1), axis=1)
     high = jnp.max(jnp.where(need, four[None], 0), axis=1)
     want = jnp.stack([low, high], axis=1)
+    mates = exchanged(perturb, 1)
     asked = jnp.concatenate([exchanged(want[q], q, back=True) for q in range(4)])
 
     k_ids = jnp.arange(K_PART, dtype=jnp.int32)[None, :, None]
@@ -419,15 +417,14 @@
     got = []
     for stage in range(STAGES):
         got.append([exchanged(chosen[stage][i], q) for i, q in enumerate((0, 2, 3))])
-    held, _ = lax.optimization_barrier((perturb, chosen[1][0]))
+    held, _, mates = lax.optimization_barrier((perturb, chosen[1][0], mates))
     at, kept, *own_parts = own_tiles(dest, held)
-    *own_parts, to_mate, below, across, above = lax.optimization_barrier((*own_parts, chosen[1][3], *got[0]))
-    mates = exchanged(to_mate, 1)
+    *own_parts, below, across, above = lax.optimization_barrier((*own_parts, *got[0]))
     got = [[below, mates, across, above], [got[1][0], mates, got[1][1], got[1][2]]]
     own_parts = spread(own_parts)
     sums = []
     for stage in range(STAGES):
-        parts = list(remote_tiles(stage, slots, dest, at, got[stage], samp))
+        parts = list(remote_tiles(stage, slots, dest, want[1], at, got[stage], samp))
         if stage == 0:
             parts, own_parts = lax.optimization_barrier((parts, own_parts))
         last = [parts[0]] + [passed_along(parts[d], "samp", d) for d in range(1, samp)]

time: 148 us -> 135 us (0.912)
  waiting for transfers between devices: 43.3 us -> 29.6 us
  Pallas kernels: 54.3 us -> 52.5 us
    ppermute x10, waiting for transfers between devices: 30.7 us -> 15 us  [passed_along(): return lax.ppermute(value, axis, pairs)]
    ppermute x10, starting transfers between devices: 15.3 us -> 17.9 us  [passed_along(): return lax.ppermute(value, axis, pairs)]
    ppermute x11, waiting for transfers between devices: 12.6 us -> 14.5 us  [exchanged(): return lax.ppermute(value, 'blk', sorted(pairs))]
    pallas_call x2, Pallas kernels: 9.15 us -> 7.29 us  [select(): pl.pallas_call(functools.partial(select_kernel, plan), grid_spec=pltpu.Pr...]
    ppermute x11, starting transfers between devices: 26.3 us -> 24.8 us  [exchanged(): return lax.ppermute(value, 'blk', sorted(pairs))]
  transfers between devices with their start and end apart: 21 -> 21, of which waited for: 8 -> 7; matrix products, arithmetic and copies ran while one was open for 4% -> 4% of each run, Pallas kernels for 31% -> 36%
where the time goes in v8:
time: 135 us; the launch traced here: 134 us
  Pallas kernels  52.5 us (39%)
  starting transfers between devices  42.6 us (32%)
  waiting for transfers between devices  29.6 us (22%)
  local copies, waits for them, and re-layouts  5.12 us (4%)
  other arithmetic  4.17 us (3%)
    ppermute x11, starting transfers between devices, exchanged(): return lax.ppermute(value, 'blk', sorted(pairs))  24.8 us
    pallas_call x2, Pallas kernels, remote_tiles(): pl.pallas_call(functools.partial(remote_kernel, stage), grid_spec=pltpu.P...  18.9 us
    ppermute x10, starting transfers between devices, passed_along(): return lax.ppermute(value, axis, pairs)  17.9 us
    pallas_call x1, Pallas kernels, own_tiles(): pl.pallas_call(own_kernel, grid_spec=pltpu.PrefetchScalarGridSpec(num_sca...  16.8 us
    ppermute x10, waiting for transfers between devices, passed_along(): return lax.ppermute(value, axis, pairs)  15 us
    ppermute x11, waiting for transfers between devices, exchanged(): return lax.ppermute(value, 'blk', sorted(pairs))  14.5 us
    pallas_call x2, Pallas kernels, final(): pl.pallas_call(functools.partial(final_kernel, half), grid_spec=pltpu.Pre...  9.12 us
    pallas_call x2, Pallas kernels, select(): pl.pallas_call(functools.partial(select_kernel, plan), grid_spec=pltpu.Pr...  7.29 us
  transfers between devices with their start and end apart: 21, of which 7 were waited for; matrix products, arithmetic and copies ran while one was open for 4% of the time, Pallas kernels for 36%

profile of v8, /device:TPU:8, one launch (start us, length us, event | category | flops | bytes accessed | tf_op | source)
XLA Modules:
  0.0 134.2 jit_solution(13846182984447281489)
XLA Ops:
  0.0 0.7 add_select_fusion
  1.4 8.1 %collective-permute-start = (s32[2]{0:T(128)S(1)}, s32[2]{0:T(128)S(1)}, u32[]{:S(2)}, u32[]{:S(2)}) collective-permute-start(s32[2]{0:T(128)S(1)} %get-tuple-element.79), channel_id=1, source_target_pairs={{0,62},{1,63},{2,0},{3,1},{4,2},{5,3},{6,4},{7,5},{8,6},{9,7},{10,... | collective-permute-start | bytes 32 | tf_op jit(solution)/shard_map/ppermute | solution.py:45
  9.6 4.9 %collective-permute-start.2 = (s32[2]{0:T(128)S(1)}, s32[2]{0:T(128)S(1)}, u32[]{:S(2)}, u32[]{:S(2)}) collective-permute-start(s32[2]{0:T(128)S(1)} %get-tuple-element.81), channel_id=1, source_target_pairs={{0,63},{1,2},{2,1},{3,4},{4,3},{5,6},{6,5},{7,8},{8,7},{9,10},{10,... | collective-permute-start | bytes 32 | tf_op jit(solution)/shard_map/ppermute | solution.py:45
  14.5 2.0 %collective-permute-done.3 = s32[2]{0:T(128)S(1)} collective-permute-done((s32[2]{0:T(128)S(1)}, s32[2]{0:T(128)S(1)}, u32[]{:S(2)}, u32[]{:S(2)}) %collective-permute-start.3) | collective-permute-done | bytes 40 | tf_op jit(solution)/shard_map/ppermute | solution.py:45
  16.4 0.6 pad_add_fusion.3.want_ref
  17.0 3.7 %shard_map.39 = (bf16[2048,256]{1,0:T(8,128)(2,1)}, bf16[2048,256]{1,0:T(8,128)(2,1)}, bf16[2048,256]{1,0:T(8,128)(2,1)}) custom-call(s32[8]{0:T(128)} %pad_add_fusion.3.want_ref, bf16[2048,1024]{1,0:T(8,128)(2,1)} %source_ref.3), custom_call_target="tpu_custom_call" | custom-call | bytes 6291456 | tf_op jit(solution)/shard_map/pallas_call | solution.py:112
  20.8 4.3 %collective-permute-start.6 = (bf16[2048,256]{1,0:T(8,128)(2,1)}, bf16[2048,256]{1,0:T(8,128)(2,1)S(1)}, u32[]{:S(2)}, u32[]{:S(2)}) collective-permute-start(bf16[2048,256]{1,0:T(8,128)(2,1)} %get-tuple-element.49), channel_id=1, source_target_pairs={{0,63},{1,2},{2,1},{3,4},{4,3},{5,6},{6,5},{7,8},{8,7},{9,10},{10,... | collective-permute-start | bytes 3145736 | tf_op jit(solution)/shard_map/ppermute | solution.py:45
  25.1 1.6 %collective-permute-start.7 = (bf16[2048,256]{1,0:T(8,128)(2,1)}, bf16[2048,256]{1,0:T(8,128)(2,1)}, u32[]{:S(2)}, u32[]{:S(2)}) collective-permute-start(bf16[2048,256]{1,0:T(8,128)(2,1)} %get-tuple-element.50), channel_id=1, source_target_pairs={{0,62},{1,63},{2,0},{3,1},{4,2},{5,3},{6,4},{7,5},{8,6},{9,7},{10,... | collective-permute-start | bytes 3145736 | tf_op jit(solution)/shard_map/ppermute | solution.py:45
  27.3 3.6 %shard_map.37 = (bf16[2048,256]{1,0:T(8,128)(2,1)}, bf16[2048,256]{1,0:T(8,128)(2,1)}, bf16[2048,256]{1,0:T(8,128)(2,1)}) custom-call(s32[8]{0:T(128)} %pad_add_fusion.3.want_ref, bf16[2048,1024]{1,0:T(8,128)(2,1)} %source_ref.3), custom_call_target="tpu_custom_call" | custom-call | bytes 6291456 | tf_op jit(solution)/shard_map/pallas_call | solution.py:112
  30.9 16.8 %shard_map.38 = (bf16[1024,2048]{1,0:T(8,128)(2,1)}, f32[1056,256]{1,0:T(8,128)}, s16[1088,256]{1,0:T(8,128)(2,1)}, s16[1088,256]{1,0:T(8,128)(2,1)}, s16[1088,256]{1,0:T(8,128)(2,1)}) custom-call(s32[4]{0:T(128)} %and_select_fusion.dest_ref, bf16[2048,1024]{1,0:T(8,128)(2,1)} %source_ref.3, bf16[2048,1024]{1,0:T(8,128)(2,1)} %source_ref.3), custom_call_target="tpu_custom_call" | custom-call | flops 4294967296 | bytes 12582912 | tf_op jit(solution)/shard_map/pallas_call | solution.py:173
  47.7 2.8 %collective-permute-done.5.refs_0_ = bf16[2048,256]{1,0:T(8,128)(2,1)S(1)} collective-permute-done((bf16[2048,256]{1,0:T(8,128)(2,1)}, bf16[2048,256]{1,0:T(8,128)(2,1)S(1)}, u32[]{:S(2)}, u32[]{:S(2)}) %collective-permute-start.5) | collective-permute-done | bytes 1048608 | tf_op jit(solution)/shard_map/ppermute | solution.py:45
  50.4 9.8 %collective-permute-done.6.refs_2_ = bf16[2048,256]{1,0:T(8,128)(2,1)S(1)} collective-permute-done((bf16[2048,256]{1,0:T(8,128)(2,1)}, bf16[2048,256]{1,0:T(8,128)(2,1)S(1)}, u32[]{:S(2)}, u32[]{:S(2)}) %collective-permute-start.6) | collective-permute-done | bytes 1048608 | tf_op jit(solution)/shard_map/ppermute | solution.py:45
  60.2 1.4 %fusion.12 = (s16[544,256]{1,0:T(8,128)(2,1)S(1)}, s16[544,256]{1,0:T(8,128)(2,1)S(1)}) fusion(s16[1088,256]{1,0:T(8,128)(2,1)} %get-tuple-element.60), kind=kLoop, calls=%fused_computation.60 | loop fusion | bytes 1114112 | tf_op jit(solution)/shard_map/slice | solution.py:51
  61.7 1.1 pad_add_fusion
  63.7 5.5 %collective-permute-start.15 = (bf16[2048,256]{1,0:T(8,128)(2,1)}, bf16[2048,256]{1,0:T(8,128)(2,1)}, u32[]{:S(2)}, u32[]{:S(2)}) collective-permute-start(bf16[2048,256]{1,0:T(8,128)(2,1)} %get-tuple-element.70), channel_id=1, source_target_pairs={{0,62},{1,63},{2,0},{3,1},{4,2},{5,3},{6,4},{7,5},{8,6},{9,7},{10,... | collective-permute-start | bytes 3145736 | tf_op jit(solution)/shard_map/ppermute | solution.py:45
  69.2 2.6 %collective-permute-start.9 = (s16[544,256]{1,0:T(8,128)(2,1)S(1)}, s16[544,256]{1,0:T(8,128)(2,1)S(1)}, u32[]{:S(2)}, u32[]{:S(2)}) collective-permute-start(s16[544,256]{1,0:T(8,128)(2,1)S(1)} %get-tuple-element.88), channel_id=1, source_target_pairs={{0,128},{64,192},{128,0},{192,64},{1,129},{65,193},{129,1},{193,65... | collective-permute-start | bytes 835592 | tf_op jit(solution)/shard_map/ppermute | solution.py:31
  72.0 0.6 reshape.142.slot_ref
  72.6 8.2 %collective-permute-done.10.down_ref = s16[1632,256]{1,0:T(8,128)(2,1)S(1)} collective-permute-done((s16[1632,256]{1,0:T(8,128)(2,1)S(1)}, s16[1632,256]{1,0:T(8,128)(2,1)S(1)}, u32[]{:S(2)}, u32[]{:S(2)}) %collective-permute-start.10) | collective-permute-done | bytes 835616 | tf_op jit(solution)/shard_map/ppermute | solution.py:31
  80.8 1.6 %collective-permute-start.8 = (s16[1088,256]{1,0:T(8,128)(2,1)}, s16[1088,256]{1,0:T(8,128)(2,1)S(1)}, u32[]{:S(2)}, u32[]{:S(2)}) collective-permute-start(s16[1088,256]{1,0:T(8,128)(2,1)} %get-tuple-element.59), channel_id=1, source_target_pairs={{0,64},{64,128},{128,192},{192,0},{1,65},{65,129},{129,193},{193,1... | collective-permute-start | bytes 1671176 | tf_op jit(solution)/shard_map/ppermute | solution.py:31
  82.4 4.4 %collective-permute-done.9.first_ref = s16[544,256]{1,0:T(8,128)(2,1)S(1)} collective-permute-done((s16[544,256]{1,0:T(8,128)(2,1)S(1)}, s16[544,256]{1,0:T(8,128)(2,1)S(1)}, u32[]{:S(2)}, u32[]{:S(2)}) %collective-permute-start.9) | collective-permute-done | bytes 278560 | tf_op jit(solution)/shard_map/ppermute | solution.py:31
  86.8 9.5 %shard_map.40 = (f32[1056,128]{1,0:T(8,128)}, s16[1088,128]{1,0:T(8,128)(2,1)}, s16[1088,128]{1,0:T(8,128)(2,1)}, s16[1088,128]{1,0:T(8,128)(2,1)}) custom-call(s32[16]{0:T(128)} %reshape.142.slot_ref, s32[4]{0:T(128)} %and_select_fusion.dest_ref, s32[2]{0:T(128)} %copy-done.6, bf16[1024,2048]{1,0:T(8,128)(2,1)} %get-tuple-element.44.at_ref, ...), custom_call_target="tpu_custom_call" | custom-call | flops 4294967296 | bytes 10485760 | tf_op jit(solution)/shard_map/pallas_call | solution.py:294
  96.3 3.8 %collective-permute-start.12 = (s16[1088,128]{1,0:T(8,128)(2,1)}, s16[1088,128]{1,0:T(8,128)(2,1)S(1)}, u32[]{:S(2)}, u32[]{:S(2)}) collective-permute-start(s16[1088,128]{1,0:T(8,128)(2,1)} %get-tuple-element.62), channel_id=1, source_target_pairs={{0,64},{64,128},{128,192},{192,0},{1,65},{65,129},{129,193},{193,1... | collective-permute-start | bytes 835592 | tf_op jit(solution)/shard_map/ppermute | solution.py:31
  100.4 1.9 %collective-permute-start.19 = (s16[1088,128]{1,0:T(8,128)(2,1)}, s16[1088,128]{1,0:T(8,128)(2,1)}, u32[]{:S(2)}, u32[]{:S(2)}) collective-permute-start(s16[1088,128]{1,0:T(8,128)(2,1)} %get-tuple-element.77), channel_id=1, source_target_pairs={{0,128},{64,192},{128,0},{192,64},{1,129},{65,193},{129,1},{193,65... | collective-permute-start | bytes 835592 | tf_op jit(solution)/shard_map/ppermute | solution.py:31
  102.3 2.2 %collective-permute-done.12.refs_0_ = s16[1088,128]{1,0:T(8,128)(2,1)S(1)} collective-permute-done((s16[1088,128]{1,0:T(8,128)(2,1)}, s16[1088,128]{1,0:T(8,128)(2,1)S(1)}, u32[]{:S(2)}, u32[]{:S(2)}) %collective-permute-start.12) | collective-permute-done | bytes 278560 | tf_op jit(solution)/shard_map/ppermute | solution.py:31
  104.5 3.3 %collective-permute-start.20 = (s16[1088,128]{1,0:T(8,128)(2,1)}, s16[1088,128]{1,0:T(8,128)(2,1)}, u32[]{:S(2)}, u32[]{:S(2)}) collective-permute-start(s16[1088,128]{1,0:T(8,128)(2,1)} %get-tuple-element.78), channel_id=1, source_target_pairs={{0,192},{64,0},{128,64},{192,128},{1,193},{65,1},{129,65},{193,129... | collective-permute-start | bytes 835592 | tf_op jit(solution)/shard_map/ppermute | solution.py:31
  107.8 9.4 %shard_map.42 = (f32[1056,128]{1,0:T(8,128)}, s16[1088,128]{1,0:T(8,128)(2,1)}, s16[1088,128]{1,0:T(8,128)(2,1)}, s16[1088,128]{1,0:T(8,128)(2,1)}) custom-call(s32[16]{0:T(128)} %reshape.142.slot_ref, s32[4]{0:T(128)} %and_select_fusion.dest_ref, s32[2]{0:T(128)} %copy-done.6, bf16[1024,2048]{1,0:T(8,128)(2,1)} %get-tuple-element.44.at_ref, ...), custom_call_target="tpu_custom_call" | custom-call | flops 4294967296 | bytes 10485760 | tf_op jit(solution)/shard_map/pallas_call | solution.py:294
  117.3 4.1 %collective-permute-start.17 = (s16[1088,128]{1,0:T(8,128)(2,1)}, s16[1088,128]{1,0:T(8,128)(2,1)}, u32[]{:S(2)}, u32[]{:S(2)}) collective-permute-start(s16[1088,128]{1,0:T(8,128)(2,1)} %get-tuple-element.73), channel_id=1, source_target_pairs={{0,128},{64,192},{128,0},{192,64},{1,129},{65,193},{129,1},{193,65... | collective-permute-start | bytes 835592 | tf_op jit(solution)/shard_map/ppermute | solution.py:31
  121.4 0.6 reshape.143.taper_ref
  122.3 0.6 add.125.place_ref
  123.4 1.0 copy-done
  124.4 4.6 %shard_map.43.refs_3_ = f32[2048,256]{1,0:T(8,128)} custom-call(s32[32]{0:T(128)} %add.125.place_ref, s32[16]{0:T(128)} %reshape.142.slot_ref, s32[4]{0:T(128)} %and_select_fusion.dest_ref, f32[32]{0:T(128)} %reshape.143.taper_ref, f32[1056,256]{1,0:T(8,128)} %copy-done, f32[1056,128]{1,0:T(8,128)} %get-tuple-element.75.kept_ref, ...), custom_call_target="tpu_custom_call" | custom-call | flops 1048576 | bytes 4194304 | tf_op jit(solution)/shard_map/pallas_call | solution.py:359
  129.7 4.6 %shard_map.44 = f32[2048,256]{1,0:T(8,128)} custom-call(s32[32]{0:T(128)} %add.125.place_ref, s32[16]{0:T(128)} %reshape.142.slot_ref, s32[4]{0:T(128)} %and_select_fusion.dest_ref, f32[32]{0:T(128)} %reshape.143.taper_ref, f32[1056,256]{1,0:T(8,128)} %copy-done, f32[1056,128]{1,0:T(8,128)} %get-tuple-element.71.kept_ref, ...), custom_call_target="tpu_custom_call", output_to_operand_aliasing={{}: (9, {})} | custom-call | flops 1048576 | bytes 4194304 | tf_op jit(solution)/shard_map/pallas_call | solution.py:359
  (66 shorter events, 4.3 us)
Async XLA Ops:
  0.0 30.9 %collective-permute-start.4 = (bf16[2048,1024]{1,0:T(8,128)(2,1)}, bf16[2048,1024]{1,0:T(8,128)(2,1)}, u32[]{:S(2)}, u32[]{:S(2)}) collective-permute-start(bf16[2048,1024]{1,0:T(8,128)(2,1)} %source_ref.3), channel_id=1, source_target_pairs={{0,1},{1,0},{2,3},{3,2},{4,5},{5,4},{6,7},{7,6},{8,9},{9,8},{10,11... | collective-permute-start | bytes 12582920 | tf_op jit(solution)/shard_map/ppermute | solution.py:45
  1.4 19.3 %copy-start.6 = (s32[2]{0:T(128)}, s32[2]{0:T(128)S(1)}, u32[]{:S(2)}) copy-start(s32[2]{0:T(128)S(1)} %get-tuple-element.82.mate_ref) | copy-start | bytes 28
  1.4 13.0 %collective-permute-start = (s32[2]{0:T(128)S(1)}, s32[2]{0:T(128)S(1)}, u32[]{:S(2)}, u32[]{:S(2)}) collective-permute-start(s32[2]{0:T(128)S(1)} %get-tuple-element.79), channel_id=1, source_target_pairs={{0,62},{1,63},{2,0},{3,1},{4,2},{5,3},{6,4},{7,5},{8,6},{9,7},{10,... | collective-permute-start | bytes 32 | tf_op jit(solution)/shard_map/ppermute | solution.py:45
  9.6 6.9 %collective-permute-start.3 = (s32[2]{0:T(128)S(1)}, s32[2]{0:T(128)S(1)}, u32[]{:S(2)}, u32[]{:S(2)}) collective-permute-start(s32[2]{0:T(128)S(1)} %get-tuple-element.80), channel_id=1, source_target_pairs={{0,2},{1,3},{2,4},{3,5},{4,6},{5,7},{6,8},{7,9},{8,10},{9,11},{10,... | collective-permute-start | bytes 32 | tf_op jit(solution)/shard_map/ppermute | solution.py:45
  9.6 6.9 %collective-permute-start.2 = (s32[2]{0:T(128)S(1)}, s32[2]{0:T(128)S(1)}, u32[]{:S(2)}, u32[]{:S(2)}) collective-permute-start(s32[2]{0:T(128)S(1)} %get-tuple-element.81), channel_id=1, source_target_pairs={{0,63},{1,2},{2,1},{3,4},{4,3},{5,6},{6,5},{7,8},{8,7},{9,10},{10,... | collective-permute-start | bytes 32 | tf_op jit(solution)/shard_map/ppermute | solution.py:45
  14.5 2.0 %collective-permute-start.1 = (s32[2]{0:T(128)S(1)}, s32[2]{0:T(128)S(1)}, u32[]{:S(2)}, u32[]{:S(2)}) collective-permute-start(s32[2]{0:T(128)S(1)} %get-tuple-element.82.mate_ref), channel_id=1, source_target_pairs={{0,1},{1,0},{2,3},{3,2},{4,5},{5,4},{6,7},{7,6},{8,9},{9,8},{10,11... | collective-permute-start | bytes 32 | tf_op jit(solution)/shard_map/ppermute | solution.py:45
  20.7 29.7 %collective-permute-start.5 = (bf16[2048,256]{1,0:T(8,128)(2,1)}, bf16[2048,256]{1,0:T(8,128)(2,1)S(1)}, u32[]{:S(2)}, u32[]{:S(2)}) collective-permute-start(bf16[2048,256]{1,0:T(8,128)(2,1)} %get-tuple-element.48), channel_id=1, source_target_pairs={{0,2},{1,3},{2,4},{3,5},{4,6},{5,7},{6,8},{7,9},{8,10},{9,11},{10,... | collective-permute-start | bytes 3145736 | tf_op jit(solution)/shard_map/ppermute | solution.py:45
  20.8 39.4 %collective-permute-start.6 = (bf16[2048,256]{1,0:T(8,128)(2,1)}, bf16[2048,256]{1,0:T(8,128)(2,1)S(1)}, u32[]{:S(2)}, u32[]{:S(2)}) collective-permute-start(bf16[2048,256]{1,0:T(8,128)(2,1)} %get-tuple-element.49), channel_id=1, source_target_pairs={{0,63},{1,2},{2,1},{3,4},{4,3},{5,6},{6,5},{7,8},{8,7},{9,10},{10,... | collective-permute-start | bytes 3145736 | tf_op jit(solution)/shard_map/ppermute | solution.py:45
  25.1 35.1 %collective-permute-start.7 = (bf16[2048,256]{1,0:T(8,128)(2,1)}, bf16[2048,256]{1,0:T(8,128)(2,1)}, u32[]{:S(2)}, u32[]{:S(2)}) collective-permute-start(bf16[2048,256]{1,0:T(8,128)(2,1)} %get-tuple-element.50), channel_id=1, source_target_pairs={{0,62},{1,63},{2,0},{3,1},{4,2},{5,3},{6,4},{7,5},{8,6},{9,7},{10,... | collective-permute-start | bytes 3145736 | tf_op jit(solution)/shard_map/ppermute | solution.py:45
  47.7 15.8 %copy-start.4 = (s32[4,8]{1,0:T(4,128)S(1)}, s32[4,8]{1,0:T(4,128)}, u32[]{:S(2)}) copy-start(s32[4,8]{1,0:T(4,128)} %param.4) | copy-start | bytes 388
  50.4 11.2 %copy-start.7 = (bf16[2048,256]{1,0:T(8,128)(2,1)}, bf16[2048,256]{1,0:T(8,128)(2,1)S(1)}, u32[]{:S(2)}) copy-start(bf16[2048,256]{1,0:T(8,128)(2,1)S(1)} %collective-permute-done.5.refs_0_) | copy-start | bytes 3145732
  60.2 3.2 %copy-start.8 = (bf16[2048,256]{1,0:T(8,128)(2,1)}, bf16[2048,256]{1,0:T(8,128)(2,1)S(1)}, u32[]{:S(2)}) copy-start(bf16[2048,256]{1,0:T(8,128)(2,1)S(1)} %collective-permute-done.6.refs_2_) | copy-start | bytes 3145732
  62.8 18.0 %collective-permute-start.10 = (s16[1632,256]{1,0:T(8,128)(2,1)S(1)}, s16[1632,256]{1,0:T(8,128)(2,1)S(1)}, u32[]{:S(2)}, u32[]{:S(2)}) collective-permute-start(s16[1632,256]{1,0:T(8,128)(2,1)S(1)} %pad_add_fusion), channel_id=1, source_target_pairs={{0,192},{64,0},{128,64},{192,128},{1,193},{65,1},{129,65},{193,129... | collective-permute-start | bytes 2506760 | tf_op jit(solution)/shard_map/ppermute | solution.py:31
  63.5 44.3 %collective-permute-start.13 = (bf16[2048,256]{1,0:T(8,128)(2,1)}, bf16[2048,256]{1,0:T(8,128)(2,1)}, u32[]{:S(2)}, u32[]{:S(2)}) collective-permute-start(bf16[2048,256]{1,0:T(8,128)(2,1)} %get-tuple-element.42), channel_id=1, source_target_pairs={{0,2},{1,3},{2,4},{3,5},{4,6},{5,7},{6,8},{7,9},{8,10},{9,11},{10,... | collective-permute-start | bytes 3145736 | tf_op jit(solution)/shard_map/ppermute | solution.py:45
  63.6 44.2 %collective-permute-start.14 = (bf16[2048,256]{1,0:T(8,128)(2,1)}, bf16[2048,256]{1,0:T(8,128)(2,1)}, u32[]{:S(2)}, u32[]{:S(2)}) collective-permute-start(bf16[2048,256]{1,0:T(8,128)(2,1)} %get-tuple-element.69), channel_id=1, source_target_pairs={{0,63},{1,2},{2,1},{3,4},{4,3},{5,6},{6,5},{7,8},{8,7},{9,10},{10,... | collective-permute-start | bytes 3145736 | tf_op jit(solution)/shard_map/ppermute | solution.py:45
  63.7 44.1 %collective-permute-start.15 = (bf16[2048,256]{1,0:T(8,128)(2,1)}, bf16[2048,256]{1,0:T(8,128)(2,1)}, u32[]{:S(2)}, u32[]{:S(2)}) collective-permute-start(bf16[2048,256]{1,0:T(8,128)(2,1)} %get-tuple-element.70), channel_id=1, source_target_pairs={{0,62},{1,63},{2,0},{3,1},{4,2},{5,3},{6,4},{7,5},{8,6},{9,7},{10,... | collective-permute-start | bytes 3145736 | tf_op jit(solution)/shard_map/ppermute | solution.py:45
  69.2 17.5 %collective-permute-start.9 = (s16[544,256]{1,0:T(8,128)(2,1)S(1)}, s16[544,256]{1,0:T(8,128)(2,1)S(1)}, u32[]{:S(2)}, u32[]{:S(2)}) collective-permute-start(s16[544,256]{1,0:T(8,128)(2,1)S(1)} %get-tuple-element.88), channel_id=1, source_target_pairs={{0,128},{64,192},{128,0},{192,64},{1,129},{65,193},{129,1},{193,65... | collective-permute-start | bytes 835592 | tf_op jit(solution)/shard_map/ppermute | solution.py:31
  80.8 15.5 %collective-permute-start.8 = (s16[1088,256]{1,0:T(8,128)(2,1)}, s16[1088,256]{1,0:T(8,128)(2,1)S(1)}, u32[]{:S(2)}, u32[]{:S(2)}) collective-permute-start(s16[1088,256]{1,0:T(8,128)(2,1)} %get-tuple-element.59), channel_id=1, source_target_pairs={{0,64},{64,128},{128,192},{192,0},{1,65},{65,129},{129,193},{193,1... | collective-permute-start | bytes 1671176 | tf_op jit(solution)/shard_map/ppermute | solution.py:31
  86.8 9.5 %collective-permute-start.11 = (s16[544,256]{1,0:T(8,128)(2,1)S(1)}, s16[544,256]{1,0:T(8,128)(2,1)S(1)}, u32[]{:S(2)}, u32[]{:S(2)}) collective-permute-start(s16[544,256]{1,0:T(8,128)(2,1)S(1)} %slice.30), channel_id=1, source_target_pairs={{0,192},{64,0},{128,64},{192,128},{1,193},{65,1},{129,65},{193,129... | collective-permute-start | bytes 835592 | tf_op jit(solution)/shard_map/ppermute | solution.py:31
  86.8 13.4 %copy-start.5 = (s32[4,8]{1,0:T(4,128)S(1)}, s32[4,8]{1,0:T(4,128)}, u32[]{:S(2)}) copy-start(s32[4,8]{1,0:T(4,128)} %param.5) | copy-start | bytes 388
  96.3 8.2 %collective-permute-start.12 = (s16[1088,128]{1,0:T(8,128)(2,1)}, s16[1088,128]{1,0:T(8,128)(2,1)S(1)}, u32[]{:S(2)}, u32[]{:S(2)}) collective-permute-start(s16[1088,128]{1,0:T(8,128)(2,1)} %get-tuple-element.62), channel_id=1, source_target_pairs={{0,64},{64,128},{128,192},{192,0},{1,65},{65,129},{129,193},{193,1... | collective-permute-start | bytes 835592 | tf_op jit(solution)/shard_map/ppermute | solution.py:31
  100.4 22.6 %copy-start.1 = (f32[1056,256]{1,0:T(8,128)S(1)}, f32[1056,256]{1,0:T(8,128)}, u32[]{:S(2)}) copy-start(f32[1056,256]{1,0:T(8,128)} %get-tuple-element.64.kept_ref) | copy-start | bytes 3244036
  100.4 24.0 %collective-permute-start.19 = (s16[1088,128]{1,0:T(8,128)(2,1)}, s16[1088,128]{1,0:T(8,128)(2,1)}, u32[]{:S(2)}, u32[]{:S(2)}) collective-permute-start(s16[1088,128]{1,0:T(8,128)(2,1)} %get-tuple-element.77), channel_id=1, source_target_pairs={{0,128},{64,192},{128,0},{192,64},{1,129},{65,193},{129,1},{193,65... | collective-permute-start | bytes 835592 | tf_op jit(solution)/shard_map/ppermute | solution.py:31
  104.5 12.8 %copy-start.2 = (s16[1088,128]{1,0:T(8,128)(2,1)}, s16[1088,128]{1,0:T(8,128)(2,1)S(1)}, u32[]{:S(2)}) copy-start(s16[1088,128]{1,0:T(8,128)(2,1)S(1)} %collective-permute-done.12.refs_0_) | copy-start | bytes 835588
  104.5 19.9 %collective-permute-start.20 = (s16[1088,128]{1,0:T(8,128)(2,1)}, s16[1088,128]{1,0:T(8,128)(2,1)}, u32[]{:S(2)}, u32[]{:S(2)}) collective-permute-start(s16[1088,128]{1,0:T(8,128)(2,1)} %get-tuple-element.78), channel_id=1, source_target_pairs={{0,192},{64,0},{128,64},{192,128},{1,193},{65,1},{129,65},{193,129... | collective-permute-start | bytes 835592 | tf_op jit(solution)/shard_map/ppermute | solution.py:31
  117.3 11.7 %collective-permute-start.16 = (s16[1088,128]{1,0:T(8,128)(2,1)}, s16[1088,128]{1,0:T(8,128)(2,1)S(1)}, u32[]{:S(2)}, u32[]{:S(2)}) collective-permute-start(s16[1088,128]{1,0:T(8,128)(2,1)} %get-tuple-element.72), channel_id=1, source_target_pairs={{0,64},{64,128},{128,192},{192,0},{1,65},{65,129},{129,193},{193,1... | collective-permute-start | bytes 835592 | tf_op jit(solution)/shard_map/ppermute | solution.py:31
  117.3 11.6 %collective-permute-start.17 = (s16[1088,128]{1,0:T(8,128)(2,1)}, s16[1088,128]{1,0:T(8,128)(2,1)}, u32[]{:S(2)}, u32[]{:S(2)}) collective-permute-start(s16[1088,128]{1,0:T(8,128)(2,1)} %get-tuple-element.73), channel_id=1, source_target_pairs={{0,128},{64,192},{128,0},{192,64},{1,129},{65,193},{129,1},{193,65... | collective-permute-start | bytes 835592 | tf_op jit(solution)/shard_map/ppermute | solution.py:31
  121.4 7.8 %collective-permute-start.18 = (s16[1088,128]{1,0:T(8,128)(2,1)}, s16[1088,128]{1,0:T(8,128)(2,1)}, u32[]{:S(2)}, u32[]{:S(2)}) collective-permute-start(s16[1088,128]{1,0:T(8,128)(2,1)} %get-tuple-element.74), channel_id=1, source_target_pairs={{0,192},{64,0},{128,64},{192,128},{1,193},{65,1},{129,65},{193,129... | collective-permute-start | bytes 835592 | tf_op jit(solution)/shard_map/ppermute | solution.py:31
  123.4 1.0 copy-start
  129.0 0.7 copy-start.3

commit v9 on v8

--- a/solution.py
+++ b/solution.py
@@ -46,12 +46,11 @@
 
 
 def spread(parts):
-    one, two, three = parts
-    count, half = three.shape[0], two.shape[0] // 2
-    down = passed_along(jnp.concatenate([three, two[half:]]), "samp", -1)
-    up = passed_along(one, "samp", 1)
-    first = passed_along(two[:half], "samp", 2)
-    second = passed_along(down[count:], "samp", -1)
+    up, first, down = parts
+    down = passed_along(down, "samp", -1)
+    up = passed_along(up, "samp", 1)
+    first = passed_along(first, "samp", 2)
+    second = passed_along(down[up.shape[0] :], "samp", -1)
     return [up, first, second, down]
 
 
@@ -108,7 +107,7 @@
 def select(stage, want, perturb):
     samples = perturb.shape[0]
     widths = [2 * HALF] * 3
-    plan = [(q, side, stage, out, side) for out, q in enumerate((0, 2, 3)) for side in range(2)]
+    plan = [(out, side, stage, out, side) for out in range(3) for side in range(2)]
     return pl.pallas_call(
         functools.partial(select_kernel, plan),
         grid_spec=pltpu.PrefetchScalarGridSpec(
@@ -136,23 +135,42 @@
     return block.astype(jnp.int32).astype(jnp.int16)
 
 
-def own_kernel(dest_ref, x_ref, row_ref, at_ref, *refs):
-    parts, tile_ref, norm_ref = refs[:-2], refs[-2], refs[-1]
-    samp = len(parts)
-    rows = BS // samp
+def own_kernel(dest_ref, x_ref, row_ref, at_ref, kept_ref, up_ref, first_ref, down_ref, tile_ref, norm_ref):
+    rows = BS // 4
+    coded = BS + CODE_EXTRA
     r = pl.program_id(0)
+    half = B_DEV // 2
     at_ref[...] = jnp.transpose(row_ref[...])
     at = at_ref[...]
-    codes = [[] for _ in range(samp - 1)]
+
+    def store(d, start, value):
+        size = value.shape[0]
+        base = pl.multiple_of(r * coded, 16) + start
+        if d == 1:
+            up_ref[pl.ds(base, size), :] = value
+        elif d == 3:
+            down_ref[pl.ds(base, size), :] = value
+        else:
+
+            @pl.when(r < half)
+            def _():
+                first_ref[pl.ds(base, size), :] = value
+
+            @pl.when(r >= half)
+            def _():
+                down_ref[pl.ds(base + half * coded, size), :] = value
+
+    codes = [[] for _ in range(3)]
     for c in range(B_DEV):
         tile_ref[...] = jnp.dot(at, x_ref[:, c * BS : (c + 1) * BS], preferred_element_type=jnp.float32)
-        for d in range(samp):
+        for d in range(4):
             piece = tile_ref[pl.ds(pl.multiple_of(dest_ref[d] * rows, rows), rows), :]
-            if d > 0:
-                piece, code = encode(piece)
-                piece = piece.astype(jnp.int32).astype(jnp.int16)
-                codes[d - 1].append(code)
-            parts[d][c * rows : (c + 1) * rows, :] = piece
+            if d == 0:
+                kept_ref[c * rows : (c + 1) * rows, :] = piece
+                continue
+            piece, code = encode(piece)
+            codes[d - 1].append(code)
+            store(d, c * rows, piece.astype(jnp.int32).astype(jnp.int16))
 
         @pl.when(r == c)
         def _():
@@ -160,16 +178,16 @@
             norm = jnp.sum(jnp.where(here, tile_ref[...], 0.0), axis=0, keepdims=True)
             norm_ref[...] = jnp.broadcast_to(norm, norm_ref.shape)
 
-    parts[0][BS : BS + EXTRA, :] = norm_ref[...]
+    kept_ref[BS : BS + EXTRA, :] = norm_ref[...]
     norm_codes = encode_norm(norm_ref[0:1, :])
-    for d in range(1, samp):
-        parts[d][BS : BS + CODE_EXTRA, :] = with_rows(CODE_EXTRA, BS, codes[d - 1] + norm_codes)
+    for d in range(1, 4):
+        store(d, BS, with_rows(CODE_EXTRA, BS, codes[d - 1] + norm_codes))
 
 
 def own_tiles(dest, perturb):
     samples, cells = perturb.shape
-    samp = dest.shape[0]
-    blocks_out = [(BS + EXTRA, jnp.float32)] + [(BS + CODE_EXTRA, jnp.int16)] * (samp - 1)
+    coded = BS + CODE_EXTRA
+    counts = [B_DEV * coded, B_DEV // 2 * coded, (B_DEV + B_DEV // 2) * coded]
     return pl.pallas_call(
         own_kernel,
         grid_spec=pltpu.PrefetchScalarGridSpec(
@@ -179,12 +197,18 @@
                 pl.BlockSpec((samples, cells), lambda r, *s: (0, 0)),
                 pl.BlockSpec((samples, BS), lambda r, *s: (0, r)),
             ],
-            out_specs=[pl.BlockSpec((BS, samples), lambda r, *s: (r, 0))]
-            + [pl.BlockSpec((block, BS), lambda r, *s: (r, 0)) for block, _ in blocks_out],
+            out_specs=[
+                pl.BlockSpec((BS, samples), lambda r, *s: (r, 0)),
+                pl.BlockSpec((BS + EXTRA, BS), lambda r, *s: (r, 0)),
+            ]
+            + [pl.BlockSpec((count, BS), lambda r, *s: (0, 0)) for count in counts],
             scratch_shapes=[pltpu.VMEM((BS, BS), jnp.float32), pltpu.VMEM((EXTRA, BS), jnp.float32)],
         ),
-        out_shape=[jax.ShapeDtypeStruct((cells, samples), perturb.dtype)]
-        + [jax.ShapeDtypeStruct((B_DEV * block, BS), dtype) for block, dtype in blocks_out],
+        out_shape=[
+            jax.ShapeDtypeStruct((cells, samples), perturb.dtype),
+            jax.ShapeDtypeStruct((B_DEV * (BS + EXTRA), BS), jnp.float32),
+        ]
+        + [jax.ShapeDtypeStruct((count, BS), jnp.int16) for count in counts],
         compiler_params=pltpu.CompilerParams(vmem_limit_bytes=BIG),
         cost_estimate=pl.CostEstimate(flops=2 * cells * cells * samples, bytes_accessed=12 * MIB, transcendentals=0),
     )(dest, perturb, perturb)
@@ -391,7 +415,7 @@
     high = jnp.max(jnp.where(need, four[None], 0), axis=1)
     want = jnp.stack([low, high], axis=1)
     mates = exchanged(perturb, 1)
-    asked = jnp.concatenate([exchanged(want[q], q, back=True) for q in range(4)])
+    asked = jnp.concatenate([exchanged(want[q], q, back=True) for q in (0, 2, 3)])
 
     k_ids = jnp.arange(K_PART, dtype=jnp.int32)[None, :, None]
     is_high = jnp.sum(jnp.where(kind[:, :, None] == four, high[None, None], 0), axis=2) == inside

time: 135 us -> 134 us (level); the launches traced: 134 us -> 132 us
  waiting for transfers between devices: 29.6 us -> 27.8 us
    slice x2 -> x1, local copies, waits for them, and re-layouts: 1.46 us -> 0.02 us  [spread(): second = passed_along(down[up.shape[0]:], 'samp', -1)]
    ppermute x11 -> x10, waiting for transfers between devices: 14.5 us -> 13.4 us  [exchanged(): return lax.ppermute(value, 'blk', sorted(pairs))]
    ppermute x11 -> x10, starting transfers between devices: 24.8 us -> 25.1 us  [exchanged(): return lax.ppermute(value, 'blk', sorted(pairs))]
  transfers between devices with their start and end apart: 21 -> 20, of which waited for: 7 -> 7; matrix products, arithmetic and copies ran while one was open for 4% -> 5% of each run, Pallas kernels for 36% -> 37%
where the time goes in v9:
time: 134 us; the launch traced here: 132 us
  Pallas kernels  53.7 us (40%)
  starting transfers between devices  42.5 us (32%)
  waiting for transfers between devices  27.8 us (21%)
  local copies, waits for them, and re-layouts  4.51 us (3%)
  other arithmetic  3.07 us (2%)
    ppermute x10, starting transfers between devices, exchanged(): return lax.ppermute(value, 'blk', sorted(pairs))  25.1 us
    pallas_call x2, Pallas kernels, remote_tiles(): pl.pallas_call(functools.partial(remote_kernel, stage), grid_spec=pltpu.P...  18.9 us
    pallas_call x1, Pallas kernels, own_tiles(): pl.pallas_call(own_kernel, grid_spec=pltpu.PrefetchScalarGridSpec(num_sca...  17.9 us
    ppermute x10, starting transfers between devices, passed_along(): return lax.ppermute(value, axis, pairs)  17.4 us
    ppermute x10, waiting for transfers between devices, passed_along(): return lax.ppermute(value, axis, pairs)  14.4 us
    ppermute x10, waiting for transfers between devices, exchanged(): return lax.ppermute(value, 'blk', sorted(pairs))  13.4 us
    pallas_call x2, Pallas kernels, final(): pl.pallas_call(functools.partial(final_kernel, half), grid_spec=pltpu.Pre...  9.12 us
    pallas_call x2, Pallas kernels, select(): pl.pallas_call(functools.partial(select_kernel, plan), grid_spec=pltpu.Pr...  7.24 us
  transfers between devices with their start and end apart: 20, of which 7 were waited for; matrix products, arithmetic and copies ran while one was open for 5% of the time, Pallas kernels for 37%

profile of v9, /device:TPU:8, one launch (start us, length us, event | category | flops | bytes accessed | tf_op | source)
XLA Modules:
  0.0 131.7 jit_solution(7057471955986739761)
XLA Ops:
  0.0 0.7 add_select_fusion
  1.2 0.8 slice_reduce_fusion.2
  2.0 8.1 %collective-permute-start = (s32[2]{0:T(128)S(1)}, s32[2]{0:T(128)S(1)}, u32[]{:S(2)}, u32[]{:S(2)}) collective-permute-start(s32[2]{0:T(128)S(1)} %get-tuple-element.79), channel_id=1, source_target_pairs={{0,62},{1,63},{2,0},{3,1},{4,2},{5,3},{6,4},{7,5},{8,6},{9,7},{10,... | collective-permute-start | bytes 32 | tf_op jit(solution)/shard_map/ppermute | solution.py:45
  10.1 4.9 %collective-permute-start.1 = (s32[2]{0:T(128)S(1)}, s32[2]{0:T(128)S(1)}, u32[]{:S(2)}, u32[]{:S(2)}) collective-permute-start(s32[2]{0:T(128)S(1)} %get-tuple-element.81), channel_id=1, source_target_pairs={{0,63},{1,2},{2,1},{3,4},{4,3},{5,6},{6,5},{7,8},{8,7},{9,10},{10,... | collective-permute-start | bytes 32 | tf_op jit(solution)/shard_map/ppermute | solution.py:45
  15.0 2.0 %collective-permute-done.2 = s32[2]{0:T(128)S(1)} collective-permute-done((s32[2]{0:T(128)S(1)}, s32[2]{0:T(128)S(1)}, u32[]{:S(2)}, u32[]{:S(2)}) %collective-permute-start.2) | collective-permute-done | bytes 40 | tf_op jit(solution)/shard_map/ppermute | solution.py:45
  16.9 0.6 pad_add_fusion.2.want_ref
  17.5 3.6 %shard_map.39 = (bf16[2048,256]{1,0:T(8,128)(2,1)}, bf16[2048,256]{1,0:T(8,128)(2,1)}, bf16[2048,256]{1,0:T(8,128)(2,1)}) custom-call(s32[6]{0:T(128)} %pad_add_fusion.2.want_ref, bf16[2048,1024]{1,0:T(8,128)(2,1)} %source_ref.3), custom_call_target="tpu_custom_call" | custom-call | bytes 6291456 | tf_op jit(solution)/shard_map/pallas_call | solution.py:111
  21.2 4.4 %collective-permute-start.5 = (bf16[2048,256]{1,0:T(8,128)(2,1)}, bf16[2048,256]{1,0:T(8,128)(2,1)}, u32[]{:S(2)}, u32[]{:S(2)}) collective-permute-start(bf16[2048,256]{1,0:T(8,128)(2,1)} %get-tuple-element.49), channel_id=1, source_target_pairs={{0,63},{1,2},{2,1},{3,4},{4,3},{5,6},{6,5},{7,8},{8,7},{9,10},{10,... | collective-permute-start | bytes 3145736 | tf_op jit(solution)/shard_map/ppermute | solution.py:45
  25.6 1.6 %collective-permute-start.6 = (bf16[2048,256]{1,0:T(8,128)(2,1)}, bf16[2048,256]{1,0:T(8,128)(2,1)}, u32[]{:S(2)}, u32[]{:S(2)}) collective-permute-start(bf16[2048,256]{1,0:T(8,128)(2,1)} %get-tuple-element.50), channel_id=1, source_target_pairs={{0,62},{1,63},{2,0},{3,1},{4,2},{5,3},{6,4},{7,5},{8,6},{9,7},{10,... | collective-permute-start | bytes 3145736 | tf_op jit(solution)/shard_map/ppermute | solution.py:45
  27.8 3.6 %shard_map.37 = (bf16[2048,256]{1,0:T(8,128)(2,1)}, bf16[2048,256]{1,0:T(8,128)(2,1)}, bf16[2048,256]{1,0:T(8,128)(2,1)}) custom-call(s32[6]{0:T(128)} %pad_add_fusion.2.want_ref, bf16[2048,1024]{1,0:T(8,128)(2,1)} %source_ref.3), custom_call_target="tpu_custom_call" | custom-call | bytes 6291456 | tf_op jit(solution)/shard_map/pallas_call | solution.py:111
  31.5 17.9 %shard_map.38 = (bf16[1024,2048]{1,0:T(8,128)(2,1)}, f32[1056,256]{1,0:T(8,128)}, s16[1088,256]{1,0:T(8,128)(2,1)}, s16[544,256]{1,0:T(8,128)(2,1)}, s16[1632,256]{1,0:T(8,128)(2,1)}) custom-call(s32[4]{0:T(128)} %and_select_fusion.dest_ref, bf16[2048,1024]{1,0:T(8,128)(2,1)} %source_ref.3, bf16[2048,1024]{1,0:T(8,128)(2,1)} %source_ref.3), custom_call_target="tpu_custom_call" | custom-call | flops 4294967296 | bytes 12582912 | tf_op jit(solution)/shard_map/pallas_call | solution.py:191
  49.4 1.4 %collective-permute-done.4.refs_0_ = bf16[2048,256]{1,0:T(8,128)(2,1)S(1)} collective-permute-done((bf16[2048,256]{1,0:T(8,128)(2,1)}, bf16[2048,256]{1,0:T(8,128)(2,1)S(1)}, u32[]{:S(2)}, u32[]{:S(2)}) %collective-permute-start.4) | collective-permute-done | bytes 1048608 | tf_op jit(solution)/shard_map/ppermute | solution.py:45
  50.8 10.0 %collective-permute-done.5.refs_2_ = bf16[2048,256]{1,0:T(8,128)(2,1)} collective-permute-done((bf16[2048,256]{1,0:T(8,128)(2,1)}, bf16[2048,256]{1,0:T(8,128)(2,1)}, u32[]{:S(2)}, u32[]{:S(2)}) %collective-permute-start.5) | collective-permute-done | bytes 1048608 | tf_op jit(solution)/shard_map/ppermute | solution.py:45
  61.7 5.8 %collective-permute-start.14 = (bf16[2048,256]{1,0:T(8,128)(2,1)}, bf16[2048,256]{1,0:T(8,128)(2,1)}, u32[]{:S(2)}, u32[]{:S(2)}) collective-permute-start(bf16[2048,256]{1,0:T(8,128)(2,1)} %get-tuple-element.70), channel_id=1, source_target_pairs={{0,62},{1,63},{2,0},{3,1},{4,2},{5,3},{6,4},{7,5},{8,6},{9,7},{10,... | collective-permute-start | bytes 3145736 | tf_op jit(solution)/shard_map/ppermute | solution.py:45
  67.5 2.6 %collective-permute-start.8 = (s16[544,256]{1,0:T(8,128)(2,1)}, s16[544,256]{1,0:T(8,128)(2,1)S(1)}, u32[]{:S(2)}, u32[]{:S(2)}) collective-permute-start(s16[544,256]{1,0:T(8,128)(2,1)} %get-tuple-element.60), channel_id=1, source_target_pairs={{0,128},{64,192},{128,0},{192,64},{1,129},{65,193},{129,1},{193,65... | collective-permute-start | bytes 835592 | tf_op jit(solution)/shard_map/ppermute | solution.py:31
  70.2 0.6 reshape.142.slot_ref
  70.8 7.8 %collective-permute-done.9.down_ref = s16[1632,256]{1,0:T(8,128)(2,1)S(1)} collective-permute-done((s16[1632,256]{1,0:T(8,128)(2,1)}, s16[1632,256]{1,0:T(8,128)(2,1)S(1)}, u32[]{:S(2)}, u32[]{:S(2)}) %collective-permute-start.9) | collective-permute-done | bytes 835616 | tf_op jit(solution)/shard_map/ppermute | solution.py:31
  78.6 1.6 %collective-permute-start.7 = (s16[1088,256]{1,0:T(8,128)(2,1)}, s16[1088,256]{1,0:T(8,128)(2,1)S(1)}, u32[]{:S(2)}, u32[]{:S(2)}) collective-permute-start(s16[1088,256]{1,0:T(8,128)(2,1)} %get-tuple-element.59), channel_id=1, source_target_pairs={{0,64},{64,128},{128,192},{192,0},{1,65},{65,129},{129,193},{193,1... | collective-permute-start | bytes 1671176 | tf_op jit(solution)/shard_map/ppermute | solution.py:31
  80.3 4.1 %collective-permute-done.8.first_ref = s16[544,256]{1,0:T(8,128)(2,1)S(1)} collective-permute-done((s16[544,256]{1,0:T(8,128)(2,1)}, s16[544,256]{1,0:T(8,128)(2,1)S(1)}, u32[]{:S(2)}, u32[]{:S(2)}) %collective-permute-start.8) | collective-permute-done | bytes 278560 | tf_op jit(solution)/shard_map/ppermute | solution.py:31
  84.4 9.5 %shard_map.40 = (f32[1056,128]{1,0:T(8,128)}, s16[1088,128]{1,0:T(8,128)(2,1)}, s16[1088,128]{1,0:T(8,128)(2,1)}, s16[1088,128]{1,0:T(8,128)(2,1)}) custom-call(s32[16]{0:T(128)} %reshape.142.slot_ref, s32[4]{0:T(128)} %and_select_fusion.dest_ref, s32[2]{0:T(128)} %get-tuple-element.82.mate_ref, bf16[1024,2048]{1,0:T(8,128)(2,1)} %get-tuple-element.44.at_ref, ...), custom_call_target="tpu_custom_call" | custom-call | flops 4294967296 | bytes 10485760 | tf_op jit(solution)/shard_map/pallas_call | solution.py:318
  93.9 3.5 %collective-permute-start.11 = (s16[1088,128]{1,0:T(8,128)(2,1)}, s16[1088,128]{1,0:T(8,128)(2,1)S(1)}, u32[]{:S(2)}, u32[]{:S(2)}) collective-permute-start(s16[1088,128]{1,0:T(8,128)(2,1)} %get-tuple-element.62), channel_id=1, source_target_pairs={{0,64},{64,128},{128,192},{192,0},{1,65},{65,129},{129,193},{193,1... | collective-permute-start | bytes 835592 | tf_op jit(solution)/shard_map/ppermute | solution.py:31
  97.7 2.0 %collective-permute-start.18 = (s16[1088,128]{1,0:T(8,128)(2,1)}, s16[1088,128]{1,0:T(8,128)(2,1)}, u32[]{:S(2)}, u32[]{:S(2)}) collective-permute-start(s16[1088,128]{1,0:T(8,128)(2,1)} %get-tuple-element.77), channel_id=1, source_target_pairs={{0,128},{64,192},{128,0},{192,64},{1,129},{65,193},{129,1},{193,65... | collective-permute-start | bytes 835592 | tf_op jit(solution)/shard_map/ppermute | solution.py:31
  99.7 2.3 %collective-permute-done.11.refs_0_ = s16[1088,128]{1,0:T(8,128)(2,1)S(1)} collective-permute-done((s16[1088,128]{1,0:T(8,128)(2,1)}, s16[1088,128]{1,0:T(8,128)(2,1)S(1)}, u32[]{:S(2)}, u32[]{:S(2)}) %collective-permute-start.11) | collective-permute-done | bytes 278560 | tf_op jit(solution)/shard_map/ppermute | solution.py:31
  102.0 3.4 %collective-permute-start.19 = (s16[1088,128]{1,0:T(8,128)(2,1)}, s16[1088,128]{1,0:T(8,128)(2,1)}, u32[]{:S(2)}, u32[]{:S(2)}) collective-permute-start(s16[1088,128]{1,0:T(8,128)(2,1)} %get-tuple-element.78), channel_id=1, source_target_pairs={{0,192},{64,0},{128,64},{192,128},{1,193},{65,1},{129,65},{193,129... | collective-permute-start | bytes 835592 | tf_op jit(solution)/shard_map/ppermute | solution.py:31
  105.4 9.4 %shard_map.42 = (f32[1056,128]{1,0:T(8,128)}, s16[1088,128]{1,0:T(8,128)(2,1)}, s16[1088,128]{1,0:T(8,128)(2,1)}, s16[1088,128]{1,0:T(8,128)(2,1)}) custom-call(s32[16]{0:T(128)} %reshape.142.slot_ref, s32[4]{0:T(128)} %and_select_fusion.dest_ref, s32[2]{0:T(128)} %get-tuple-element.82.mate_ref, bf16[1024,2048]{1,0:T(8,128)(2,1)} %get-tuple-element.44.at_ref, ...), custom_call_target="tpu_custom_call" | custom-call | flops 4294967296 | bytes 10485760 | tf_op jit(solution)/shard_map/pallas_call | solution.py:318
  114.9 3.8 %collective-permute-start.16 = (s16[1088,128]{1,0:T(8,128)(2,1)}, s16[1088,128]{1,0:T(8,128)(2,1)}, u32[]{:S(2)}, u32[]{:S(2)}) collective-permute-start(s16[1088,128]{1,0:T(8,128)(2,1)} %get-tuple-element.73), channel_id=1, source_target_pairs={{0,128},{64,192},{128,0},{192,64},{1,129},{65,193},{129,1},{193,65... | collective-permute-start | bytes 835592 | tf_op jit(solution)/shard_map/ppermute | solution.py:31
  118.7 0.7 reshape.143.taper_ref
  119.7 0.7 add.125.place_ref
  120.8 1.0 copy-done
  121.8 4.6 %shard_map.43.refs_3_ = f32[2048,256]{1,0:T(8,128)} custom-call(s32[32]{0:T(128)} %add.125.place_ref, s32[16]{0:T(128)} %reshape.142.slot_ref, s32[4]{0:T(128)} %and_select_fusion.dest_ref, f32[32]{0:T(128)} %reshape.143.taper_ref, f32[1056,256]{1,0:T(8,128)} %copy-done, f32[1056,128]{1,0:T(8,128)} %get-tuple-element.75.kept_ref, ...), custom_call_target="tpu_custom_call" | custom-call | flops 1048576 | bytes 4194304 | tf_op jit(solution)/shard_map/pallas_call | solution.py:383
  126.5 0.6 copy-done.3
  127.1 4.6 %shard_map.44 = f32[2048,256]{1,0:T(8,128)} custom-call(s32[32]{0:T(128)} %add.125.place_ref, s32[16]{0:T(128)} %reshape.142.slot_ref, s32[4]{0:T(128)} %and_select_fusion.dest_ref, f32[32]{0:T(128)} %reshape.143.taper_ref, f32[1056,256]{1,0:T(8,128)} %copy-done, f32[1056,128]{1,0:T(8,128)} %get-tuple-element.71.kept_ref, ...), custom_call_target="tpu_custom_call", output_to_operand_aliasing={{}: (9, {})} | custom-call | flops 1048576 | bytes 4194304 | tf_op jit(solution)/shard_map/pallas_call | solution.py:383
  (58 shorter events, 3.4 us)
Async XLA Ops:
  0.0 31.4 %collective-permute-start.3 = (bf16[2048,1024]{1,0:T(8,128)(2,1)}, bf16[2048,1024]{1,0:T(8,128)(2,1)}, u32[]{:S(2)}, u32[]{:S(2)}) collective-permute-start(bf16[2048,1024]{1,0:T(8,128)(2,1)} %source_ref.3), channel_id=1, source_target_pairs={{0,1},{1,0},{2,3},{3,2},{4,5},{5,4},{6,7},{7,6},{8,9},{9,8},{10,11... | collective-permute-start | bytes 12582920 | tf_op jit(solution)/shard_map/ppermute | solution.py:45
  2.0 13.0 %collective-permute-start = (s32[2]{0:T(128)S(1)}, s32[2]{0:T(128)S(1)}, u32[]{:S(2)}, u32[]{:S(2)}) collective-permute-start(s32[2]{0:T(128)S(1)} %get-tuple-element.79), channel_id=1, source_target_pairs={{0,62},{1,63},{2,0},{3,1},{4,2},{5,3},{6,4},{7,5},{8,6},{9,7},{10,... | collective-permute-start | bytes 32 | tf_op jit(solution)/shard_map/ppermute | solution.py:45
  10.1 6.9 %collective-permute-start.2 = (s32[2]{0:T(128)S(1)}, s32[2]{0:T(128)S(1)}, u32[]{:S(2)}, u32[]{:S(2)}) collective-permute-start(s32[2]{0:T(128)S(1)} %get-tuple-element.80), channel_id=1, source_target_pairs={{0,2},{1,3},{2,4},{3,5},{4,6},{5,7},{6,8},{7,9},{8,10},{9,11},{10,... | collective-permute-start | bytes 32 | tf_op jit(solution)/shard_map/ppermute | solution.py:45
  10.1 6.9 %collective-permute-start.1 = (s32[2]{0:T(128)S(1)}, s32[2]{0:T(128)S(1)}, u32[]{:S(2)}, u32[]{:S(2)}) collective-permute-start(s32[2]{0:T(128)S(1)} %get-tuple-element.81), channel_id=1, source_target_pairs={{0,63},{1,2},{2,1},{3,4},{4,3},{5,6},{6,5},{7,8},{8,7},{9,10},{10,... | collective-permute-start | bytes 32 | tf_op jit(solution)/shard_map/ppermute | solution.py:45
  21.1 29.7 %collective-permute-start.4 = (bf16[2048,256]{1,0:T(8,128)(2,1)}, bf16[2048,256]{1,0:T(8,128)(2,1)S(1)}, u32[]{:S(2)}, u32[]{:S(2)}) collective-permute-start(bf16[2048,256]{1,0:T(8,128)(2,1)} %get-tuple-element.48), channel_id=1, source_target_pairs={{0,2},{1,3},{2,4},{3,5},{4,6},{5,7},{6,8},{7,9},{8,10},{9,11},{10,... | collective-permute-start | bytes 3145736 | tf_op jit(solution)/shard_map/ppermute | solution.py:45
  21.2 39.6 %collective-permute-start.5 = (bf16[2048,256]{1,0:T(8,128)(2,1)}, bf16[2048,256]{1,0:T(8,128)(2,1)}, u32[]{:S(2)}, u32[]{:S(2)}) collective-permute-start(bf16[2048,256]{1,0:T(8,128)(2,1)} %get-tuple-element.49), channel_id=1, source_target_pairs={{0,63},{1,2},{2,1},{3,4},{4,3},{5,6},{6,5},{7,8},{8,7},{9,10},{10,... | collective-permute-start | bytes 3145736 | tf_op jit(solution)/shard_map/ppermute | solution.py:45
  25.6 35.2 %collective-permute-start.6 = (bf16[2048,256]{1,0:T(8,128)(2,1)}, bf16[2048,256]{1,0:T(8,128)(2,1)}, u32[]{:S(2)}, u32[]{:S(2)}) collective-permute-start(bf16[2048,256]{1,0:T(8,128)(2,1)} %get-tuple-element.50), channel_id=1, source_target_pairs={{0,62},{1,63},{2,0},{3,1},{4,2},{5,3},{6,4},{7,5},{8,6},{9,7},{10,... | collective-permute-start | bytes 3145736 | tf_op jit(solution)/shard_map/ppermute | solution.py:45
  31.4 30.0 %copy-start.4 = (s32[4,8]{1,0:T(4,128)S(1)}, s32[4,8]{1,0:T(4,128)}, u32[]{:S(2)}) copy-start(s32[4,8]{1,0:T(4,128)} %param.4) | copy-start | bytes 388
  50.8 29.4 %copy-start.6 = (bf16[2048,256]{1,0:T(8,128)(2,1)}, bf16[2048,256]{1,0:T(8,128)(2,1)S(1)}, u32[]{:S(2)}) copy-start(bf16[2048,256]{1,0:T(8,128)(2,1)S(1)} %collective-permute-done.4.refs_0_) | copy-start | bytes 3145732
  60.8 17.8 %collective-permute-start.9 = (s16[1632,256]{1,0:T(8,128)(2,1)}, s16[1632,256]{1,0:T(8,128)(2,1)S(1)}, u32[]{:S(2)}, u32[]{:S(2)}) collective-permute-start(s16[1632,256]{1,0:T(8,128)(2,1)} %get-tuple-element.61), channel_id=1, source_target_pairs={{0,192},{64,0},{128,64},{192,128},{1,193},{65,1},{129,65},{193,129... | collective-permute-start | bytes 2506760 | tf_op jit(solution)/shard_map/ppermute | solution.py:31
  61.5 44.0 %collective-permute-start.12 = (bf16[2048,256]{1,0:T(8,128)(2,1)}, bf16[2048,256]{1,0:T(8,128)(2,1)}, u32[]{:S(2)}, u32[]{:S(2)}) collective-permute-start(bf16[2048,256]{1,0:T(8,128)(2,1)} %get-tuple-element.42), channel_id=1, source_target_pairs={{0,2},{1,3},{2,4},{3,5},{4,6},{5,7},{6,8},{7,9},{8,10},{9,11},{10,... | collective-permute-start | bytes 3145736 | tf_op jit(solution)/shard_map/ppermute | solution.py:45
  61.5 43.9 %collective-permute-start.13 = (bf16[2048,256]{1,0:T(8,128)(2,1)}, bf16[2048,256]{1,0:T(8,128)(2,1)}, u32[]{:S(2)}, u32[]{:S(2)}) collective-permute-start(bf16[2048,256]{1,0:T(8,128)(2,1)} %get-tuple-element.69), channel_id=1, source_target_pairs={{0,63},{1,2},{2,1},{3,4},{4,3},{5,6},{6,5},{7,8},{8,7},{9,10},{10,... | collective-permute-start | bytes 3145736 | tf_op jit(solution)/shard_map/ppermute | solution.py:45
  61.7 43.8 %collective-permute-start.14 = (bf16[2048,256]{1,0:T(8,128)(2,1)}, bf16[2048,256]{1,0:T(8,128)(2,1)}, u32[]{:S(2)}, u32[]{:S(2)}) collective-permute-start(bf16[2048,256]{1,0:T(8,128)(2,1)} %get-tuple-element.70), channel_id=1, source_target_pairs={{0,62},{1,63},{2,0},{3,1},{4,2},{5,3},{6,4},{7,5},{8,6},{9,7},{10,... | collective-permute-start | bytes 3145736 | tf_op jit(solution)/shard_map/ppermute | solution.py:45
  67.5 16.9 %collective-permute-start.8 = (s16[544,256]{1,0:T(8,128)(2,1)}, s16[544,256]{1,0:T(8,128)(2,1)S(1)}, u32[]{:S(2)}, u32[]{:S(2)}) collective-permute-start(s16[544,256]{1,0:T(8,128)(2,1)} %get-tuple-element.60), channel_id=1, source_target_pairs={{0,128},{64,192},{128,0},{192,64},{1,129},{65,193},{129,1},{193,65... | collective-permute-start | bytes 835592 | tf_op jit(solution)/shard_map/ppermute | solution.py:31
  78.6 15.3 %collective-permute-start.7 = (s16[1088,256]{1,0:T(8,128)(2,1)}, s16[1088,256]{1,0:T(8,128)(2,1)S(1)}, u32[]{:S(2)}, u32[]{:S(2)}) collective-permute-start(s16[1088,256]{1,0:T(8,128)(2,1)} %get-tuple-element.59), channel_id=1, source_target_pairs={{0,64},{64,128},{128,192},{192,0},{1,65},{65,129},{129,193},{193,1... | collective-permute-start | bytes 1671176 | tf_op jit(solution)/shard_map/ppermute | solution.py:31
  84.4 9.5 %collective-permute-start.10 = (s16[544,256]{1,0:T(8,128)(2,1)S(1)}, s16[544,256]{1,0:T(8,128)(2,1)S(1)}, u32[]{:S(2)}, u32[]{:S(2)}) collective-permute-start(s16[544,256]{1,0:T(8,128)(2,1)S(1)} %slice.21), channel_id=1, source_target_pairs={{0,192},{64,0},{128,64},{192,128},{1,193},{65,1},{129,65},{193,129... | collective-permute-start | bytes 835592 | tf_op jit(solution)/shard_map/ppermute | solution.py:31
  84.4 13.1 %copy-start.5 = (s32[4,8]{1,0:T(4,128)S(1)}, s32[4,8]{1,0:T(4,128)}, u32[]{:S(2)}) copy-start(s32[4,8]{1,0:T(4,128)} %param.5) | copy-start | bytes 388
  93.9 8.0 %collective-permute-start.11 = (s16[1088,128]{1,0:T(8,128)(2,1)}, s16[1088,128]{1,0:T(8,128)(2,1)S(1)}, u32[]{:S(2)}, u32[]{:S(2)}) collective-permute-start(s16[1088,128]{1,0:T(8,128)(2,1)} %get-tuple-element.62), channel_id=1, source_target_pairs={{0,64},{64,128},{128,192},{192,0},{1,65},{65,129},{129,193},{193,1... | collective-permute-start | bytes 835592 | tf_op jit(solution)/shard_map/ppermute | solution.py:31
  97.7 22.7 %copy-start.1 = (f32[1056,256]{1,0:T(8,128)S(1)}, f32[1056,256]{1,0:T(8,128)}, u32[]{:S(2)}) copy-start(f32[1056,256]{1,0:T(8,128)} %get-tuple-element.64.kept_ref) | copy-start | bytes 3244036
  97.7 24.1 %collective-permute-start.18 = (s16[1088,128]{1,0:T(8,128)(2,1)}, s16[1088,128]{1,0:T(8,128)(2,1)}, u32[]{:S(2)}, u32[]{:S(2)}) collective-permute-start(s16[1088,128]{1,0:T(8,128)(2,1)} %get-tuple-element.77), channel_id=1, source_target_pairs={{0,128},{64,192},{128,0},{192,64},{1,129},{65,193},{129,1},{193,65... | collective-permute-start | bytes 835592 | tf_op jit(solution)/shard_map/ppermute | solution.py:31
  102.0 12.9 %copy-start.2 = (s16[1088,128]{1,0:T(8,128)(2,1)}, s16[1088,128]{1,0:T(8,128)(2,1)S(1)}, u32[]{:S(2)}) copy-start(s16[1088,128]{1,0:T(8,128)(2,1)S(1)} %collective-permute-done.11.refs_0_) | copy-start | bytes 835588
  102.0 19.9 %collective-permute-start.19 = (s16[1088,128]{1,0:T(8,128)(2,1)}, s16[1088,128]{1,0:T(8,128)(2,1)}, u32[]{:S(2)}, u32[]{:S(2)}) collective-permute-start(s16[1088,128]{1,0:T(8,128)(2,1)} %get-tuple-element.78), channel_id=1, source_target_pairs={{0,192},{64,0},{128,64},{192,128},{1,193},{65,1},{129,65},{193,129... | collective-permute-start | bytes 835592 | tf_op jit(solution)/shard_map/ppermute | solution.py:31
  114.8 11.6 %collective-permute-start.15 = (s16[1088,128]{1,0:T(8,128)(2,1)}, s16[1088,128]{1,0:T(8,128)(2,1)S(1)}, u32[]{:S(2)}, u32[]{:S(2)}) collective-permute-start(s16[1088,128]{1,0:T(8,128)(2,1)} %get-tuple-element.72), channel_id=1, source_target_pairs={{0,64},{64,128},{128,192},{192,0},{1,65},{65,129},{129,193},{193,1... | collective-permute-start | bytes 835592 | tf_op jit(solution)/shard_map/ppermute | solution.py:31
  114.9 11.5 %collective-permute-start.16 = (s16[1088,128]{1,0:T(8,128)(2,1)}, s16[1088,128]{1,0:T(8,128)(2,1)}, u32[]{:S(2)}, u32[]{:S(2)}) collective-permute-start(s16[1088,128]{1,0:T(8,128)(2,1)} %get-tuple-element.73), channel_id=1, source_target_pairs={{0,128},{64,192},{128,0},{192,64},{1,129},{65,193},{129,1},{193,65... | collective-permute-start | bytes 835592 | tf_op jit(solution)/shard_map/ppermute | solution.py:31
  118.7 7.8 %collective-permute-start.17 = (s16[1088,128]{1,0:T(8,128)(2,1)}, s16[1088,128]{1,0:T(8,128)(2,1)}, u32[]{:S(2)}, u32[]{:S(2)}) collective-permute-start(s16[1088,128]{1,0:T(8,128)(2,1)} %get-tuple-element.74), channel_id=1, source_target_pairs={{0,192},{64,0},{128,64},{192,128},{1,193},{65,1},{129,65},{193,129... | collective-permute-start | bytes 835592 | tf_op jit(solution)/shard_map/ppermute | solution.py:31
  120.8 1.0 copy-start
  126.4 0.7 copy-start.3

commit v10 on v9

--- a/solution.py
+++ b/solution.py
@@ -248,7 +248,7 @@
 
 
 def remote_kernel(stage, slot_ref, dest_ref, mate_ref, at_ref, *refs):
-    blocks, parts, (cols_ref, tile_ref, sems) = refs[:4], refs[4:-3], refs[-3:]
+    blocks, parts, (cols_ref, tile_ref, norm_ref, sems) = refs[:4], refs[4:-4], refs[-4:]
     samp = len(parts)
     samples = cols_ref.shape[1]
     rows = BS // samp
@@ -269,8 +269,16 @@
                 )
         for copy in copies:
             copy.start()
-        for copy in copies:
+        step, lanes = 256, 32
+        for slot, copy in enumerate(copies):
             copy.wait()
+
+            def add(i, total):
+                x = cols_ref[slot, pl.ds(pl.multiple_of(i * step, step), step), :].astype(jnp.float32)
+                return total + jnp.sum(jnp.square(x).reshape(step // lanes, lanes, HALF), axis=0)
+
+            total = lax.fori_loop(0, samples // step, add, jnp.zeros((lanes, HALF), jnp.float32))
+            norm_ref[slot // 2, slot % 2 : slot % 2 + 1, :] = jnp.sum(total, axis=0, keepdims=True)
 
     at = at_ref[...]
     codes = [[] for _ in range(samp - 1)]
@@ -290,20 +298,10 @@
                     codes[d - 1].append(code)
                 parts[d][j * rows : (j + 1) * rows, :] = piece
 
-    step, lanes = 256, 32
-
-    def add(i, totals):
-        at_rows = pl.ds(pl.multiple_of(i * step, step), step)
-        squares = [jnp.square(cols_ref[2 * r + side, at_rows, :].astype(jnp.float32)) for side in range(2)]
-        return [
-            total + jnp.sum(square.reshape(step // lanes, lanes, HALF), axis=0)
-            for total, square in zip(totals, squares)
-        ]
-
-    totals = lax.fori_loop(0, samples // step, add, [jnp.zeros((lanes, HALF), jnp.float32)] * 2)
+    norms = norm_ref[r]
     norm_codes = []
-    for side, total in enumerate(totals):
-        norm = jnp.sum(total, axis=0, keepdims=True)
+    for side in range(2):
+        norm = norms[side : side + 1, :]
         norm_codes += encode_norm(norm)
         parts[0][BS + side * 4 : BS + side * 4 + 4, :] = jnp.broadcast_to(norm, (4, HALF))
     for d in range(1, samp):
@@ -325,6 +323,7 @@
             scratch_shapes=[
                 pltpu.VMEM((8, samples, HALF), at.dtype),
                 pltpu.VMEM((BS, BS), jnp.float32),
+                pltpu.VMEM((B_DEV, 8, HALF), jnp.float32),
                 pltpu.SemaphoreType.DMA((8,)),
             ],
         ),
@@ -378,20 +377,19 @@
 
 
 def final(half, place, slots, dest, tapers, own, rems, out, rows):
-    full = lambda shape: pl.BlockSpec(shape, lambda i, *s: (0,) * len(shape))
     before = [] if out is None else [out]
     return pl.pallas_call(
         functools.partial(final_kernel, half),
         grid_spec=pltpu.PrefetchScalarGridSpec(
             num_scalar_prefetch=4,
             grid=(1,),
-            in_specs=[full(own.shape)]
-            + [full(rem.shape) for rem in rems]
+            in_specs=[pl.BlockSpec(memory_space=pltpu.VMEM)] * (1 + len(rems))
             + [pl.BlockSpec(memory_space=pl.ANY)] * len(before),
             out_specs=pl.BlockSpec((rows * PAIR_DEV, HALF), lambda i, *s: (0, half)),
             scratch_shapes=[pltpu.VMEM((8, HALF), jnp.float32)],
         ),
         out_shape=jax.ShapeDtypeStruct((rows * PAIR_DEV, BS), jnp.float32),
+        compiler_params=pltpu.CompilerParams(vmem_limit_bytes=16 * MIB),
         input_output_aliases={5 + len(rems): 0} if before else {},
         cost_estimate=pl.CostEstimate(flops=MIB, bytes_accessed=4 * MIB, transcendentals=0),
     )(place, slots, dest, tapers, own, *rems, *before)

time: 134 us -> 133 us (level)
  Pallas kernels: 53.7 us -> 51.5 us
    unnamed x14 -> x24, local copies, waits for them, and re-layouts: 1.56 us -> 2.83 us
  transfers between devices with their start and end apart: 20 -> 20, of which waited for: 7 -> 7; matrix products, arithmetic and copies ran while one was open for 5% -> 4% of each run, Pallas kernels for 37% -> 36%
where the time goes in v10:
time: 133 us; the launch traced here: 131 us
  Pallas kernels  51.5 us (39%)
  starting transfers between devices  42.8 us (32%)
  waiting for transfers between devices  28.9 us (22%)
  local copies, waits for them, and re-layouts  4.61 us (3%)
  other arithmetic  3.07 us (2%)
    ppermute x10, starting transfers between devices, exchanged(): return lax.ppermute(value, 'blk', sorted(pairs))  25.1 us
    pallas_call x2, Pallas kernels, remote_tiles(): pl.pallas_call(functools.partial(remote_kernel, stage), grid_spec=pltpu.P...  18.1 us
    pallas_call x1, Pallas kernels, own_tiles(): pl.pallas_call(own_kernel, grid_spec=pltpu.PrefetchScalarGridSpec(num_sca...  17.9 us
    ppermute x10, starting transfers between devices, passed_along(): return lax.ppermute(value, axis, pairs)  17.8 us
    ppermute x10, waiting for transfers between devices, passed_along(): return lax.ppermute(value, axis, pairs)  15.5 us
    ppermute x10, waiting for transfers between devices, exchanged(): return lax.ppermute(value, 'blk', sorted(pairs))  13.4 us
    pallas_call x2, Pallas kernels, final(): pl.pallas_call(functools.partial(final_kernel, half), grid_spec=pltpu.Pre...  7.8 us
    pallas_call x2, Pallas kernels, select(): pl.pallas_call(functools.partial(select_kernel, plan), grid_spec=pltpu.Pr...  7.21 us
  transfers between devices with their start and end apart: 20, of which 7 were waited for; matrix products, arithmetic and copies ran while one was open for 4% of the time, Pallas kernels for 36%

profile of v10, /device:TPU:8, one launch (start us, length us, event | category | flops | bytes accessed | tf_op | source)
XLA Modules:
  0.0 131.1 jit_solution(1985272240613485259)
XLA Ops:
  0.0 0.7 add_select_fusion
  1.2 0.8 slice_reduce_fusion.2
  2.0 8.1 %collective-permute-start = (s32[2]{0:T(128)S(1)}, s32[2]{0:T(128)S(1)}, u32[]{:S(2)}, u32[]{:S(2)}) collective-permute-start(s32[2]{0:T(128)S(1)} %get-tuple-element.79), channel_id=1, source_target_pairs={{0,62},{1,63},{2,0},{3,1},{4,2},{5,3},{6,4},{7,5},{8,6},{9,7},{10,... | collective-permute-start | bytes 32 | tf_op jit(solution)/shard_map/ppermute | solution.py:45
  10.0 4.9 %collective-permute-start.1 = (s32[2]{0:T(128)S(1)}, s32[2]{0:T(128)S(1)}, u32[]{:S(2)}, u32[]{:S(2)}) collective-permute-start(s32[2]{0:T(128)S(1)} %get-tuple-element.81), channel_id=1, source_target_pairs={{0,63},{1,2},{2,1},{3,4},{4,3},{5,6},{6,5},{7,8},{8,7},{9,10},{10,... | collective-permute-start | bytes 32 | tf_op jit(solution)/shard_map/ppermute | solution.py:45
  14.9 2.0 %collective-permute-done.2 = s32[2]{0:T(128)S(1)} collective-permute-done((s32[2]{0:T(128)S(1)}, s32[2]{0:T(128)S(1)}, u32[]{:S(2)}, u32[]{:S(2)}) %collective-permute-start.2) | collective-permute-done | bytes 40 | tf_op jit(solution)/shard_map/ppermute | solution.py:45
  16.9 0.6 pad_add_fusion.2.want_ref
  17.5 3.6 %shard_map.39 = (bf16[2048,256]{1,0:T(8,128)(2,1)}, bf16[2048,256]{1,0:T(8,128)(2,1)}, bf16[2048,256]{1,0:T(8,128)(2,1)}) custom-call(s32[6]{0:T(128)} %pad_add_fusion.2.want_ref, bf16[2048,1024]{1,0:T(8,128)(2,1)} %source_ref.3), custom_call_target="tpu_custom_call" | custom-call | bytes 6291456 | tf_op jit(solution)/shard_map/pallas_call | solution.py:111
  21.2 4.4 %collective-permute-start.5 = (bf16[2048,256]{1,0:T(8,128)(2,1)}, bf16[2048,256]{1,0:T(8,128)(2,1)}, u32[]{:S(2)}, u32[]{:S(2)}) collective-permute-start(bf16[2048,256]{1,0:T(8,128)(2,1)} %get-tuple-element.49), channel_id=1, source_target_pairs={{0,63},{1,2},{2,1},{3,4},{4,3},{5,6},{6,5},{7,8},{8,7},{9,10},{10,... | collective-permute-start | bytes 3145736 | tf_op jit(solution)/shard_map/ppermute | solution.py:45
  25.6 1.6 %collective-permute-start.6 = (bf16[2048,256]{1,0:T(8,128)(2,1)}, bf16[2048,256]{1,0:T(8,128)(2,1)}, u32[]{:S(2)}, u32[]{:S(2)}) collective-permute-start(bf16[2048,256]{1,0:T(8,128)(2,1)} %get-tuple-element.50), channel_id=1, source_target_pairs={{0,62},{1,63},{2,0},{3,1},{4,2},{5,3},{6,4},{7,5},{8,6},{9,7},{10,... | collective-permute-start | bytes 3145736 | tf_op jit(solution)/shard_map/ppermute | solution.py:45
  27.8 3.6 %shard_map.37 = (bf16[2048,256]{1,0:T(8,128)(2,1)}, bf16[2048,256]{1,0:T(8,128)(2,1)}, bf16[2048,256]{1,0:T(8,128)(2,1)}) custom-call(s32[6]{0:T(128)} %pad_add_fusion.2.want_ref, bf16[2048,1024]{1,0:T(8,128)(2,1)} %source_ref.3), custom_call_target="tpu_custom_call" | custom-call | bytes 6291456 | tf_op jit(solution)/shard_map/pallas_call | solution.py:111
  31.4 17.9 %shard_map.38 = (bf16[1024,2048]{1,0:T(8,128)(2,1)}, f32[1056,256]{1,0:T(8,128)}, s16[1088,256]{1,0:T(8,128)(2,1)}, s16[544,256]{1,0:T(8,128)(2,1)}, s16[1632,256]{1,0:T(8,128)(2,1)}) custom-call(s32[4]{0:T(128)} %and_select_fusion.dest_ref, bf16[2048,1024]{1,0:T(8,128)(2,1)} %source_ref.3, bf16[2048,1024]{1,0:T(8,128)(2,1)} %source_ref.3), custom_call_target="tpu_custom_call" | custom-call | flops 4294967296 | bytes 12582912 | tf_op jit(solution)/shard_map/pallas_call | solution.py:191
  49.3 1.4 %collective-permute-done.4.refs_0_ = bf16[2048,256]{1,0:T(8,128)(2,1)S(1)} collective-permute-done((bf16[2048,256]{1,0:T(8,128)(2,1)}, bf16[2048,256]{1,0:T(8,128)(2,1)S(1)}, u32[]{:S(2)}, u32[]{:S(2)}) %collective-permute-start.4) | collective-permute-done | bytes 1048608 | tf_op jit(solution)/shard_map/ppermute | solution.py:45
  50.8 10.0 %collective-permute-done.5.refs_2_ = bf16[2048,256]{1,0:T(8,128)(2,1)} collective-permute-done((bf16[2048,256]{1,0:T(8,128)(2,1)}, bf16[2048,256]{1,0:T(8,128)(2,1)}, u32[]{:S(2)}, u32[]{:S(2)}) %collective-permute-start.5) | collective-permute-done | bytes 1048608 | tf_op jit(solution)/shard_map/ppermute | solution.py:45
  61.6 5.8 %collective-permute-start.14 = (bf16[2048,256]{1,0:T(8,128)(2,1)}, bf16[2048,256]{1,0:T(8,128)(2,1)}, u32[]{:S(2)}, u32[]{:S(2)}) collective-permute-start(bf16[2048,256]{1,0:T(8,128)(2,1)} %get-tuple-element.70), channel_id=1, source_target_pairs={{0,62},{1,63},{2,0},{3,1},{4,2},{5,3},{6,4},{7,5},{8,6},{9,7},{10,... | collective-permute-start | bytes 3145736 | tf_op jit(solution)/shard_map/ppermute | solution.py:45
  67.4 2.6 %collective-permute-start.8 = (s16[544,256]{1,0:T(8,128)(2,1)}, s16[544,256]{1,0:T(8,128)(2,1)S(1)}, u32[]{:S(2)}, u32[]{:S(2)}) collective-permute-start(s16[544,256]{1,0:T(8,128)(2,1)} %get-tuple-element.60), channel_id=1, source_target_pairs={{0,128},{64,192},{128,0},{192,64},{1,129},{65,193},{129,1},{193,65... | collective-permute-start | bytes 835592 | tf_op jit(solution)/shard_map/ppermute | solution.py:31
  70.1 0.7 reshape.142.slot_ref
  70.8 7.7 %collective-permute-done.9.down_ref = s16[1632,256]{1,0:T(8,128)(2,1)S(1)} collective-permute-done((s16[1632,256]{1,0:T(8,128)(2,1)}, s16[1632,256]{1,0:T(8,128)(2,1)S(1)}, u32[]{:S(2)}, u32[]{:S(2)}) %collective-permute-start.9) | collective-permute-done | bytes 835616 | tf_op jit(solution)/shard_map/ppermute | solution.py:31
  78.5 1.6 %collective-permute-start.7 = (s16[1088,256]{1,0:T(8,128)(2,1)}, s16[1088,256]{1,0:T(8,128)(2,1)S(1)}, u32[]{:S(2)}, u32[]{:S(2)}) collective-permute-start(s16[1088,256]{1,0:T(8,128)(2,1)} %get-tuple-element.59), channel_id=1, source_target_pairs={{0,64},{64,128},{128,192},{192,0},{1,65},{65,129},{129,193},{193,1... | collective-permute-start | bytes 1671176 | tf_op jit(solution)/shard_map/ppermute | solution.py:31
  80.1 4.0 %collective-permute-done.8.first_ref = s16[544,256]{1,0:T(8,128)(2,1)S(1)} collective-permute-done((s16[544,256]{1,0:T(8,128)(2,1)}, s16[544,256]{1,0:T(8,128)(2,1)S(1)}, u32[]{:S(2)}, u32[]{:S(2)}) %collective-permute-start.8) | collective-permute-done | bytes 278560 | tf_op jit(solution)/shard_map/ppermute | solution.py:31
  84.1 9.1 %shard_map.40 = (f32[1056,128]{1,0:T(8,128)}, s16[1088,128]{1,0:T(8,128)(2,1)}, s16[1088,128]{1,0:T(8,128)(2,1)}, s16[1088,128]{1,0:T(8,128)(2,1)}) custom-call(s32[16]{0:T(128)} %reshape.142.slot_ref, s32[4]{0:T(128)} %and_select_fusion.dest_ref, s32[2]{0:T(128)} %get-tuple-element.82.mate_ref, bf16[1024,2048]{1,0:T(8,128)(2,1)} %get-tuple-element.44.at_ref, ...), custom_call_target="tpu_custom_call" | custom-call | flops 4294967296 | bytes 10485760 | tf_op jit(solution)/shard_map/pallas_call | solution.py:316
  93.2 0.7 copy-done.3
  93.9 3.7 %collective-permute-start.11 = (s16[1088,128]{1,0:T(8,128)(2,1)}, s16[1088,128]{1,0:T(8,128)(2,1)S(1)}, u32[]{:S(2)}, u32[]{:S(2)}) collective-permute-start(s16[1088,128]{1,0:T(8,128)(2,1)} %get-tuple-element.62), channel_id=1, source_target_pairs={{0,64},{64,128},{128,192},{192,0},{1,65},{65,129},{129,193},{193,1... | collective-permute-start | bytes 835592 | tf_op jit(solution)/shard_map/ppermute | solution.py:31
  98.0 1.9 %collective-permute-start.18 = (s16[1088,128]{1,0:T(8,128)(2,1)}, s16[1088,128]{1,0:T(8,128)(2,1)}, u32[]{:S(2)}, u32[]{:S(2)}) collective-permute-start(s16[1088,128]{1,0:T(8,128)(2,1)} %get-tuple-element.77), channel_id=1, source_target_pairs={{0,128},{64,192},{128,0},{192,64},{1,129},{65,193},{129,1},{193,65... | collective-permute-start | bytes 835592 | tf_op jit(solution)/shard_map/ppermute | solution.py:31
  99.9 2.2 %collective-permute-done.11.refs_0_ = s16[1088,128]{1,0:T(8,128)(2,1)S(1)} collective-permute-done((s16[1088,128]{1,0:T(8,128)(2,1)}, s16[1088,128]{1,0:T(8,128)(2,1)S(1)}, u32[]{:S(2)}, u32[]{:S(2)}) %collective-permute-start.11) | collective-permute-done | bytes 278560 | tf_op jit(solution)/shard_map/ppermute | solution.py:31
  102.1 0.7 copy-done.5
  102.8 3.3 %collective-permute-start.19 = (s16[1088,128]{1,0:T(8,128)(2,1)}, s16[1088,128]{1,0:T(8,128)(2,1)}, u32[]{:S(2)}, u32[]{:S(2)}) collective-permute-start(s16[1088,128]{1,0:T(8,128)(2,1)} %get-tuple-element.78), channel_id=1, source_target_pairs={{0,192},{64,0},{128,64},{192,128},{1,193},{65,1},{129,65},{193,129... | collective-permute-start | bytes 835592 | tf_op jit(solution)/shard_map/ppermute | solution.py:31
  106.1 9.0 %shard_map.42 = (f32[1056,128]{1,0:T(8,128)}, s16[1088,128]{1,0:T(8,128)(2,1)}, s16[1088,128]{1,0:T(8,128)(2,1)}, s16[1088,128]{1,0:T(8,128)(2,1)}) custom-call(s32[16]{0:T(128)} %reshape.142.slot_ref, s32[4]{0:T(128)} %and_select_fusion.dest_ref, s32[2]{0:T(128)} %get-tuple-element.82.mate_ref, bf16[1024,2048]{1,0:T(8,128)(2,1)} %get-tuple-element.44.at_ref, ...), custom_call_target="tpu_custom_call" | custom-call | flops 4294967296 | bytes 10485760 | tf_op jit(solution)/shard_map/pallas_call | solution.py:316
  115.3 4.1 %collective-permute-start.16 = (s16[1088,128]{1,0:T(8,128)(2,1)}, s16[1088,128]{1,0:T(8,128)(2,1)}, u32[]{:S(2)}, u32[]{:S(2)}) collective-permute-start(s16[1088,128]{1,0:T(8,128)(2,1)} %get-tuple-element.73), channel_id=1, source_target_pairs={{0,128},{64,192},{128,0},{192,64},{1,129},{65,193},{129,1},{193,65... | collective-permute-start | bytes 835592 | tf_op jit(solution)/shard_map/ppermute | solution.py:31
  119.9 1.0 copy-done.4
  121.8 3.8 %shard_map.43.refs_3_ = f32[2048,256]{1,0:T(8,128)} custom-call(s32[32]{0:T(128)S(1)} %add.125.place_ref, s32[16]{0:T(128)S(1)} %copy-done.7, s32[4]{0:T(128)S(1)} %copy-done.8, f32[32]{0:T(128)S(1)} %reshape.143.taper_ref, f32[1056,256]{1,0:T(8,128)S(1)} %shard_map.41.own_ref, f32[1056,128]{1,0:T(8,128)S(1)} %copy-done.2, s16[1088,128]{1,0:T(8,128)(2,1)S(1)} %copy-done.6, ...), custom_call_target="tpu_custom_call" | custom-call | flops 1048576 | bytes 4194304 | tf_op jit(solution)/shard_map/pallas_call | solution.py:381
  125.6 1.6 %collective-permute-done.17.refs_2_ = s16[1088,128]{1,0:T(8,128)(2,1)} collective-permute-done((s16[1088,128]{1,0:T(8,128)(2,1)}, s16[1088,128]{1,0:T(8,128)(2,1)}, u32[]{:S(2)}, u32[]{:S(2)}) %collective-permute-start.17) | collective-permute-done | bytes 278560 | tf_op jit(solution)/shard_map/ppermute | solution.py:31
  127.2 3.9 %shard_map.44 = f32[2048,256]{1,0:T(8,128)} custom-call(s32[32]{0:T(128)S(1)} %add.125.place_ref, s32[16]{0:T(128)S(1)} %copy-done.7, s32[4]{0:T(128)S(1)} %copy-done.8, f32[32]{0:T(128)S(1)} %reshape.143.taper_ref, f32[1056,256]{1,0:T(8,128)S(1)} %shard_map.41.own_ref, f32[1056,128]{1,0:T(8,128)S(1)} %copy-done.1, ...), custom_call_target="tpu_custom_call", output_to_operand_aliasing={{}: (9, {})} | custom-call | flops 1048576 | bytes 4194304 | tf_op jit(solution)/shard_map/pallas_call | solution.py:381
  (68 shorter events, 3.9 us)
Async XLA Ops:
  0.0 31.4 %collective-permute-start.3 = (bf16[2048,1024]{1,0:T(8,128)(2,1)}, bf16[2048,1024]{1,0:T(8,128)(2,1)}, u32[]{:S(2)}, u32[]{:S(2)}) collective-permute-start(bf16[2048,1024]{1,0:T(8,128)(2,1)} %source_ref.3), channel_id=1, source_target_pairs={{0,1},{1,0},{2,3},{3,2},{4,5},{5,4},{6,7},{7,6},{8,9},{9,8},{10,11... | collective-permute-start | bytes 12582920 | tf_op jit(solution)/shard_map/ppermute | solution.py:45
  2.0 13.0 %collective-permute-start = (s32[2]{0:T(128)S(1)}, s32[2]{0:T(128)S(1)}, u32[]{:S(2)}, u32[]{:S(2)}) collective-permute-start(s32[2]{0:T(128)S(1)} %get-tuple-element.79), channel_id=1, source_target_pairs={{0,62},{1,63},{2,0},{3,1},{4,2},{5,3},{6,4},{7,5},{8,6},{9,7},{10,... | collective-permute-start | bytes 32 | tf_op jit(solution)/shard_map/ppermute | solution.py:45
  10.0 6.9 %collective-permute-start.2 = (s32[2]{0:T(128)S(1)}, s32[2]{0:T(128)S(1)}, u32[]{:S(2)}, u32[]{:S(2)}) collective-permute-start(s32[2]{0:T(128)S(1)} %get-tuple-element.80), channel_id=1, source_target_pairs={{0,2},{1,3},{2,4},{3,5},{4,6},{5,7},{6,8},{7,9},{8,10},{9,11},{10,... | collective-permute-start | bytes 32 | tf_op jit(solution)/shard_map/ppermute | solution.py:45
  10.0 6.9 %collective-permute-start.1 = (s32[2]{0:T(128)S(1)}, s32[2]{0:T(128)S(1)}, u32[]{:S(2)}, u32[]{:S(2)}) collective-permute-start(s32[2]{0:T(128)S(1)} %get-tuple-element.81), channel_id=1, source_target_pairs={{0,63},{1,2},{2,1},{3,4},{4,3},{5,6},{6,5},{7,8},{8,7},{9,10},{10,... | collective-permute-start | bytes 32 | tf_op jit(solution)/shard_map/ppermute | solution.py:45
  21.1 29.7 %collective-permute-start.4 = (bf16[2048,256]{1,0:T(8,128)(2,1)}, bf16[2048,256]{1,0:T(8,128)(2,1)S(1)}, u32[]{:S(2)}, u32[]{:S(2)}) collective-permute-start(bf16[2048,256]{1,0:T(8,128)(2,1)} %get-tuple-element.48), channel_id=1, source_target_pairs={{0,2},{1,3},{2,4},{3,5},{4,6},{5,7},{6,8},{7,9},{8,10},{9,11},{10,... | collective-permute-start | bytes 3145736 | tf_op jit(solution)/shard_map/ppermute | solution.py:45
  21.2 39.6 %collective-permute-start.5 = (bf16[2048,256]{1,0:T(8,128)(2,1)}, bf16[2048,256]{1,0:T(8,128)(2,1)}, u32[]{:S(2)}, u32[]{:S(2)}) collective-permute-start(bf16[2048,256]{1,0:T(8,128)(2,1)} %get-tuple-element.49), channel_id=1, source_target_pairs={{0,63},{1,2},{2,1},{3,4},{4,3},{5,6},{6,5},{7,8},{8,7},{9,10},{10,... | collective-permute-start | bytes 3145736 | tf_op jit(solution)/shard_map/ppermute | solution.py:45
  25.6 35.2 %collective-permute-start.6 = (bf16[2048,256]{1,0:T(8,128)(2,1)}, bf16[2048,256]{1,0:T(8,128)(2,1)}, u32[]{:S(2)}, u32[]{:S(2)}) collective-permute-start(bf16[2048,256]{1,0:T(8,128)(2,1)} %get-tuple-element.50), channel_id=1, source_target_pairs={{0,62},{1,63},{2,0},{3,1},{4,2},{5,3},{6,4},{7,5},{8,6},{9,7},{10,... | collective-permute-start | bytes 3145736 | tf_op jit(solution)/shard_map/ppermute | solution.py:45
  31.4 30.0 %copy-start.9 = (s32[4,8]{1,0:T(4,128)S(1)}, s32[4,8]{1,0:T(4,128)}, u32[]{:S(2)}) copy-start(s32[4,8]{1,0:T(4,128)} %param.4) | copy-start | bytes 388
  50.8 29.3 %copy-start.11 = (bf16[2048,256]{1,0:T(8,128)(2,1)}, bf16[2048,256]{1,0:T(8,128)(2,1)S(1)}, u32[]{:S(2)}) copy-start(bf16[2048,256]{1,0:T(8,128)(2,1)S(1)} %collective-permute-done.4.refs_0_) | copy-start | bytes 3145732
  60.8 17.7 %collective-permute-start.9 = (s16[1632,256]{1,0:T(8,128)(2,1)}, s16[1632,256]{1,0:T(8,128)(2,1)S(1)}, u32[]{:S(2)}, u32[]{:S(2)}) collective-permute-start(s16[1632,256]{1,0:T(8,128)(2,1)} %get-tuple-element.61), channel_id=1, source_target_pairs={{0,192},{64,0},{128,64},{192,128},{1,193},{65,1},{129,65},{193,129... | collective-permute-start | bytes 2506760 | tf_op jit(solution)/shard_map/ppermute | solution.py:31
  61.4 44.7 %collective-permute-start.12 = (bf16[2048,256]{1,0:T(8,128)(2,1)}, bf16[2048,256]{1,0:T(8,128)(2,1)}, u32[]{:S(2)}, u32[]{:S(2)}) collective-permute-start(bf16[2048,256]{1,0:T(8,128)(2,1)} %get-tuple-element.42), channel_id=1, source_target_pairs={{0,2},{1,3},{2,4},{3,5},{4,6},{5,7},{6,8},{7,9},{8,10},{9,11},{10,... | collective-permute-start | bytes 3145736 | tf_op jit(solution)/shard_map/ppermute | solution.py:45
  61.5 44.6 %collective-permute-start.13 = (bf16[2048,256]{1,0:T(8,128)(2,1)}, bf16[2048,256]{1,0:T(8,128)(2,1)}, u32[]{:S(2)}, u32[]{:S(2)}) collective-permute-start(bf16[2048,256]{1,0:T(8,128)(2,1)} %get-tuple-element.69), channel_id=1, source_target_pairs={{0,63},{1,2},{2,1},{3,4},{4,3},{5,6},{6,5},{7,8},{8,7},{9,10},{10,... | collective-permute-start | bytes 3145736 | tf_op jit(solution)/shard_map/ppermute | solution.py:45
  61.6 44.5 %collective-permute-start.14 = (bf16[2048,256]{1,0:T(8,128)(2,1)}, bf16[2048,256]{1,0:T(8,128)(2,1)}, u32[]{:S(2)}, u32[]{:S(2)}) collective-permute-start(bf16[2048,256]{1,0:T(8,128)(2,1)} %get-tuple-element.70), channel_id=1, source_target_pairs={{0,62},{1,63},{2,0},{3,1},{4,2},{5,3},{6,4},{7,5},{8,6},{9,7},{10,... | collective-permute-start | bytes 3145736 | tf_op jit(solution)/shard_map/ppermute | solution.py:45
  67.4 16.7 %collective-permute-start.8 = (s16[544,256]{1,0:T(8,128)(2,1)}, s16[544,256]{1,0:T(8,128)(2,1)S(1)}, u32[]{:S(2)}, u32[]{:S(2)}) collective-permute-start(s16[544,256]{1,0:T(8,128)(2,1)} %get-tuple-element.60), channel_id=1, source_target_pairs={{0,128},{64,192},{128,0},{192,64},{1,129},{65,193},{129,1},{193,65... | collective-permute-start | bytes 835592 | tf_op jit(solution)/shard_map/ppermute | solution.py:31
  78.5 14.7 %collective-permute-start.7 = (s16[1088,256]{1,0:T(8,128)(2,1)}, s16[1088,256]{1,0:T(8,128)(2,1)S(1)}, u32[]{:S(2)}, u32[]{:S(2)}) collective-permute-start(s16[1088,256]{1,0:T(8,128)(2,1)} %get-tuple-element.59), channel_id=1, source_target_pairs={{0,64},{64,128},{128,192},{192,0},{1,65},{65,129},{129,193},{193,1... | collective-permute-start | bytes 1671176 | tf_op jit(solution)/shard_map/ppermute | solution.py:31
  84.1 9.1 %collective-permute-start.10 = (s16[544,256]{1,0:T(8,128)(2,1)S(1)}, s16[544,256]{1,0:T(8,128)(2,1)S(1)}, u32[]{:S(2)}, u32[]{:S(2)}) collective-permute-start(s16[544,256]{1,0:T(8,128)(2,1)S(1)} %slice.21), channel_id=1, source_target_pairs={{0,192},{64,0},{128,64},{192,128},{1,193},{65,1},{129,65},{193,129... | collective-permute-start | bytes 835592 | tf_op jit(solution)/shard_map/ppermute | solution.py:31
  84.1 13.6 %copy-start.10 = (s32[4,8]{1,0:T(4,128)S(1)}, s32[4,8]{1,0:T(4,128)}, u32[]{:S(2)}) copy-start(s32[4,8]{1,0:T(4,128)} %param.5) | copy-start | bytes 388
  93.2 0.7 copy-start.3
  93.9 8.1 %collective-permute-start.11 = (s16[1088,128]{1,0:T(8,128)(2,1)}, s16[1088,128]{1,0:T(8,128)(2,1)S(1)}, u32[]{:S(2)}, u32[]{:S(2)}) collective-permute-start(s16[1088,128]{1,0:T(8,128)(2,1)} %get-tuple-element.62), channel_id=1, source_target_pairs={{0,64},{64,128},{128,192},{192,0},{1,65},{65,129},{129,193},{193,1... | collective-permute-start | bytes 835592 | tf_op jit(solution)/shard_map/ppermute | solution.py:31
  98.0 21.9 %copy-start = (f32[1056,256]{1,0:T(8,128)S(1)}, f32[1056,256]{1,0:T(8,128)}, u32[]{:S(2)}) copy-start(f32[1056,256]{1,0:T(8,128)} %get-tuple-element.64.kept_ref) | copy-start | bytes 3244036
  98.0 23.3 %collective-permute-start.18 = (s16[1088,128]{1,0:T(8,128)(2,1)}, s16[1088,128]{1,0:T(8,128)(2,1)}, u32[]{:S(2)}, u32[]{:S(2)}) collective-permute-start(s16[1088,128]{1,0:T(8,128)(2,1)} %get-tuple-element.77), channel_id=1, source_target_pairs={{0,128},{64,192},{128,0},{192,64},{1,129},{65,193},{129,1},{193,65... | collective-permute-start | bytes 835592 | tf_op jit(solution)/shard_map/ppermute | solution.py:31
  102.1 0.7 copy-start.5
  102.8 18.5 %collective-permute-start.19 = (s16[1088,128]{1,0:T(8,128)(2,1)}, s16[1088,128]{1,0:T(8,128)(2,1)}, u32[]{:S(2)}, u32[]{:S(2)}) collective-permute-start(s16[1088,128]{1,0:T(8,128)(2,1)} %get-tuple-element.78), channel_id=1, source_target_pairs={{0,192},{64,0},{128,64},{192,128},{1,193},{65,1},{129,65},{193,129... | collective-permute-start | bytes 835592 | tf_op jit(solution)/shard_map/ppermute | solution.py:31
  106.1 15.2 %copy-start.7 = (s32[16]{0:T(128)S(1)}, s32[16]{0:T(128)}, u32[]{:S(2)}) copy-start(s32[16]{0:T(128)} %reshape.142.slot_ref) | copy-start | bytes 196
  106.1 15.2 %copy-start.8 = (s32[4]{0:T(128)S(1)}, s32[4]{0:T(128)}, u32[]{:S(2)}) copy-start(s32[4]{0:T(128)} %and_select_fusion.dest_ref) | copy-start | bytes 52
  115.2 6.2 %copy-start.2 = (f32[1056,128]{1,0:T(8,128)S(1)}, f32[1056,128]{1,0:T(8,128)}, u32[]{:S(2)}) copy-start(f32[1056,128]{1,0:T(8,128)} %get-tuple-element.75.kept_ref) | copy-start | bytes 1622020
  115.2 10.4 %collective-permute-start.15 = (s16[1088,128]{1,0:T(8,128)(2,1)}, s16[1088,128]{1,0:T(8,128)(2,1)}, u32[]{:S(2)}, u32[]{:S(2)}) collective-permute-start(s16[1088,128]{1,0:T(8,128)(2,1)} %get-tuple-element.72), channel_id=1, source_target_pairs={{0,64},{64,128},{128,192},{192,0},{1,65},{65,129},{129,193},{193,1... | collective-permute-start | bytes 835592 | tf_op jit(solution)/shard_map/ppermute | solution.py:31
  115.3 10.3 %collective-permute-start.16 = (s16[1088,128]{1,0:T(8,128)(2,1)}, s16[1088,128]{1,0:T(8,128)(2,1)}, u32[]{:S(2)}, u32[]{:S(2)}) collective-permute-start(s16[1088,128]{1,0:T(8,128)(2,1)} %get-tuple-element.73), channel_id=1, source_target_pairs={{0,128},{64,192},{128,0},{192,64},{1,129},{65,193},{129,1},{193,65... | collective-permute-start | bytes 835592 | tf_op jit(solution)/shard_map/ppermute | solution.py:31
  119.4 7.8 %collective-permute-start.17 = (s16[1088,128]{1,0:T(8,128)(2,1)}, s16[1088,128]{1,0:T(8,128)(2,1)}, u32[]{:S(2)}, u32[]{:S(2)}) collective-permute-start(s16[1088,128]{1,0:T(8,128)(2,1)} %get-tuple-element.74), channel_id=1, source_target_pairs={{0,192},{64,0},{128,64},{192,128},{1,193},{65,1},{129,65},{193,129... | collective-permute-start | bytes 835592 | tf_op jit(solution)/shard_map/ppermute | solution.py:31
  119.8 1.0 copy-start.4
  120.8 1.0 copy-start.6
  121.3 5.9 %copy-start.1 = (f32[1056,128]{1,0:T(8,128)S(1)}, f32[1056,128]{1,0:T(8,128)}, u32[]{:S(2)}) copy-start(f32[1056,128]{1,0:T(8,128)} %get-tuple-element.71.kept_ref) | copy-start | bytes 1622020

commit v11 on v10

--- a/solution.py
+++ b/solution.py
@@ -378,18 +378,21 @@
 
 def final(half, place, slots, dest, tapers, own, rems, out, rows):
     before = [] if out is None else [out]
+    vmem = pl.BlockSpec(memory_space=pltpu.VMEM)
+    whole = lambda shape: vmem if before else pl.BlockSpec(shape, lambda i, *s: (0,) * len(shape))
     return pl.pallas_call(
         functools.partial(final_kernel, half),
         grid_spec=pltpu.PrefetchScalarGridSpec(
             num_scalar_prefetch=4,
             grid=(1,),
-            in_specs=[pl.BlockSpec(memory_space=pltpu.VMEM)] * (1 + len(rems))
+            in_specs=[whole(own.shape)]
+            + [whole(rem.shape) for rem in rems]
             + [pl.BlockSpec(memory_space=pl.ANY)] * len(before),
             out_specs=pl.BlockSpec((rows * PAIR_DEV, HALF), lambda i, *s: (0, half)),
             scratch_shapes=[pltpu.VMEM((8, HALF), jnp.float32)],
         ),
         out_shape=jax.ShapeDtypeStruct((rows * PAIR_DEV, BS), jnp.float32),
-        compiler_params=pltpu.CompilerParams(vmem_limit_bytes=16 * MIB),
+        compiler_params=pltpu.CompilerParams(vmem_limit_bytes=16 * MIB if before else BIG),
         input_output_aliases={5 + len(rems): 0} if before else {},
         cost_estimate=pl.CostEstimate(flops=MIB, bytes_accessed=4 * MIB, transcendentals=0),
     )(place, slots, dest, tapers, own, *rems, *before)

time: 133 us -> 133 us (level)
  waiting for transfers between devices: 28.9 us -> 27.5 us
    unnamed x24 -> x22, local copies, waits for them, and re-layouts: 2.83 us -> 1.02 us
  transfers between devices with their start and end apart: 20 -> 20, of which waited for: 7 -> 6; matrix products, arithmetic and copies ran while one was open for 4% -> 5% of each run, Pallas kernels for 36% -> 37%
where the time goes in v11:
time: 133 us; the launch traced here: 130 us
  Pallas kernels  52.2 us (39%)
  starting transfers between devices  43.6 us (33%)
  waiting for transfers between devices  27.5 us (21%)
  local copies, waits for them, and re-layouts  3.84 us (3%)
  other arithmetic  3.08 us (2%)
    ppermute x10, starting transfers between devices, exchanged(): return lax.ppermute(value, 'blk', sorted(pairs))  25.1 us
    ppermute x10, starting transfers between devices, passed_along(): return lax.ppermute(value, axis, pairs)  18.5 us
    pallas_call x2, Pallas kernels, remote_tiles(): pl.pallas_call(functools.partial(remote_kernel, stage), grid_spec=pltpu.P...  18.1 us
    pallas_call x1, Pallas kernels, own_tiles(): pl.pallas_call(own_kernel, grid_spec=pltpu.PrefetchScalarGridSpec(num_sca...  18 us
    ppermute x10, waiting for transfers between devices, passed_along(): return lax.ppermute(value, axis, pairs)  14.2 us
    ppermute x10, waiting for transfers between devices, exchanged(): return lax.ppermute(value, 'blk', sorted(pairs))  13.4 us
    pallas_call x2, Pallas kernels, final(): pl.pallas_call(functools.partial(final_kernel, half), grid_spec=pltpu.Pre...  8.55 us
    pallas_call x2, Pallas kernels, select(): pl.pallas_call(functools.partial(select_kernel, plan), grid_spec=pltpu.Pr...  7.21 us
  transfers between devices with their start and end apart: 20, of which 6 were waited for; matrix products, arithmetic and copies ran while one was open for 5% of the time, Pallas kernels for 37%

profile of v11, /device:TPU:8, one launch (start us, length us, event | category | flops | bytes accessed | tf_op | source)
XLA Modules:
  0.0 130.5 jit_solution(16133626497349671658)
XLA Ops:
  0.0 0.7 add_select_fusion
  1.2 0.7 slice_reduce_fusion.2
  1.9 8.1 %collective-permute-start = (s32[2]{0:T(128)S(1)}, s32[2]{0:T(128)S(1)}, u32[]{:S(2)}, u32[]{:S(2)}) collective-permute-start(s32[2]{0:T(128)S(1)} %get-tuple-element.79), channel_id=1, source_target_pairs={{0,62},{1,63},{2,0},{3,1},{4,2},{5,3},{6,4},{7,5},{8,6},{9,7},{10,... | collective-permute-start | bytes 32 | tf_op jit(solution)/shard_map/ppermute | solution.py:45
  10.0 4.9 %collective-permute-start.1 = (s32[2]{0:T(128)S(1)}, s32[2]{0:T(128)S(1)}, u32[]{:S(2)}, u32[]{:S(2)}) collective-permute-start(s32[2]{0:T(128)S(1)} %get-tuple-element.81), channel_id=1, source_target_pairs={{0,63},{1,2},{2,1},{3,4},{4,3},{5,6},{6,5},{7,8},{8,7},{9,10},{10,... | collective-permute-start | bytes 32 | tf_op jit(solution)/shard_map/ppermute | solution.py:45
  14.9 2.0 %collective-permute-done.2 = s32[2]{0:T(128)S(1)} collective-permute-done((s32[2]{0:T(128)S(1)}, s32[2]{0:T(128)S(1)}, u32[]{:S(2)}, u32[]{:S(2)}) %collective-permute-start.2) | collective-permute-done | bytes 40 | tf_op jit(solution)/shard_map/ppermute | solution.py:45
  16.8 0.6 pad_add_fusion.2.want_ref
  17.4 3.6 %shard_map.39 = (bf16[2048,256]{1,0:T(8,128)(2,1)}, bf16[2048,256]{1,0:T(8,128)(2,1)}, bf16[2048,256]{1,0:T(8,128)(2,1)}) custom-call(s32[6]{0:T(128)} %pad_add_fusion.2.want_ref, bf16[2048,1024]{1,0:T(8,128)(2,1)} %source_ref.3), custom_call_target="tpu_custom_call" | custom-call | bytes 6291456 | tf_op jit(solution)/shard_map/pallas_call | solution.py:111
  21.1 4.4 %collective-permute-start.5 = (bf16[2048,256]{1,0:T(8,128)(2,1)}, bf16[2048,256]{1,0:T(8,128)(2,1)}, u32[]{:S(2)}, u32[]{:S(2)}) collective-permute-start(bf16[2048,256]{1,0:T(8,128)(2,1)} %get-tuple-element.49), channel_id=1, source_target_pairs={{0,63},{1,2},{2,1},{3,4},{4,3},{5,6},{6,5},{7,8},{8,7},{9,10},{10,... | collective-permute-start | bytes 3145736 | tf_op jit(solution)/shard_map/ppermute | solution.py:45
  25.6 1.6 %collective-permute-start.6 = (bf16[2048,256]{1,0:T(8,128)(2,1)}, bf16[2048,256]{1,0:T(8,128)(2,1)}, u32[]{:S(2)}, u32[]{:S(2)}) collective-permute-start(bf16[2048,256]{1,0:T(8,128)(2,1)} %get-tuple-element.50), channel_id=1, source_target_pairs={{0,62},{1,63},{2,0},{3,1},{4,2},{5,3},{6,4},{7,5},{8,6},{9,7},{10,... | collective-permute-start | bytes 3145736 | tf_op jit(solution)/shard_map/ppermute | solution.py:45
  27.2 0.5 and_select_fusion.dest_ref
  27.8 3.6 %shard_map.37 = (bf16[2048,256]{1,0:T(8,128)(2,1)}, bf16[2048,256]{1,0:T(8,128)(2,1)}, bf16[2048,256]{1,0:T(8,128)(2,1)}) custom-call(s32[6]{0:T(128)} %pad_add_fusion.2.want_ref, bf16[2048,1024]{1,0:T(8,128)(2,1)} %source_ref.3), custom_call_target="tpu_custom_call" | custom-call | bytes 6291456 | tf_op jit(solution)/shard_map/pallas_call | solution.py:111
  31.4 18.0 %shard_map.38 = (bf16[1024,2048]{1,0:T(8,128)(2,1)}, f32[1056,256]{1,0:T(8,128)}, s16[1088,256]{1,0:T(8,128)(2,1)}, s16[544,256]{1,0:T(8,128)(2,1)}, s16[1632,256]{1,0:T(8,128)(2,1)}) custom-call(s32[4]{0:T(128)} %and_select_fusion.dest_ref, bf16[2048,1024]{1,0:T(8,128)(2,1)} %source_ref.3, bf16[2048,1024]{1,0:T(8,128)(2,1)} %source_ref.3), custom_call_target="tpu_custom_call" | custom-call | flops 4294967296 | bytes 12582912 | tf_op jit(solution)/shard_map/pallas_call | solution.py:191
  49.3 1.4 %collective-permute-done.4.refs_0_ = bf16[2048,256]{1,0:T(8,128)(2,1)S(1)} collective-permute-done((bf16[2048,256]{1,0:T(8,128)(2,1)}, bf16[2048,256]{1,0:T(8,128)(2,1)S(1)}, u32[]{:S(2)}, u32[]{:S(2)}) %collective-permute-start.4) | collective-permute-done | bytes 1048608 | tf_op jit(solution)/shard_map/ppermute | solution.py:45
  50.7 10.0 %collective-permute-done.5.refs_2_ = bf16[2048,256]{1,0:T(8,128)(2,1)} collective-permute-done((bf16[2048,256]{1,0:T(8,128)(2,1)}, bf16[2048,256]{1,0:T(8,128)(2,1)}, u32[]{:S(2)}, u32[]{:S(2)}) %collective-permute-start.5) | collective-permute-done | bytes 1048608 | tf_op jit(solution)/shard_map/ppermute | solution.py:45
  61.6 5.8 %collective-permute-start.14 = (bf16[2048,256]{1,0:T(8,128)(2,1)}, bf16[2048,256]{1,0:T(8,128)(2,1)}, u32[]{:S(2)}, u32[]{:S(2)}) collective-permute-start(bf16[2048,256]{1,0:T(8,128)(2,1)} %get-tuple-element.70), channel_id=1, source_target_pairs={{0,62},{1,63},{2,0},{3,1},{4,2},{5,3},{6,4},{7,5},{8,6},{9,7},{10,... | collective-permute-start | bytes 3145736 | tf_op jit(solution)/shard_map/ppermute | solution.py:45
  67.4 2.6 %collective-permute-start.8 = (s16[544,256]{1,0:T(8,128)(2,1)}, s16[544,256]{1,0:T(8,128)(2,1)S(1)}, u32[]{:S(2)}, u32[]{:S(2)}) collective-permute-start(s16[544,256]{1,0:T(8,128)(2,1)} %get-tuple-element.60), channel_id=1, source_target_pairs={{0,128},{64,192},{128,0},{192,64},{1,129},{65,193},{129,1},{193,65... | collective-permute-start | bytes 835592 | tf_op jit(solution)/shard_map/ppermute | solution.py:31
  70.1 0.7 reshape.142.slot_ref
  70.8 7.8 %collective-permute-done.9.down_ref = s16[1632,256]{1,0:T(8,128)(2,1)S(1)} collective-permute-done((s16[1632,256]{1,0:T(8,128)(2,1)}, s16[1632,256]{1,0:T(8,128)(2,1)S(1)}, u32[]{:S(2)}, u32[]{:S(2)}) %collective-permute-start.9) | collective-permute-done | bytes 835616 | tf_op jit(solution)/shard_map/ppermute | solution.py:31
  78.6 1.6 %collective-permute-start.7 = (s16[1088,256]{1,0:T(8,128)(2,1)}, s16[1088,256]{1,0:T(8,128)(2,1)S(1)}, u32[]{:S(2)}, u32[]{:S(2)}) collective-permute-start(s16[1088,256]{1,0:T(8,128)(2,1)} %get-tuple-element.59), channel_id=1, source_target_pairs={{0,64},{64,128},{128,192},{192,0},{1,65},{65,129},{129,193},{193,1... | collective-permute-start | bytes 1671176 | tf_op jit(solution)/shard_map/ppermute | solution.py:31
  80.2 4.1 %collective-permute-done.8.first_ref = s16[544,256]{1,0:T(8,128)(2,1)S(1)} collective-permute-done((s16[544,256]{1,0:T(8,128)(2,1)}, s16[544,256]{1,0:T(8,128)(2,1)S(1)}, u32[]{:S(2)}, u32[]{:S(2)}) %collective-permute-start.8) | collective-permute-done | bytes 278560 | tf_op jit(solution)/shard_map/ppermute | solution.py:31
  84.3 9.1 %shard_map.40 = (f32[1056,128]{1,0:T(8,128)}, s16[1088,128]{1,0:T(8,128)(2,1)}, s16[1088,128]{1,0:T(8,128)(2,1)}, s16[1088,128]{1,0:T(8,128)(2,1)}) custom-call(s32[16]{0:T(128)} %reshape.142.slot_ref, s32[4]{0:T(128)} %and_select_fusion.dest_ref, s32[2]{0:T(128)} %get-tuple-element.82.mate_ref, bf16[1024,2048]{1,0:T(8,128)(2,1)} %get-tuple-element.44.at_ref, ...), custom_call_target="tpu_custom_call" | custom-call | flops 4294967296 | bytes 10485760 | tf_op jit(solution)/shard_map/pallas_call | solution.py:316
  93.4 4.3 %collective-permute-start.11 = (s16[1088,128]{1,0:T(8,128)(2,1)}, s16[1088,128]{1,0:T(8,128)(2,1)}, u32[]{:S(2)}, u32[]{:S(2)}) collective-permute-start(s16[1088,128]{1,0:T(8,128)(2,1)} %get-tuple-element.62), channel_id=1, source_target_pairs={{0,64},{64,128},{128,192},{192,0},{1,65},{65,129},{129,193},{193,1... | collective-permute-start | bytes 835592 | tf_op jit(solution)/shard_map/ppermute | solution.py:31
  98.1 1.9 %collective-permute-start.18 = (s16[1088,128]{1,0:T(8,128)(2,1)}, s16[1088,128]{1,0:T(8,128)(2,1)}, u32[]{:S(2)}, u32[]{:S(2)}) collective-permute-start(s16[1088,128]{1,0:T(8,128)(2,1)} %get-tuple-element.77), channel_id=1, source_target_pairs={{0,128},{64,192},{128,0},{192,64},{1,129},{65,193},{129,1},{193,65... | collective-permute-start | bytes 835592 | tf_op jit(solution)/shard_map/ppermute | solution.py:31
  100.0 2.2 %collective-permute-done.11.refs_0_ = s16[1088,128]{1,0:T(8,128)(2,1)} collective-permute-done((s16[1088,128]{1,0:T(8,128)(2,1)}, s16[1088,128]{1,0:T(8,128)(2,1)}, u32[]{:S(2)}, u32[]{:S(2)}) %collective-permute-start.11) | collective-permute-done | bytes 278560 | tf_op jit(solution)/shard_map/ppermute | solution.py:31
  102.2 3.4 %collective-permute-start.19 = (s16[1088,128]{1,0:T(8,128)(2,1)}, s16[1088,128]{1,0:T(8,128)(2,1)}, u32[]{:S(2)}, u32[]{:S(2)}) collective-permute-start(s16[1088,128]{1,0:T(8,128)(2,1)} %get-tuple-element.78), channel_id=1, source_target_pairs={{0,192},{64,0},{128,64},{192,128},{1,193},{65,1},{129,65},{193,129... | collective-permute-start | bytes 835592 | tf_op jit(solution)/shard_map/ppermute | solution.py:31
  105.6 9.0 %shard_map.42 = (f32[1056,128]{1,0:T(8,128)}, s16[1088,128]{1,0:T(8,128)(2,1)}, s16[1088,128]{1,0:T(8,128)(2,1)}, s16[1088,128]{1,0:T(8,128)(2,1)}) custom-call(s32[16]{0:T(128)} %reshape.142.slot_ref, s32[4]{0:T(128)} %and_select_fusion.dest_ref, s32[2]{0:T(128)} %get-tuple-element.82.mate_ref, bf16[1024,2048]{1,0:T(8,128)(2,1)} %get-tuple-element.44.at_ref, ...), custom_call_target="tpu_custom_call" | custom-call | flops 4294967296 | bytes 10485760 | tf_op jit(solution)/shard_map/pallas_call | solution.py:316
  114.7 4.1 %collective-permute-start.16 = (s16[1088,128]{1,0:T(8,128)(2,1)}, s16[1088,128]{1,0:T(8,128)(2,1)}, u32[]{:S(2)}, u32[]{:S(2)}) collective-permute-start(s16[1088,128]{1,0:T(8,128)(2,1)} %get-tuple-element.73), channel_id=1, source_target_pairs={{0,128},{64,192},{128,0},{192,64},{1,129},{65,193},{129,1},{193,65... | collective-permute-start | bytes 835592 | tf_op jit(solution)/shard_map/ppermute | solution.py:31
  118.8 0.6 reshape.143.taper_ref
  119.7 0.7 add.125.place_ref
  120.8 1.0 copy-done
  121.8 4.7 %shard_map.43.refs_3_ = f32[2048,256]{1,0:T(8,128)} custom-call(s32[32]{0:T(128)} %add.125.place_ref, s32[16]{0:T(128)} %reshape.142.slot_ref, s32[4]{0:T(128)} %and_select_fusion.dest_ref, f32[32]{0:T(128)} %reshape.143.taper_ref, f32[1056,256]{1,0:T(8,128)} %copy-done, f32[1056,128]{1,0:T(8,128)} %get-tuple-element.75.kept_ref, ...), custom_call_target="tpu_custom_call" | custom-call | flops 1048576 | bytes 4194304 | tf_op jit(solution)/shard_map/pallas_call | solution.py:383
  126.6 3.9 %shard_map.44 = f32[2048,256]{1,0:T(8,128)} custom-call(s32[32]{0:T(128)S(1)} %copy-done.6, s32[16]{0:T(128)S(1)} %copy-done.4, s32[4]{0:T(128)S(1)} %copy-done.7, f32[32]{0:T(128)S(1)} %copy-done.5, f32[1056,256]{1,0:T(8,128)S(1)} %copy-done.1, f32[1056,128]{1,0:T(8,128)S(1)} %copy-done.3, ...), custom_call_target="tpu_custom_call", output_to_operand_aliasing={{}: (9, {})} | custom-call | flops 1048576 | bytes 4194304 | tf_op jit(solution)/shard_map/pallas_call | solution.py:383
  (66 shorter events, 2.8 us)
Async XLA Ops:
  0.0 31.4 %collective-permute-start.3 = (bf16[2048,1024]{1,0:T(8,128)(2,1)}, bf16[2048,1024]{1,0:T(8,128)(2,1)}, u32[]{:S(2)}, u32[]{:S(2)}) collective-permute-start(bf16[2048,1024]{1,0:T(8,128)(2,1)} %source_ref.3), channel_id=1, source_target_pairs={{0,1},{1,0},{2,3},{3,2},{4,5},{5,4},{6,7},{7,6},{8,9},{9,8},{10,11... | collective-permute-start | bytes 12582920 | tf_op jit(solution)/shard_map/ppermute | solution.py:45
  1.9 13.0 %collective-permute-start = (s32[2]{0:T(128)S(1)}, s32[2]{0:T(128)S(1)}, u32[]{:S(2)}, u32[]{:S(2)}) collective-permute-start(s32[2]{0:T(128)S(1)} %get-tuple-element.79), channel_id=1, source_target_pairs={{0,62},{1,63},{2,0},{3,1},{4,2},{5,3},{6,4},{7,5},{8,6},{9,7},{10,... | collective-permute-start | bytes 32 | tf_op jit(solution)/shard_map/ppermute | solution.py:45
  10.0 6.9 %collective-permute-start.2 = (s32[2]{0:T(128)S(1)}, s32[2]{0:T(128)S(1)}, u32[]{:S(2)}, u32[]{:S(2)}) collective-permute-start(s32[2]{0:T(128)S(1)} %get-tuple-element.80), channel_id=1, source_target_pairs={{0,2},{1,3},{2,4},{3,5},{4,6},{5,7},{6,8},{7,9},{8,10},{9,11},{10,... | collective-permute-start | bytes 32 | tf_op jit(solution)/shard_map/ppermute | solution.py:45
  10.0 6.9 %collective-permute-start.1 = (s32[2]{0:T(128)S(1)}, s32[2]{0:T(128)S(1)}, u32[]{:S(2)}, u32[]{:S(2)}) collective-permute-start(s32[2]{0:T(128)S(1)} %get-tuple-element.81), channel_id=1, source_target_pairs={{0,63},{1,2},{2,1},{3,4},{4,3},{5,6},{6,5},{7,8},{8,7},{9,10},{10,... | collective-permute-start | bytes 32 | tf_op jit(solution)/shard_map/ppermute | solution.py:45
  21.0 29.7 %collective-permute-start.4 = (bf16[2048,256]{1,0:T(8,128)(2,1)}, bf16[2048,256]{1,0:T(8,128)(2,1)S(1)}, u32[]{:S(2)}, u32[]{:S(2)}) collective-permute-start(bf16[2048,256]{1,0:T(8,128)(2,1)} %get-tuple-element.48), channel_id=1, source_target_pairs={{0,2},{1,3},{2,4},{3,5},{4,6},{5,7},{6,8},{7,9},{8,10},{9,11},{10,... | collective-permute-start | bytes 3145736 | tf_op jit(solution)/shard_map/ppermute | solution.py:45
  21.1 39.6 %collective-permute-start.5 = (bf16[2048,256]{1,0:T(8,128)(2,1)}, bf16[2048,256]{1,0:T(8,128)(2,1)}, u32[]{:S(2)}, u32[]{:S(2)}) collective-permute-start(bf16[2048,256]{1,0:T(8,128)(2,1)} %get-tuple-element.49), channel_id=1, source_target_pairs={{0,63},{1,2},{2,1},{3,4},{4,3},{5,6},{6,5},{7,8},{8,7},{9,10},{10,... | collective-permute-start | bytes 3145736 | tf_op jit(solution)/shard_map/ppermute | solution.py:45
  25.6 35.2 %collective-permute-start.6 = (bf16[2048,256]{1,0:T(8,128)(2,1)}, bf16[2048,256]{1,0:T(8,128)(2,1)}, u32[]{:S(2)}, u32[]{:S(2)}) collective-permute-start(bf16[2048,256]{1,0:T(8,128)(2,1)} %get-tuple-element.50), channel_id=1, source_target_pairs={{0,62},{1,63},{2,0},{3,1},{4,2},{5,3},{6,4},{7,5},{8,6},{9,7},{10,... | collective-permute-start | bytes 3145736 | tf_op jit(solution)/shard_map/ppermute | solution.py:45
  31.4 30.0 %copy-start.8 = (s32[4,8]{1,0:T(4,128)S(1)}, s32[4,8]{1,0:T(4,128)}, u32[]{:S(2)}) copy-start(s32[4,8]{1,0:T(4,128)} %param.4) | copy-start | bytes 388
  50.7 29.4 %copy-start.10 = (bf16[2048,256]{1,0:T(8,128)(2,1)}, bf16[2048,256]{1,0:T(8,128)(2,1)S(1)}, u32[]{:S(2)}) copy-start(bf16[2048,256]{1,0:T(8,128)(2,1)S(1)} %collective-permute-done.4.refs_0_) | copy-start | bytes 3145732
  60.7 17.8 %collective-permute-start.9 = (s16[1632,256]{1,0:T(8,128)(2,1)}, s16[1632,256]{1,0:T(8,128)(2,1)S(1)}, u32[]{:S(2)}, u32[]{:S(2)}) collective-permute-start(s16[1632,256]{1,0:T(8,128)(2,1)} %get-tuple-element.61), channel_id=1, source_target_pairs={{0,192},{64,0},{128,64},{192,128},{1,193},{65,1},{129,65},{193,129... | collective-permute-start | bytes 2506760 | tf_op jit(solution)/shard_map/ppermute | solution.py:31
  61.4 44.2 %collective-permute-start.12 = (bf16[2048,256]{1,0:T(8,128)(2,1)}, bf16[2048,256]{1,0:T(8,128)(2,1)}, u32[]{:S(2)}, u32[]{:S(2)}) collective-permute-start(bf16[2048,256]{1,0:T(8,128)(2,1)} %get-tuple-element.42), channel_id=1, source_target_pairs={{0,2},{1,3},{2,4},{3,5},{4,6},{5,7},{6,8},{7,9},{8,10},{9,11},{10,... | collective-permute-start | bytes 3145736 | tf_op jit(solution)/shard_map/ppermute | solution.py:45
  61.5 44.1 %collective-permute-start.13 = (bf16[2048,256]{1,0:T(8,128)(2,1)}, bf16[2048,256]{1,0:T(8,128)(2,1)}, u32[]{:S(2)}, u32[]{:S(2)}) collective-permute-start(bf16[2048,256]{1,0:T(8,128)(2,1)} %get-tuple-element.69), channel_id=1, source_target_pairs={{0,63},{1,2},{2,1},{3,4},{4,3},{5,6},{6,5},{7,8},{8,7},{9,10},{10,... | collective-permute-start | bytes 3145736 | tf_op jit(solution)/shard_map/ppermute | solution.py:45
  61.6 44.0 %collective-permute-start.14 = (bf16[2048,256]{1,0:T(8,128)(2,1)}, bf16[2048,256]{1,0:T(8,128)(2,1)}, u32[]{:S(2)}, u32[]{:S(2)}) collective-permute-start(bf16[2048,256]{1,0:T(8,128)(2,1)} %get-tuple-element.70), channel_id=1, source_target_pairs={{0,62},{1,63},{2,0},{3,1},{4,2},{5,3},{6,4},{7,5},{8,6},{9,7},{10,... | collective-permute-start | bytes 3145736 | tf_op jit(solution)/shard_map/ppermute | solution.py:45
  67.4 16.9 %collective-permute-start.8 = (s16[544,256]{1,0:T(8,128)(2,1)}, s16[544,256]{1,0:T(8,128)(2,1)S(1)}, u32[]{:S(2)}, u32[]{:S(2)}) collective-permute-start(s16[544,256]{1,0:T(8,128)(2,1)} %get-tuple-element.60), channel_id=1, source_target_pairs={{0,128},{64,192},{128,0},{192,64},{1,129},{65,193},{129,1},{193,65... | collective-permute-start | bytes 835592 | tf_op jit(solution)/shard_map/ppermute | solution.py:31
  78.6 14.8 %collective-permute-start.7 = (s16[1088,256]{1,0:T(8,128)(2,1)}, s16[1088,256]{1,0:T(8,128)(2,1)S(1)}, u32[]{:S(2)}, u32[]{:S(2)}) collective-permute-start(s16[1088,256]{1,0:T(8,128)(2,1)} %get-tuple-element.59), channel_id=1, source_target_pairs={{0,64},{64,128},{128,192},{192,0},{1,65},{65,129},{129,193},{193,1... | collective-permute-start | bytes 1671176 | tf_op jit(solution)/shard_map/ppermute | solution.py:31
  84.3 9.1 %collective-permute-start.10 = (s16[544,256]{1,0:T(8,128)(2,1)S(1)}, s16[544,256]{1,0:T(8,128)(2,1)S(1)}, u32[]{:S(2)}, u32[]{:S(2)}) collective-permute-start(s16[544,256]{1,0:T(8,128)(2,1)S(1)} %slice.21), channel_id=1, source_target_pairs={{0,192},{64,0},{128,64},{192,128},{1,193},{65,1},{129,65},{193,129... | collective-permute-start | bytes 835592 | tf_op jit(solution)/shard_map/ppermute | solution.py:31
  84.3 13.5 %copy-start.9 = (s32[4,8]{1,0:T(4,128)S(1)}, s32[4,8]{1,0:T(4,128)}, u32[]{:S(2)}) copy-start(s32[4,8]{1,0:T(4,128)} %param.5) | copy-start | bytes 388
  93.4 8.7 %collective-permute-start.11 = (s16[1088,128]{1,0:T(8,128)(2,1)}, s16[1088,128]{1,0:T(8,128)(2,1)}, u32[]{:S(2)}, u32[]{:S(2)}) collective-permute-start(s16[1088,128]{1,0:T(8,128)(2,1)} %get-tuple-element.62), channel_id=1, source_target_pairs={{0,64},{64,128},{128,192},{192,0},{1,65},{65,129},{129,193},{193,1... | collective-permute-start | bytes 835592 | tf_op jit(solution)/shard_map/ppermute | solution.py:31
  98.1 22.3 %copy-start.2 = (f32[1056,256]{1,0:T(8,128)S(1)}, f32[1056,256]{1,0:T(8,128)}, u32[]{:S(2)}) copy-start(f32[1056,256]{1,0:T(8,128)} %get-tuple-element.64.kept_ref) | copy-start | bytes 3244036
  98.1 23.7 %collective-permute-start.18 = (s16[1088,128]{1,0:T(8,128)(2,1)}, s16[1088,128]{1,0:T(8,128)(2,1)}, u32[]{:S(2)}, u32[]{:S(2)}) collective-permute-start(s16[1088,128]{1,0:T(8,128)(2,1)} %get-tuple-element.77), channel_id=1, source_target_pairs={{0,128},{64,192},{128,0},{192,64},{1,129},{65,193},{129,1},{193,65... | collective-permute-start | bytes 835592 | tf_op jit(solution)/shard_map/ppermute | solution.py:31
  102.2 19.7 %collective-permute-start.19 = (s16[1088,128]{1,0:T(8,128)(2,1)}, s16[1088,128]{1,0:T(8,128)(2,1)}, u32[]{:S(2)}, u32[]{:S(2)}) collective-permute-start(s16[1088,128]{1,0:T(8,128)(2,1)} %get-tuple-element.78), channel_id=1, source_target_pairs={{0,192},{64,0},{128,64},{192,128},{1,193},{65,1},{129,65},{193,129... | collective-permute-start | bytes 835592 | tf_op jit(solution)/shard_map/ppermute | solution.py:31
  114.6 12.0 %collective-permute-start.15 = (s16[1088,128]{1,0:T(8,128)(2,1)}, s16[1088,128]{1,0:T(8,128)(2,1)S(1)}, u32[]{:S(2)}, u32[]{:S(2)}) collective-permute-start(s16[1088,128]{1,0:T(8,128)(2,1)} %get-tuple-element.72), channel_id=1, source_target_pairs={{0,64},{64,128},{128,192},{192,0},{1,65},{65,129},{129,193},{193,1... | collective-permute-start | bytes 835592 | tf_op jit(solution)/shard_map/ppermute | solution.py:31
  114.7 11.9 %collective-permute-start.16 = (s16[1088,128]{1,0:T(8,128)(2,1)}, s16[1088,128]{1,0:T(8,128)(2,1)}, u32[]{:S(2)}, u32[]{:S(2)}) collective-permute-start(s16[1088,128]{1,0:T(8,128)(2,1)} %get-tuple-element.73), channel_id=1, source_target_pairs={{0,128},{64,192},{128,0},{192,64},{1,129},{65,193},{129,1},{193,65... | collective-permute-start | bytes 835592 | tf_op jit(solution)/shard_map/ppermute | solution.py:31
  118.8 7.8 %collective-permute-start.17 = (s16[1088,128]{1,0:T(8,128)(2,1)}, s16[1088,128]{1,0:T(8,128)(2,1)}, u32[]{:S(2)}, u32[]{:S(2)}) collective-permute-start(s16[1088,128]{1,0:T(8,128)(2,1)} %get-tuple-element.74), channel_id=1, source_target_pairs={{0,192},{64,0},{128,64},{192,128},{1,193},{65,1},{129,65},{193,129... | collective-permute-start | bytes 835592 | tf_op jit(solution)/shard_map/ppermute | solution.py:31
  120.8 1.0 copy-start
  121.8 4.8 %copy-start.3 = (f32[1056,128]{1,0:T(8,128)S(1)}, f32[1056,128]{1,0:T(8,128)}, u32[]{:S(2)}) copy-start(f32[1056,128]{1,0:T(8,128)} %get-tuple-element.71.kept_ref) | copy-start | bytes 1622020
  121.8 4.8 %copy-start.4 = (s32[16]{0:T(128)S(1)}, s32[16]{0:T(128)}, u32[]{:S(2)}) copy-start(s32[16]{0:T(128)} %reshape.142.slot_ref) | copy-start | bytes 196
  121.8 4.8 %copy-start.5 = (f32[32]{0:T(128)S(1)}, f32[32]{0:T(128)}, u32[]{:S(2)}) copy-start(f32[32]{0:T(128)} %reshape.143.taper_ref) | copy-start | bytes 388
  121.8 4.8 %copy-start.6 = (s32[32]{0:T(128)S(1)}, s32[32]{0:T(128)}, u32[]{:S(2)}) copy-start(s32[32]{0:T(128)} %add.125.place_ref) | copy-start | bytes 388
  121.8 4.8 %copy-start.7 = (s32[4]{0:T(128)S(1)}, s32[4]{0:T(128)}, u32[]{:S(2)}) copy-start(s32[4]{0:T(128)} %and_select_fusion.dest_ref) | copy-start | bytes 52
  121.8 4.8 %copy-start.1 = (f32[1056,256]{1,0:T(8,128)S(1)}, f32[1056,256]{1,0:T(8,128)}, u32[]{:S(2)}) copy-start(f32[1056,256]{1,0:T(8,128)} %copy-done) | copy-start | bytes 3244036

commit v12 on v11

--- a/solution.py
+++ b/solution.py
@@ -18,6 +18,7 @@
 EXTRA = 8
 CODE_EXTRA = 16
 TOP = 32766.0
+PIECES = 4
 STEPS = 256.0
 
 EPSILON = 1e-06
@@ -89,12 +90,17 @@
 def select_kernel(plan, want_ref, source_ref, *refs):
     outs, held_ref, in_sems, out_sems = refs[:-3], refs[-3], refs[-2], refs[-1]
     reads, writes = [], []
+    samples = held_ref.shape[1]
+    size = samples // PIECES
     for i, (q, side, half, out, column) in enumerate(plan):
         start = pl.multiple_of(want_ref[q * 2 + side] * BS + half * HALF, HALF)
-        reads.append(pltpu.make_async_copy(source_ref.at[:, pl.ds(start, HALF)], held_ref.at[i], in_sems.at[i]))
-        writes.append(
-            pltpu.make_async_copy(held_ref.at[i], outs[out].at[:, pl.ds(column * HALF, HALF)], out_sems.at[i])
-        )
+        for piece in range(PIECES):
+            at = slice(piece * size, (piece + 1) * size)
+            held = held_ref.at[i, at]
+            n = i * PIECES + piece
+            reads.append(pltpu.make_async_copy(source_ref.at[at, pl.ds(start, HALF)], held, in_sems.at[n]))
+            target = outs[out].at[at, pl.ds(column * HALF, HALF)]
+            writes.append(pltpu.make_async_copy(held, target, out_sems.at[n]))
     for read in reads:
         read.start()
     for read, write in zip(reads, writes):
@@ -117,8 +123,8 @@
             out_specs=[pl.BlockSpec(memory_space=pltpu.HBM)] * len(widths),
             scratch_shapes=[
                 pltpu.VMEM((len(plan), samples, HALF), perturb.dtype),
-                pltpu.SemaphoreType.DMA((len(plan),)),
-                pltpu.SemaphoreType.DMA((len(plan),)),
+                pltpu.SemaphoreType.DMA((len(plan) * PIECES,)),
+                pltpu.SemaphoreType.DMA((len(plan) * PIECES,)),
             ],
         ),
         out_shape=[jax.ShapeDtypeStruct((samples, width), perturb.dtype) for width in widths],

time: 133 us -> 133 us (level)
  transfers between devices with their start and end apart: 20 -> 20, of which waited for: 6 -> 6; matrix products, arithmetic and copies ran while one was open for 5% -> 5% of each run, Pallas kernels for 37% -> 38%
where the time goes in v12:
time: 133 us; the launch traced here: 131 us
  Pallas kernels  53.5 us (40%)
  starting transfers between devices  43.6 us (33%)
  waiting for transfers between devices  26.7 us (20%)
  local copies, waits for them, and re-layouts  3.84 us (3%)
  other arithmetic  3.08 us (2%)
    ppermute x10, starting transfers between devices, exchanged(): return lax.ppermute(value, 'blk', sorted(pairs))  25.1 us
    ppermute x10, starting transfers between devices, passed_along(): return lax.ppermute(value, axis, pairs)  18.5 us
    pallas_call x2, Pallas kernels, remote_tiles(): pl.pallas_call(functools.partial(remote_kernel, stage), grid_spec=pltpu.P...  18.1 us
    pallas_call x1, Pallas kernels, own_tiles(): pl.pallas_call(own_kernel, grid_spec=pltpu.PrefetchScalarGridSpec(num_sca...  18 us
    ppermute x10, waiting for transfers between devices, passed_along(): return lax.ppermute(value, axis, pairs)  13.9 us
    ppermute x10, waiting for transfers between devices, exchanged(): return lax.ppermute(value, 'blk', sorted(pairs))  12.7 us
    pallas_call x2, Pallas kernels, final(): pl.pallas_call(functools.partial(final_kernel, half), grid_spec=pltpu.Pre...  8.55 us
    pallas_call x2, Pallas kernels, select(): pl.pallas_call(functools.partial(select_kernel, plan), grid_spec=pltpu.Pr...  8.5 us
  transfers between devices with their start and end apart: 20, of which 6 were waited for; matrix products, arithmetic and copies ran while one was open for 5% of the time, Pallas kernels for 38%

profile of v12, /device:TPU:8, one launch (start us, length us, event | category | flops | bytes accessed | tf_op | source)
XLA Modules:
  0.0 130.9 jit_solution(12746731945522946948)
XLA Ops:
  0.0 0.7 add_select_fusion
  1.2 0.7 slice_reduce_fusion.2
  1.9 8.1 %collective-permute-start = (s32[2]{0:T(128)S(1)}, s32[2]{0:T(128)S(1)}, u32[]{:S(2)}, u32[]{:S(2)}) collective-permute-start(s32[2]{0:T(128)S(1)} %get-tuple-element.79), channel_id=1, source_target_pairs={{0,62},{1,63},{2,0},{3,1},{4,2},{5,3},{6,4},{7,5},{8,6},{9,7},{10,... | collective-permute-start | bytes 32 | tf_op jit(solution)/shard_map/ppermute | solution.py:46
  10.0 4.9 %collective-permute-start.1 = (s32[2]{0:T(128)S(1)}, s32[2]{0:T(128)S(1)}, u32[]{:S(2)}, u32[]{:S(2)}) collective-permute-start(s32[2]{0:T(128)S(1)} %get-tuple-element.81), channel_id=1, source_target_pairs={{0,63},{1,2},{2,1},{3,4},{4,3},{5,6},{6,5},{7,8},{8,7},{9,10},{10,... | collective-permute-start | bytes 32 | tf_op jit(solution)/shard_map/ppermute | solution.py:46
  14.9 2.0 %collective-permute-done.2 = s32[2]{0:T(128)S(1)} collective-permute-done((s32[2]{0:T(128)S(1)}, s32[2]{0:T(128)S(1)}, u32[]{:S(2)}, u32[]{:S(2)}) %collective-permute-start.2) | collective-permute-done | bytes 40 | tf_op jit(solution)/shard_map/ppermute | solution.py:46
  16.8 0.6 pad_add_fusion.2.want_ref
  17.4 4.2 %shard_map.39 = (bf16[2048,256]{1,0:T(8,128)(2,1)}, bf16[2048,256]{1,0:T(8,128)(2,1)}, bf16[2048,256]{1,0:T(8,128)(2,1)}) custom-call(s32[6]{0:T(128)} %pad_add_fusion.2.want_ref, bf16[2048,1024]{1,0:T(8,128)(2,1)} %source_ref.3), custom_call_target="tpu_custom_call" | custom-call | bytes 6291456 | tf_op jit(solution)/shard_map/pallas_call | solution.py:117
  21.8 4.4 %collective-permute-start.5 = (bf16[2048,256]{1,0:T(8,128)(2,1)}, bf16[2048,256]{1,0:T(8,128)(2,1)}, u32[]{:S(2)}, u32[]{:S(2)}) collective-permute-start(bf16[2048,256]{1,0:T(8,128)(2,1)} %get-tuple-element.49), channel_id=1, source_target_pairs={{0,63},{1,2},{2,1},{3,4},{4,3},{5,6},{6,5},{7,8},{8,7},{9,10},{10,... | collective-permute-start | bytes 3145736 | tf_op jit(solution)/shard_map/ppermute | solution.py:46
  26.2 1.6 %collective-permute-start.6 = (bf16[2048,256]{1,0:T(8,128)(2,1)}, bf16[2048,256]{1,0:T(8,128)(2,1)}, u32[]{:S(2)}, u32[]{:S(2)}) collective-permute-start(bf16[2048,256]{1,0:T(8,128)(2,1)} %get-tuple-element.50), channel_id=1, source_target_pairs={{0,62},{1,63},{2,0},{3,1},{4,2},{5,3},{6,4},{7,5},{8,6},{9,7},{10,... | collective-permute-start | bytes 3145736 | tf_op jit(solution)/shard_map/ppermute | solution.py:46
  27.8 0.5 and_select_fusion.dest_ref
  28.4 4.3 %shard_map.37 = (bf16[2048,256]{1,0:T(8,128)(2,1)}, bf16[2048,256]{1,0:T(8,128)(2,1)}, bf16[2048,256]{1,0:T(8,128)(2,1)}) custom-call(s32[6]{0:T(128)} %pad_add_fusion.2.want_ref, bf16[2048,1024]{1,0:T(8,128)(2,1)} %source_ref.3), custom_call_target="tpu_custom_call" | custom-call | bytes 6291456 | tf_op jit(solution)/shard_map/pallas_call | solution.py:117
  32.7 18.0 %shard_map.38 = (bf16[1024,2048]{1,0:T(8,128)(2,1)}, f32[1056,256]{1,0:T(8,128)}, s16[1088,256]{1,0:T(8,128)(2,1)}, s16[544,256]{1,0:T(8,128)(2,1)}, s16[1632,256]{1,0:T(8,128)(2,1)}) custom-call(s32[4]{0:T(128)} %and_select_fusion.dest_ref, bf16[2048,1024]{1,0:T(8,128)(2,1)} %source_ref.3, bf16[2048,1024]{1,0:T(8,128)(2,1)} %source_ref.3), custom_call_target="tpu_custom_call" | custom-call | flops 4294967296 | bytes 12582912 | tf_op jit(solution)/shard_map/pallas_call | solution.py:197
  50.6 0.8 collective-permute-done.4.refs_0_
  51.4 10.0 %collective-permute-done.5.refs_2_ = bf16[2048,256]{1,0:T(8,128)(2,1)} collective-permute-done((bf16[2048,256]{1,0:T(8,128)(2,1)}, bf16[2048,256]{1,0:T(8,128)(2,1)}, u32[]{:S(2)}, u32[]{:S(2)}) %collective-permute-start.5) | collective-permute-done | bytes 1048608 | tf_op jit(solution)/shard_map/ppermute | solution.py:46
  62.2 5.8 %collective-permute-start.14 = (bf16[2048,256]{1,0:T(8,128)(2,1)}, bf16[2048,256]{1,0:T(8,128)(2,1)}, u32[]{:S(2)}, u32[]{:S(2)}) collective-permute-start(bf16[2048,256]{1,0:T(8,128)(2,1)} %get-tuple-element.70), channel_id=1, source_target_pairs={{0,62},{1,63},{2,0},{3,1},{4,2},{5,3},{6,4},{7,5},{8,6},{9,7},{10,... | collective-permute-start | bytes 3145736 | tf_op jit(solution)/shard_map/ppermute | solution.py:46
  68.0 2.6 %collective-permute-start.8 = (s16[544,256]{1,0:T(8,128)(2,1)}, s16[544,256]{1,0:T(8,128)(2,1)S(1)}, u32[]{:S(2)}, u32[]{:S(2)}) collective-permute-start(s16[544,256]{1,0:T(8,128)(2,1)} %get-tuple-element.60), channel_id=1, source_target_pairs={{0,128},{64,192},{128,0},{192,64},{1,129},{65,193},{129,1},{193,65... | collective-permute-start | bytes 835592 | tf_op jit(solution)/shard_map/ppermute | solution.py:32
  70.7 0.7 reshape.142.slot_ref
  71.4 7.7 %collective-permute-done.9.down_ref = s16[1632,256]{1,0:T(8,128)(2,1)S(1)} collective-permute-done((s16[1632,256]{1,0:T(8,128)(2,1)}, s16[1632,256]{1,0:T(8,128)(2,1)S(1)}, u32[]{:S(2)}, u32[]{:S(2)}) %collective-permute-start.9) | collective-permute-done | bytes 835616 | tf_op jit(solution)/shard_map/ppermute | solution.py:32
  79.1 1.6 %collective-permute-start.7 = (s16[1088,256]{1,0:T(8,128)(2,1)}, s16[1088,256]{1,0:T(8,128)(2,1)S(1)}, u32[]{:S(2)}, u32[]{:S(2)}) collective-permute-start(s16[1088,256]{1,0:T(8,128)(2,1)} %get-tuple-element.59), channel_id=1, source_target_pairs={{0,64},{64,128},{128,192},{192,0},{1,65},{65,129},{129,193},{193,1... | collective-permute-start | bytes 1671176 | tf_op jit(solution)/shard_map/ppermute | solution.py:32
  80.7 4.0 %collective-permute-done.8.first_ref = s16[544,256]{1,0:T(8,128)(2,1)S(1)} collective-permute-done((s16[544,256]{1,0:T(8,128)(2,1)}, s16[544,256]{1,0:T(8,128)(2,1)S(1)}, u32[]{:S(2)}, u32[]{:S(2)}) %collective-permute-start.8) | collective-permute-done | bytes 278560 | tf_op jit(solution)/shard_map/ppermute | solution.py:32
  84.7 9.1 %shard_map.40 = (f32[1056,128]{1,0:T(8,128)}, s16[1088,128]{1,0:T(8,128)(2,1)}, s16[1088,128]{1,0:T(8,128)(2,1)}, s16[1088,128]{1,0:T(8,128)(2,1)}) custom-call(s32[16]{0:T(128)} %reshape.142.slot_ref, s32[4]{0:T(128)} %and_select_fusion.dest_ref, s32[2]{0:T(128)} %get-tuple-element.82.mate_ref, bf16[1024,2048]{1,0:T(8,128)(2,1)} %get-tuple-element.44.at_ref, ...), custom_call_target="tpu_custom_call" | custom-call | flops 4294967296 | bytes 10485760 | tf_op jit(solution)/shard_map/pallas_call | solution.py:322
  93.8 4.4 %collective-permute-start.11 = (s16[1088,128]{1,0:T(8,128)(2,1)}, s16[1088,128]{1,0:T(8,128)(2,1)}, u32[]{:S(2)}, u32[]{:S(2)}) collective-permute-start(s16[1088,128]{1,0:T(8,128)(2,1)} %get-tuple-element.62), channel_id=1, source_target_pairs={{0,64},{64,128},{128,192},{192,0},{1,65},{65,129},{129,193},{193,1... | collective-permute-start | bytes 835592 | tf_op jit(solution)/shard_map/ppermute | solution.py:32
  98.5 1.9 %collective-permute-start.18 = (s16[1088,128]{1,0:T(8,128)(2,1)}, s16[1088,128]{1,0:T(8,128)(2,1)}, u32[]{:S(2)}, u32[]{:S(2)}) collective-permute-start(s16[1088,128]{1,0:T(8,128)(2,1)} %get-tuple-element.77), channel_id=1, source_target_pairs={{0,128},{64,192},{128,0},{192,64},{1,129},{65,193},{129,1},{193,65... | collective-permute-start | bytes 835592 | tf_op jit(solution)/shard_map/ppermute | solution.py:32
  100.4 2.2 %collective-permute-done.11.refs_0_ = s16[1088,128]{1,0:T(8,128)(2,1)} collective-permute-done((s16[1088,128]{1,0:T(8,128)(2,1)}, s16[1088,128]{1,0:T(8,128)(2,1)}, u32[]{:S(2)}, u32[]{:S(2)}) %collective-permute-start.11) | collective-permute-done | bytes 278560 | tf_op jit(solution)/shard_map/ppermute | solution.py:32
  102.6 3.4 %collective-permute-start.19 = (s16[1088,128]{1,0:T(8,128)(2,1)}, s16[1088,128]{1,0:T(8,128)(2,1)}, u32[]{:S(2)}, u32[]{:S(2)}) collective-permute-start(s16[1088,128]{1,0:T(8,128)(2,1)} %get-tuple-element.78), channel_id=1, source_target_pairs={{0,192},{64,0},{128,64},{192,128},{1,193},{65,1},{129,65},{193,129... | collective-permute-start | bytes 835592 | tf_op jit(solution)/shard_map/ppermute | solution.py:32
  106.0 9.0 %shard_map.42 = (f32[1056,128]{1,0:T(8,128)}, s16[1088,128]{1,0:T(8,128)(2,1)}, s16[1088,128]{1,0:T(8,128)(2,1)}, s16[1088,128]{1,0:T(8,128)(2,1)}) custom-call(s32[16]{0:T(128)} %reshape.142.slot_ref, s32[4]{0:T(128)} %and_select_fusion.dest_ref, s32[2]{0:T(128)} %get-tuple-element.82.mate_ref, bf16[1024,2048]{1,0:T(8,128)(2,1)} %get-tuple-element.44.at_ref, ...), custom_call_target="tpu_custom_call" | custom-call | flops 4294967296 | bytes 10485760 | tf_op jit(solution)/shard_map/pallas_call | solution.py:322
  115.1 4.1 %collective-permute-start.16 = (s16[1088,128]{1,0:T(8,128)(2,1)}, s16[1088,128]{1,0:T(8,128)(2,1)}, u32[]{:S(2)}, u32[]{:S(2)}) collective-permute-start(s16[1088,128]{1,0:T(8,128)(2,1)} %get-tuple-element.73), channel_id=1, source_target_pairs={{0,128},{64,192},{128,0},{192,64},{1,129},{65,193},{129,1},{193,65... | collective-permute-start | bytes 835592 | tf_op jit(solution)/shard_map/ppermute | solution.py:32
  119.2 0.6 reshape.143.taper_ref
  120.1 0.7 add.125.place_ref
  121.2 1.0 copy-done
  122.3 4.7 %shard_map.43.refs_3_ = f32[2048,256]{1,0:T(8,128)} custom-call(s32[32]{0:T(128)} %add.125.place_ref, s32[16]{0:T(128)} %reshape.142.slot_ref, s32[4]{0:T(128)} %and_select_fusion.dest_ref, f32[32]{0:T(128)} %reshape.143.taper_ref, f32[1056,256]{1,0:T(8,128)} %copy-done, f32[1056,128]{1,0:T(8,128)} %get-tuple-element.75.kept_ref, ...), custom_call_target="tpu_custom_call" | custom-call | flops 1048576 | bytes 4194304 | tf_op jit(solution)/shard_map/pallas_call | solution.py:389
  127.0 3.9 %shard_map.44 = f32[2048,256]{1,0:T(8,128)} custom-call(s32[32]{0:T(128)S(1)} %copy-done.6, s32[16]{0:T(128)S(1)} %copy-done.4, s32[4]{0:T(128)S(1)} %copy-done.7, f32[32]{0:T(128)S(1)} %copy-done.5, f32[1056,256]{1,0:T(8,128)S(1)} %copy-done.1, f32[1056,128]{1,0:T(8,128)S(1)} %copy-done.3, ...), custom_call_target="tpu_custom_call", output_to_operand_aliasing={{}: (9, {})} | custom-call | flops 1048576 | bytes 4194304 | tf_op jit(solution)/shard_map/pallas_call | solution.py:389
  (66 shorter events, 2.8 us)
Async XLA Ops:
  0.0 32.6 %collective-permute-start.3 = (bf16[2048,1024]{1,0:T(8,128)(2,1)}, bf16[2048,1024]{1,0:T(8,128)(2,1)}, u32[]{:S(2)}, u32[]{:S(2)}) collective-permute-start(bf16[2048,1024]{1,0:T(8,128)(2,1)} %source_ref.3), channel_id=1, source_target_pairs={{0,1},{1,0},{2,3},{3,2},{4,5},{5,4},{6,7},{7,6},{8,9},{9,8},{10,11... | collective-permute-start | bytes 12582920 | tf_op jit(solution)/shard_map/ppermute | solution.py:46
  1.9 13.0 %collective-permute-start = (s32[2]{0:T(128)S(1)}, s32[2]{0:T(128)S(1)}, u32[]{:S(2)}, u32[]{:S(2)}) collective-permute-start(s32[2]{0:T(128)S(1)} %get-tuple-element.79), channel_id=1, source_target_pairs={{0,62},{1,63},{2,0},{3,1},{4,2},{5,3},{6,4},{7,5},{8,6},{9,7},{10,... | collective-permute-start | bytes 32 | tf_op jit(solution)/shard_map/ppermute | solution.py:46
  10.0 6.9 %collective-permute-start.2 = (s32[2]{0:T(128)S(1)}, s32[2]{0:T(128)S(1)}, u32[]{:S(2)}, u32[]{:S(2)}) collective-permute-start(s32[2]{0:T(128)S(1)} %get-tuple-element.80), channel_id=1, source_target_pairs={{0,2},{1,3},{2,4},{3,5},{4,6},{5,7},{6,8},{7,9},{8,10},{9,11},{10,... | collective-permute-start | bytes 32 | tf_op jit(solution)/shard_map/ppermute | solution.py:46
  10.0 6.9 %collective-permute-start.1 = (s32[2]{0:T(128)S(1)}, s32[2]{0:T(128)S(1)}, u32[]{:S(2)}, u32[]{:S(2)}) collective-permute-start(s32[2]{0:T(128)S(1)} %get-tuple-element.81), channel_id=1, source_target_pairs={{0,63},{1,2},{2,1},{3,4},{4,3},{5,6},{6,5},{7,8},{8,7},{9,10},{10,... | collective-permute-start | bytes 32 | tf_op jit(solution)/shard_map/ppermute | solution.py:46
  21.7 29.7 %collective-permute-start.4 = (bf16[2048,256]{1,0:T(8,128)(2,1)}, bf16[2048,256]{1,0:T(8,128)(2,1)S(1)}, u32[]{:S(2)}, u32[]{:S(2)}) collective-permute-start(bf16[2048,256]{1,0:T(8,128)(2,1)} %get-tuple-element.48), channel_id=1, source_target_pairs={{0,2},{1,3},{2,4},{3,5},{4,6},{5,7},{6,8},{7,9},{8,10},{9,11},{10,... | collective-permute-start | bytes 3145736 | tf_op jit(solution)/shard_map/ppermute | solution.py:46
  21.8 39.6 %collective-permute-start.5 = (bf16[2048,256]{1,0:T(8,128)(2,1)}, bf16[2048,256]{1,0:T(8,128)(2,1)}, u32[]{:S(2)}, u32[]{:S(2)}) collective-permute-start(bf16[2048,256]{1,0:T(8,128)(2,1)} %get-tuple-element.49), channel_id=1, source_target_pairs={{0,63},{1,2},{2,1},{3,4},{4,3},{5,6},{6,5},{7,8},{8,7},{9,10},{10,... | collective-permute-start | bytes 3145736 | tf_op jit(solution)/shard_map/ppermute | solution.py:46
  26.2 35.2 %collective-permute-start.6 = (bf16[2048,256]{1,0:T(8,128)(2,1)}, bf16[2048,256]{1,0:T(8,128)(2,1)}, u32[]{:S(2)}, u32[]{:S(2)}) collective-permute-start(bf16[2048,256]{1,0:T(8,128)(2,1)} %get-tuple-element.50), channel_id=1, source_target_pairs={{0,62},{1,63},{2,0},{3,1},{4,2},{5,3},{6,4},{7,5},{8,6},{9,7},{10,... | collective-permute-start | bytes 3145736 | tf_op jit(solution)/shard_map/ppermute | solution.py:46
  32.6 29.4 %copy-start.8 = (s32[4,8]{1,0:T(4,128)S(1)}, s32[4,8]{1,0:T(4,128)}, u32[]{:S(2)}) copy-start(s32[4,8]{1,0:T(4,128)} %param.4) | copy-start | bytes 388
  51.4 29.3 %copy-start.10 = (bf16[2048,256]{1,0:T(8,128)(2,1)}, bf16[2048,256]{1,0:T(8,128)(2,1)S(1)}, u32[]{:S(2)}) copy-start(bf16[2048,256]{1,0:T(8,128)(2,1)S(1)} %collective-permute-done.4.refs_0_) | copy-start | bytes 3145732
  61.4 17.7 %collective-permute-start.9 = (s16[1632,256]{1,0:T(8,128)(2,1)}, s16[1632,256]{1,0:T(8,128)(2,1)S(1)}, u32[]{:S(2)}, u32[]{:S(2)}) collective-permute-start(s16[1632,256]{1,0:T(8,128)(2,1)} %get-tuple-element.61), channel_id=1, source_target_pairs={{0,192},{64,0},{128,64},{192,128},{1,193},{65,1},{129,65},{193,129... | collective-permute-start | bytes 2506760 | tf_op jit(solution)/shard_map/ppermute | solution.py:32
  62.0 44.0 %collective-permute-start.12 = (bf16[2048,256]{1,0:T(8,128)(2,1)}, bf16[2048,256]{1,0:T(8,128)(2,1)}, u32[]{:S(2)}, u32[]{:S(2)}) collective-permute-start(bf16[2048,256]{1,0:T(8,128)(2,1)} %get-tuple-element.42), channel_id=1, source_target_pairs={{0,2},{1,3},{2,4},{3,5},{4,6},{5,7},{6,8},{7,9},{8,10},{9,11},{10,... | collective-permute-start | bytes 3145736 | tf_op jit(solution)/shard_map/ppermute | solution.py:46
  62.1 43.9 %collective-permute-start.13 = (bf16[2048,256]{1,0:T(8,128)(2,1)}, bf16[2048,256]{1,0:T(8,128)(2,1)}, u32[]{:S(2)}, u32[]{:S(2)}) collective-permute-start(bf16[2048,256]{1,0:T(8,128)(2,1)} %get-tuple-element.69), channel_id=1, source_target_pairs={{0,63},{1,2},{2,1},{3,4},{4,3},{5,6},{6,5},{7,8},{8,7},{9,10},{10,... | collective-permute-start | bytes 3145736 | tf_op jit(solution)/shard_map/ppermute | solution.py:46
  62.2 43.8 %collective-permute-start.14 = (bf16[2048,256]{1,0:T(8,128)(2,1)}, bf16[2048,256]{1,0:T(8,128)(2,1)}, u32[]{:S(2)}, u32[]{:S(2)}) collective-permute-start(bf16[2048,256]{1,0:T(8,128)(2,1)} %get-tuple-element.70), channel_id=1, source_target_pairs={{0,62},{1,63},{2,0},{3,1},{4,2},{5,3},{6,4},{7,5},{8,6},{9,7},{10,... | collective-permute-start | bytes 3145736 | tf_op jit(solution)/shard_map/ppermute | solution.py:46
  68.0 16.7 %collective-permute-start.8 = (s16[544,256]{1,0:T(8,128)(2,1)}, s16[544,256]{1,0:T(8,128)(2,1)S(1)}, u32[]{:S(2)}, u32[]{:S(2)}) collective-permute-start(s16[544,256]{1,0:T(8,128)(2,1)} %get-tuple-element.60), channel_id=1, source_target_pairs={{0,128},{64,192},{128,0},{192,64},{1,129},{65,193},{129,1},{193,65... | collective-permute-start | bytes 835592 | tf_op jit(solution)/shard_map/ppermute | solution.py:32
  79.1 14.7 %collective-permute-start.7 = (s16[1088,256]{1,0:T(8,128)(2,1)}, s16[1088,256]{1,0:T(8,128)(2,1)S(1)}, u32[]{:S(2)}, u32[]{:S(2)}) collective-permute-start(s16[1088,256]{1,0:T(8,128)(2,1)} %get-tuple-element.59), channel_id=1, source_target_pairs={{0,64},{64,128},{128,192},{192,0},{1,65},{65,129},{129,193},{193,1... | collective-permute-start | bytes 1671176 | tf_op jit(solution)/shard_map/ppermute | solution.py:32
  84.7 9.1 %collective-permute-start.10 = (s16[544,256]{1,0:T(8,128)(2,1)S(1)}, s16[544,256]{1,0:T(8,128)(2,1)S(1)}, u32[]{:S(2)}, u32[]{:S(2)}) collective-permute-start(s16[544,256]{1,0:T(8,128)(2,1)S(1)} %slice.21), channel_id=1, source_target_pairs={{0,192},{64,0},{128,64},{192,128},{1,193},{65,1},{129,65},{193,129... | collective-permute-start | bytes 835592 | tf_op jit(solution)/shard_map/ppermute | solution.py:32
  84.7 13.5 %copy-start.9 = (s32[4,8]{1,0:T(4,128)S(1)}, s32[4,8]{1,0:T(4,128)}, u32[]{:S(2)}) copy-start(s32[4,8]{1,0:T(4,128)} %param.5) | copy-start | bytes 388
  93.8 8.7 %collective-permute-start.11 = (s16[1088,128]{1,0:T(8,128)(2,1)}, s16[1088,128]{1,0:T(8,128)(2,1)}, u32[]{:S(2)}, u32[]{:S(2)}) collective-permute-start(s16[1088,128]{1,0:T(8,128)(2,1)} %get-tuple-element.62), channel_id=1, source_target_pairs={{0,64},{64,128},{128,192},{192,0},{1,65},{65,129},{129,193},{193,1... | collective-permute-start | bytes 835592 | tf_op jit(solution)/shard_map/ppermute | solution.py:32
  98.5 22.3 %copy-start.2 = (f32[1056,256]{1,0:T(8,128)S(1)}, f32[1056,256]{1,0:T(8,128)}, u32[]{:S(2)}) copy-start(f32[1056,256]{1,0:T(8,128)} %get-tuple-element.64.kept_ref) | copy-start | bytes 3244036
  98.5 23.7 %collective-permute-start.18 = (s16[1088,128]{1,0:T(8,128)(2,1)}, s16[1088,128]{1,0:T(8,128)(2,1)}, u32[]{:S(2)}, u32[]{:S(2)}) collective-permute-start(s16[1088,128]{1,0:T(8,128)(2,1)} %get-tuple-element.77), channel_id=1, source_target_pairs={{0,128},{64,192},{128,0},{192,64},{1,129},{65,193},{129,1},{193,65... | collective-permute-start | bytes 835592 | tf_op jit(solution)/shard_map/ppermute | solution.py:32
  102.6 19.7 %collective-permute-start.19 = (s16[1088,128]{1,0:T(8,128)(2,1)}, s16[1088,128]{1,0:T(8,128)(2,1)}, u32[]{:S(2)}, u32[]{:S(2)}) collective-permute-start(s16[1088,128]{1,0:T(8,128)(2,1)} %get-tuple-element.78), channel_id=1, source_target_pairs={{0,192},{64,0},{128,64},{192,128},{1,193},{65,1},{129,65},{193,129... | collective-permute-start | bytes 835592 | tf_op jit(solution)/shard_map/ppermute | solution.py:32
  115.0 12.0 %collective-permute-start.15 = (s16[1088,128]{1,0:T(8,128)(2,1)}, s16[1088,128]{1,0:T(8,128)(2,1)S(1)}, u32[]{:S(2)}, u32[]{:S(2)}) collective-permute-start(s16[1088,128]{1,0:T(8,128)(2,1)} %get-tuple-element.72), channel_id=1, source_target_pairs={{0,64},{64,128},{128,192},{192,0},{1,65},{65,129},{129,193},{193,1... | collective-permute-start | bytes 835592 | tf_op jit(solution)/shard_map/ppermute | solution.py:32
  115.1 11.9 %collective-permute-start.16 = (s16[1088,128]{1,0:T(8,128)(2,1)}, s16[1088,128]{1,0:T(8,128)(2,1)}, u32[]{:S(2)}, u32[]{:S(2)}) collective-permute-start(s16[1088,128]{1,0:T(8,128)(2,1)} %get-tuple-element.73), channel_id=1, source_target_pairs={{0,128},{64,192},{128,0},{192,64},{1,129},{65,193},{129,1},{193,65... | collective-permute-start | bytes 835592 | tf_op jit(solution)/shard_map/ppermute | solution.py:32
  119.2 7.8 %collective-permute-start.17 = (s16[1088,128]{1,0:T(8,128)(2,1)}, s16[1088,128]{1,0:T(8,128)(2,1)}, u32[]{:S(2)}, u32[]{:S(2)}) collective-permute-start(s16[1088,128]{1,0:T(8,128)(2,1)} %get-tuple-element.74), channel_id=1, source_target_pairs={{0,192},{64,0},{128,64},{192,128},{1,193},{65,1},{129,65},{193,129... | collective-permute-start | bytes 835592 | tf_op jit(solution)/shard_map/ppermute | solution.py:32
  121.2 1.0 copy-start
  122.2 4.8 %copy-start.3 = (f32[1056,128]{1,0:T(8,128)S(1)}, f32[1056,128]{1,0:T(8,128)}, u32[]{:S(2)}) copy-start(f32[1056,128]{1,0:T(8,128)} %get-tuple-element.71.kept_ref) | copy-start | bytes 1622020
  122.2 4.8 %copy-start.4 = (s32[16]{0:T(128)S(1)}, s32[16]{0:T(128)}, u32[]{:S(2)}) copy-start(s32[16]{0:T(128)} %reshape.142.slot_ref) | copy-start | bytes 196
  122.2 4.8 %copy-start.5 = (f32[32]{0:T(128)S(1)}, f32[32]{0:T(128)}, u32[]{:S(2)}) copy-start(f32[32]{0:T(128)} %reshape.143.taper_ref) | copy-start | bytes 388
  122.2 4.8 %copy-start.6 = (s32[32]{0:T(128)S(1)}, s32[32]{0:T(128)}, u32[]{:S(2)}) copy-start(s32[32]{0:T(128)} %add.125.place_ref) | copy-start | bytes 388
  122.2 4.8 %copy-start.7 = (s32[4]{0:T(128)S(1)}, s32[4]{0:T(128)}, u32[]{:S(2)}) copy-start(s32[4]{0:T(128)} %and_select_fusion.dest_ref) | copy-start | bytes 52
  122.2 4.8 %copy-start.1 = (f32[1056,256]{1,0:T(8,128)S(1)}, f32[1056,256]{1,0:T(8,128)}, u32[]{:S(2)}) copy-start(f32[1056,256]{1,0:T(8,128)} %copy-done) | copy-start | bytes 3244036
